TPU v7x, 32 devices: a whole 2x2x4 slice. The times are simulated.
32 devices in a mesh: row: 4 (over z), col: 8 (over y, x, core).
Axes of the slice: x: 2, y: 2, z: 4, core: 2. Of those that a mesh axis runs over, the one named last changes fastest.
Arguments:
- tangents: float32 [3, 256, 256, 128], P(None, 'row', 'col'), may hold values from -400 to 400
- sea_mask: int32 [256, 256], P('row', 'col'), may hold values 0 or 1
- levels: int32 [256, 256], P('row', 'col'), may hold values from 0 to 49
- current: float32 [256, 256], P('row', 'col'), may hold values from -0.6 to 0.6
Outputs:
- new_tangents: float32 [3, 256, 256, 128], P(None, 'row', 'col')
- growth: float32 [128], replicated
All inputs are finite; a program needn't handle non-finite values. No bound on the sum of `sea_mask` on one device may be relied on, other than what follows from the above.
Results may differ from a plain program's by a relative error of at most 0.00014.
Values sent between devices are 32-bit elements; how exact they have to be, the bound alone decides.
No kernel may reach another device: no remote copies, remote signals or barrier semaphores. Data moves between devices by JAX's collectives and lax.ppermute only.
A program may use at most 64 MiB of HBM per device.

v0:
```python
import functools

import jax
import jax.numpy as jnp
from jax import lax
from jax.experimental import pallas as pl
from jax.experimental.pallas import tpu as pltpu
from jax.sharding import PartitionSpec as P

STEPS = 2
RENORMS = 2
LEVELS = 50

viscosity = 0.15
gravity = 0.5
rotation = 0.4

SUB = 8
LANES = 128
FIELDS = 3
TILES = 8
VMEM_LIMIT = 16 * 1024 * 1024

HBM = pl.BlockSpec(memory_space=pltpu.HBM)
VMEM = pl.BlockSpec(memory_space=pltpu.VMEM)
SMEM = pl.BlockSpec(memory_space=pltpu.SMEM)


def params():
    return pltpu.CompilerParams(vmem_limit_bytes=VMEM_LIMIT)


def shape_of(*dims):
    return jax.ShapeDtypeStruct(dims, jnp.float32)


def lane_spread(block, lane):
    return jnp.broadcast_to(block[:, lane : lane + 1], (block.shape[0], LANES))


def spread_fields(sea_ref, levels_ref, current_ref, out_ref):
    rows = sea_ref.shape[1]
    fields = (
        sea_ref[...].astype(jnp.float32),
        0.5 * current_ref[...],
        0.5 * ((levels_ref[...] + 1).astype(jnp.float32) / LEVELS),
    )
    for field, value in enumerate(fields):
        for row in range(rows):
            out_ref[field, row] = lane_spread(value, row)


def sides_of(par):
    odd_row, odd_col = par[0] % 2, par[1] % 2
    return (1 - odd_row, odd_row), (1 - odd_col, odd_col)


def pack_first(par, t_ref, col_a, col_b, row_a, row_b, edges, sems):
    comps, rows, cols, _ = t_ref.shape
    norths, easts = sides_of(par)
    copies = []
    for slot in (0, 1):
        start = pl.multiple_of(easts[slot] * (cols - SUB), SUB)
        copies.append(
            pltpu.make_async_copy(t_ref.at[:, :, pl.ds(start, SUB), :], edges.at[slot], sems.at[slot])
        )
        copies[-1].start()
    for slot, msg in ((0, row_a), (1, row_b)):
        copies.append(
            pltpu.make_async_copy(t_ref.at[:, norths[slot] * (rows - 1)], msg, sems.at[2 + slot])
        )
        copies[-1].start()
    for slot, msg in ((0, col_a), (1, col_b)):
        copies[slot].wait()
        flat = edges.at[slot].reshape(comps * rows * SUB, LANES)
        for comp in range(comps):
            for row in range(0, rows, SUB):
                at = (comp * rows + row) * SUB + easts[slot] * (SUB - 1)
                msg[comp, pl.ds(row, SUB), :] = flat[pl.ds(at, SUB, stride=SUB), :]
    copies[2].wait()
    copies[3].wait()


def pack_edges(par, state, col_a, col_b, row_a, row_b):
    comps, rows, cols, _ = state.shape
    norths, easts = sides_of(par)
    flat = state.reshape(comps * rows * cols, LANES)
    for slot, msg in ((0, col_a), (1, col_b)):
        for comp in range(comps):
            for row in range(0, rows, SUB):
                at = (comp * rows + row) * cols + easts[slot] * (cols - 1)
                msg[comp, pl.ds(row, SUB), :] = flat[pl.ds(at, SUB, stride=cols), :]
    for slot, msg in ((0, row_a), (1, row_b)):
        for comp in range(comps):
            msg[comp] = state[comp, norths[slot] * (rows - 1)]


def apply_inside(t_ref, coef_ref, spin_ref, out_ref):
    comps, rows, cols, _ = t_ref.shape
    flat = t_ref.reshape(comps * rows * cols, LANES)
    sub = lax.broadcasted_iota(jnp.int32, (SUB, LANES), 0)
    zero = jnp.zeros((SUB, LANES), jnp.float32)
    keep, half = 1.0 - 4.0 * viscosity, 0.5 * gravity

    def line_of(line, south, north):
        spin = jnp.broadcast_to(spin_ref[pl.ds(line, 1), :], (SUB, LANES))
        for lon in range(0, cols, SUB):
            at = [(comp * rows + line) * cols + lon for comp in range(comps)]
            sea, flow, depth = (coef_ref[field, line, pl.ds(lon, SUB), :] for field in range(FIELDS))
            own = [t_ref[comp, line, pl.ds(lon, SUB), :] for comp in range(comps)]
            if lon == 0:
                west = [jnp.where(sub == 0, 0.0, pltpu.roll(x, 1, 0)) for x in own]
            else:
                west = [flat[pl.ds(a - 1, SUB), :] for a in at]
            if lon == cols - SUB:
                east = [jnp.where(sub == SUB - 1, 0.0, pltpu.roll(x, SUB - 1, 0)) for x in own]
            else:
                east = [flat[pl.ds(a + 1, SUB), :] for a in at]
            above = [
                t_ref[comp, line + 1, pl.ds(lon, SUB), :] if north else zero for comp in range(comps)
            ]
            below = [
                t_ref[comp, line - 1, pl.ds(lon, SUB), :] if south else zero for comp in range(comps)
            ]
            x_diff = [e - w for e, w in zip(east, west)]
            mixed = [
                keep * c + viscosity * ((e + w) + (n + s)) - flow * x
                for c, e, w, n, s, x in zip(own, east, west, above, below, x_diff)
            ]
            v_y, h_y = above[1] - below[1], above[2] - below[2]
            out_ref[0, line, pl.ds(lon, SUB), :] = sea * (mixed[0] - half * x_diff[2] + spin * own[1])
            out_ref[1, line, pl.ds(lon, SUB), :] = sea * (mixed[1] - half * h_y - spin * own[0])
            out_ref[2, line, pl.ds(lon, SUB), :] = sea * (mixed[2] - depth * (x_diff[0] + v_y))

    line_of(0, False, True)
    line_of(rows - 1, True, False)

    @pl.loop(0, (rows - 2) // 2)
    def _(pair):
        line_of(1 + 2 * pair, True, True)
        line_of(2 + 2 * pair, True, True)


def add_halos(par, state, coef_ref, col_a, col_b, row_a, row_b):
    comps, rows, cols, _ = state.shape
    norths, easts = sides_of(par)
    half = 0.5 * gravity
    flat = state.reshape(comps * rows * cols, LANES)
    flat_coef = coef_ref.reshape(FIELDS * rows * cols, LANES)
    for slot, halo in ((0, col_a), (1, col_b)):
        sign = (1 - 2 * easts[slot]).astype(jnp.float32)
        for row in range(0, rows, SUB):
            spots = [
                pl.ds((comp * rows + row) * cols + easts[slot] * (cols - 1), SUB, stride=cols)
                for comp in range(comps)
            ]
            sea, flow, depth = (flat_coef[spot, :] for spot in spots)
            u, v, h = (halo[comp, pl.ds(row, SUB), :] for comp in range(comps))
            mix = viscosity + sign * flow
            flat[spots[0], :] += sea * (mix * u + (sign * half) * h)
            flat[spots[1], :] += sea * (mix * v)
            flat[spots[2], :] += sea * (mix * h + (sign * depth) * u)
    for slot, halo in ((0, row_a), (1, row_b)):
        sign = (1 - 2 * norths[slot]).astype(jnp.float32)
        line = norths[slot] * (rows - 1)
        for lon in range(0, cols, SUB):
            cells = pl.ds(lon, SUB)
            sea, _, depth = (coef_ref[field, line, cells, :] for field in range(FIELDS))
            u, v, h = (halo[comp, cells, :] for comp in range(comps))
            state[0, line, cells, :] += sea * (viscosity * u)
            state[1, line, cells, :] += sea * (viscosity * v + (sign * half) * h)
            state[2, line, cells, :] += sea * (viscosity * h + (sign * depth) * v)


def join_step(par, state_in, coef_ref, a, b, c, d, state, col_a, col_b, row_a, row_b):
    add_halos(par, state, coef_ref, a, b, c, d)
    pack_edges(par, state, col_a, col_b, row_a, row_b)


def join_gram(
    scale, par, state_in, coef_ref, a, b, c, d, state, col_a, col_b, row_a, row_b, kept, sent, total
):
    add_halos(par, state, coef_ref, a, b, c, d)
    pack_edges(par, state, col_a, col_b, row_a, row_b)
    total[...] = jnp.zeros_like(total)
    flat = state.reshape(state.shape[0] * state.shape[1] * state.shape[2], LANES)
    height = flat.shape[0] // TILES

    @pl.loop(0, TILES)
    def _(tile):
        total[...] += gram_of(split_halves(flat[pl.ds(tile * height, height), :]))

    write_halves(par, total, scale, kept, sent)


def split_halves(value):
    high = value.astype(jnp.bfloat16)
    low = (value - high.astype(jnp.float32)).astype(jnp.bfloat16)
    return jnp.concatenate([high, low], axis=1)


def gram_of(pair):
    return lax.dot_general(pair, pair, (((0,), (0,)), ((), ())), preferred_element_type=jnp.float32)


def write_halves(par, total, scale, kept, sent):
    odd = par[1] % 2
    rows = LANES // 2
    for out, start in ((kept, odd * rows), (sent, (1 - odd) * rows)):
        top, low = pl.ds(start, rows), pl.ds(LANES + start, rows)
        out[...] = scale * (
            (total[top, :LANES] + total[low, LANES:]) + (total[top, LANES:] + total[low, :LANES])
        )


def invert_factor(gram_ref, work):
    count = LANES // SUB
    lane = lax.broadcasted_iota(jnp.int32, (SUB, LANES), 1)
    sub = lax.broadcasted_iota(jnp.int32, (SUB, LANES), 0)
    rows = [gram_ref[pl.ds(SUB * i, SUB), :] for i in range(count)]
    for block in range(count):
        base = SUB * block
        here = (lane >= base) & (lane < base + SUB)
        spread = [lane_spread(rows[block], base + l) for l in range(SUB)]
        low = [
            [jnp.broadcast_to(spread[l][k : k + 1, :], (SUB, LANES)) for l in range(k + 1)]
            for k in range(SUB)
        ]
        pivot = jnp.where(here, jnp.where(lane - base == sub, 1.0, 0.0), rows[block])
        inv, scaled = [], []
        for k in range(SUB):
            inv.append(lax.rsqrt(low[k][k]))
            for i in range(k + 1, SUB):
                low[i][k] = low[i][k] * inv[k]
            for i in range(k + 1, SUB):
                for m in range(k + 1, i + 1):
                    low[i][m] = low[i][m] - low[i][k] * low[m][k]
            line = jnp.broadcast_to(pivot[k : k + 1, :], (SUB, LANES))
            for l in range(k):
                line = line - low[k][l] * scaled[l]
            scaled.append(line * inv[k])
        merged = scaled[0]
        for k in range(1, SUB):
            merged = jnp.where(sub == k, scaled[k], merged)
        work[pl.ds(base, SUB), :] = merged
        for i in range(block + 1, count):
            weights = []
            rest = jnp.where(here, 0.0, rows[i])
            for l in range(SUB):
                weight = lane_spread(rows[i], base + l)
                for m in range(l):
                    weight = weight - weights[m] * low[l][m]
                weights.append(weight * inv[l])
            for l in range(SUB):
                rest = rest - weights[l] * scaled[l]
            rows[i] = rest


def factorize(par, mine_ref, other_ref, gram, work):
    rows = LANES // 2
    odd = par[1] % 2
    gram[pl.ds(odd * rows, rows), :] = mine_ref[...]
    gram[pl.ds((1 - odd) * rows, rows), :] = other_ref[...]
    invert_factor(gram, work)
    row = lax.broadcasted_iota(jnp.int32, (LANES, LANES), 0)
    col = lax.broadcasted_iota(jnp.int32, (LANES, LANES), 1)
    inverse = jnp.where(row >= col, work[...], 0.0)
    diagonal = jnp.sum(jnp.where(row == col, inverse, 0.0), axis=0, keepdims=True)
    return inverse, diagonal


def paired(inverse):
    high = inverse.astype(jnp.bfloat16)
    low = (inverse - high.astype(jnp.float32)).astype(jnp.bfloat16)
    return jnp.concatenate(
        [jnp.concatenate([high, high], axis=1), jnp.concatenate([low, low], axis=1)], axis=0
    )


def times_factor(cells, factor):
    both = lax.dot_general(
        split_halves(cells), factor, (((1,), (1,)), ((), ())), preferred_element_type=jnp.float32
    )
    return both[:, :LANES] + both[:, LANES:]


def factor_only(par, mine_ref, other_ref, prior_ref, inverse_ref, logs_ref, gram, work):
    inverse, diagonal = factorize(par, mine_ref, other_ref, gram, work)
    inverse_ref[...] = inverse
    logs_ref[...] = prior_ref[...] - jnp.log(diagonal)


def join_update(
    scale, par, state_in, coef_ref, a, b, c, d, inverse_ref, state, kept, sent, factor, total
):
    add_halos(par, state, coef_ref, a, b, c, d)
    factor[...] = paired(inverse_ref[...])
    total[...] = jnp.zeros_like(total)
    flat = state.reshape(state.shape[0] * state.shape[1] * state.shape[2], LANES)
    height = flat.shape[0] // TILES

    @pl.loop(0, TILES)
    def _(tile):
        cells = pl.ds(tile * height, height)
        new = times_factor(flat[cells, :], factor[...])
        flat[cells, :] = new
        total[...] += gram_of(split_halves(new))

    write_halves(par, total, scale, kept, sent)


def finish(par, mine_ref, other_ref, prior_ref, t_ref, out_ref, logs_ref, gram, work, factor, fresh, sems):
    inverse, diagonal = factorize(par, mine_ref, other_ref, gram, work)
    logs_ref[...] = prior_ref[...] - jnp.log(diagonal)
    factor[...] = paired(inverse)

    def out_copy(tile):
        return pltpu.make_async_copy(fresh.at[tile], out_ref.at[tile], sems.at[tile])

    @pl.loop(0, TILES)
    def _(tile):
        fresh[tile] = times_factor(t_ref[tile], factor[...])
        out_copy(tile).start()

    for tile in range(TILES):
        out_copy(tile).wait()


def swap_pairs(near_value, far_value, axis, closed):
    count = lax.axis_size(axis)
    near = [(i, i ^ 1) for i in range(count)]
    far = [(i, (i + 1 if i % 2 else i - 1) % count) for i in range(count)]
    if not closed:
        far = far[1:-1]
    return lax.ppermute(near_value, axis, near), lax.ppermute(far_value, axis, far)


def exchanged(messages):
    col_a, col_b, row_a, row_b = messages
    return swap_pairs(col_a, col_b, "col", True) + swap_pairs(row_a, row_b, "row", False)


def swapped(value, axis, mask):
    return lax.ppermute(value, axis, [(i, i ^ mask) for i in range(lax.axis_size(axis))])


def sum_over(value, axis, first_bit):
    bits = lax.axis_size(axis).bit_length() - 1
    while first_bit < bits:
        low = 1 << first_bit
        if first_bit + 1 < bits:
            high = low << 1
            one, two, three = (swapped(value, axis, mask) for mask in (low, high, low | high))
            value = (value + one) + (two + three)
            first_bit += 2
        else:
            value = value + swapped(value, axis, low)
            first_bit += 1
    return value


def sum_devices(kept, sent):
    mine = kept + swapped(sent, "col", 1)
    mine = sum_over(mine, "col", 1)
    mine = sum_over(mine, "row", 0)
    return mine, swapped(mine, "col", 1)


def body(tangents, sea_mask, levels, current):
    comps, rows, cols, modes = tangents.shape
    total_rows = rows * lax.axis_size("row")
    total_cells = total_rows * cols * lax.axis_size("col")
    scale = 1.0 / total_cells
    row_at, col_at = lax.axis_index("row"), lax.axis_index("col")
    par = jnp.stack([row_at, col_at]).astype(jnp.int32)

    lat = (row_at * rows + jnp.arange(rows)).astype(jnp.float32)
    angle = (-70.0 + 140.0 * (lat + 0.5) / total_rows) * (jnp.pi / 180.0)
    spin = jnp.broadcast_to((rotation * jnp.sin(angle))[:, None], (rows, LANES))

    block = shape_of(comps, rows, cols, modes)
    messages = (shape_of(comps, rows, modes),) * 2 + (shape_of(comps, cols, modes),) * 2
    halves = (shape_of(modes // 2, modes),) * 2
    square = pltpu.VMEM((modes, modes), jnp.float32)
    factor = pltpu.VMEM((2 * modes, 2 * modes), jnp.bfloat16)
    total = pltpu.VMEM((2 * modes, 2 * modes), jnp.float32)

    def call(kernel, outs, *operands, specs=None, out_specs=None, scratch=(), aliases=None):
        return pl.pallas_call(
            kernel,
            out_shape=outs,
            in_specs=specs or [SMEM] + [VMEM] * (len(operands) - 1),
            out_specs=out_specs or (VMEM,) * len(outs),
            scratch_shapes=scratch,
            input_output_aliases=aliases or {},
            compiler_params=params(),
        )(*operands)

    coef = call(
        spread_fields,
        (shape_of(FIELDS, rows, cols, LANES),),
        sea_mask.T,
        levels.T,
        current.T,
        specs=[VMEM] * 3,
    )[0]

    def inside(state):
        return call(apply_inside, (block,), state, coef, spin, specs=[VMEM] * 3)[0]

    packed = call(
        pack_first,
        messages,
        par,
        tangents,
        specs=[SMEM, HBM],
        scratch=[
            pltpu.VMEM((2, comps, rows, SUB, modes), jnp.float32),
            pltpu.SemaphoreType.DMA((4,)),
        ],
    )
    halos = exchanged(packed)
    state, *packed = call(
        join_step, (block,) + messages, par, inside(tangents), coef, *halos, aliases={1: 0}
    )
    halos = exchanged(packed)
    state, *packed, kept, sent = call(
        functools.partial(join_gram, scale),
        (block,) + messages + halves,
        par,
        inside(state),
        coef,
        *halos,
        scratch=[total],
        aliases={1: 0},
    )
    halos = exchanged(packed)
    mine, other = sum_devices(kept, sent)
    state, *packed = call(
        join_step, (block,) + messages, par, inside(state), coef, *halos, aliases={1: 0}
    )
    halos = exchanged(packed)
    logs = jnp.zeros((1, modes), jnp.float32)
    inverse, logs = call(
        factor_only,
        (shape_of(modes, modes), shape_of(1, modes)),
        par,
        mine,
        other,
        logs,
        scratch=[square, square],
    )
    state, kept, sent = call(
        functools.partial(join_update, scale),
        (block,) + halves,
        par,
        inside(state),
        coef,
        *halos,
        inverse,
        scratch=[factor, total],
        aliases={1: 0},
    )
    mine, other = sum_devices(kept, sent)
    height = comps * rows * cols // TILES
    tiled = shape_of(TILES, height, modes)
    out, logs = call(
        finish,
        (tiled, shape_of(1, modes)),
        par,
        mine,
        other,
        logs,
        state.reshape(TILES, height, modes),
        out_specs=(HBM, VMEM),
        scratch=[
            square,
            square,
            factor,
            pltpu.VMEM((TILES, height, modes), jnp.float32),
            pltpu.SemaphoreType.DMA((TILES,)),
        ],
    )
    return out.reshape(tangents.shape), logs.reshape(modes)


def solution(mesh):
    placed = (P(None, "row", "col", None), P("row", "col"), P("row", "col"), P("row", "col"))
    return jax.shard_map(
        body,
        mesh=mesh,
        in_specs=placed,
        out_specs=(P(None, "row", "col", None), P()),
        check_vma=False,
    )
```

profile of v0, /device:TPU:0, one launch (start us, length us, event | category | flops | bytes accessed | tf_op | source)
XLA Modules:
  0.0 89.3 jit_solution(3700388047554341264)
XLA Ops:
  0.7 1.9 %copy-done = f32[3,64,32,128]{3,2,1,0:T(8,128)S(1)} copy-done((f32[3,64,32,128]{3,2,1,0:T(8,128)S(1)}, f32[3,64,32,128]{3,2,1,0:T(8,128)}, u32[]{:S(2)}) %copy-start) | copy-done | bytes 3145752
  2.6 1.6 %shard_map.61 = (f32[3,64,128]{2,1,0:T(8,128)}, f32[3,64,128]{2,1,0:T(8,128)}, f32[3,32,128]{2,1,0:T(8,128)}, f32[3,32,128]{2,1,0:T(8,128)S(1)}) custom-call(s32[2]{0:T(128)S(1)} %pad_add_fusion.par, f32[3,64,32,128]{3,2,1,0:T(8,128)S(1)} %copy-done), custom_call_target="tpu_custom_call" | custom-call | tf_op jit(solution)/shard_map/pallas_call | solution.py:389
  4.7 3.6 %collective-permute-start.1 = (f32[3,64,128]{2,1,0:T(8,128)}, f32[3,64,128]{2,1,0:T(8,128)S(1)}, u32[]{:S(2)}, u32[]{:S(2)}) collective-permute-start(f32[3,64,128]{2,1,0:T(8,128)} %get-tuple-element.31), channel_id=1, source_target_pairs={{0,7},{1,2},{2,1},{3,4},{4,3},{5,6},{6,5},{7,0},{8,15},{9,10},{10,... | collective-permute-start | bytes 294920 | tf_op jit(solution)/shard_map/ppermute | solution.py:335
  8.3 1.6 %collective-permute-start.2 = (f32[3,32,128]{2,1,0:T(8,128)}, f32[3,32,128]{2,1,0:T(8,128)S(1)}, u32[]{:S(2)}, u32[]{:S(2)}) collective-permute-start(f32[3,32,128]{2,1,0:T(8,128)} %get-tuple-element.32), channel_id=1, source_target_pairs={{0,8},{8,0},{16,24},{24,16},{1,9},{9,1},{17,25},{25,17},{2,10},{10... | collective-permute-start | bytes 147464 | tf_op jit(solution)/shard_map/ppermute | solution.py:335
  11.3 1.2 %shard_map.59.coef_ref = f32[3,64,32,128]{3,2,1,0:T(8,128)S(1)} custom-call(s32[32,64]{1,0:T(8,128)S(1)} %bitcast.9, s32[32,64]{1,0:T(8,128)S(1)} %bitcast.10, f32[32,64]{1,0:T(8,128)S(1)} %bitcast.11), custom_call_target="tpu_custom_call" | custom-call | tf_op jit(solution)/shard_map/pallas_call | solution.py:389
  12.6 1.8 %shard_map.60.state_in = f32[3,64,32,128]{3,2,1,0:T(8,128)S(1)} custom-call(f32[3,64,32,128]{3,2,1,0:T(8,128)S(1)} %copy-done.1, f32[3,64,32,128]{3,2,1,0:T(8,128)S(1)} %shard_map.59.coef_ref, f32[64,128]{1,0:T(8,128)S(1)} %broadcast_in_dim.4.spin_ref), custom_call_target="tpu_custom_call" | custom-call | tf_op jit(solution)/shard_map/pallas_call | solution.py:389
  14.4 1.2 %shard_map.62 = (f32[3,64,32,128]{3,2,1,0:T(8,128)S(1)}, f32[3,64,128]{2,1,0:T(8,128)S(1)}, f32[3,64,128]{2,1,0:T(8,128)S(1)}, f32[3,32,128]{2,1,0:T(8,128)S(1)}, f32[3,32,128]{2,1,0:T(8,128)S(1)}) custom-call(s32[2]{0:T(128)S(1)} %pad_add_fusion.par, f32[3,64,32,128]{3,2,1,0:T(8,128)S(1)} %shard_map.60.state_in, ...), custom_call_target="tpu_custom_call", output_to_operand_aliasing={{0}: (1, {})} | custom-call | tf_op jit(solution)/shard_map/pallas_call | solution.py:389
  16.4 4.4 %collective-permute-start.6 = (f32[3,32,128]{2,1,0:T(8,128)S(1)}, f32[3,32,128]{2,1,0:T(8,128)S(1)}, u32[]{:S(2)}, u32[]{:S(2)}) collective-permute-start(f32[3,32,128]{2,1,0:T(8,128)S(1)} %get-tuple-element.37), channel_id=1, source_target_pairs={{0,8},{8,0},{16,24},{24,16},{1,9},{9,1},{17,25},{25,17},{2,10},{10... | collective-permute-start | bytes 147464 | tf_op jit(solution)/shard_map/ppermute | solution.py:335
  21.4 1.8 %shard_map.63.state_in = f32[3,64,32,128]{3,2,1,0:T(8,128)S(1)} custom-call(f32[3,64,32,128]{3,2,1,0:T(8,128)S(1)} %get-tuple-element.34.t_ref, f32[3,64,32,128]{3,2,1,0:T(8,128)S(1)} %shard_map.59.coef_ref, f32[64,128]{1,0:T(8,128)S(1)} %broadcast_in_dim.4.spin_ref), custom_call_target="tpu_custom_call" | custom-call | tf_op jit(solution)/shard_map/pallas_call | solution.py:389
  23.3 3.7 %shard_map.64 = (f32[3,64,32,128]{3,2,1,0:T(8,128)S(1)}, f32[3,64,128]{2,1,0:T(8,128)S(1)}, f32[3,64,128]{2,1,0:T(8,128)S(1)}, f32[3,32,128]{2,1,0:T(8,128)S(1)}...) custom-call(s32[2]{0:T(128)S(1)} %pad_add_fusion.par, ...), custom_call_target="tpu_custom_call", output_to_operand_aliasing={{0}: (1, {})} | custom-call | tf_op jit(solution)/shard_map/pallas_call | solution.py:389
  27.1 1.2 %collective-permute-done.16 = f32[64,128]{1,0:T(8,128)S(1)} collective-permute-done((f32[64,128]{1,0:T(8,128)S(1)}, f32[64,128]{1,0:T(8,128)S(1)}, u32[]{:S(2)}, u32[]{:S(2)}) %collective-permute-start.16) | collective-permute-done | bytes 32800 | tf_op jit(solution)/shard_map/ppermute | solution.py:344
  28.8 2.4 %collective-permute-start.19 = (f32[64,128]{1,0:T(8,128)S(1)}, f32[64,128]{1,0:T(8,128)S(1)}, u32[]{:S(2)}, u32[]{:S(2)}) collective-permute-start(f32[64,128]{1,0:T(8,128)S(1)} %add.78), channel_id=1, source_target_pairs={{0,6},{1,7},{2,4},{3,5},{4,2},{5,3},{6,0},{7,1},{8,14},{9,15},{10,... | collective-permute-start | bytes 98312 | tf_op jit(solution)/shard_map/ppermute | solution.py:344
  31.8 2.0 %collective-permute-start.9 = (f32[3,64,128]{2,1,0:T(8,128)S(1)}, f32[3,64,128]{2,1,0:T(8,128)S(1)}, u32[]{:S(2)}, u32[]{:S(2)}) collective-permute-start(f32[3,64,128]{2,1,0:T(8,128)S(1)} %get-tuple-element.41), channel_id=1, source_target_pairs={{0,7},{1,2},{2,1},{3,4},{4,3},{5,6},{6,5},{7,0},{8,15},{9,10},{10,... | collective-permute-start | bytes 294920 | tf_op jit(solution)/shard_map/ppermute | solution.py:335
  33.7 3.5 %collective-permute-start.10 = (f32[3,32,128]{2,1,0:T(8,128)S(1)}, f32[3,32,128]{2,1,0:T(8,128)S(1)}, u32[]{:S(2)}, u32[]{:S(2)}) collective-permute-start(f32[3,32,128]{2,1,0:T(8,128)S(1)} %get-tuple-element.42), channel_id=1, source_target_pairs={{0,8},{8,0},{16,24},{24,16},{1,9},{9,1},{17,25},{25,17},{2,10},{10... | collective-permute-start | bytes 147464 | tf_op jit(solution)/shard_map/ppermute | solution.py:335
  37.9 2.8 %collective-permute-start.21 = (f32[64,128]{1,0:T(8,128)S(1)}, f32[64,128]{1,0:T(8,128)S(1)}, u32[]{:S(2)}, u32[]{:S(2)}) collective-permute-start(f32[64,128]{1,0:T(8,128)S(1)} %add_add_fusion.3), channel_id=1, source_target_pairs={{0,16},{8,24},{16,0},{24,8},{1,17},{9,25},{17,1},{25,9},{2,18},{10... | collective-permute-start | bytes 98312 | tf_op jit(solution)/shard_map/ppermute | solution.py:344
  40.7 1.4 %collective-permute-start.22 = (f32[64,128]{1,0:T(8,128)S(1)}, f32[64,128]{1,0:T(8,128)S(1)}, u32[]{:S(2)}, u32[]{:S(2)}) collective-permute-start(f32[64,128]{1,0:T(8,128)S(1)} %add_add_fusion.3), channel_id=1, source_target_pairs={{0,24},{8,16},{16,8},{24,0},{1,25},{9,17},{17,9},{25,1},{2,26},{10... | collective-permute-start | bytes 98312 | tf_op jit(solution)/shard_map/ppermute | solution.py:344
  42.1 1.5 %collective-permute-start.20 = (f32[64,128]{1,0:T(8,128)S(1)}, f32[64,128]{1,0:T(8,128)S(1)}, u32[]{:S(2)}, u32[]{:S(2)}) collective-permute-start(f32[64,128]{1,0:T(8,128)S(1)} %add_add_fusion.3), channel_id=1, source_target_pairs={{0,8},{8,0},{16,24},{24,16},{1,9},{9,1},{17,25},{25,17},{2,10},{10... | collective-permute-start | bytes 98312 | tf_op jit(solution)/shard_map/ppermute | solution.py:344
  43.6 1.8 %shard_map.65.state_in = f32[3,64,32,128]{3,2,1,0:T(8,128)S(1)} custom-call(f32[3,64,32,128]{3,2,1,0:T(8,128)S(1)} %get-tuple-element.39.t_ref, f32[3,64,32,128]{3,2,1,0:T(8,128)S(1)} %shard_map.59.coef_ref, f32[64,128]{1,0:T(8,128)S(1)} %broadcast_in_dim.4.spin_ref), custom_call_target="tpu_custom_call" | custom-call | tf_op jit(solution)/shard_map/pallas_call | solution.py:389
  45.4 1.2 %shard_map.66 = (f32[3,64,32,128]{3,2,1,0:T(8,128)S(1)}, f32[3,64,128]{2,1,0:T(8,128)S(1)}, f32[3,64,128]{2,1,0:T(8,128)S(1)}, f32[3,32,128]{2,1,0:T(8,128)S(1)}, f32[3,32,128]{2,1,0:T(8,128)S(1)}) custom-call(s32[2]{0:T(128)S(1)} %pad_add_fusion.par, f32[3,64,32,128]{3,2,1,0:T(8,128)S(1)} %shard_map.65.state_in, ...), custom_call_target="tpu_custom_call", output_to_operand_aliasing={{0}: (1, {})} | custom-call | tf_op jit(solution)/shard_map/pallas_call | solution.py:389
  46.7 2.0 %collective-permute-start.13 = (f32[3,64,128]{2,1,0:T(8,128)S(1)}, f32[3,64,128]{2,1,0:T(8,128)S(1)}, u32[]{:S(2)}, u32[]{:S(2)}) collective-permute-start(f32[3,64,128]{2,1,0:T(8,128)S(1)} %get-tuple-element.46), channel_id=1, source_target_pairs={{0,7},{1,2},{2,1},{3,4},{4,3},{5,6},{6,5},{7,0},{8,15},{9,10},{10,... | collective-permute-start | bytes 294920 | tf_op jit(solution)/shard_map/ppermute | solution.py:335
  50.3 1.8 %shard_map.67.state_in = f32[3,64,32,128]{3,2,1,0:T(8,128)S(1)} custom-call(f32[3,64,32,128]{3,2,1,0:T(8,128)S(1)} %get-tuple-element.44.t_ref, f32[3,64,32,128]{3,2,1,0:T(8,128)S(1)} %shard_map.59.coef_ref, f32[64,128]{1,0:T(8,128)S(1)} %broadcast_in_dim.4.spin_ref), custom_call_target="tpu_custom_call" | custom-call | tf_op jit(solution)/shard_map/pallas_call | solution.py:389
  52.1 4.4 %shard_map.68 = (f32[128,128]{1,0:T(8,128)S(1)}, f32[1,128]{1,0:T(1,128)S(1)}) custom-call(s32[2]{0:T(128)S(1)} %pad_add_fusion.par, f32[64,128]{1,0:T(8,128)S(1)} %add_add_fusion.2.mine_ref, f32[64,128]{1,0:T(8,128)S(1)} %collective-permute-done.23.other_ref, f32[1,128]{1,0:T(1,128)S(1)} %broadcast_in_dim.10.prior_ref), custom_call_target="tpu_custom_call" | custom-call | tf_op jit(solution)/shard_map/pallas_call | solution.py:389
  56.5 5.9 %shard_map.69 = (f32[3,64,32,128]{3,2,1,0:T(8,128)S(1)}, f32[64,128]{1,0:T(8,128)S(1)}, f32[64,128]{1,0:T(8,128)S(1)}) custom-call(s32[2]{0:T(128)S(1)} %pad_add_fusion.par, f32[3,64,32,128]{3,2,1,0:T(8,128)S(1)} %shard_map.67.state_in, f32[3,64,32,128]{3,2,1,0:T(8,128)S(1)} %shard_map.59.coef_ref, ...), custom_call_target="tpu_custom_call", output_to_operand_aliasing={{0}: (1, {})} | custom-call | tf_op jit(solution)/shard_map/pallas_call | solution.py:389
  63.9 0.9 collective-permute-start.26
  64.8 1.0 %collective-permute-start.27 = (f32[64,128]{1,0:T(8,128)S(1)}, f32[64,128]{1,0:T(8,128)S(1)}, u32[]{:S(2)}, u32[]{:S(2)}) collective-permute-start(f32[64,128]{1,0:T(8,128)S(1)} %add.85), channel_id=1, source_target_pairs={{0,6},{1,7},{2,4},{3,5},{4,2},{5,3},{6,0},{7,1},{8,14},{9,15},{10,... | collective-permute-start | bytes 98312 | tf_op jit(solution)/shard_map/ppermute | solution.py:344
  65.8 1.6 %collective-permute-start.25 = (f32[64,128]{1,0:T(8,128)S(1)}, f32[64,128]{1,0:T(8,128)S(1)}, u32[]{:S(2)}, u32[]{:S(2)}) collective-permute-start(f32[64,128]{1,0:T(8,128)S(1)} %add.85), channel_id=1, source_target_pairs={{0,2},{1,3},{2,0},{3,1},{4,6},{5,7},{6,4},{7,5},{8,10},{9,11},{10,... | collective-permute-start | bytes 98312 | tf_op jit(solution)/shard_map/ppermute | solution.py:344
  67.8 1.8 %collective-permute-done.27 = f32[64,128]{1,0:T(8,128)S(1)} collective-permute-done((f32[64,128]{1,0:T(8,128)S(1)}, f32[64,128]{1,0:T(8,128)S(1)}, u32[]{:S(2)}, u32[]{:S(2)}) %collective-permute-start.27) | collective-permute-done | bytes 32800 | tf_op jit(solution)/shard_map/ppermute | solution.py:344
  69.7 4.2 %collective-permute-start.29 = (f32[64,128]{1,0:T(8,128)S(1)}, f32[64,128]{1,0:T(8,128)S(1)}, u32[]{:S(2)}, u32[]{:S(2)}) collective-permute-start(f32[64,128]{1,0:T(8,128)S(1)} %add_add_fusion.1), channel_id=1, source_target_pairs={{0,16},{8,24},{16,0},{24,8},{1,17},{9,25},{17,1},{25,9},{2,18},{10... | collective-permute-start | bytes 98312 | tf_op jit(solution)/shard_map/ppermute | solution.py:344
  73.9 1.4 %collective-permute-start.30 = (f32[64,128]{1,0:T(8,128)S(1)}, f32[64,128]{1,0:T(8,128)S(1)}, u32[]{:S(2)}, u32[]{:S(2)}) collective-permute-start(f32[64,128]{1,0:T(8,128)S(1)} %add_add_fusion.1), channel_id=1, source_target_pairs={{0,24},{8,16},{16,8},{24,0},{1,25},{9,17},{17,9},{25,1},{2,26},{10... | collective-permute-start | bytes 98312 | tf_op jit(solution)/shard_map/ppermute | solution.py:344
  75.8 3.8 %collective-permute-done.30 = f32[64,128]{1,0:T(8,128)S(1)} collective-permute-done((f32[64,128]{1,0:T(8,128)S(1)}, f32[64,128]{1,0:T(8,128)S(1)}, u32[]{:S(2)}, u32[]{:S(2)}) %collective-permute-start.30) | collective-permute-done | bytes 32800 | tf_op jit(solution)/shard_map/ppermute | solution.py:344
  79.7 1.2 %collective-permute-done.31.other_ref = f32[64,128]{1,0:T(8,128)S(1)} collective-permute-done((f32[64,128]{1,0:T(8,128)S(1)}, f32[64,128]{1,0:T(8,128)S(1)}, u32[]{:S(2)}, u32[]{:S(2)}) %collective-permute-start.31) | collective-permute-done | bytes 32800 | tf_op jit(solution)/shard_map/ppermute | solution.py:344
  80.9 8.2 %shard_map.70 = (f32[8,768,128]{2,1,0:T(8,128)}, f32[1,128]{1,0:T(1,128)}) custom-call(s32[2]{0:T(128)S(1)} %pad_add_fusion.par, f32[64,128]{1,0:T(8,128)S(1)} %add_add_fusion.mine_ref, f32[64,128]{1,0:T(8,128)S(1)} %collective-permute-done.31.other_ref, f32[1,128]{1,0:T(1,128)S(1)} %get-tuple-element.54.prior_ref, f32[8,768,128]{2,1,0:T(8,128)S(1)} %bitcast.8), custom_call_target="tpu_custom_call" | custom-call | tf_op jit(solution)/shard_map/pallas_call | solution.py:389
  (64 shorter events, 9.5 us)
Async XLA Ops:
  4.2 10.2 %collective-permute-start = (f32[3,64,128]{2,1,0:T(8,128)}, f32[3,64,128]{2,1,0:T(8,128)S(1)}, u32[]{:S(2)}, u32[]{:S(2)}) collective-permute-start(f32[3,64,128]{2,1,0:T(8,128)} %get-tuple-element.30), channel_id=1, source_target_pairs={{0,1},{1,0},{2,3},{3,2},{4,5},{5,4},{6,7},{7,6},{8,9},{9,8},{10,11... | collective-permute-start | bytes 294920 | tf_op jit(solution)/shard_map/ppermute | solution.py:335
  4.7 9.7 %collective-permute-start.1 = (f32[3,64,128]{2,1,0:T(8,128)}, f32[3,64,128]{2,1,0:T(8,128)S(1)}, u32[]{:S(2)}, u32[]{:S(2)}) collective-permute-start(f32[3,64,128]{2,1,0:T(8,128)} %get-tuple-element.31), channel_id=1, source_target_pairs={{0,7},{1,2},{2,1},{3,4},{4,3},{5,6},{6,5},{7,0},{8,15},{9,10},{10,... | collective-permute-start | bytes 294920 | tf_op jit(solution)/shard_map/ppermute | solution.py:335
  8.3 6.1 %collective-permute-start.2 = (f32[3,32,128]{2,1,0:T(8,128)}, f32[3,32,128]{2,1,0:T(8,128)S(1)}, u32[]{:S(2)}, u32[]{:S(2)}) collective-permute-start(f32[3,32,128]{2,1,0:T(8,128)} %get-tuple-element.32), channel_id=1, source_target_pairs={{0,8},{8,0},{16,24},{24,16},{1,9},{9,1},{17,25},{25,17},{2,10},{10... | collective-permute-start | bytes 147464 | tf_op jit(solution)/shard_map/ppermute | solution.py:335
  9.9 4.5 %collective-permute-start.3 = (f32[3,32,128]{2,1,0:T(8,128)S(1)}, f32[3,32,128]{2,1,0:T(8,128)S(1)}, u32[]{:S(2)}, u32[]{:S(2)}) collective-permute-start(f32[3,32,128]{2,1,0:T(8,128)S(1)} %get-tuple-element.33), channel_id=1, source_target_pairs={{8,16},{16,8},{9,17},{17,9},{10,18},{18,10},{11,19},{19,11},{12,20... | collective-permute-start | bytes 147464 | tf_op jit(solution)/shard_map/ppermute | solution.py:335
  15.6 7.6 %collective-permute-start.4 = (f32[3,64,128]{2,1,0:T(8,128)S(1)}, f32[3,64,128]{2,1,0:T(8,128)S(1)}, u32[]{:S(2)}, u32[]{:S(2)}) collective-permute-start(f32[3,64,128]{2,1,0:T(8,128)S(1)} %get-tuple-element.35), channel_id=1, source_target_pairs={{0,1},{1,0},{2,3},{3,2},{4,5},{5,4},{6,7},{7,6},{8,9},{9,8},{10,11... | collective-permute-start | bytes 294920 | tf_op jit(solution)/shard_map/ppermute | solution.py:335
  15.7 7.5 %collective-permute-start.5 = (f32[3,64,128]{2,1,0:T(8,128)S(1)}, f32[3,64,128]{2,1,0:T(8,128)S(1)}, u32[]{:S(2)}, u32[]{:S(2)}) collective-permute-start(f32[3,64,128]{2,1,0:T(8,128)S(1)} %get-tuple-element.36), channel_id=1, source_target_pairs={{0,7},{1,2},{2,1},{3,4},{4,3},{5,6},{6,5},{7,0},{8,15},{9,10},{10,... | collective-permute-start | bytes 294920 | tf_op jit(solution)/shard_map/ppermute | solution.py:335
  16.4 6.9 %collective-permute-start.6 = (f32[3,32,128]{2,1,0:T(8,128)S(1)}, f32[3,32,128]{2,1,0:T(8,128)S(1)}, u32[]{:S(2)}, u32[]{:S(2)}) collective-permute-start(f32[3,32,128]{2,1,0:T(8,128)S(1)} %get-tuple-element.37), channel_id=1, source_target_pairs={{0,8},{8,0},{16,24},{24,16},{1,9},{9,1},{17,25},{25,17},{2,10},{10... | collective-permute-start | bytes 147464 | tf_op jit(solution)/shard_map/ppermute | solution.py:335
  20.7 2.5 %collective-permute-start.7 = (f32[3,32,128]{2,1,0:T(8,128)S(1)}, f32[3,32,128]{2,1,0:T(8,128)S(1)}, u32[]{:S(2)}, u32[]{:S(2)}) collective-permute-start(f32[3,32,128]{2,1,0:T(8,128)S(1)} %get-tuple-element.38), channel_id=1, source_target_pairs={{8,16},{16,8},{9,17},{17,9},{10,18},{18,10},{11,19},{19,11},{12,20... | collective-permute-start | bytes 147464 | tf_op jit(solution)/shard_map/ppermute | solution.py:335
  27.0 1.3 %collective-permute-start.16 = (f32[64,128]{1,0:T(8,128)S(1)}, f32[64,128]{1,0:T(8,128)S(1)}, u32[]{:S(2)}, u32[]{:S(2)}) collective-permute-start(f32[64,128]{1,0:T(8,128)S(1)} %get-tuple-element.50), channel_id=1, source_target_pairs={{0,1},{1,0},{2,3},{3,2},{4,5},{5,4},{6,7},{7,6},{8,9},{9,8},{10,11... | collective-permute-start | bytes 98312 | tf_op jit(solution)/shard_map/ppermute | solution.py:344
  28.3 5.5 %collective-permute-start.18 = (f32[64,128]{1,0:T(8,128)S(1)}, f32[64,128]{1,0:T(8,128)S(1)}, u32[]{:S(2)}, u32[]{:S(2)}) collective-permute-start(f32[64,128]{1,0:T(8,128)S(1)} %add.78), channel_id=1, source_target_pairs={{0,4},{1,5},{2,6},{3,7},{4,0},{5,1},{6,2},{7,3},{8,12},{9,13},{10,... | collective-permute-start | bytes 98312 | tf_op jit(solution)/shard_map/ppermute | solution.py:344
  28.8 8.4 %collective-permute-start.19 = (f32[64,128]{1,0:T(8,128)S(1)}, f32[64,128]{1,0:T(8,128)S(1)}, u32[]{:S(2)}, u32[]{:S(2)}) collective-permute-start(f32[64,128]{1,0:T(8,128)S(1)} %add.78), channel_id=1, source_target_pairs={{0,6},{1,7},{2,4},{3,5},{4,2},{5,3},{6,0},{7,1},{8,14},{9,15},{10,... | collective-permute-start | bytes 98312 | tf_op jit(solution)/shard_map/ppermute | solution.py:344
  31.2 6.7 %collective-permute-start.17 = (f32[64,128]{1,0:T(8,128)S(1)}, f32[64,128]{1,0:T(8,128)S(1)}, u32[]{:S(2)}, u32[]{:S(2)}) collective-permute-start(f32[64,128]{1,0:T(8,128)S(1)} %add.78), channel_id=1, source_target_pairs={{0,2},{1,3},{2,0},{3,1},{4,6},{5,7},{6,4},{7,5},{8,10},{9,11},{10,... | collective-permute-start | bytes 98312 | tf_op jit(solution)/shard_map/ppermute | solution.py:344
  31.8 13.6 %collective-permute-start.8 = (f32[3,64,128]{2,1,0:T(8,128)S(1)}, f32[3,64,128]{2,1,0:T(8,128)S(1)}, u32[]{:S(2)}, u32[]{:S(2)}) collective-permute-start(f32[3,64,128]{2,1,0:T(8,128)S(1)} %get-tuple-element.40), channel_id=1, source_target_pairs={{0,1},{1,0},{2,3},{3,2},{4,5},{5,4},{6,7},{7,6},{8,9},{9,8},{10,11... | collective-permute-start | bytes 294920 | tf_op jit(solution)/shard_map/ppermute | solution.py:335
  31.8 13.6 %collective-permute-start.9 = (f32[3,64,128]{2,1,0:T(8,128)S(1)}, f32[3,64,128]{2,1,0:T(8,128)S(1)}, u32[]{:S(2)}, u32[]{:S(2)}) collective-permute-start(f32[3,64,128]{2,1,0:T(8,128)S(1)} %get-tuple-element.41), channel_id=1, source_target_pairs={{0,7},{1,2},{2,1},{3,4},{4,3},{5,6},{6,5},{7,0},{8,15},{9,10},{10,... | collective-permute-start | bytes 294920 | tf_op jit(solution)/shard_map/ppermute | solution.py:335
  33.7 7.0 %collective-permute-start.10 = (f32[3,32,128]{2,1,0:T(8,128)S(1)}, f32[3,32,128]{2,1,0:T(8,128)S(1)}, u32[]{:S(2)}, u32[]{:S(2)}) collective-permute-start(f32[3,32,128]{2,1,0:T(8,128)S(1)} %get-tuple-element.42), channel_id=1, source_target_pairs={{0,8},{8,0},{16,24},{24,16},{1,9},{9,1},{17,25},{25,17},{2,10},{10... | collective-permute-start | bytes 147464 | tf_op jit(solution)/shard_map/ppermute | solution.py:335
  37.3 4.9 %collective-permute-start.11 = (f32[3,32,128]{2,1,0:T(8,128)S(1)}, f32[3,32,128]{2,1,0:T(8,128)S(1)}, u32[]{:S(2)}, u32[]{:S(2)}) collective-permute-start(f32[3,32,128]{2,1,0:T(8,128)S(1)} %get-tuple-element.43), channel_id=1, source_target_pairs={{8,16},{16,8},{9,17},{17,9},{10,18},{18,10},{11,19},{19,11},{12,20... | collective-permute-start | bytes 147464 | tf_op jit(solution)/shard_map/ppermute | solution.py:335
  37.9 10.8 %collective-permute-start.21 = (f32[64,128]{1,0:T(8,128)S(1)}, f32[64,128]{1,0:T(8,128)S(1)}, u32[]{:S(2)}, u32[]{:S(2)}) collective-permute-start(f32[64,128]{1,0:T(8,128)S(1)} %add_add_fusion.3), channel_id=1, source_target_pairs={{0,16},{8,24},{16,0},{24,8},{1,17},{9,25},{17,1},{25,9},{2,18},{10... | collective-permute-start | bytes 98312 | tf_op jit(solution)/shard_map/ppermute | solution.py:344
  40.7 8.6 %collective-permute-start.22 = (f32[64,128]{1,0:T(8,128)S(1)}, f32[64,128]{1,0:T(8,128)S(1)}, u32[]{:S(2)}, u32[]{:S(2)}) collective-permute-start(f32[64,128]{1,0:T(8,128)S(1)} %add_add_fusion.3), channel_id=1, source_target_pairs={{0,24},{8,16},{16,8},{24,0},{1,25},{9,17},{17,9},{25,1},{2,26},{10... | collective-permute-start | bytes 98312 | tf_op jit(solution)/shard_map/ppermute | solution.py:344
  42.1 8.1 %collective-permute-start.20 = (f32[64,128]{1,0:T(8,128)S(1)}, f32[64,128]{1,0:T(8,128)S(1)}, u32[]{:S(2)}, u32[]{:S(2)}) collective-permute-start(f32[64,128]{1,0:T(8,128)S(1)} %add_add_fusion.3), channel_id=1, source_target_pairs={{0,8},{8,0},{16,24},{24,16},{1,9},{9,1},{17,25},{25,17},{2,10},{10... | collective-permute-start | bytes 98312 | tf_op jit(solution)/shard_map/ppermute | solution.py:344
  46.7 9.9 %collective-permute-start.12 = (f32[3,64,128]{2,1,0:T(8,128)S(1)}, f32[3,64,128]{2,1,0:T(8,128)S(1)}, u32[]{:S(2)}, u32[]{:S(2)}) collective-permute-start(f32[3,64,128]{2,1,0:T(8,128)S(1)} %get-tuple-element.45), channel_id=1, source_target_pairs={{0,1},{1,0},{2,3},{3,2},{4,5},{5,4},{6,7},{7,6},{8,9},{9,8},{10,11... | collective-permute-start | bytes 294920 | tf_op jit(solution)/shard_map/ppermute | solution.py:335
  46.7 9.8 %collective-permute-start.13 = (f32[3,64,128]{2,1,0:T(8,128)S(1)}, f32[3,64,128]{2,1,0:T(8,128)S(1)}, u32[]{:S(2)}, u32[]{:S(2)}) collective-permute-start(f32[3,64,128]{2,1,0:T(8,128)S(1)} %get-tuple-element.46), channel_id=1, source_target_pairs={{0,7},{1,2},{2,1},{3,4},{4,3},{5,6},{6,5},{7,0},{8,15},{9,10},{10,... | collective-permute-start | bytes 294920 | tf_op jit(solution)/shard_map/ppermute | solution.py:335
  48.7 7.8 %collective-permute-start.14 = (f32[3,32,128]{2,1,0:T(8,128)S(1)}, f32[3,32,128]{2,1,0:T(8,128)S(1)}, u32[]{:S(2)}, u32[]{:S(2)}) collective-permute-start(f32[3,32,128]{2,1,0:T(8,128)S(1)} %get-tuple-element.47), channel_id=1, source_target_pairs={{0,8},{8,0},{16,24},{24,16},{1,9},{9,1},{17,25},{25,17},{2,10},{10... | collective-permute-start | bytes 147464 | tf_op jit(solution)/shard_map/ppermute | solution.py:335
  49.3 7.2 %collective-permute-start.15 = (f32[3,32,128]{2,1,0:T(8,128)S(1)}, f32[3,32,128]{2,1,0:T(8,128)S(1)}, u32[]{:S(2)}, u32[]{:S(2)}) collective-permute-start(f32[3,32,128]{2,1,0:T(8,128)S(1)} %get-tuple-element.48), channel_id=1, source_target_pairs={{8,16},{16,8},{9,17},{17,9},{10,18},{18,10},{11,19},{19,11},{12,20... | collective-permute-start | bytes 147464 | tf_op jit(solution)/shard_map/ppermute | solution.py:335
  50.2 1.9 %collective-permute-start.23 = (f32[64,128]{1,0:T(8,128)S(1)}, f32[64,128]{1,0:T(8,128)S(1)}, u32[]{:S(2)}, u32[]{:S(2)}) collective-permute-start(f32[64,128]{1,0:T(8,128)S(1)} %add_add_fusion.2.mine_ref), channel_id=1, source_target_pairs={{0,1},{1,0},{2,3},{3,2},{4,5},{5,4},{6,7},{7,6},{8,9},{9,8},{10,11... | collective-permute-start | bytes 98312 | tf_op jit(solution)/shard_map/ppermute | solution.py:344
  62.5 1.4 %collective-permute-start.24 = (f32[64,128]{1,0:T(8,128)S(1)}, f32[64,128]{1,0:T(8,128)S(1)}, u32[]{:S(2)}, u32[]{:S(2)}) collective-permute-start(f32[64,128]{1,0:T(8,128)S(1)} %get-tuple-element.53), channel_id=1, source_target_pairs={{0,1},{1,0},{2,3},{3,2},{4,5},{5,4},{6,7},{7,6},{8,9},{9,8},{10,11... | collective-permute-start | bytes 98312 | tf_op jit(solution)/shard_map/ppermute | solution.py:344
  63.9 3.9 %collective-permute-start.26 = (f32[64,128]{1,0:T(8,128)S(1)}, f32[64,128]{1,0:T(8,128)S(1)}, u32[]{:S(2)}, u32[]{:S(2)}) collective-permute-start(f32[64,128]{1,0:T(8,128)S(1)} %add.85), channel_id=1, source_target_pairs={{0,4},{1,5},{2,6},{3,7},{4,0},{5,1},{6,2},{7,3},{8,12},{9,13},{10,... | collective-permute-start | bytes 98312 | tf_op jit(solution)/shard_map/ppermute | solution.py:344
  64.8 4.8 %collective-permute-start.27 = (f32[64,128]{1,0:T(8,128)S(1)}, f32[64,128]{1,0:T(8,128)S(1)}, u32[]{:S(2)}, u32[]{:S(2)}) collective-permute-start(f32[64,128]{1,0:T(8,128)S(1)} %add.85), channel_id=1, source_target_pairs={{0,6},{1,7},{2,4},{3,5},{4,2},{5,3},{6,0},{7,1},{8,14},{9,15},{10,... | collective-permute-start | bytes 98312 | tf_op jit(solution)/shard_map/ppermute | solution.py:344
  65.8 3.9 %collective-permute-start.25 = (f32[64,128]{1,0:T(8,128)S(1)}, f32[64,128]{1,0:T(8,128)S(1)}, u32[]{:S(2)}, u32[]{:S(2)}) collective-permute-start(f32[64,128]{1,0:T(8,128)S(1)} %add.85), channel_id=1, source_target_pairs={{0,2},{1,3},{2,0},{3,1},{4,6},{5,7},{6,4},{7,5},{8,10},{9,11},{10,... | collective-permute-start | bytes 98312 | tf_op jit(solution)/shard_map/ppermute | solution.py:344
  69.7 6.1 %collective-permute-start.29 = (f32[64,128]{1,0:T(8,128)S(1)}, f32[64,128]{1,0:T(8,128)S(1)}, u32[]{:S(2)}, u32[]{:S(2)}) collective-permute-start(f32[64,128]{1,0:T(8,128)S(1)} %add_add_fusion.1), channel_id=1, source_target_pairs={{0,16},{8,24},{16,0},{24,8},{1,17},{9,25},{17,1},{25,9},{2,18},{10... | collective-permute-start | bytes 98312 | tf_op jit(solution)/shard_map/ppermute | solution.py:344
  73.9 5.7 %collective-permute-start.30 = (f32[64,128]{1,0:T(8,128)S(1)}, f32[64,128]{1,0:T(8,128)S(1)}, u32[]{:S(2)}, u32[]{:S(2)}) collective-permute-start(f32[64,128]{1,0:T(8,128)S(1)} %add_add_fusion.1), channel_id=1, source_target_pairs={{0,24},{8,16},{16,8},{24,0},{1,25},{9,17},{17,9},{25,1},{2,26},{10... | collective-permute-start | bytes 98312 | tf_op jit(solution)/shard_map/ppermute | solution.py:344
  75.3 4.3 %collective-permute-start.28 = (f32[64,128]{1,0:T(8,128)S(1)}, f32[64,128]{1,0:T(8,128)S(1)}, u32[]{:S(2)}, u32[]{:S(2)}) collective-permute-start(f32[64,128]{1,0:T(8,128)S(1)} %add_add_fusion.1), channel_id=1, source_target_pairs={{0,8},{8,0},{16,24},{24,16},{1,9},{9,1},{17,25},{25,17},{2,10},{10... | collective-permute-start | bytes 98312 | tf_op jit(solution)/shard_map/ppermute | solution.py:344
  79.6 1.3 %collective-permute-start.31 = (f32[64,128]{1,0:T(8,128)S(1)}, f32[64,128]{1,0:T(8,128)S(1)}, u32[]{:S(2)}, u32[]{:S(2)}) collective-permute-start(f32[64,128]{1,0:T(8,128)S(1)} %add_add_fusion.mine_ref), channel_id=1, source_target_pairs={{0,1},{1,0},{2,3},{3,2},{4,5},{5,4},{6,7},{7,6},{8,9},{9,8},{10,11... | collective-permute-start | bytes 98312 | tf_op jit(solution)/shard_map/ppermute | solution.py:344
  (5 other events, 30.5 us)
where the time goes:
time: 89.6 us; the launch traced here: 89.3 us
  starting transfers between devices  40.7 us (45%)
  Pallas kernels  34.7 us (39%)
  waiting for transfers between devices  9.93 us (11%)
  local copies, waits for them, and re-layouts  2.69 us (3%)
  between operations  1.17 us (1%)
    pallas_call x12, Pallas kernels, call(): pl.pallas_call(kernel, out_shape=outs, in_specs=specs or [SMEM] + [VMEM]...  34.7 us
    ppermute x16, starting transfers between devices, swapped(): lax.ppermute(value, axis, [(i, i ^ mask) for i in range(lax.axis_size(axi...  19 us
    ppermute x8, starting transfers between devices, swap_pairs(): lax.ppermute(far_value, axis, far)  10.9 us
    ppermute x8, starting transfers between devices, swap_pairs(): lax.ppermute(near_value, axis, near)  10.8 us
    ppermute x16, waiting for transfers between devices, swapped(): lax.ppermute(value, axis, [(i, i ^ mask) for i in range(lax.axis_size(axi...  9.89 us
    unnamed x10, local copies, waits for them, and re-layouts  2.61 us
  transfers between devices with their start and end apart: 32, of which 8 were waited for; matrix products, arithmetic and copies ran while one was open for 0% of the time, Pallas kernels for 16%

commit v1 on v0

v1 whole, which is shorter than its diff:
```python
import functools

import jax
import jax.numpy as jnp
from jax import lax
from jax.experimental import pallas as pl
from jax.experimental.pallas import tpu as pltpu
from jax.sharding import PartitionSpec as P

STEPS = 2
RENORMS = 2
LEVELS = 50

viscosity = 0.15
gravity = 0.5
rotation = 0.4

SUB = 8
LANES = 128
FIELDS = 3
HALO = STEPS * RENORMS
TILES = 6
VMEM_LIMIT = 16 * 1024 * 1024

HBM = pl.BlockSpec(memory_space=pltpu.HBM)
VMEM = pl.BlockSpec(memory_space=pltpu.VMEM)
SMEM = pl.BlockSpec(memory_space=pltpu.SMEM)


def params():
    return pltpu.CompilerParams(vmem_limit_bytes=VMEM_LIMIT)


def shape_of(*dims):
    return jax.ShapeDtypeStruct(dims, jnp.float32)


def lane_spread(block, lane):
    return jnp.broadcast_to(block[:, lane : lane + 1], (block.shape[0], LANES))


def fields_of(sea_ref, levels_ref, current_ref):
    return (
        sea_ref[...].astype(jnp.float32),
        0.5 * current_ref[...],
        0.5 * ((levels_ref[...] + 1).astype(jnp.float32) / LEVELS),
    )


def sides_of(par):
    odd_row, odd_col = par[0] % 2, par[1] % 2
    return (1 - odd_row, odd_row), (1 - odd_col, odd_col)


def pack_rows(par, t_ref, sea_ref, levels_ref, current_ref, row_a, row_b, wide, sems):
    comps, rows, cols, _ = t_ref.shape
    norths, _ = sides_of(par)
    copies = []
    for slot, msg in ((0, row_a), (1, row_b)):
        for comp in range(comps):
            copies.append(
                pltpu.make_async_copy(
                    t_ref.at[comp, pl.ds(norths[slot] * (rows - HALO), HALO)],
                    msg.at[pl.ds(comp * HALO, HALO)],
                    sems.at[slot * comps + comp],
                )
            )
            copies[-1].start()
    lane = lax.broadcasted_iota(jnp.int32, (cols, LANES), 1)
    wide[...] = jnp.zeros_like(wide)
    packed = [jnp.zeros((cols, LANES), jnp.float32)] * 2
    for field, value in enumerate(fields_of(sea_ref, levels_ref, current_ref)):
        wide[:, pl.ds(0, rows)] = value
        whole = wide[...]
        for north in (0, 1):
            shift = (field * SUB - north * (rows - HALO)) % LANES
            moved = pltpu.roll(whole, shift, 1) if shift else whole
            here = (lane >= field * SUB) & (lane < field * SUB + HALO)
            packed[north] = jnp.where(here, moved, packed[north])
    for slot, msg in ((0, row_a), (1, row_b)):
        msg[comps * HALO] = jnp.where(norths[slot] == 1, packed[1], packed[0])
    for copy in copies:
        copy.wait()


def spread_fields(t_ref, sea_ref, levels_ref, current_ref, state, coef, sems):
    comps, rows, _, _ = t_ref.shape
    copies = [
        pltpu.make_async_copy(t_ref.at[comp], state.at[comp, pl.ds(HALO, rows)], sems.at[comp])
        for comp in range(comps)
    ]
    for copy in copies:
        copy.start()
    for field, value in enumerate(fields_of(sea_ref, levels_ref, current_ref)):
        for row in range(rows):
            coef[field, HALO + row] = lane_spread(value, row)
    for copy in copies:
        copy.wait()


def pack_columns(par, state, col_a, col_b):
    comps, tall, cols, _ = state.shape
    _, easts = sides_of(par)
    flat = state.reshape(comps * tall * cols, LANES)
    for slot, msg in ((0, col_a), (1, col_b)):
        for comp in range(comps):
            for row in range(0, tall, SUB):
                at = (comp * tall + row) * cols + easts[slot] * (cols - 1)
                msg[comp, pl.ds(row, SUB), :] = flat[pl.ds(at, SUB, stride=cols), :]


def join_rows(par, state_in, coef_in, row_a, row_b, state, coef, col_a, col_b):
    comps, tall, _, _ = state.shape
    norths, _ = sides_of(par)
    for slot, msg in ((0, row_a), (1, row_b)):
        line = norths[slot] * (tall - HALO)
        fields = msg[comps * HALO]
        for h in range(HALO):
            for comp in range(comps):
                state[comp, line + h] = msg[comp * HALO + h]
            for field in range(FIELDS):
                coef[field, line + h] = lane_spread(fields, field * SUB + h)
    pack_columns(par, state, col_a, col_b)


def apply_inside(step, t_ref, coef_ref, spin_ref, out_ref):
    comps, tall, cols, _ = t_ref.shape
    flat = t_ref.reshape(comps * tall * cols, LANES)
    sub = lax.broadcasted_iota(jnp.int32, (SUB, LANES), 0)
    keep, half = 1.0 - 4.0 * viscosity, 0.5 * gravity
    first, last = step + 1, tall - step - 1

    def line_of(line):
        spin = jnp.broadcast_to(spin_ref[pl.ds(line, 1), :], (SUB, LANES))
        for lon in range(0, cols, SUB):
            at = [(comp * tall + line) * cols + lon for comp in range(comps)]
            cells = pl.ds(lon, SUB)
            sea, flow, depth = (coef_ref[field, line, cells, :] for field in range(FIELDS))
            own = [t_ref[comp, line, cells, :] for comp in range(comps)]
            if lon == 0:
                west = [jnp.where(sub == 0, 0.0, pltpu.roll(x, 1, 0)) for x in own]
            else:
                west = [flat[pl.ds(a - 1, SUB), :] for a in at]
            if lon == cols - SUB:
                east = [jnp.where(sub == SUB - 1, 0.0, pltpu.roll(x, SUB - 1, 0)) for x in own]
            else:
                east = [flat[pl.ds(a + 1, SUB), :] for a in at]
            above = [t_ref[comp, line + 1, cells, :] for comp in range(comps)]
            below = [t_ref[comp, line - 1, cells, :] for comp in range(comps)]
            x_diff = [e - w for e, w in zip(east, west)]
            mixed = [
                keep * c + viscosity * ((e + w) + (n + s)) - flow * x
                for c, e, w, n, s, x in zip(own, east, west, above, below, x_diff)
            ]
            v_y, h_y = above[1] - below[1], above[2] - below[2]
            out_ref[0, line, cells, :] = sea * (mixed[0] - half * x_diff[2] + spin * own[1])
            out_ref[1, line, cells, :] = sea * (mixed[1] - half * h_y - spin * own[0])
            out_ref[2, line, cells, :] = sea * (mixed[2] - depth * (x_diff[0] + v_y))

    @pl.loop(0, (last - first) // 2)
    def _(pair):
        line_of(first + 2 * pair)
        line_of(first + 1 + 2 * pair)


def add_columns(par, state, coef_ref, col_a, col_b):
    comps, tall, cols, _ = state.shape
    _, easts = sides_of(par)
    half = 0.5 * gravity
    flat = state.reshape(comps * tall * cols, LANES)
    flat_coef = coef_ref.reshape(FIELDS * tall * cols, LANES)
    for slot, halo in ((0, col_a), (1, col_b)):
        sign = (1 - 2 * easts[slot]).astype(jnp.float32)
        for row in range(0, tall, SUB):
            spots = [
                pl.ds((comp * tall + row) * cols + easts[slot] * (cols - 1), SUB, stride=cols)
                for comp in range(comps)
            ]
            sea, flow, depth = (flat_coef[spot, :] for spot in spots)
            u, v, h = (halo[comp, pl.ds(row, SUB), :] for comp in range(comps))
            mix = viscosity + sign * flow
            flat[spots[0], :] += sea * (mix * u + (sign * half) * h)
            flat[spots[1], :] += sea * (mix * v)
            flat[spots[2], :] += sea * (mix * h + (sign * depth) * u)


def tiles_of(state):
    comps, tall, cols, _ = state.shape
    flat = state.reshape(comps * tall * cols, LANES)
    parts = TILES // comps
    height = (tall - 2 * HALO) * cols // parts
    for tile in range(TILES):
        start = ((tile // parts) * tall + HALO) * cols + (tile % parts) * height
        yield flat, pl.ds(start, height)


def join_step(par, state_in, coef_ref, a, b, state, col_a, col_b):
    add_columns(par, state, coef_ref, a, b)
    pack_columns(par, state, col_a, col_b)


def join_gram(scale, par, state_in, coef_ref, a, b, state, col_a, col_b, kept, sent, total):
    add_columns(par, state, coef_ref, a, b)
    pack_columns(par, state, col_a, col_b)
    gram = sum(gram_of(*split_halves(flat[cells, :])) for flat, cells in tiles_of(state))
    write_halves(par, gram, scale, kept, sent, total)


def split_halves(value):
    high = value.astype(jnp.bfloat16)
    return high, (value - high.astype(jnp.float32)).astype(jnp.bfloat16)


def gram_of(high, low):
    return lax.dot_general(
        high,
        jnp.concatenate([high, low], axis=1),
        (((0,), (0,)), ((), ())),
        preferred_element_type=jnp.float32,
    )


def write_halves(par, gram, scale, kept, sent, total):
    odd = par[1] % 2
    rows = LANES // 2
    mixed = gram[:, LANES:]
    total[...] = scale * (gram[:, :LANES] + (mixed + jnp.transpose(mixed)))
    kept[...] = total[pl.ds(odd * rows, rows), :]
    sent[...] = total[pl.ds((1 - odd) * rows, rows), :]


def invert_factor(gram_ref, work):
    count = LANES // SUB
    lane = lax.broadcasted_iota(jnp.int32, (SUB, LANES), 1)
    sub = lax.broadcasted_iota(jnp.int32, (SUB, LANES), 0)
    rows = [gram_ref[pl.ds(SUB * i, SUB), :] for i in range(count)]
    for block in range(count):
        base = SUB * block
        here = (lane >= base) & (lane < base + SUB)
        spread = [lane_spread(rows[block], base + l) for l in range(SUB)]
        low = [
            [jnp.broadcast_to(spread[l][k : k + 1, :], (SUB, LANES)) for l in range(k + 1)]
            for k in range(SUB)
        ]
        pivot = jnp.where(here, jnp.where(lane - base == sub, 1.0, 0.0), rows[block])
        inv, scaled = [], []
        for k in range(SUB):
            inv.append(lax.rsqrt(low[k][k]))
            for i in range(k + 1, SUB):
                low[i][k] = low[i][k] * inv[k]
            for i in range(k + 1, SUB):
                for m in range(k + 1, i + 1):
                    low[i][m] = low[i][m] - low[i][k] * low[m][k]
            line = jnp.broadcast_to(pivot[k : k + 1, :], (SUB, LANES))
            for l in range(k):
                line = line - low[k][l] * scaled[l]
            scaled.append(line * inv[k])
        merged = scaled[0]
        for k in range(1, SUB):
            merged = jnp.where(sub == k, scaled[k], merged)
        work[pl.ds(base, SUB), :] = merged
        for i in range(block + 1, count):
            weights = []
            rest = jnp.where(here, 0.0, rows[i])
            for l in range(SUB):
                weight = lane_spread(rows[i], base + l)
                for m in range(l):
                    weight = weight - weights[m] * low[l][m]
                weights.append(weight * inv[l])
            for l in range(SUB):
                rest = rest - weights[l] * scaled[l]
            rows[i] = rest


def factorize(par, mine_ref, other_ref, gram, work):
    rows = LANES // 2
    odd = par[1] % 2
    gram[pl.ds(odd * rows, rows), :] = mine_ref[...]
    gram[pl.ds((1 - odd) * rows, rows), :] = other_ref[...]
    invert_factor(gram, work)
    row = lax.broadcasted_iota(jnp.int32, (LANES, LANES), 0)
    col = lax.broadcasted_iota(jnp.int32, (LANES, LANES), 1)
    inverse = jnp.where(row >= col, work[...], 0.0)
    diagonal = jnp.sum(jnp.where(row == col, inverse, 0.0), axis=0, keepdims=True)
    return inverse, diagonal


def paired(inverse):
    high = inverse.astype(jnp.bfloat16)
    low = (inverse - high.astype(jnp.float32)).astype(jnp.bfloat16)
    return jnp.concatenate(
        [jnp.concatenate([high, high], axis=1), jnp.concatenate([low, low], axis=1)], axis=0
    )


def times_factor(cells, factor):
    pair = jnp.concatenate(split_halves(cells), axis=1)
    both = lax.dot_general(
        pair, factor, (((1,), (1,)), ((), ())), preferred_element_type=jnp.float32
    )
    return both[:, :LANES] + both[:, LANES:]


def factor_only(par, mine_ref, other_ref, prior_ref, inverse_ref, logs_ref, gram, work):
    inverse, diagonal = factorize(par, mine_ref, other_ref, gram, work)
    inverse_ref[...] = inverse
    logs_ref[...] = prior_ref[...] - jnp.log(diagonal)


def join_update(
    scale, par, state_in, coef_ref, a, b, inverse_ref, state, out_ref, kept, sent, factor, total
):
    add_columns(par, state, coef_ref, a, b)
    factor[...] = paired(inverse_ref[...])
    gram = 0.0
    for tile, (flat, cells) in enumerate(tiles_of(state)):
        new = times_factor(flat[cells, :], factor[...])
        out_ref[tile] = new
        gram += gram_of(*split_halves(new))
    write_halves(par, gram, scale, kept, sent, total)


def finish(par, mine_ref, other_ref, prior_ref, t_ref, out_ref, logs_ref, gram, work, factor, fresh, sems):
    inverse, diagonal = factorize(par, mine_ref, other_ref, gram, work)
    logs_ref[...] = prior_ref[...] - jnp.log(diagonal)
    factor[...] = paired(inverse)

    def out_copy(tile):
        return pltpu.make_async_copy(fresh.at[tile], out_ref.at[tile], sems.at[tile])

    for tile in range(TILES):
        fresh[tile] = times_factor(t_ref[tile], factor[...])
        out_copy(tile).start()

    for tile in range(TILES):
        out_copy(tile).wait()


def swap_pairs(near_value, far_value, axis, closed):
    count = lax.axis_size(axis)
    near = [(i, i ^ 1) for i in range(count)]
    far = [(i, (i + 1 if i % 2 else i - 1) % count) for i in range(count)]
    if not closed:
        far = far[1:-1]
    return lax.ppermute(near_value, axis, near), lax.ppermute(far_value, axis, far)


def swapped(value, axis, mask):
    return lax.ppermute(value, axis, [(i, i ^ mask) for i in range(lax.axis_size(axis))])


def sum_over(value, axis, first_bit):
    bits = lax.axis_size(axis).bit_length() - 1
    while first_bit < bits:
        low = 1 << first_bit
        if first_bit + 1 < bits:
            high = low << 1
            one, two, three = (swapped(value, axis, mask) for mask in (low, high, low | high))
            value = (value + one) + (two + three)
            first_bit += 2
        else:
            value = value + swapped(value, axis, low)
            first_bit += 1
    return value


def sum_devices(kept, sent):
    mine = kept + swapped(sent, "col", 1)
    mine = sum_over(mine, "col", 1)
    mine = sum_over(mine, "row", 0)
    return mine, swapped(mine, "col", 1)


def body(tangents, sea_mask, levels, current):
    comps, rows, cols, modes = tangents.shape
    total_rows = rows * lax.axis_size("row")
    total_cells = total_rows * cols * lax.axis_size("col")
    scale = 1.0 / total_cells
    row_at, col_at = lax.axis_index("row"), lax.axis_index("col")
    par = jnp.stack([row_at, col_at]).astype(jnp.int32)

    tall = rows + 2 * HALO
    lat = (row_at * rows - HALO + jnp.arange(tall)).astype(jnp.float32)
    angle = (-70.0 + 140.0 * (lat + 0.5) / total_rows) * (jnp.pi / 180.0)
    spin = jnp.broadcast_to((rotation * jnp.sin(angle))[:, None], (tall, LANES))

    height = comps * rows * cols // TILES
    block = shape_of(comps, tall, cols, modes)
    columns = (shape_of(comps, tall, modes),) * 2
    rows_sent = (shape_of(comps * HALO + 1, cols, modes),) * 2
    halves = (shape_of(modes // 2, modes),) * 2
    tiled = shape_of(TILES, height, modes)
    square = pltpu.VMEM((modes, modes), jnp.float32)
    factor = pltpu.VMEM((2 * modes, 2 * modes), jnp.bfloat16)

    def call(kernel, outs, *operands, specs=None, out_specs=None, scratch=(), aliases=None):
        return pl.pallas_call(
            kernel,
            out_shape=outs,
            in_specs=specs or [SMEM] + [VMEM] * (len(operands) - 1),
            out_specs=out_specs or (VMEM,) * len(outs),
            scratch_shapes=scratch,
            input_output_aliases=aliases or {},
            compiler_params=params(),
        )(*operands)

    def inside(step, state):
        kernel = functools.partial(apply_inside, step)
        return call(kernel, (block,), state, coef, spin, specs=[VMEM] * 3)[0]

    def swap_columns(packed):
        return swap_pairs(*packed, "col", True)

    source = pltpu.with_memory_space_constraint(tangents, pltpu.HBM)
    fields = (sea_mask.T, levels.T, current.T)
    packed = call(
        pack_rows,
        rows_sent,
        par,
        source,
        *fields,
        specs=[SMEM, HBM] + [VMEM] * 3,
        scratch=[pltpu.VMEM((cols, LANES), jnp.float32), pltpu.SemaphoreType.DMA((2 * comps,))],
    )
    row_halos = swap_pairs(*packed, "row", False)
    state, coef = call(
        spread_fields,
        (block, shape_of(FIELDS, tall, cols, LANES)),
        source,
        *fields,
        specs=[HBM] + [VMEM] * 3,
        scratch=[pltpu.SemaphoreType.DMA((comps,))],
    )
    state, coef, *packed = call(
        join_rows,
        (block, shape_of(FIELDS, tall, cols, LANES)) + columns,
        par,
        state,
        coef,
        *row_halos,
        aliases={1: 0, 2: 1},
    )
    logs = jnp.zeros((1, modes), jnp.float32)
    for step in range(STEPS * RENORMS):
        halos = swap_columns(packed)
        state = inside(step, state)
        if step == STEPS * RENORMS - 1:
            break
        if step == STEPS - 1:
            state, *packed, kept, sent = call(
                functools.partial(join_gram, scale),
                (block,) + columns + halves,
                par,
                state,
                coef,
                *halos,
                scratch=[square],
                aliases={1: 0},
            )
            mine, other = sum_devices(kept, sent)
            inverse, logs = call(
                factor_only,
                (shape_of(modes, modes), shape_of(1, modes)),
                par,
                mine,
                other,
                logs,
                scratch=[square, square],
            )
        else:
            state, *packed = call(
                join_step, (block,) + columns, par, state, coef, *halos, aliases={1: 0}
            )
    _, state, kept, sent = call(
        functools.partial(join_update, scale),
        (block, tiled) + halves,
        par,
        state,
        coef,
        *halos,
        inverse,
        scratch=[factor, square],
        aliases={1: 0},
    )
    mine, other = sum_devices(kept, sent)
    out, logs = call(
        finish,
        (tiled, shape_of(1, modes)),
        par,
        mine,
        other,
        logs,
        state,
        out_specs=(HBM, VMEM),
        scratch=[
            square,
            square,
            factor,
            pltpu.VMEM((TILES, height, modes), jnp.float32),
            pltpu.SemaphoreType.DMA((TILES,)),
        ],
    )
    return out.reshape(tangents.shape), logs.reshape(modes)


def solution(mesh):
    placed = (P(None, "row", "col", None), P("row", "col"), P("row", "col"), P("row", "col"))
    return jax.shard_map(
        body,
        mesh=mesh,
        in_specs=placed,
        out_specs=(P(None, "row", "col", None), P()),
        check_vma=False,
    )
```

time: 89.6 us -> 89.5 us (level)
  starting transfers between devices: 40.7 us -> 32.8 us
  waiting for transfers between devices: 9.93 us -> 15.9 us
  local copies, waits for them, and re-layouts: 2.69 us -> 5.95 us
  Pallas kernels: 34.7 us -> 33.2 us
    ppermute x8 -> x5, starting transfers between devices: 10.8 us -> 3.42 us  [swap_pairs(): lax.ppermute(near_value, axis, near)]
    ppermute x16, waiting for transfers between devices: 9.89 us -> 13.8 us  [swapped(): lax.ppermute(value, axis, [(i, i ^ mask) for i in range(lax.axis_size(axi...]
    unnamed x10, local copies, waits for them, and re-layouts: 2.61 us -> 5.88 us
    ppermute x8 -> x5, waiting for transfers between devices: 0.02 us -> 1.65 us  [swap_pairs(): lax.ppermute(far_value, axis, far)]
    ppermute x8 -> x5, starting transfers between devices: 10.9 us -> 9.33 us  [swap_pairs(): lax.ppermute(far_value, axis, far)]
    pallas_call x12 -> x13, Pallas kernels: 34.7 us -> 33.2 us  [call(): pl.pallas_call(kernel, out_shape=outs, in_specs=specs or [SMEM] + [VMEM]...]
    ppermute x16, starting transfers between devices: 19 us -> 20 us  [swapped(): lax.ppermute(value, axis, [(i, i ^ mask) for i in range(lax.axis_size(axi...]
  transfers between devices with their start and end apart: 32 -> 26, of which waited for: 8 -> 13; matrix products, arithmetic and copies ran while one was open for 0% -> 0% of each run, Pallas kernels for 16% -> 17%
where the time goes in v1:
time: 89.5 us; the launch traced here: 89 us
  Pallas kernels  33.2 us (37%)
  starting transfers between devices  32.8 us (37%)
  waiting for transfers between devices  15.9 us (18%)
  local copies, waits for them, and re-layouts  5.95 us (7%)
  between operations  1 us (1%)
    pallas_call x13, Pallas kernels, call(): pl.pallas_call(kernel, out_shape=outs, in_specs=specs or [SMEM] + [VMEM]...  33.2 us
    ppermute x16, starting transfers between devices, swapped(): lax.ppermute(value, axis, [(i, i ^ mask) for i in range(lax.axis_size(axi...  20 us
    ppermute x16, waiting for transfers between devices, swapped(): lax.ppermute(value, axis, [(i, i ^ mask) for i in range(lax.axis_size(axi...  13.8 us
    ppermute x5, starting transfers between devices, swap_pairs(): lax.ppermute(far_value, axis, far)  9.33 us
    unnamed x10, local copies, waits for them, and re-layouts  5.88 us
    ppermute x5, starting transfers between devices, swap_pairs(): lax.ppermute(near_value, axis, near)  3.42 us
  transfers between devices with their start and end apart: 26, of which 13 were waited for; matrix products, arithmetic and copies ran while one was open for 0% of the time, Pallas kernels for 17%

profile of v1, /device:TPU:0, one launch (start us, length us, event | category | flops | bytes accessed | tf_op | source)
XLA Modules:
  0.0 89.0 jit_solution(6210415499556801123)
XLA Ops:
  2.9 2.4 %shard_map.60 = (f32[13,32,128]{2,1,0:T(8,128)}, f32[13,32,128]{2,1,0:T(8,128)}) custom-call(s32[2]{0:T(128)S(1)} %pad_add_fusion.par, f32[3,64,32,128]{3,2,1,0:T(8,128)} %t_ref.3, s32[32,64]{1,0:T(8,128)S(1)} %bitcast.7, s32[32,64]{1,0:T(8,128)S(1)} %bitcast.9, f32[32,64]{1,0:T(8,128)S(1)} %bitcast.11), custom_call_target="tpu_custom_call" | custom-call | tf_op jit(solution)/shard_map/pallas_call | solution.py:397
  5.2 3.1 %collective-permute-start = (f32[13,32,128]{2,1,0:T(8,128)}, f32[13,32,128]{2,1,0:T(8,128)}, u32[]{:S(2)}, u32[]{:S(2)}) collective-permute-start(f32[13,32,128]{2,1,0:T(8,128)} %get-tuple-element.30), channel_id=1, source_target_pairs={{0,8},{8,0},{16,24},{24,16},{1,9},{9,1},{17,25},{25,17},{2,10},{10... | collective-permute-start | bytes 638984 | tf_op jit(solution)/shard_map/ppermute | solution.py:345
  8.3 1.3 %collective-permute-start.1 = (f32[13,32,128]{2,1,0:T(8,128)}, f32[13,32,128]{2,1,0:T(8,128)}, u32[]{:S(2)}, u32[]{:S(2)}) collective-permute-start(f32[13,32,128]{2,1,0:T(8,128)} %get-tuple-element.31), channel_id=1, source_target_pairs={{8,16},{16,8},{9,17},{17,9},{10,18},{18,10},{11,19},{19,11},{12,20... | collective-permute-start | bytes 638984 | tf_op jit(solution)/shard_map/ppermute | solution.py:345
  9.7 2.0 %shard_map.59 = (f32[3,72,32,128]{3,2,1,0:T(8,128)S(1)}, f32[3,72,32,128]{3,2,1,0:T(8,128)S(1)}) custom-call(f32[3,64,32,128]{3,2,1,0:T(8,128)} %t_ref.3, s32[32,64]{1,0:T(8,128)S(1)} %bitcast.8, s32[32,64]{1,0:T(8,128)S(1)} %bitcast.10, f32[32,64]{1,0:T(8,128)S(1)} %bitcast.12), custom_call_target="tpu_custom_call" | custom-call | tf_op jit(solution)/shard_map/pallas_call | solution.py:397
  11.7 1.7 %copy-done = f32[3,72,32,128]{3,2,1,0:T(8,128)} copy-done((f32[3,72,32,128]{3,2,1,0:T(8,128)}, f32[3,72,32,128]{3,2,1,0:T(8,128)S(1)}, u32[]{:S(2)}) %copy-start) | copy-done | bytes 3538968
  13.9 2.0 %copy-done.1 = f32[3,72,32,128]{3,2,1,0:T(8,128)S(1)} copy-done((f32[3,72,32,128]{3,2,1,0:T(8,128)S(1)}, f32[3,72,32,128]{3,2,1,0:T(8,128)}, u32[]{:S(2)}) %copy-start.1) | copy-done | bytes 3538968
  15.9 1.4 %shard_map.61 = (f32[3,72,32,128]{3,2,1,0:T(8,128)S(1)}, f32[3,72,32,128]{3,2,1,0:T(8,128)S(1)}, f32[3,72,128]{2,1,0:T(8,128)S(1)}, f32[3,72,128]{2,1,0:T(8,128)S(1)}) custom-call(s32[2]{0:T(128)S(1)} %pad_add_fusion.par, f32[3,72,32,128]{3,2,1,0:T(8,128)S(1)} %copy-done.1, ...), custom_call_target="tpu_custom_call", output_to_operand_aliasing={{0}: (1, {}), {1}: (2, {})} | custom-call | tf_op jit(solution)/shard_map/pallas_call | solution.py:397
  17.3 2.7 %collective-permute-start.3 = (f32[3,72,128]{2,1,0:T(8,128)S(1)}, f32[3,72,128]{2,1,0:T(8,128)S(1)}, u32[]{:S(2)}, u32[]{:S(2)}) collective-permute-start(f32[3,72,128]{2,1,0:T(8,128)S(1)} %get-tuple-element.35), channel_id=1, source_target_pairs={{0,7},{1,2},{2,1},{3,4},{4,3},{5,6},{6,5},{7,0},{8,15},{9,10},{10,... | collective-permute-start | bytes 331784 | tf_op jit(solution)/shard_map/ppermute | solution.py:345
  20.2 2.0 %shard_map.62.state_in = f32[3,72,32,128]{3,2,1,0:T(8,128)S(1)} custom-call(f32[3,72,32,128]{3,2,1,0:T(8,128)S(1)} %get-tuple-element.32.t_ref, f32[3,72,32,128]{3,2,1,0:T(8,128)S(1)} %get-tuple-element.33.coef_ref, f32[72,128]{1,0:T(8,128)S(1)} %broadcast_in_dim.4.spin_ref), custom_call_target="tpu_custom_call" | custom-call | tf_op jit(solution)/shard_map/pallas_call | solution.py:397
  22.9 1.3 %shard_map.63 = (f32[3,72,32,128]{3,2,1,0:T(8,128)S(1)}, f32[3,72,128]{2,1,0:T(8,128)S(1)}, f32[3,72,128]{2,1,0:T(8,128)S(1)}) custom-call(s32[2]{0:T(128)S(1)} %pad_add_fusion.par, f32[3,72,32,128]{3,2,1,0:T(8,128)S(1)} %shard_map.62.state_in, f32[3,72,32,128]{3,2,1,0:T(8,128)S(1)} %get-tuple-element.33.coef_ref, ...), custom_call_target="tpu_custom_call", output_to_operand_aliasing={{0}: (1, {})} | custom-call | tf_op jit(solution)/shard_map/pallas_call | solution.py:397
  24.3 2.2 %collective-permute-start.5 = (f32[3,72,128]{2,1,0:T(8,128)S(1)}, f32[3,72,128]{2,1,0:T(8,128)S(1)}, u32[]{:S(2)}, u32[]{:S(2)}) collective-permute-start(f32[3,72,128]{2,1,0:T(8,128)S(1)} %get-tuple-element.38), channel_id=1, source_target_pairs={{0,7},{1,2},{2,1},{3,4},{4,3},{5,6},{6,5},{7,0},{8,15},{9,10},{10,... | collective-permute-start | bytes 331784 | tf_op jit(solution)/shard_map/ppermute | solution.py:345
  26.5 2.0 %shard_map.64.state_in = f32[3,72,32,128]{3,2,1,0:T(8,128)S(1)} custom-call(f32[3,72,32,128]{3,2,1,0:T(8,128)S(1)} %get-tuple-element.36.t_ref, f32[3,72,32,128]{3,2,1,0:T(8,128)S(1)} %get-tuple-element.33.coef_ref, f32[72,128]{1,0:T(8,128)S(1)} %broadcast_in_dim.4.spin_ref), custom_call_target="tpu_custom_call" | custom-call | tf_op jit(solution)/shard_map/pallas_call | solution.py:397
  29.5 2.1 %shard_map.65 = (f32[3,72,32,128]{3,2,1,0:T(8,128)S(1)}, f32[3,72,128]{2,1,0:T(8,128)S(1)}, f32[3,72,128]{2,1,0:T(8,128)S(1)}, f32[64,128]{1,0:T(8,128)S(1)}, f32[64,128]{1,0:T(8,128)S(1)}) custom-call(s32[2]{0:T(128)S(1)} %pad_add_fusion.par, f32[3,72,32,128]{3,2,1,0:T(8,128)S(1)} %shard_map.64.state_in, ...), custom_call_target="tpu_custom_call", output_to_operand_aliasing={{0}: (1, {})} | custom-call | tf_op jit(solution)/shard_map/pallas_call | solution.py:397
  32.8 2.2 %collective-permute-start.11 = (f32[64,128]{1,0:T(8,128)S(1)}, f32[64,128]{1,0:T(8,128)S(1)}, u32[]{:S(2)}, u32[]{:S(2)}) collective-permute-start(f32[64,128]{1,0:T(8,128)S(1)} %add.79), channel_id=1, source_target_pairs={{0,2},{1,3},{2,0},{3,1},{4,6},{5,7},{6,4},{7,5},{8,10},{9,11},{10,... | collective-permute-start | bytes 98312 | tf_op jit(solution)/shard_map/ppermute | solution.py:349
  36.7 2.5 %collective-permute-start.7 = (f32[3,72,128]{2,1,0:T(8,128)S(1)}, f32[3,72,128]{2,1,0:T(8,128)S(1)}, u32[]{:S(2)}, u32[]{:S(2)}) collective-permute-start(f32[3,72,128]{2,1,0:T(8,128)S(1)} %get-tuple-element.41), channel_id=1, source_target_pairs={{0,7},{1,2},{2,1},{3,4},{4,3},{5,6},{6,5},{7,0},{8,15},{9,10},{10,... | collective-permute-start | bytes 331784 | tf_op jit(solution)/shard_map/ppermute | solution.py:345
  39.2 2.1 %collective-permute-done.13 = f32[64,128]{1,0:T(8,128)S(1)} collective-permute-done((f32[64,128]{1,0:T(8,128)S(1)}, f32[64,128]{1,0:T(8,128)S(1)}, u32[]{:S(2)}, u32[]{:S(2)}) %collective-permute-start.13) | collective-permute-done | bytes 32800 | tf_op jit(solution)/shard_map/ppermute | solution.py:349
  41.4 4.5 %collective-permute-start.14 = (f32[64,128]{1,0:T(8,128)S(1)}, f32[64,128]{1,0:T(8,128)S(1)}, u32[]{:S(2)}, u32[]{:S(2)}) collective-permute-start(f32[64,128]{1,0:T(8,128)S(1)} %add_add_fusion.3), channel_id=1, source_target_pairs={{0,8},{8,0},{16,24},{24,16},{1,9},{9,1},{17,25},{25,17},{2,10},{10... | collective-permute-start | bytes 98312 | tf_op jit(solution)/shard_map/ppermute | solution.py:349
  45.9 1.2 %collective-permute-start.15 = (f32[64,128]{1,0:T(8,128)S(1)}, f32[64,128]{1,0:T(8,128)S(1)}, u32[]{:S(2)}, u32[]{:S(2)}) collective-permute-start(f32[64,128]{1,0:T(8,128)S(1)} %add_add_fusion.3), channel_id=1, source_target_pairs={{0,16},{8,24},{16,0},{24,8},{1,17},{9,25},{17,1},{25,9},{2,18},{10... | collective-permute-start | bytes 98312 | tf_op jit(solution)/shard_map/ppermute | solution.py:349
  47.2 1.4 %collective-permute-start.16 = (f32[64,128]{1,0:T(8,128)S(1)}, f32[64,128]{1,0:T(8,128)S(1)}, u32[]{:S(2)}, u32[]{:S(2)}) collective-permute-start(f32[64,128]{1,0:T(8,128)S(1)} %add_add_fusion.3), channel_id=1, source_target_pairs={{0,24},{8,16},{16,8},{24,0},{1,25},{9,17},{17,9},{25,1},{2,26},{10... | collective-permute-start | bytes 98312 | tf_op jit(solution)/shard_map/ppermute | solution.py:349
  48.5 1.9 %shard_map.66.state_in = f32[3,72,32,128]{3,2,1,0:T(8,128)S(1)} custom-call(f32[3,72,32,128]{3,2,1,0:T(8,128)S(1)} %get-tuple-element.39.t_ref, f32[3,72,32,128]{3,2,1,0:T(8,128)S(1)} %get-tuple-element.33.coef_ref, f32[72,128]{1,0:T(8,128)S(1)} %broadcast_in_dim.4.spin_ref), custom_call_target="tpu_custom_call" | custom-call | tf_op jit(solution)/shard_map/pallas_call | solution.py:397
  50.4 1.3 %shard_map.67 = (f32[3,72,32,128]{3,2,1,0:T(8,128)S(1)}, f32[3,72,128]{2,1,0:T(8,128)S(1)}, f32[3,72,128]{2,1,0:T(8,128)S(1)}) custom-call(s32[2]{0:T(128)S(1)} %pad_add_fusion.par, f32[3,72,32,128]{3,2,1,0:T(8,128)S(1)} %shard_map.66.state_in, f32[3,72,32,128]{3,2,1,0:T(8,128)S(1)} %get-tuple-element.33.coef_ref, ...), custom_call_target="tpu_custom_call", output_to_operand_aliasing={{0}: (1, {})} | custom-call | tf_op jit(solution)/shard_map/pallas_call | solution.py:397
  53.2 2.0 %shard_map.68.state_in = f32[3,72,32,128]{3,2,1,0:T(8,128)S(1)} custom-call(f32[3,72,32,128]{3,2,1,0:T(8,128)S(1)} %get-tuple-element.42.t_ref, f32[3,72,32,128]{3,2,1,0:T(8,128)S(1)} %get-tuple-element.33.coef_ref, f32[72,128]{1,0:T(8,128)S(1)} %broadcast_in_dim.4.spin_ref), custom_call_target="tpu_custom_call" | custom-call | tf_op jit(solution)/shard_map/pallas_call | solution.py:397
  55.3 4.4 %shard_map.69 = (f32[128,128]{1,0:T(8,128)S(1)}, f32[1,128]{1,0:T(1,128)S(1)}) custom-call(s32[2]{0:T(128)S(1)} %pad_add_fusion.par, f32[64,128]{1,0:T(8,128)S(1)} %add_add_fusion.2.mine_ref, f32[64,128]{1,0:T(8,128)S(1)} %collective-permute-done.17.other_ref, f32[1,128]{1,0:T(1,128)S(1)} %broadcast_in_dim.10.prior_ref), custom_call_target="tpu_custom_call" | custom-call | tf_op jit(solution)/shard_map/pallas_call | solution.py:397
  59.7 2.9 %shard_map.70 = (f32[3,72,32,128]{3,2,1,0:T(8,128)S(1)}, f32[6,1024,128]{2,1,0:T(8,128)S(1)}, f32[64,128]{1,0:T(8,128)S(1)}, f32[64,128]{1,0:T(8,128)S(1)}) custom-call(s32[2]{0:T(128)S(1)} %pad_add_fusion.par, f32[3,72,32,128]{3,2,1,0:T(8,128)S(1)} %shard_map.68.state_in, ...), custom_call_target="tpu_custom_call", output_to_operand_aliasing={{0}: (1, {})} | custom-call | tf_op jit(solution)/shard_map/pallas_call | solution.py:397
  64.9 1.3 %collective-permute-start.20 = (f32[64,128]{1,0:T(8,128)S(1)}, f32[64,128]{1,0:T(8,128)S(1)}, u32[]{:S(2)}, u32[]{:S(2)}) collective-permute-start(f32[64,128]{1,0:T(8,128)S(1)} %add.86), channel_id=1, source_target_pairs={{0,4},{1,5},{2,6},{3,7},{4,0},{5,1},{6,2},{7,3},{8,12},{9,13},{10,... | collective-permute-start | bytes 98312 | tf_op jit(solution)/shard_map/ppermute | solution.py:349
  68.8 2.2 %collective-permute-done.21 = f32[64,128]{1,0:T(8,128)S(1)} collective-permute-done((f32[64,128]{1,0:T(8,128)S(1)}, f32[64,128]{1,0:T(8,128)S(1)}, u32[]{:S(2)}, u32[]{:S(2)}) %collective-permute-start.21) | collective-permute-done | bytes 32800 | tf_op jit(solution)/shard_map/ppermute | solution.py:349
  71.9 2.1 %collective-permute-start.23 = (f32[64,128]{1,0:T(8,128)S(1)}, f32[64,128]{1,0:T(8,128)S(1)}, u32[]{:S(2)}, u32[]{:S(2)}) collective-permute-start(f32[64,128]{1,0:T(8,128)S(1)} %add_add_fusion.1), channel_id=1, source_target_pairs={{0,16},{8,24},{16,0},{24,8},{1,17},{9,25},{17,1},{25,9},{2,18},{10... | collective-permute-start | bytes 98312 | tf_op jit(solution)/shard_map/ppermute | solution.py:349
  74.1 1.4 %collective-permute-start.24 = (f32[64,128]{1,0:T(8,128)S(1)}, f32[64,128]{1,0:T(8,128)S(1)}, u32[]{:S(2)}, u32[]{:S(2)}) collective-permute-start(f32[64,128]{1,0:T(8,128)S(1)} %add_add_fusion.1), channel_id=1, source_target_pairs={{0,24},{8,16},{16,8},{24,0},{1,25},{9,17},{17,9},{25,1},{2,26},{10... | collective-permute-start | bytes 98312 | tf_op jit(solution)/shard_map/ppermute | solution.py:349
  75.5 2.0 %collective-permute-done.23 = f32[64,128]{1,0:T(8,128)S(1)} collective-permute-done((f32[64,128]{1,0:T(8,128)S(1)}, f32[64,128]{1,0:T(8,128)S(1)}, u32[]{:S(2)}, u32[]{:S(2)}) %collective-permute-start.23) | collective-permute-done | bytes 32800 | tf_op jit(solution)/shard_map/ppermute | solution.py:349
  77.4 2.4 %collective-permute-done.24 = f32[64,128]{1,0:T(8,128)S(1)} collective-permute-done((f32[64,128]{1,0:T(8,128)S(1)}, f32[64,128]{1,0:T(8,128)S(1)}, u32[]{:S(2)}, u32[]{:S(2)}) %collective-permute-start.24) | collective-permute-done | bytes 32800 | tf_op jit(solution)/shard_map/ppermute | solution.py:349
  79.9 1.2 %collective-permute-done.25.other_ref = f32[64,128]{1,0:T(8,128)S(1)} collective-permute-done((f32[64,128]{1,0:T(8,128)S(1)}, f32[64,128]{1,0:T(8,128)S(1)}, u32[]{:S(2)}, u32[]{:S(2)}) %collective-permute-start.25) | collective-permute-done | bytes 32800 | tf_op jit(solution)/shard_map/ppermute | solution.py:349
  81.1 7.8 %shard_map.71 = (f32[6,1024,128]{2,1,0:T(8,128)}, f32[1,128]{1,0:T(1,128)}) custom-call(s32[2]{0:T(128)S(1)} %pad_add_fusion.par, f32[64,128]{1,0:T(8,128)S(1)} %add_add_fusion.mine_ref, f32[64,128]{1,0:T(8,128)S(1)} %collective-permute-done.25.other_ref, f32[1,128]{1,0:T(1,128)S(1)} %get-tuple-element.50.prior_ref, f32[6,1024,128]{2,1,0:T(8,128)S(1)} %get-tuple-element.51.t_ref), custom_call_target="tpu_custom_call" | custom-call | tf_op jit(solution)/shard_map/pallas_call | solution.py:397
  (53 shorter events, 15.2 us)
Async XLA Ops:
  0.7 0.7 copy-start.2
  1.4 0.7 copy-start.3
  2.1 0.7 copy-start.4
  5.2 8.7 %collective-permute-start = (f32[13,32,128]{2,1,0:T(8,128)}, f32[13,32,128]{2,1,0:T(8,128)}, u32[]{:S(2)}, u32[]{:S(2)}) collective-permute-start(f32[13,32,128]{2,1,0:T(8,128)} %get-tuple-element.30), channel_id=1, source_target_pairs={{0,8},{8,0},{16,24},{24,16},{1,9},{9,1},{17,25},{25,17},{2,10},{10... | collective-permute-start | bytes 638984 | tf_op jit(solution)/shard_map/ppermute | solution.py:345
  8.3 5.6 %collective-permute-start.1 = (f32[13,32,128]{2,1,0:T(8,128)}, f32[13,32,128]{2,1,0:T(8,128)}, u32[]{:S(2)}, u32[]{:S(2)}) collective-permute-start(f32[13,32,128]{2,1,0:T(8,128)} %get-tuple-element.31), channel_id=1, source_target_pairs={{8,16},{16,8},{9,17},{17,9},{10,18},{18,10},{11,19},{19,11},{12,20... | collective-permute-start | bytes 638984 | tf_op jit(solution)/shard_map/ppermute | solution.py:345
  11.6 1.7 %copy-start = (f32[3,72,32,128]{3,2,1,0:T(8,128)}, f32[3,72,32,128]{3,2,1,0:T(8,128)S(1)}, u32[]{:S(2)}) copy-start(f32[3,72,32,128]{3,2,1,0:T(8,128)S(1)} %get-tuple-element.28.state_in) | copy-start | bytes 10616836
  13.9 2.0 %copy-start.1 = (f32[3,72,32,128]{3,2,1,0:T(8,128)S(1)}, f32[3,72,32,128]{3,2,1,0:T(8,128)}, u32[]{:S(2)}) copy-start(f32[3,72,32,128]{3,2,1,0:T(8,128)} %copy-done) | copy-start | bytes 10616836
  17.3 4.9 %collective-permute-start.2 = (f32[3,72,128]{2,1,0:T(8,128)S(1)}, f32[3,72,128]{2,1,0:T(8,128)S(1)}, u32[]{:S(2)}, u32[]{:S(2)}) collective-permute-start(f32[3,72,128]{2,1,0:T(8,128)S(1)} %get-tuple-element.34), channel_id=1, source_target_pairs={{0,1},{1,0},{2,3},{3,2},{4,5},{5,4},{6,7},{7,6},{8,9},{9,8},{10,11... | collective-permute-start | bytes 331784 | tf_op jit(solution)/shard_map/ppermute | solution.py:345
  17.3 5.5 %collective-permute-start.3 = (f32[3,72,128]{2,1,0:T(8,128)S(1)}, f32[3,72,128]{2,1,0:T(8,128)S(1)}, u32[]{:S(2)}, u32[]{:S(2)}) collective-permute-start(f32[3,72,128]{2,1,0:T(8,128)S(1)} %get-tuple-element.35), channel_id=1, source_target_pairs={{0,7},{1,2},{2,1},{3,4},{4,3},{5,6},{6,5},{7,0},{8,15},{9,10},{10,... | collective-permute-start | bytes 331784 | tf_op jit(solution)/shard_map/ppermute | solution.py:345
  24.1 4.4 %collective-permute-start.4 = (f32[3,72,128]{2,1,0:T(8,128)S(1)}, f32[3,72,128]{2,1,0:T(8,128)S(1)}, u32[]{:S(2)}, u32[]{:S(2)}) collective-permute-start(f32[3,72,128]{2,1,0:T(8,128)S(1)} %get-tuple-element.37), channel_id=1, source_target_pairs={{0,1},{1,0},{2,3},{3,2},{4,5},{5,4},{6,7},{7,6},{8,9},{9,8},{10,11... | collective-permute-start | bytes 331784 | tf_op jit(solution)/shard_map/ppermute | solution.py:345
  24.3 5.2 %collective-permute-start.5 = (f32[3,72,128]{2,1,0:T(8,128)S(1)}, f32[3,72,128]{2,1,0:T(8,128)S(1)}, u32[]{:S(2)}, u32[]{:S(2)}) collective-permute-start(f32[3,72,128]{2,1,0:T(8,128)S(1)} %get-tuple-element.38), channel_id=1, source_target_pairs={{0,7},{1,2},{2,1},{3,4},{4,3},{5,6},{6,5},{7,0},{8,15},{9,10},{10,... | collective-permute-start | bytes 331784 | tf_op jit(solution)/shard_map/ppermute | solution.py:345
  31.6 1.3 %collective-permute-start.10 = (f32[64,128]{1,0:T(8,128)S(1)}, f32[64,128]{1,0:T(8,128)S(1)}, u32[]{:S(2)}, u32[]{:S(2)}) collective-permute-start(f32[64,128]{1,0:T(8,128)S(1)} %get-tuple-element.46), channel_id=1, source_target_pairs={{0,1},{1,0},{2,3},{3,2},{4,5},{5,4},{6,7},{7,6},{8,9},{9,8},{10,11... | collective-permute-start | bytes 98312 | tf_op jit(solution)/shard_map/ppermute | solution.py:349
  32.8 6.4 %collective-permute-start.11 = (f32[64,128]{1,0:T(8,128)S(1)}, f32[64,128]{1,0:T(8,128)S(1)}, u32[]{:S(2)}, u32[]{:S(2)}) collective-permute-start(f32[64,128]{1,0:T(8,128)S(1)} %add.79), channel_id=1, source_target_pairs={{0,2},{1,3},{2,0},{3,1},{4,6},{5,7},{6,4},{7,5},{8,10},{9,11},{10,... | collective-permute-start | bytes 98312 | tf_op jit(solution)/shard_map/ppermute | solution.py:349
  35.1 4.2 %collective-permute-start.12 = (f32[64,128]{1,0:T(8,128)S(1)}, f32[64,128]{1,0:T(8,128)S(1)}, u32[]{:S(2)}, u32[]{:S(2)}) collective-permute-start(f32[64,128]{1,0:T(8,128)S(1)} %add.79), channel_id=1, source_target_pairs={{0,4},{1,5},{2,6},{3,7},{4,0},{5,1},{6,2},{7,3},{8,12},{9,13},{10,... | collective-permute-start | bytes 98312 | tf_op jit(solution)/shard_map/ppermute | solution.py:349
  36.2 5.2 %collective-permute-start.13 = (f32[64,128]{1,0:T(8,128)S(1)}, f32[64,128]{1,0:T(8,128)S(1)}, u32[]{:S(2)}, u32[]{:S(2)}) collective-permute-start(f32[64,128]{1,0:T(8,128)S(1)} %add.79), channel_id=1, source_target_pairs={{0,6},{1,7},{2,4},{3,5},{4,2},{5,3},{6,0},{7,1},{8,14},{9,15},{10,... | collective-permute-start | bytes 98312 | tf_op jit(solution)/shard_map/ppermute | solution.py:349
  36.7 13.7 %collective-permute-start.6 = (f32[3,72,128]{2,1,0:T(8,128)S(1)}, f32[3,72,128]{2,1,0:T(8,128)S(1)}, u32[]{:S(2)}, u32[]{:S(2)}) collective-permute-start(f32[3,72,128]{2,1,0:T(8,128)S(1)} %get-tuple-element.40), channel_id=1, source_target_pairs={{0,1},{1,0},{2,3},{3,2},{4,5},{5,4},{6,7},{7,6},{8,9},{9,8},{10,11... | collective-permute-start | bytes 331784 | tf_op jit(solution)/shard_map/ppermute | solution.py:345
  36.7 13.7 %collective-permute-start.7 = (f32[3,72,128]{2,1,0:T(8,128)S(1)}, f32[3,72,128]{2,1,0:T(8,128)S(1)}, u32[]{:S(2)}, u32[]{:S(2)}) collective-permute-start(f32[3,72,128]{2,1,0:T(8,128)S(1)} %get-tuple-element.41), channel_id=1, source_target_pairs={{0,7},{1,2},{2,1},{3,4},{4,3},{5,6},{6,5},{7,0},{8,15},{9,10},{10,... | collective-permute-start | bytes 331784 | tf_op jit(solution)/shard_map/ppermute | solution.py:345
  41.4 11.0 %collective-permute-start.14 = (f32[64,128]{1,0:T(8,128)S(1)}, f32[64,128]{1,0:T(8,128)S(1)}, u32[]{:S(2)}, u32[]{:S(2)}) collective-permute-start(f32[64,128]{1,0:T(8,128)S(1)} %add_add_fusion.3), channel_id=1, source_target_pairs={{0,8},{8,0},{16,24},{24,16},{1,9},{9,1},{17,25},{25,17},{2,10},{10... | collective-permute-start | bytes 98312 | tf_op jit(solution)/shard_map/ppermute | solution.py:349
  45.9 6.4 %collective-permute-start.15 = (f32[64,128]{1,0:T(8,128)S(1)}, f32[64,128]{1,0:T(8,128)S(1)}, u32[]{:S(2)}, u32[]{:S(2)}) collective-permute-start(f32[64,128]{1,0:T(8,128)S(1)} %add_add_fusion.3), channel_id=1, source_target_pairs={{0,16},{8,24},{16,0},{24,8},{1,17},{9,25},{17,1},{25,9},{2,18},{10... | collective-permute-start | bytes 98312 | tf_op jit(solution)/shard_map/ppermute | solution.py:349
  47.2 5.7 %collective-permute-start.16 = (f32[64,128]{1,0:T(8,128)S(1)}, f32[64,128]{1,0:T(8,128)S(1)}, u32[]{:S(2)}, u32[]{:S(2)}) collective-permute-start(f32[64,128]{1,0:T(8,128)S(1)} %add_add_fusion.3), channel_id=1, source_target_pairs={{0,24},{8,16},{16,8},{24,0},{1,25},{9,17},{17,9},{25,1},{2,26},{10... | collective-permute-start | bytes 98312 | tf_op jit(solution)/shard_map/ppermute | solution.py:349
  51.7 8.0 %collective-permute-start.8 = (f32[3,72,128]{2,1,0:T(8,128)S(1)}, f32[3,72,128]{2,1,0:T(8,128)S(1)}, u32[]{:S(2)}, u32[]{:S(2)}) collective-permute-start(f32[3,72,128]{2,1,0:T(8,128)S(1)} %get-tuple-element.43), channel_id=1, source_target_pairs={{0,1},{1,0},{2,3},{3,2},{4,5},{5,4},{6,7},{7,6},{8,9},{9,8},{10,11... | collective-permute-start | bytes 331784 | tf_op jit(solution)/shard_map/ppermute | solution.py:345
  51.8 7.9 %collective-permute-start.9 = (f32[3,72,128]{2,1,0:T(8,128)S(1)}, f32[3,72,128]{2,1,0:T(8,128)S(1)}, u32[]{:S(2)}, u32[]{:S(2)}) collective-permute-start(f32[3,72,128]{2,1,0:T(8,128)S(1)} %get-tuple-element.44), channel_id=1, source_target_pairs={{0,7},{1,2},{2,1},{3,4},{4,3},{5,6},{6,5},{7,0},{8,15},{9,10},{10,... | collective-permute-start | bytes 331784 | tf_op jit(solution)/shard_map/ppermute | solution.py:345
  52.9 2.4 %collective-permute-start.17 = (f32[64,128]{1,0:T(8,128)S(1)}, f32[64,128]{1,0:T(8,128)S(1)}, u32[]{:S(2)}, u32[]{:S(2)}) collective-permute-start(f32[64,128]{1,0:T(8,128)S(1)} %add_add_fusion.2.mine_ref), channel_id=1, source_target_pairs={{0,1},{1,0},{2,3},{3,2},{4,5},{5,4},{6,7},{7,6},{8,9},{9,8},{10,11... | collective-permute-start | bytes 98312 | tf_op jit(solution)/shard_map/ppermute | solution.py:349
  62.6 1.3 %collective-permute-start.18 = (f32[64,128]{1,0:T(8,128)S(1)}, f32[64,128]{1,0:T(8,128)S(1)}, u32[]{:S(2)}, u32[]{:S(2)}) collective-permute-start(f32[64,128]{1,0:T(8,128)S(1)} %get-tuple-element.49), channel_id=1, source_target_pairs={{0,1},{1,0},{2,3},{3,2},{4,5},{5,4},{6,7},{7,6},{8,9},{9,8},{10,11... | collective-permute-start | bytes 98312 | tf_op jit(solution)/shard_map/ppermute | solution.py:349
  63.9 3.9 %collective-permute-start.19 = (f32[64,128]{1,0:T(8,128)S(1)}, f32[64,128]{1,0:T(8,128)S(1)}, u32[]{:S(2)}, u32[]{:S(2)}) collective-permute-start(f32[64,128]{1,0:T(8,128)S(1)} %add.86), channel_id=1, source_target_pairs={{0,2},{1,3},{2,0},{3,1},{4,6},{5,7},{6,4},{7,5},{8,10},{9,11},{10,... | collective-permute-start | bytes 98312 | tf_op jit(solution)/shard_map/ppermute | solution.py:349
  64.9 3.9 %collective-permute-start.20 = (f32[64,128]{1,0:T(8,128)S(1)}, f32[64,128]{1,0:T(8,128)S(1)}, u32[]{:S(2)}, u32[]{:S(2)}) collective-permute-start(f32[64,128]{1,0:T(8,128)S(1)} %add.86), channel_id=1, source_target_pairs={{0,4},{1,5},{2,6},{3,7},{4,0},{5,1},{6,2},{7,3},{8,12},{9,13},{10,... | collective-permute-start | bytes 98312 | tf_op jit(solution)/shard_map/ppermute | solution.py:349
  66.2 4.8 %collective-permute-start.21 = (f32[64,128]{1,0:T(8,128)S(1)}, f32[64,128]{1,0:T(8,128)S(1)}, u32[]{:S(2)}, u32[]{:S(2)}) collective-permute-start(f32[64,128]{1,0:T(8,128)S(1)} %add.86), channel_id=1, source_target_pairs={{0,6},{1,7},{2,4},{3,5},{4,2},{5,3},{6,0},{7,1},{8,14},{9,15},{10,... | collective-permute-start | bytes 98312 | tf_op jit(solution)/shard_map/ppermute | solution.py:349
  71.0 4.5 %collective-permute-start.22 = (f32[64,128]{1,0:T(8,128)S(1)}, f32[64,128]{1,0:T(8,128)S(1)}, u32[]{:S(2)}, u32[]{:S(2)}) collective-permute-start(f32[64,128]{1,0:T(8,128)S(1)} %add_add_fusion.1), channel_id=1, source_target_pairs={{0,8},{8,0},{16,24},{24,16},{1,9},{9,1},{17,25},{25,17},{2,10},{10... | collective-permute-start | bytes 98312 | tf_op jit(solution)/shard_map/ppermute | solution.py:349
  71.9 5.5 %collective-permute-start.23 = (f32[64,128]{1,0:T(8,128)S(1)}, f32[64,128]{1,0:T(8,128)S(1)}, u32[]{:S(2)}, u32[]{:S(2)}) collective-permute-start(f32[64,128]{1,0:T(8,128)S(1)} %add_add_fusion.1), channel_id=1, source_target_pairs={{0,16},{8,24},{16,0},{24,8},{1,17},{9,25},{17,1},{25,9},{2,18},{10... | collective-permute-start | bytes 98312 | tf_op jit(solution)/shard_map/ppermute | solution.py:349
  74.1 5.7 %collective-permute-start.24 = (f32[64,128]{1,0:T(8,128)S(1)}, f32[64,128]{1,0:T(8,128)S(1)}, u32[]{:S(2)}, u32[]{:S(2)}) collective-permute-start(f32[64,128]{1,0:T(8,128)S(1)} %add_add_fusion.1), channel_id=1, source_target_pairs={{0,24},{8,16},{16,8},{24,0},{1,25},{9,17},{17,9},{25,1},{2,26},{10... | collective-permute-start | bytes 98312 | tf_op jit(solution)/shard_map/ppermute | solution.py:349
  79.8 1.3 %collective-permute-start.25 = (f32[64,128]{1,0:T(8,128)S(1)}, f32[64,128]{1,0:T(8,128)S(1)}, u32[]{:S(2)}, u32[]{:S(2)}) collective-permute-start(f32[64,128]{1,0:T(8,128)S(1)} %add_add_fusion.mine_ref), channel_id=1, source_target_pairs={{0,1},{1,0},{2,3},{3,2},{4,5},{5,4},{6,7},{7,6},{8,9},{9,8},{10,11... | collective-permute-start | bytes 98312 | tf_op jit(solution)/shard_map/ppermute | solution.py:349

commit v2 on v1

--- a/solution.py
+++ b/solution.py
@@ -19,7 +19,7 @@
 LANES = 128
 FIELDS = 3
 HALO = STEPS * RENORMS
-TILES = 6
+TILES = 12
 VMEM_LIMIT = 16 * 1024 * 1024
 
 HBM = pl.BlockSpec(memory_space=pltpu.HBM)
@@ -37,6 +37,21 @@
 
 def lane_spread(block, lane):
     return jnp.broadcast_to(block[:, lane : lane + 1], (block.shape[0], LANES))
+
+
+def fetch(sources, places, sems):
+    copies = [
+        pltpu.make_async_copy(source, place, sems.at[i])
+        for i, (source, place) in enumerate(zip(sources, places))
+    ]
+    for copy in copies:
+        copy.start()
+    return copies
+
+
+def finish_all(copies):
+    for copy in copies:
+        copy.wait()
 
 
 def fields_of(sea_ref, levels_ref, current_ref):
@@ -52,24 +67,23 @@
     return (1 - odd_row, odd_row), (1 - odd_col, odd_col)
 
 
-def pack_rows(par, t_ref, sea_ref, levels_ref, current_ref, row_a, row_b, wide, sems):
+def pack_rows(
+    par, t_ref, sea_ref, levels_ref, current_ref, row_a, row_b, sea, levels, current, wide, sems, field_sems
+):
     comps, rows, cols, _ = t_ref.shape
     norths, _ = sides_of(par)
-    copies = []
-    for slot, msg in ((0, row_a), (1, row_b)):
-        for comp in range(comps):
-            copies.append(
-                pltpu.make_async_copy(
-                    t_ref.at[comp, pl.ds(norths[slot] * (rows - HALO), HALO)],
-                    msg.at[pl.ds(comp * HALO, HALO)],
-                    sems.at[slot * comps + comp],
-                )
-            )
-            copies[-1].start()
+    field_copies = fetch((sea_ref, levels_ref, current_ref), (sea, levels, current), field_sems)
+    slots = [(slot, msg, comp) for slot, msg in ((0, row_a), (1, row_b)) for comp in range(comps)]
+    copies = fetch(
+        [t_ref.at[comp, pl.ds(norths[slot] * (rows - HALO), HALO)] for slot, _, comp in slots],
+        [msg.at[pl.ds(comp * HALO, HALO)] for _, msg, comp in slots],
+        sems,
+    )
     lane = lax.broadcasted_iota(jnp.int32, (cols, LANES), 1)
     wide[...] = jnp.zeros_like(wide)
     packed = [jnp.zeros((cols, LANES), jnp.float32)] * 2
-    for field, value in enumerate(fields_of(sea_ref, levels_ref, current_ref)):
+    finish_all(field_copies)
+    for field, value in enumerate(fields_of(sea, levels, current)):
         wide[:, pl.ds(0, rows)] = value
         whole = wide[...]
         for north in (0, 1):
@@ -79,23 +93,15 @@
             packed[north] = jnp.where(here, moved, packed[north])
     for slot, msg in ((0, row_a), (1, row_b)):
         msg[comps * HALO] = jnp.where(norths[slot] == 1, packed[1], packed[0])
-    for copy in copies:
-        copy.wait()
-
-
-def spread_fields(t_ref, sea_ref, levels_ref, current_ref, state, coef, sems):
-    comps, rows, _, _ = t_ref.shape
-    copies = [
-        pltpu.make_async_copy(t_ref.at[comp], state.at[comp, pl.ds(HALO, rows)], sems.at[comp])
-        for comp in range(comps)
-    ]
-    for copy in copies:
-        copy.start()
-    for field, value in enumerate(fields_of(sea_ref, levels_ref, current_ref)):
+    finish_all(copies)
+
+
+def spread_fields(sea_ref, levels_ref, current_ref, coef, sea, levels, current, sems):
+    rows = sea_ref.shape[1]
+    finish_all(fetch((sea_ref, levels_ref, current_ref), (sea, levels, current), sems))
+    for field, value in enumerate(fields_of(sea, levels, current)):
         for row in range(rows):
             coef[field, HALO + row] = lane_spread(value, row)
-    for copy in copies:
-        copy.wait()
 
 
 def pack_columns(par, state, col_a, col_b):
@@ -109,9 +115,15 @@
                 msg[comp, pl.ds(row, SUB), :] = flat[pl.ds(at, SUB, stride=cols), :]
 
 
-def join_rows(par, state_in, coef_in, row_a, row_b, state, coef, col_a, col_b):
+def join_rows(par, t_ref, coef_in, row_a, row_b, state, coef, col_a, col_b, sems):
     comps, tall, _, _ = state.shape
+    rows = tall - 2 * HALO
     norths, _ = sides_of(par)
+    copies = fetch(
+        [t_ref.at[comp] for comp in range(comps)],
+        [state.at[comp, pl.ds(HALO, rows)] for comp in range(comps)],
+        sems,
+    )
     for slot, msg in ((0, row_a), (1, row_b)):
         line = norths[slot] * (tall - HALO)
         fields = msg[comps * HALO]
@@ -120,6 +132,7 @@
                 state[comp, line + h] = msg[comp * HALO + h]
             for field in range(FIELDS):
                 coef[field, line + h] = lane_spread(fields, field * SUB + h)
+    finish_all(copies)
     pack_columns(par, state, col_a, col_b)
 
 
@@ -364,10 +377,29 @@
     return value
 
 
-def sum_devices(kept, sent):
+def sum_groups(value, axis, low_bits, bits):
+    count = lax.axis_size(axis)
+    low, size = 1 << low_bits, 1 << bits
+    groups = [
+        [high * low * size + i * low + rest for i in range(size)]
+        for high in range(count // (low * size))
+        for rest in range(low)
+    ]
+    copies = jnp.broadcast_to(value, (size,) + value.shape)
+    if size == count:
+        groups = None
+    got = lax.all_to_all(copies, axis, 0, 0, axis_index_groups=groups)
+    return jnp.sum(got, axis=0)
+
+
+def sum_devices(kept, sent, grouped):
     mine = kept + swapped(sent, "col", 1)
-    mine = sum_over(mine, "col", 1)
-    mine = sum_over(mine, "row", 0)
+    if grouped:
+        mine = sum_groups(mine, "col", 1, lax.axis_size("col").bit_length() - 2)
+        mine = sum_groups(mine, "row", 0, lax.axis_size("row").bit_length() - 1)
+    else:
+        mine = sum_over(mine, "col", 1)
+        mine = sum_over(mine, "row", 0)
     return mine, swapped(mine, "col", 1)
 
 
@@ -411,34 +443,43 @@
     def swap_columns(packed):
         return swap_pairs(*packed, "col", True)
 
-    source = pltpu.with_memory_space_constraint(tangents, pltpu.HBM)
-    fields = (sea_mask.T, levels.T, current.T)
+    source, *fields = (
+        pltpu.with_memory_space_constraint(x, pltpu.HBM)
+        for x in (tangents, sea_mask.T, levels.T, current.T)
+    )
+    upright = [pltpu.VMEM(x.shape, x.dtype) for x in fields]
     packed = call(
         pack_rows,
         rows_sent,
         par,
         source,
         *fields,
-        specs=[SMEM, HBM] + [VMEM] * 3,
-        scratch=[pltpu.VMEM((cols, LANES), jnp.float32), pltpu.SemaphoreType.DMA((2 * comps,))],
+        specs=[SMEM] + [HBM] * 4,
+        scratch=upright
+        + [
+            pltpu.VMEM((cols, LANES), jnp.float32),
+            pltpu.SemaphoreType.DMA((2 * comps,)),
+            pltpu.SemaphoreType.DMA((FIELDS,)),
+        ],
     )
     row_halos = swap_pairs(*packed, "row", False)
-    state, coef = call(
+    coef = call(
         spread_fields,
-        (block, shape_of(FIELDS, tall, cols, LANES)),
-        source,
+        (shape_of(FIELDS, tall, cols, LANES),),
         *fields,
-        specs=[HBM] + [VMEM] * 3,
-        scratch=[pltpu.SemaphoreType.DMA((comps,))],
-    )
+        specs=[HBM] * 3,
+        scratch=upright + [pltpu.SemaphoreType.DMA((FIELDS,))],
+    )[0]
     state, coef, *packed = call(
         join_rows,
         (block, shape_of(FIELDS, tall, cols, LANES)) + columns,
         par,
-        state,
+        source,
         coef,
         *row_halos,
-        aliases={1: 0, 2: 1},
+        specs=[SMEM, HBM] + [VMEM] * 3,
+        scratch=[pltpu.SemaphoreType.DMA((comps,))],
+        aliases={2: 1},
     )
     logs = jnp.zeros((1, modes), jnp.float32)
     for step in range(STEPS * RENORMS):
@@ -457,7 +498,7 @@
                 scratch=[square],
                 aliases={1: 0},
             )
-            mine, other = sum_devices(kept, sent)
+            mine, other = sum_devices(kept, sent, False)
             inverse, logs = call(
                 factor_only,
                 (shape_of(modes, modes), shape_of(1, modes)),
@@ -482,7 +523,7 @@
         scratch=[factor, square],
         aliases={1: 0},
     )
-    mine, other = sum_devices(kept, sent)
+    mine, other = sum_devices(kept, sent, True)
     out, logs = call(
         finish,
         (tiled, shape_of(1, modes)),

time: 89.5 us -> 91.1 us (1.018)
  blocking collectives: 0 us -> 17.4 us
  waiting for transfers between devices: 15.9 us -> 8.15 us
  starting transfers between devices: 32.8 us -> 25.5 us
  local copies, waits for them, and re-layouts: 5.95 us -> 3.65 us
  Pallas kernels: 33.2 us -> 34.7 us
    all_to_all x0 -> x2, blocking collectives: none -> 17.4 us  [sum_groups(): got = lax.all_to_all(copies, axis, 0, 0, axis_index_groups=groups)]
    ppermute x16 -> x10, waiting for transfers between devices: 13.8 us -> 4.24 us  [swapped(): lax.ppermute(value, axis, [(i, i ^ mask) for i in range(lax.axis_size(axi...]
    ppermute x16 -> x10, starting transfers between devices: 20 us -> 11.2 us  [swapped(): lax.ppermute(value, axis, [(i, i ^ mask) for i in range(lax.axis_size(axi...]
    unnamed x10 -> x4, local copies, waits for them, and re-layouts: 5.88 us -> 3.55 us
    ppermute x5, waiting for transfers between devices: 0.53 us -> 2.26 us  [swap_pairs(): lax.ppermute(near_value, axis, near)]
    ppermute x5, starting transfers between devices: 9.33 us -> 10.9 us  [swap_pairs(): lax.ppermute(far_value, axis, far)]
    pallas_call x13, Pallas kernels: 33.2 us -> 34.7 us  [call(): pl.pallas_call(kernel, out_shape=outs, in_specs=specs or [SMEM] + [VMEM]...]
  transfers between devices with their start and end apart: 26 -> 20, of which waited for: 13 -> 8; matrix products, arithmetic and copies ran while one was open for 0% -> 0% of each run, Pallas kernels for 17% -> 17%
where the time goes in v2:
time: 91.1 us; the launch traced here: 90.6 us
  Pallas kernels  34.7 us (38%)
  starting transfers between devices  25.5 us (28%)
  blocking collectives  17.4 us (19%)
  waiting for transfers between devices  8.15 us (9%)
  local copies, waits for them, and re-layouts  3.65 us (4%)
  between operations  1.02 us (1%)
    pallas_call x13, Pallas kernels, call(): pl.pallas_call(kernel, out_shape=outs, in_specs=specs or [SMEM] + [VMEM]...  34.7 us
    all_to_all x2, blocking collectives, sum_groups(): got = lax.all_to_all(copies, axis, 0, 0, axis_index_groups=groups)  17.4 us
    ppermute x10, starting transfers between devices, swapped(): lax.ppermute(value, axis, [(i, i ^ mask) for i in range(lax.axis_size(axi...  11.2 us
    ppermute x5, starting transfers between devices, swap_pairs(): lax.ppermute(far_value, axis, far)  10.9 us
    ppermute x10, waiting for transfers between devices, swapped(): lax.ppermute(value, axis, [(i, i ^ mask) for i in range(lax.axis_size(axi...  4.24 us
    unnamed x4, local copies, waits for them, and re-layouts  3.55 us
    ppermute x5, starting transfers between devices, swap_pairs(): lax.ppermute(near_value, axis, near)  3.42 us
    ppermute x5, waiting for transfers between devices, swap_pairs(): lax.ppermute(near_value, axis, near)  2.26 us
  transfers between devices with their start and end apart: 20, of which 8 were waited for; matrix products, arithmetic and copies ran while one was open for 0% of the time, Pallas kernels for 17%

profile of v2, /device:TPU:0, one launch (start us, length us, event | category | flops | bytes accessed | tf_op | source)
XLA Modules:
  0.0 90.6 jit_solution(7430367740355572999)
XLA Ops:
  0.7 2.4 %shard_map.60 = (f32[13,32,128]{2,1,0:T(8,128)}, f32[13,32,128]{2,1,0:T(8,128)}) custom-call(s32[2]{0:T(128)S(1)} %pad_add_fusion.par, f32[3,64,32,128]{3,2,1,0:T(8,128)} %t_ref.3, s32[32,64]{1,0:T(8,128)} %bitcast.7, s32[32,64]{1,0:T(8,128)} %bitcast.9, f32[32,64]{1,0:T(8,128)} %bitcast.11), custom_call_target="tpu_custom_call" | custom-call | tf_op jit(solution)/shard_map/pallas_call | solution.py:429
  3.1 3.1 %collective-permute-start = (f32[13,32,128]{2,1,0:T(8,128)}, f32[13,32,128]{2,1,0:T(8,128)}, u32[]{:S(2)}, u32[]{:S(2)}) collective-permute-start(f32[13,32,128]{2,1,0:T(8,128)} %get-tuple-element.26), channel_id=1, source_target_pairs={{0,8},{8,0},{16,24},{24,16},{1,9},{9,1},{17,25},{25,17},{2,10},{10... | collective-permute-start | bytes 638984 | tf_op jit(solution)/shard_map/ppermute | solution.py:358
  6.2 1.4 %collective-permute-start.1 = (f32[13,32,128]{2,1,0:T(8,128)}, f32[13,32,128]{2,1,0:T(8,128)}, u32[]{:S(2)}, u32[]{:S(2)}) collective-permute-start(f32[13,32,128]{2,1,0:T(8,128)} %get-tuple-element.27), channel_id=1, source_target_pairs={{8,16},{16,8},{9,17},{17,9},{10,18},{18,10},{11,19},{19,11},{12,20... | collective-permute-start | bytes 638984 | tf_op jit(solution)/shard_map/ppermute | solution.py:358
  7.6 2.0 %shard_map.59.coef_in = f32[3,72,32,128]{3,2,1,0:T(8,128)S(1)} custom-call(s32[32,64]{1,0:T(8,128)} %bitcast.8, s32[32,64]{1,0:T(8,128)} %bitcast.10, f32[32,64]{1,0:T(8,128)} %bitcast.12), custom_call_target="tpu_custom_call" | custom-call | tf_op jit(solution)/shard_map/pallas_call | solution.py:429
  9.5 2.2 %collective-permute-done.row_a = f32[13,32,128]{2,1,0:T(8,128)} collective-permute-done((f32[13,32,128]{2,1,0:T(8,128)}, f32[13,32,128]{2,1,0:T(8,128)}, u32[]{:S(2)}, u32[]{:S(2)}) %collective-permute-start) | collective-permute-done | bytes 213024 | tf_op jit(solution)/shard_map/ppermute | solution.py:358
  11.8 3.2 %shard_map.61 = (f32[3,72,32,128]{3,2,1,0:T(8,128)S(1)}, f32[3,72,32,128]{3,2,1,0:T(8,128)S(1)}, f32[3,72,128]{2,1,0:T(8,128)S(1)}, f32[3,72,128]{2,1,0:T(8,128)S(1)}) custom-call(s32[2]{0:T(128)S(1)} %pad_add_fusion.par, f32[3,64,32,128]{3,2,1,0:T(8,128)} %t_ref.3, f32[3,72,32,128]{3,2,1,0:T(8,128)S(1)} %shard_map.59.coef_in, ...), custom_call_target="tpu_custom_call", output_to_operand_aliasing={{1}: (2, {})} | custom-call | tf_op jit(solution)/shard_map/pallas_call | solution.py:429
  15.0 2.7 %collective-permute-start.3 = (f32[3,72,128]{2,1,0:T(8,128)S(1)}, f32[3,72,128]{2,1,0:T(8,128)S(1)}, u32[]{:S(2)}, u32[]{:S(2)}) collective-permute-start(f32[3,72,128]{2,1,0:T(8,128)S(1)} %get-tuple-element.31), channel_id=1, source_target_pairs={{0,7},{1,2},{2,1},{3,4},{4,3},{5,6},{6,5},{7,0},{8,15},{9,10},{10,... | collective-permute-start | bytes 331784 | tf_op jit(solution)/shard_map/ppermute | solution.py:358
  17.9 2.0 %shard_map.62.state_in = f32[3,72,32,128]{3,2,1,0:T(8,128)S(1)} custom-call(f32[3,72,32,128]{3,2,1,0:T(8,128)S(1)} %get-tuple-element.28.t_ref, f32[3,72,32,128]{3,2,1,0:T(8,128)S(1)} %get-tuple-element.29.coef_ref, f32[72,128]{1,0:T(8,128)S(1)} %broadcast_in_dim.15.spin_ref), custom_call_target="tpu_custom_call" | custom-call | tf_op jit(solution)/shard_map/pallas_call | solution.py:429
  20.6 1.3 %shard_map.63 = (f32[3,72,32,128]{3,2,1,0:T(8,128)S(1)}, f32[3,72,128]{2,1,0:T(8,128)S(1)}, f32[3,72,128]{2,1,0:T(8,128)S(1)}) custom-call(s32[2]{0:T(128)S(1)} %pad_add_fusion.par, f32[3,72,32,128]{3,2,1,0:T(8,128)S(1)} %shard_map.62.state_in, f32[3,72,32,128]{3,2,1,0:T(8,128)S(1)} %get-tuple-element.29.coef_ref, ...), custom_call_target="tpu_custom_call", output_to_operand_aliasing={{0}: (1, {})} | custom-call | tf_op jit(solution)/shard_map/pallas_call | solution.py:429
  22.0 2.2 %collective-permute-start.5 = (f32[3,72,128]{2,1,0:T(8,128)S(1)}, f32[3,72,128]{2,1,0:T(8,128)S(1)}, u32[]{:S(2)}, u32[]{:S(2)}) collective-permute-start(f32[3,72,128]{2,1,0:T(8,128)S(1)} %get-tuple-element.34), channel_id=1, source_target_pairs={{0,7},{1,2},{2,1},{3,4},{4,3},{5,6},{6,5},{7,0},{8,15},{9,10},{10,... | collective-permute-start | bytes 331784 | tf_op jit(solution)/shard_map/ppermute | solution.py:358
  24.2 2.0 %shard_map.64.state_in = f32[3,72,32,128]{3,2,1,0:T(8,128)S(1)} custom-call(f32[3,72,32,128]{3,2,1,0:T(8,128)S(1)} %get-tuple-element.32.t_ref, f32[3,72,32,128]{3,2,1,0:T(8,128)S(1)} %get-tuple-element.29.coef_ref, f32[72,128]{1,0:T(8,128)S(1)} %broadcast_in_dim.15.spin_ref), custom_call_target="tpu_custom_call" | custom-call | tf_op jit(solution)/shard_map/pallas_call | solution.py:429
  26.2 1.0 %collective-permute-done.5.b = f32[3,72,128]{2,1,0:T(8,128)S(1)} collective-permute-done((f32[3,72,128]{2,1,0:T(8,128)S(1)}, f32[3,72,128]{2,1,0:T(8,128)S(1)}, u32[]{:S(2)}, u32[]{:S(2)}) %collective-permute-start.5) | collective-permute-done | bytes 110624 | tf_op jit(solution)/shard_map/ppermute | solution.py:358
  27.2 2.1 %shard_map.65 = (f32[3,72,32,128]{3,2,1,0:T(8,128)S(1)}, f32[3,72,128]{2,1,0:T(8,128)S(1)}, f32[3,72,128]{2,1,0:T(8,128)S(1)}, f32[64,128]{1,0:T(8,128)S(1)}, f32[64,128]{1,0:T(8,128)S(1)}) custom-call(s32[2]{0:T(128)S(1)} %pad_add_fusion.par, f32[3,72,32,128]{3,2,1,0:T(8,128)S(1)} %shard_map.64.state_in, ...), custom_call_target="tpu_custom_call", output_to_operand_aliasing={{0}: (1, {})} | custom-call | tf_op jit(solution)/shard_map/pallas_call | solution.py:429
  29.6 1.0 %collective-permute-done.10 = f32[64,128]{1,0:T(8,128)S(1)} collective-permute-done((f32[64,128]{1,0:T(8,128)S(1)}, f32[64,128]{1,0:T(8,128)S(1)}, u32[]{:S(2)}, u32[]{:S(2)}) %collective-permute-start.10) | collective-permute-done | bytes 32800 | tf_op jit(solution)/shard_map/ppermute | solution.py:362
  30.6 2.8 %collective-permute-start.13 = (f32[64,128]{1,0:T(8,128)S(1)}, f32[64,128]{1,0:T(8,128)S(1)}, u32[]{:S(2)}, u32[]{:S(2)}) collective-permute-start(f32[64,128]{1,0:T(8,128)S(1)} %add.61), channel_id=1, source_target_pairs={{0,6},{1,7},{2,4},{3,5},{4,2},{5,3},{6,0},{7,1},{8,14},{9,15},{10,... | collective-permute-start | bytes 98312 | tf_op jit(solution)/shard_map/ppermute | solution.py:362
  33.4 0.9 collective-permute-start.12
  34.5 2.5 %collective-permute-start.7 = (f32[3,72,128]{2,1,0:T(8,128)S(1)}, f32[3,72,128]{2,1,0:T(8,128)S(1)}, u32[]{:S(2)}, u32[]{:S(2)}) collective-permute-start(f32[3,72,128]{2,1,0:T(8,128)S(1)} %get-tuple-element.37), channel_id=1, source_target_pairs={{0,7},{1,2},{2,1},{3,4},{4,3},{5,6},{6,5},{7,0},{8,15},{9,10},{10,... | collective-permute-start | bytes 331784 | tf_op jit(solution)/shard_map/ppermute | solution.py:358
  37.3 0.9 collective-permute-done.11
  38.2 3.7 %collective-permute-start.16 = (f32[64,128]{1,0:T(8,128)S(1)}, f32[64,128]{1,0:T(8,128)S(1)}, u32[]{:S(2)}, u32[]{:S(2)}) collective-permute-start(f32[64,128]{1,0:T(8,128)S(1)} %add_add_fusion.1), channel_id=1, source_target_pairs={{0,24},{8,16},{16,8},{24,0},{1,25},{9,17},{17,9},{25,1},{2,26},{10... | collective-permute-start | bytes 98312 | tf_op jit(solution)/shard_map/ppermute | solution.py:362
  41.9 2.5 %collective-permute-start.15 = (f32[64,128]{1,0:T(8,128)S(1)}, f32[64,128]{1,0:T(8,128)S(1)}, u32[]{:S(2)}, u32[]{:S(2)}) collective-permute-start(f32[64,128]{1,0:T(8,128)S(1)} %add_add_fusion.1), channel_id=1, source_target_pairs={{0,16},{8,24},{16,0},{24,8},{1,17},{9,25},{17,1},{25,9},{2,18},{10... | collective-permute-start | bytes 98312 | tf_op jit(solution)/shard_map/ppermute | solution.py:362
  44.6 1.9 %shard_map.66.state_in = f32[3,72,32,128]{3,2,1,0:T(8,128)S(1)} custom-call(f32[3,72,32,128]{3,2,1,0:T(8,128)S(1)} %get-tuple-element.35.t_ref, f32[3,72,32,128]{3,2,1,0:T(8,128)S(1)} %get-tuple-element.29.coef_ref, f32[72,128]{1,0:T(8,128)S(1)} %broadcast_in_dim.15.spin_ref), custom_call_target="tpu_custom_call" | custom-call | tf_op jit(solution)/shard_map/pallas_call | solution.py:429
  46.5 1.3 %shard_map.67 = (f32[3,72,32,128]{3,2,1,0:T(8,128)S(1)}, f32[3,72,128]{2,1,0:T(8,128)S(1)}, f32[3,72,128]{2,1,0:T(8,128)S(1)}) custom-call(s32[2]{0:T(128)S(1)} %pad_add_fusion.par, f32[3,72,32,128]{3,2,1,0:T(8,128)S(1)} %shard_map.66.state_in, f32[3,72,32,128]{3,2,1,0:T(8,128)S(1)} %get-tuple-element.29.coef_ref, ...), custom_call_target="tpu_custom_call", output_to_operand_aliasing={{0}: (1, {})} | custom-call | tf_op jit(solution)/shard_map/pallas_call | solution.py:429
  47.9 2.1 %collective-permute-start.9 = (f32[3,72,128]{2,1,0:T(8,128)S(1)}, f32[3,72,128]{2,1,0:T(8,128)S(1)}, u32[]{:S(2)}, u32[]{:S(2)}) collective-permute-start(f32[3,72,128]{2,1,0:T(8,128)S(1)} %get-tuple-element.40), channel_id=1, source_target_pairs={{0,7},{1,2},{2,1},{3,4},{4,3},{5,6},{6,5},{7,0},{8,15},{9,10},{10,... | collective-permute-start | bytes 331784 | tf_op jit(solution)/shard_map/ppermute | solution.py:358
  50.0 1.8 %shard_map.68.state_in = f32[3,72,32,128]{3,2,1,0:T(8,128)S(1)} custom-call(f32[3,72,32,128]{3,2,1,0:T(8,128)S(1)} %get-tuple-element.38.t_ref, f32[3,72,32,128]{3,2,1,0:T(8,128)S(1)} %get-tuple-element.29.coef_ref, f32[72,128]{1,0:T(8,128)S(1)} %broadcast_in_dim.15.spin_ref), custom_call_target="tpu_custom_call" | custom-call | tf_op jit(solution)/shard_map/pallas_call | solution.py:429
  51.9 4.4 %shard_map.69 = (f32[128,128]{1,0:T(8,128)S(1)}, f32[1,128]{1,0:T(1,128)S(1)}) custom-call(s32[2]{0:T(128)S(1)} %pad_add_fusion.par, f32[64,128]{1,0:T(8,128)S(1)} %add_add_fusion.mine_ref, f32[64,128]{1,0:T(8,128)S(1)} %collective-permute-done.17.other_ref, f32[1,128]{1,0:T(1,128)S(1)} %broadcast_in_dim.16.prior_ref), custom_call_target="tpu_custom_call" | custom-call | tf_op jit(solution)/shard_map/pallas_call | solution.py:429
  56.3 2.8 %shard_map.70 = (f32[3,72,32,128]{3,2,1,0:T(8,128)S(1)}, f32[12,512,128]{2,1,0:T(8,128)S(1)}, f32[64,128]{1,0:T(8,128)S(1)}, f32[64,128]{1,0:T(8,128)S(1)}) custom-call(s32[2]{0:T(128)S(1)} %pad_add_fusion.par, f32[3,72,32,128]{3,2,1,0:T(8,128)S(1)} %shard_map.68.state_in, ...), custom_call_target="tpu_custom_call", output_to_operand_aliasing={{0}: (1, {})} | custom-call | tf_op jit(solution)/shard_map/pallas_call | solution.py:429
  59.1 1.7 %copy-done = f32[12,512,128]{2,1,0:T(8,128)} copy-done((f32[12,512,128]{2,1,0:T(8,128)}, f32[12,512,128]{2,1,0:T(8,128)S(1)}, u32[]{:S(2)}) %copy-start) | copy-done | bytes 3145752
  62.2 7.5 %all_to_all.10 = f32[4,64,128]{2,1,0:T(8,128)S(1)} all-to-all(f32[4,64,128]{2,1,0:T(8,128)S(1)} %broadcast_in_dim.17), channel_id=1, replica_groups={{0,2,4,6},{1,3,5,7},{8,10,12,14},{9,11,13,15},{16,18,20,22},{17,19,21,2..., dimensions={0} | all-to-all | bytes 262144 | tf_op jit(solution)/shard_map/all_to_all | solution.py:391
  69.7 9.9 %all_to_all.11 = f32[4,64,128]{2,1,0:T(8,128)S(1)} all-to-all(f32[4,64,128]{2,1,0:T(8,128)S(1)} %broadcast_in_dim.18), channel_id=1, replica_groups=mesh['row'=4,'col'=8] {'row'}, dimensions={0} | all-to-all | bytes 262144 | tf_op jit(solution)/shard_map/all_to_all | solution.py:391
  79.7 1.2 %collective-permute-done.19.other_ref = f32[64,128]{1,0:T(8,128)S(1)} collective-permute-done((f32[64,128]{1,0:T(8,128)S(1)}, f32[64,128]{1,0:T(8,128)S(1)}, u32[]{:S(2)}, u32[]{:S(2)}) %collective-permute-start.19) | collective-permute-done | bytes 32800 | tf_op jit(solution)/shard_map/ppermute | solution.py:362
  80.9 1.9 %copy-done.1 = f32[12,512,128]{2,1,0:T(8,128)S(1)} copy-done((f32[12,512,128]{2,1,0:T(8,128)S(1)}, f32[12,512,128]{2,1,0:T(8,128)}, u32[]{:S(2)}) %copy-start.1) | copy-done | bytes 3145752
  82.8 7.7 %shard_map.71 = (f32[12,512,128]{2,1,0:T(8,128)}, f32[1,128]{1,0:T(1,128)}) custom-call(s32[2]{0:T(128)S(1)} %pad_add_fusion.par, f32[64,128]{1,0:T(8,128)S(1)} %reduce_sum.19.mine_ref, f32[64,128]{1,0:T(8,128)S(1)} %collective-permute-done.19.other_ref, f32[1,128]{1,0:T(1,128)S(1)} %get-tuple-element.46.prior_ref, f32[12,512,128]{2,1,0:T(8,128)S(1)} %copy-done.1), custom_call_target="tpu_custom_call" | custom-call | tf_op jit(solution)/shard_map/pallas_call | solution.py:429
  (39 shorter events, 3.9 us)
Async XLA Ops:
  3.1 8.7 %collective-permute-start = (f32[13,32,128]{2,1,0:T(8,128)}, f32[13,32,128]{2,1,0:T(8,128)}, u32[]{:S(2)}, u32[]{:S(2)}) collective-permute-start(f32[13,32,128]{2,1,0:T(8,128)} %get-tuple-element.26), channel_id=1, source_target_pairs={{0,8},{8,0},{16,24},{24,16},{1,9},{9,1},{17,25},{25,17},{2,10},{10... | collective-permute-start | bytes 638984 | tf_op jit(solution)/shard_map/ppermute | solution.py:358
  6.2 5.6 %collective-permute-start.1 = (f32[13,32,128]{2,1,0:T(8,128)}, f32[13,32,128]{2,1,0:T(8,128)}, u32[]{:S(2)}, u32[]{:S(2)}) collective-permute-start(f32[13,32,128]{2,1,0:T(8,128)} %get-tuple-element.27), channel_id=1, source_target_pairs={{8,16},{16,8},{9,17},{17,9},{10,18},{18,10},{11,19},{19,11},{12,20... | collective-permute-start | bytes 638984 | tf_op jit(solution)/shard_map/ppermute | solution.py:358
  15.0 4.9 %collective-permute-start.2 = (f32[3,72,128]{2,1,0:T(8,128)S(1)}, f32[3,72,128]{2,1,0:T(8,128)S(1)}, u32[]{:S(2)}, u32[]{:S(2)}) collective-permute-start(f32[3,72,128]{2,1,0:T(8,128)S(1)} %get-tuple-element.30), channel_id=1, source_target_pairs={{0,1},{1,0},{2,3},{3,2},{4,5},{5,4},{6,7},{7,6},{8,9},{9,8},{10,11... | collective-permute-start | bytes 331784 | tf_op jit(solution)/shard_map/ppermute | solution.py:358
  15.0 5.5 %collective-permute-start.3 = (f32[3,72,128]{2,1,0:T(8,128)S(1)}, f32[3,72,128]{2,1,0:T(8,128)S(1)}, u32[]{:S(2)}, u32[]{:S(2)}) collective-permute-start(f32[3,72,128]{2,1,0:T(8,128)S(1)} %get-tuple-element.31), channel_id=1, source_target_pairs={{0,7},{1,2},{2,1},{3,4},{4,3},{5,6},{6,5},{7,0},{8,15},{9,10},{10,... | collective-permute-start | bytes 331784 | tf_op jit(solution)/shard_map/ppermute | solution.py:358
  21.8 4.4 %collective-permute-start.4 = (f32[3,72,128]{2,1,0:T(8,128)S(1)}, f32[3,72,128]{2,1,0:T(8,128)S(1)}, u32[]{:S(2)}, u32[]{:S(2)}) collective-permute-start(f32[3,72,128]{2,1,0:T(8,128)S(1)} %get-tuple-element.33), channel_id=1, source_target_pairs={{0,1},{1,0},{2,3},{3,2},{4,5},{5,4},{6,7},{7,6},{8,9},{9,8},{10,11... | collective-permute-start | bytes 331784 | tf_op jit(solution)/shard_map/ppermute | solution.py:358
  22.0 5.2 %collective-permute-start.5 = (f32[3,72,128]{2,1,0:T(8,128)S(1)}, f32[3,72,128]{2,1,0:T(8,128)S(1)}, u32[]{:S(2)}, u32[]{:S(2)}) collective-permute-start(f32[3,72,128]{2,1,0:T(8,128)S(1)} %get-tuple-element.34), channel_id=1, source_target_pairs={{0,7},{1,2},{2,1},{3,4},{4,3},{5,6},{6,5},{7,0},{8,15},{9,10},{10,... | collective-permute-start | bytes 331784 | tf_op jit(solution)/shard_map/ppermute | solution.py:358
  29.3 1.3 %collective-permute-start.10 = (f32[64,128]{1,0:T(8,128)S(1)}, f32[64,128]{1,0:T(8,128)S(1)}, u32[]{:S(2)}, u32[]{:S(2)}) collective-permute-start(f32[64,128]{1,0:T(8,128)S(1)} %get-tuple-element.42), channel_id=1, source_target_pairs={{0,1},{1,0},{2,3},{3,2},{4,5},{5,4},{6,7},{7,6},{8,9},{9,8},{10,11... | collective-permute-start | bytes 98312 | tf_op jit(solution)/shard_map/ppermute | solution.py:362
  30.6 6.4 %collective-permute-start.13 = (f32[64,128]{1,0:T(8,128)S(1)}, f32[64,128]{1,0:T(8,128)S(1)}, u32[]{:S(2)}, u32[]{:S(2)}) collective-permute-start(f32[64,128]{1,0:T(8,128)S(1)} %add.61), channel_id=1, source_target_pairs={{0,6},{1,7},{2,4},{3,5},{4,2},{5,3},{6,0},{7,1},{8,14},{9,15},{10,... | collective-permute-start | bytes 98312 | tf_op jit(solution)/shard_map/ppermute | solution.py:362
  33.4 3.9 %collective-permute-start.12 = (f32[64,128]{1,0:T(8,128)S(1)}, f32[64,128]{1,0:T(8,128)S(1)}, u32[]{:S(2)}, u32[]{:S(2)}) collective-permute-start(f32[64,128]{1,0:T(8,128)S(1)} %add.61), channel_id=1, source_target_pairs={{0,4},{1,5},{2,6},{3,7},{4,0},{5,1},{6,2},{7,3},{8,12},{9,13},{10,... | collective-permute-start | bytes 98312 | tf_op jit(solution)/shard_map/ppermute | solution.py:362
  34.3 3.9 %collective-permute-start.11 = (f32[64,128]{1,0:T(8,128)S(1)}, f32[64,128]{1,0:T(8,128)S(1)}, u32[]{:S(2)}, u32[]{:S(2)}) collective-permute-start(f32[64,128]{1,0:T(8,128)S(1)} %add.61), channel_id=1, source_target_pairs={{0,2},{1,3},{2,0},{3,1},{4,6},{5,7},{6,4},{7,5},{8,10},{9,11},{10,... | collective-permute-start | bytes 98312 | tf_op jit(solution)/shard_map/ppermute | solution.py:362
  34.5 12.0 %collective-permute-start.6 = (f32[3,72,128]{2,1,0:T(8,128)S(1)}, f32[3,72,128]{2,1,0:T(8,128)S(1)}, u32[]{:S(2)}, u32[]{:S(2)}) collective-permute-start(f32[3,72,128]{2,1,0:T(8,128)S(1)} %get-tuple-element.36), channel_id=1, source_target_pairs={{0,1},{1,0},{2,3},{3,2},{4,5},{5,4},{6,7},{7,6},{8,9},{9,8},{10,11... | collective-permute-start | bytes 331784 | tf_op jit(solution)/shard_map/ppermute | solution.py:358
  34.5 12.0 %collective-permute-start.7 = (f32[3,72,128]{2,1,0:T(8,128)S(1)}, f32[3,72,128]{2,1,0:T(8,128)S(1)}, u32[]{:S(2)}, u32[]{:S(2)}) collective-permute-start(f32[3,72,128]{2,1,0:T(8,128)S(1)} %get-tuple-element.37), channel_id=1, source_target_pairs={{0,7},{1,2},{2,1},{3,4},{4,3},{5,6},{6,5},{7,0},{8,15},{9,10},{10,... | collective-permute-start | bytes 331784 | tf_op jit(solution)/shard_map/ppermute | solution.py:358
  38.2 11.7 %collective-permute-start.16 = (f32[64,128]{1,0:T(8,128)S(1)}, f32[64,128]{1,0:T(8,128)S(1)}, u32[]{:S(2)}, u32[]{:S(2)}) collective-permute-start(f32[64,128]{1,0:T(8,128)S(1)} %add_add_fusion.1), channel_id=1, source_target_pairs={{0,24},{8,16},{16,8},{24,0},{1,25},{9,17},{17,9},{25,1},{2,26},{10... | collective-permute-start | bytes 98312 | tf_op jit(solution)/shard_map/ppermute | solution.py:362
  41.9 8.1 %collective-permute-start.15 = (f32[64,128]{1,0:T(8,128)S(1)}, f32[64,128]{1,0:T(8,128)S(1)}, u32[]{:S(2)}, u32[]{:S(2)}) collective-permute-start(f32[64,128]{1,0:T(8,128)S(1)} %add_add_fusion.1), channel_id=1, source_target_pairs={{0,16},{8,24},{16,0},{24,8},{1,17},{9,25},{17,1},{25,9},{2,18},{10... | collective-permute-start | bytes 98312 | tf_op jit(solution)/shard_map/ppermute | solution.py:362
  44.3 5.6 %collective-permute-start.14 = (f32[64,128]{1,0:T(8,128)S(1)}, f32[64,128]{1,0:T(8,128)S(1)}, u32[]{:S(2)}, u32[]{:S(2)}) collective-permute-start(f32[64,128]{1,0:T(8,128)S(1)} %add_add_fusion.1), channel_id=1, source_target_pairs={{0,8},{8,0},{16,24},{24,16},{1,9},{9,1},{17,25},{25,17},{2,10},{10... | collective-permute-start | bytes 98312 | tf_op jit(solution)/shard_map/ppermute | solution.py:362
  47.8 8.5 %collective-permute-start.8 = (f32[3,72,128]{2,1,0:T(8,128)S(1)}, f32[3,72,128]{2,1,0:T(8,128)S(1)}, u32[]{:S(2)}, u32[]{:S(2)}) collective-permute-start(f32[3,72,128]{2,1,0:T(8,128)S(1)} %get-tuple-element.39), channel_id=1, source_target_pairs={{0,1},{1,0},{2,3},{3,2},{4,5},{5,4},{6,7},{7,6},{8,9},{9,8},{10,11... | collective-permute-start | bytes 331784 | tf_op jit(solution)/shard_map/ppermute | solution.py:358
  47.9 8.5 %collective-permute-start.9 = (f32[3,72,128]{2,1,0:T(8,128)S(1)}, f32[3,72,128]{2,1,0:T(8,128)S(1)}, u32[]{:S(2)}, u32[]{:S(2)}) collective-permute-start(f32[3,72,128]{2,1,0:T(8,128)S(1)} %get-tuple-element.40), channel_id=1, source_target_pairs={{0,7},{1,2},{2,1},{3,4},{4,3},{5,6},{6,5},{7,0},{8,15},{9,10},{10,... | collective-permute-start | bytes 331784 | tf_op jit(solution)/shard_map/ppermute | solution.py:358
  50.0 1.9 %collective-permute-start.17 = (f32[64,128]{1,0:T(8,128)S(1)}, f32[64,128]{1,0:T(8,128)S(1)}, u32[]{:S(2)}, u32[]{:S(2)}) collective-permute-start(f32[64,128]{1,0:T(8,128)S(1)} %add_add_fusion.mine_ref), channel_id=1, source_target_pairs={{0,1},{1,0},{2,3},{3,2},{4,5},{5,4},{6,7},{7,6},{8,9},{9,8},{10,11... | collective-permute-start | bytes 98312 | tf_op jit(solution)/shard_map/ppermute | solution.py:362
  59.1 1.7 %copy-start = (f32[12,512,128]{2,1,0:T(8,128)}, f32[12,512,128]{2,1,0:T(8,128)S(1)}, u32[]{:S(2)}) copy-start(f32[12,512,128]{2,1,0:T(8,128)S(1)} %get-tuple-element.47.t_ref) | copy-start | bytes 9437188
  60.8 1.4 %collective-permute-start.18 = (f32[64,128]{1,0:T(8,128)S(1)}, f32[64,128]{1,0:T(8,128)S(1)}, u32[]{:S(2)}, u32[]{:S(2)}) collective-permute-start(f32[64,128]{1,0:T(8,128)S(1)} %get-tuple-element.45), channel_id=1, source_target_pairs={{0,1},{1,0},{2,3},{3,2},{4,5},{5,4},{6,7},{7,6},{8,9},{9,8},{10,11... | collective-permute-start | bytes 98312 | tf_op jit(solution)/shard_map/ppermute | solution.py:362
  79.6 1.3 %collective-permute-start.19 = (f32[64,128]{1,0:T(8,128)S(1)}, f32[64,128]{1,0:T(8,128)S(1)}, u32[]{:S(2)}, u32[]{:S(2)}) collective-permute-start(f32[64,128]{1,0:T(8,128)S(1)} %reduce_sum.19.mine_ref), channel_id=1, source_target_pairs={{0,1},{1,0},{2,3},{3,2},{4,5},{5,4},{6,7},{7,6},{8,9},{9,8},{10,11... | collective-permute-start | bytes 98312 | tf_op jit(solution)/shard_map/ppermute | solution.py:362
  80.9 1.9 %copy-start.1 = (f32[12,512,128]{2,1,0:T(8,128)S(1)}, f32[12,512,128]{2,1,0:T(8,128)}, u32[]{:S(2)}) copy-start(f32[12,512,128]{2,1,0:T(8,128)} %copy-done) | copy-start | bytes 9437188

commit v3 on v2

--- a/solution.py
+++ b/solution.py
@@ -19,6 +19,8 @@
 LANES = 128
 FIELDS = 3
 HALO = STEPS * RENORMS
+SIDE = STEPS
+STRIP = 2 * STEPS + 2
 TILES = 12
 VMEM_LIMIT = 16 * 1024 * 1024
 
@@ -96,29 +98,24 @@
     finish_all(copies)
 
 
-def spread_fields(sea_ref, levels_ref, current_ref, coef, sea, levels, current, sems):
+def spread_fields(sea_ref, levels_ref, current_ref, coef, wide, sea, levels, current, sems):
     rows = sea_ref.shape[1]
     finish_all(fetch((sea_ref, levels_ref, current_ref), (sea, levels, current), sems))
+    wide[...] = jnp.zeros_like(wide)
     for field, value in enumerate(fields_of(sea, levels, current)):
+        wide[field, :, pl.ds(0, rows)] = value
         for row in range(rows):
             coef[field, HALO + row] = lane_spread(value, row)
 
 
-def pack_columns(par, state, col_a, col_b):
+def column_at(east, cols, depth):
+    return depth + east * (cols - 1 - 2 * depth)
+
+
+def join_rows(par, t_ref, coef_in, wide, row_a, row_b, state, coef, col_a, col_b, sems):
     comps, tall, cols, _ = state.shape
-    _, easts = sides_of(par)
-    flat = state.reshape(comps * tall * cols, LANES)
-    for slot, msg in ((0, col_a), (1, col_b)):
-        for comp in range(comps):
-            for row in range(0, tall, SUB):
-                at = (comp * tall + row) * cols + easts[slot] * (cols - 1)
-                msg[comp, pl.ds(row, SUB), :] = flat[pl.ds(at, SUB, stride=cols), :]
-
-
-def join_rows(par, t_ref, coef_in, row_a, row_b, state, coef, col_a, col_b, sems):
-    comps, tall, _, _ = state.shape
     rows = tall - 2 * HALO
-    norths, _ = sides_of(par)
+    norths, easts = sides_of(par)
     copies = fetch(
         [t_ref.at[comp] for comp in range(comps)],
         [state.at[comp, pl.ds(HALO, rows)] for comp in range(comps)],
@@ -132,15 +129,44 @@
                 state[comp, line + h] = msg[comp * HALO + h]
             for field in range(FIELDS):
                 coef[field, line + h] = lane_spread(fields, field * SUB + h)
+    tail = comps * SIDE * tall
+    for slot, msg in ((0, col_a), (1, col_b)):
+        lon = column_at(easts[slot], cols, 0)
+        msg[pl.ds(tail, SUB), :] = jnp.zeros((SUB, LANES), jnp.float32)
+        for field in range(FIELDS):
+            msg[pl.ds(tail + field, 1), :] = wide[field, pl.ds(lon, 1), :]
+        for i, got in enumerate((row_a, row_b)):
+            msg[pl.ds(tail + FIELDS + i, 1), :] = got[comps * HALO, pl.ds(lon, 1), :]
     finish_all(copies)
-    pack_columns(par, state, col_a, col_b)
+    flat = state.reshape(comps * tall * cols, LANES)
+    for slot, msg in ((0, col_a), (1, col_b)):
+        for comp in range(comps):
+            for j in range(SIDE):
+                for row in range(0, tall, SUB):
+                    at = (comp * tall + row) * cols + column_at(easts[slot], cols, j)
+                    msg[pl.ds((comp * SIDE + j) * tall + row, SUB), :] = flat[
+                        pl.ds(at, SUB, stride=cols), :
+                    ]
+
+
+def model(own, x_diff, x_sum, above, below, sea, flow, depth, spin):
+    keep, half = 1.0 - 4.0 * viscosity, 0.5 * gravity
+    mixed = [
+        keep * c + viscosity * (x + (n + s)) - flow * d
+        for c, d, x, n, s in zip(own, x_diff, x_sum, above, below)
+    ]
+    v_y, h_y = above[1] - below[1], above[2] - below[2]
+    return (
+        sea * (mixed[0] - half * x_diff[2] + spin * own[1]),
+        sea * (mixed[1] - half * h_y - spin * own[0]),
+        sea * (mixed[2] - depth * (x_diff[0] + v_y)),
+    )
 
 
 def apply_inside(step, t_ref, coef_ref, spin_ref, out_ref):
     comps, tall, cols, _ = t_ref.shape
     flat = t_ref.reshape(comps * tall * cols, LANES)
     sub = lax.broadcasted_iota(jnp.int32, (SUB, LANES), 0)
-    keep, half = 1.0 - 4.0 * viscosity, 0.5 * gravity
     first, last = step + 1, tall - step - 1
 
     def line_of(line):
@@ -161,14 +187,10 @@
             above = [t_ref[comp, line + 1, cells, :] for comp in range(comps)]
             below = [t_ref[comp, line - 1, cells, :] for comp in range(comps)]
             x_diff = [e - w for e, w in zip(east, west)]
-            mixed = [
-                keep * c + viscosity * ((e + w) + (n + s)) - flow * x
-                for c, e, w, n, s, x in zip(own, east, west, above, below, x_diff)
-            ]
-            v_y, h_y = above[1] - below[1], above[2] - below[2]
-            out_ref[0, line, cells, :] = sea * (mixed[0] - half * x_diff[2] + spin * own[1])
-            out_ref[1, line, cells, :] = sea * (mixed[1] - half * h_y - spin * own[0])
-            out_ref[2, line, cells, :] = sea * (mixed[2] - depth * (x_diff[0] + v_y))
+            x_sum = [e + w for e, w in zip(east, west)]
+            new = model(own, x_diff, x_sum, above, below, sea, flow, depth, spin)
+            for comp in range(comps):
+                out_ref[comp, line, cells, :] = new[comp]
 
     @pl.loop(0, (last - first) // 2)
     def _(pair):
@@ -176,25 +198,93 @@
         line_of(first + 1 + 2 * pair)
 
 
-def add_columns(par, state, coef_ref, col_a, col_b):
+def fill_edge(par, coef_ref, cols_got, edge):
+    _, tall, cols, _ = coef_ref.shape
+    rows = tall - 2 * HALO
+    norths, easts = sides_of(par)
+    flat = coef_ref.reshape(FIELDS * tall * cols, LANES)
+    for slot, msg in enumerate(cols_got):
+        upright = jnp.transpose(msg[pl.ds(msg.shape[0] - SUB, SUB), :])
+        for field in range(FIELDS):
+            edge[slot, field, 0, pl.ds(HALO, rows), :] = lane_spread(upright[:rows], field)
+            for i in (0, 1):
+                beyond = lane_spread(upright[field * SUB : (field + 1) * SUB], FIELDS + i)
+                line = norths[i] * (tall - HALO)
+                edge[slot, field, 0, pl.ds(line, HALO), :] = beyond[:HALO]
+            for depth in range(STRIP - 3):
+                lon = column_at(easts[slot], cols, depth)
+                for row in range(0, tall, SUB):
+                    at = (field * tall + row) * cols + lon
+                    edge[slot, field, 1 + depth, pl.ds(row, SUB), :] = flat[
+                        pl.ds(at, SUB, stride=cols), :
+                    ]
+
+
+def mend_columns(par, old, state, spin_ref, edge, cols_got, sent, strips):
     comps, tall, cols, _ = state.shape
     _, easts = sides_of(par)
-    half = 0.5 * gravity
+    flat_old = old.reshape(comps * tall * cols, LANES)
     flat = state.reshape(comps * tall * cols, LANES)
-    flat_coef = coef_ref.reshape(FIELDS * tall * cols, LANES)
-    for slot, halo in ((0, col_a), (1, col_b)):
-        sign = (1 - 2 * easts[slot]).astype(jnp.float32)
-        for row in range(0, tall, SUB):
-            spots = [
-                pl.ds((comp * tall + row) * cols + easts[slot] * (cols - 1), SUB, stride=cols)
-                for comp in range(comps)
-            ]
-            sea, flow, depth = (flat_coef[spot, :] for spot in spots)
-            u, v, h = (halo[comp, pl.ds(row, SUB), :] for comp in range(comps))
-            mix = viscosity + sign * flow
-            flat[spots[0], :] += sea * (mix * u + (sign * half) * h)
-            flat[spots[1], :] += sea * (mix * v)
-            flat[spots[2], :] += sea * (mix * h + (sign * depth) * u)
+    signs = [(1 - 2 * east).astype(jnp.float32) for east in easts]
+    first, second = strips
+
+    def neighbours(strip, slot, column, row):
+        def load(comp, shift, lat):
+            return strip[slot, comp, column + shift, pl.ds(SUB + row + lat, SUB), :]
+
+        inner, outer = ([load(comp, shift, 0) for comp in range(comps)] for shift in (1, -1))
+        return (
+            [load(comp, 0, 0) for comp in range(comps)],
+            [signs[slot] * (i - o) for i, o in zip(inner, outer)],
+            [i + o for i, o in zip(inner, outer)],
+            [load(comp, 0, 1) for comp in range(comps)],
+            [load(comp, 0, -1) for comp in range(comps)],
+        )
+
+    def coefs(slot, column, row):
+        return [edge[slot, field, column, pl.ds(row, SUB), :] for field in range(FIELDS)]
+
+    @pl.loop(0, tall // SUB)
+    def _(group):
+        row = pl.multiple_of(group * SUB, SUB)
+        for slot, got in enumerate(cols_got):
+            for comp in range(comps):
+                for j in range(SIDE):
+                    first[slot, comp, SIDE - 1 - j, pl.ds(SUB + row, SUB), :] = got[
+                        pl.ds((comp * SIDE + j) * tall + row, SUB), :
+                    ]
+                for depth in range(STRIP - SIDE):
+                    at = (comp * tall + row) * cols + column_at(easts[slot], cols, depth)
+                    first[slot, comp, SIDE + depth, pl.ds(SUB + row, SUB), :] = flat_old[
+                        pl.ds(at, SUB, stride=cols), :
+                    ]
+
+    @pl.loop(0, tall // SUB)
+    def _(group):
+        row = pl.multiple_of(group * SUB, SUB)
+        spin = spin_ref[pl.ds(row, SUB), :]
+        for slot in (0, 1):
+            for column in range(STRIP - 2):
+                new = model(
+                    *neighbours(first, slot, column + 1, row), *coefs(slot, column, row), spin
+                )
+                for comp in range(comps):
+                    second[slot, comp, column, pl.ds(SUB + row, SUB), :] = new[comp]
+
+    @pl.loop(0, tall // SUB)
+    def _(group):
+        row = pl.multiple_of(group * SUB, SUB)
+        spin = spin_ref[pl.ds(row, SUB), :]
+        for slot in (0, 1):
+            for j in range(SIDE):
+                new = model(
+                    *neighbours(second, slot, j + 1, row), *coefs(slot, j + 1, row), spin
+                )
+                for comp in range(comps):
+                    at = (comp * tall + row) * cols + column_at(easts[slot], cols, j)
+                    flat[pl.ds(at, SUB, stride=cols), :] = new[comp]
+                    if sent is not None:
+                        sent[slot][pl.ds((comp * SIDE + j) * tall + row, SUB), :] = new[comp]
 
 
 def tiles_of(state):
@@ -207,14 +297,11 @@
         yield flat, pl.ds(start, height)
 
 
-def join_step(par, state_in, coef_ref, a, b, state, col_a, col_b):
-    add_columns(par, state, coef_ref, a, b)
-    pack_columns(par, state, col_a, col_b)
-
-
-def join_gram(scale, par, state_in, coef_ref, a, b, state, col_a, col_b, kept, sent, total):
-    add_columns(par, state, coef_ref, a, b)
-    pack_columns(par, state, col_a, col_b)
+def join_gram(
+    scale, par, old, state_in, coef_ref, spin_ref, a, b, state, edge, col_a, col_b, kept, sent, total, *strips
+):
+    fill_edge(par, coef_ref, (a, b), edge)
+    mend_columns(par, old, state, spin_ref, edge, (a, b), (col_a, col_b), strips)
     gram = sum(gram_of(*split_halves(flat[cells, :])) for flat, cells in tiles_of(state))
     write_halves(par, gram, scale, kept, sent, total)
 
@@ -321,10 +408,25 @@
 
 
 def join_update(
-    scale, par, state_in, coef_ref, a, b, inverse_ref, state, out_ref, kept, sent, factor, total
+    scale,
+    par,
+    old,
+    state_in,
+    edge,
+    spin_ref,
+    a,
+    b,
+    inverse_ref,
+    state,
+    out_ref,
+    kept,
+    sent,
+    factor,
+    total,
+    *strips,
 ):
-    add_columns(par, state, coef_ref, a, b)
     factor[...] = paired(inverse_ref[...])
+    mend_columns(par, old, state, spin_ref, edge, (a, b), None, strips)
     gram = 0.0
     for tile, (flat, cells) in enumerate(tiles_of(state)):
         new = times_factor(flat[cells, :], factor[...])
@@ -377,29 +479,10 @@
     return value
 
 
-def sum_groups(value, axis, low_bits, bits):
-    count = lax.axis_size(axis)
-    low, size = 1 << low_bits, 1 << bits
-    groups = [
-        [high * low * size + i * low + rest for i in range(size)]
-        for high in range(count // (low * size))
-        for rest in range(low)
-    ]
-    copies = jnp.broadcast_to(value, (size,) + value.shape)
-    if size == count:
-        groups = None
-    got = lax.all_to_all(copies, axis, 0, 0, axis_index_groups=groups)
-    return jnp.sum(got, axis=0)
-
-
-def sum_devices(kept, sent, grouped):
+def sum_devices(kept, sent):
     mine = kept + swapped(sent, "col", 1)
-    if grouped:
-        mine = sum_groups(mine, "col", 1, lax.axis_size("col").bit_length() - 2)
-        mine = sum_groups(mine, "row", 0, lax.axis_size("row").bit_length() - 1)
-    else:
-        mine = sum_over(mine, "col", 1)
-        mine = sum_over(mine, "row", 0)
+    mine = sum_over(mine, "col", 1)
+    mine = sum_over(mine, "row", 0)
     return mine, swapped(mine, "col", 1)
 
 
@@ -418,7 +501,13 @@
 
     height = comps * rows * cols // TILES
     block = shape_of(comps, tall, cols, modes)
-    columns = (shape_of(comps, tall, modes),) * 2
+    columns = (shape_of(comps * SIDE * tall, modes),) * 2
+    first_columns = (shape_of(comps * SIDE * tall + SUB, modes),) * 2
+    edges = shape_of(2, FIELDS, STRIP - 2, tall, LANES)
+    strips = [
+        pltpu.VMEM((2, comps, columns_of, tall + 2 * SUB, modes), jnp.float32)
+        for columns_of in (STRIP, STRIP - 2)
+    ]
     rows_sent = (shape_of(comps * HALO + 1, cols, modes),) * 2
     halves = (shape_of(modes // 2, modes),) * 2
     tiled = shape_of(TILES, height, modes)
@@ -463,67 +552,66 @@
         ],
     )
     row_halos = swap_pairs(*packed, "row", False)
-    coef = call(
+    coef, wide = call(
         spread_fields,
-        (shape_of(FIELDS, tall, cols, LANES),),
+        (shape_of(FIELDS, tall, cols, LANES), shape_of(FIELDS, cols, LANES)),
         *fields,
         specs=[HBM] * 3,
         scratch=upright + [pltpu.SemaphoreType.DMA((FIELDS,))],
-    )[0]
-    state, coef, *packed = call(
+    )
+    start, coef, *packed = call(
         join_rows,
-        (block, shape_of(FIELDS, tall, cols, LANES)) + columns,
+        (block, shape_of(FIELDS, tall, cols, LANES)) + first_columns,
         par,
-        source,
+        tangents,
         coef,
+        wide,
         *row_halos,
-        specs=[SMEM, HBM] + [VMEM] * 3,
         scratch=[pltpu.SemaphoreType.DMA((comps,))],
         aliases={2: 1},
     )
     logs = jnp.zeros((1, modes), jnp.float32)
-    for step in range(STEPS * RENORMS):
-        halos = swap_columns(packed)
-        state = inside(step, state)
-        if step == STEPS * RENORMS - 1:
-            break
-        if step == STEPS - 1:
-            state, *packed, kept, sent = call(
-                functools.partial(join_gram, scale),
-                (block,) + columns + halves,
-                par,
-                state,
-                coef,
-                *halos,
-                scratch=[square],
-                aliases={1: 0},
-            )
-            mine, other = sum_devices(kept, sent, False)
-            inverse, logs = call(
-                factor_only,
-                (shape_of(modes, modes), shape_of(1, modes)),
-                par,
-                mine,
-                other,
-                logs,
-                scratch=[square, square],
-            )
-        else:
-            state, *packed = call(
-                join_step, (block,) + columns, par, state, coef, *halos, aliases={1: 0}
-            )
+
+    halos = swap_columns(packed)
+    state = inside(1, inside(0, start))
+    start, edge, *packed, kept, sent = call(
+        functools.partial(join_gram, scale),
+        (block, edges) + columns + halves,
+        par,
+        start,
+        state,
+        coef,
+        spin,
+        *halos,
+        scratch=[square] + strips,
+        aliases={2: 0},
+    )
+    halos = swap_columns(packed)
+    mine, other = sum_devices(kept, sent)
+    state = inside(3, inside(2, start))
+    inverse, logs = call(
+        factor_only,
+        (shape_of(modes, modes), shape_of(1, modes)),
+        par,
+        mine,
+        other,
+        logs,
+        scratch=[square, square],
+    )
     _, state, kept, sent = call(
         functools.partial(join_update, scale),
         (block, tiled) + halves,
         par,
+        start,
         state,
-        coef,
+        edge,
+        spin,
         *halos,
         inverse,
-        scratch=[factor, square],
-        aliases={1: 0},
-    )
-    mine, other = sum_devices(kept, sent, True)
+        scratch=[factor, square] + strips,
+        aliases={2: 0},
+    )
+    mine, other = sum_devices(kept, sent)
     out, logs = call(
         finish,
         (tiled, shape_of(1, modes)),

time: 91.1 us -> 85.7 us (0.941)
  blocking collectives: 17.4 us -> 0 us
  waiting for transfers between devices: 8.15 us -> 18.5 us
  starting transfers between devices: 25.5 us -> 27.7 us
    all_to_all x2 -> x0, blocking collectives: 17.4 us -> none  [sum_groups(): got = lax.all_to_all(copies, axis, 0, 0, axis_index_groups=groups)]
    ppermute x10 -> x16, waiting for transfers between devices: 4.24 us -> 15.8 us  [swapped(): lax.ppermute(value, axis, [(i, i ^ mask) for i in range(lax.axis_size(axi...]
    ppermute x10 -> x16, starting transfers between devices: 11.2 us -> 19.5 us  [swapped(): lax.ppermute(value, axis, [(i, i ^ mask) for i in range(lax.axis_size(axi...]
    ppermute x5 -> x3, starting transfers between devices: 10.9 us -> 5.09 us  [swap_pairs(): lax.ppermute(far_value, axis, far)]
    ppermute x5 -> x3, waiting for transfers between devices: 1.65 us -> 0.01 us  [swap_pairs(): lax.ppermute(far_value, axis, far)]
    pallas_call x13 -> x11, Pallas kernels: 34.7 us -> 34.3 us  [call(): pl.pallas_call(kernel, out_shape=outs, in_specs=specs or [SMEM] + [VMEM]...]
    ppermute x5 -> x3, waiting for transfers between devices: 2.26 us -> 2.62 us  [swap_pairs(): lax.ppermute(near_value, axis, near)]
    ppermute x5 -> x3, starting transfers between devices: 3.42 us -> 3.09 us  [swap_pairs(): lax.ppermute(near_value, axis, near)]
  transfers between devices with their start and end apart: 20 -> 22, of which waited for: 8 -> 14; matrix products, arithmetic and copies ran while one was open for 0% -> 0% of each run, Pallas kernels for 17% -> 16%
where the time goes in v3:
time: 85.7 us; the launch traced here: 85.4 us
  Pallas kernels  34.3 us (40%)
  starting transfers between devices  27.7 us (32%)
  waiting for transfers between devices  18.5 us (22%)
  local copies, waits for them, and re-layouts  3.84 us (4%)
  between operations  0.99 us (1%)
    pallas_call x11, Pallas kernels, call(): pl.pallas_call(kernel, out_shape=outs, in_specs=specs or [SMEM] + [VMEM]...  34.3 us
    ppermute x16, starting transfers between devices, swapped(): lax.ppermute(value, axis, [(i, i ^ mask) for i in range(lax.axis_size(axi...  19.5 us
    ppermute x16, waiting for transfers between devices, swapped(): lax.ppermute(value, axis, [(i, i ^ mask) for i in range(lax.axis_size(axi...  15.8 us
    ppermute x3, starting transfers between devices, swap_pairs(): lax.ppermute(far_value, axis, far)  5.09 us
    unnamed x6, local copies, waits for them, and re-layouts  3.76 us
    ppermute x3, starting transfers between devices, swap_pairs(): lax.ppermute(near_value, axis, near)  3.09 us
    ppermute x3, waiting for transfers between devices, swap_pairs(): lax.ppermute(near_value, axis, near)  2.62 us
  transfers between devices with their start and end apart: 22, of which 14 were waited for; matrix products, arithmetic and copies ran while one was open for 0% of the time, Pallas kernels for 16%

profile of v3, /device:TPU:0, one launch (start us, length us, event | category | flops | bytes accessed | tf_op | source)
XLA Modules:
  0.0 85.4 jit_solution(7779838917945806225)
XLA Ops:
  0.7 2.0 %shard_map.60 = (f32[13,32,128]{2,1,0:T(8,128)S(1)}, f32[13,32,128]{2,1,0:T(8,128)S(1)}) custom-call(s32[2]{0:T(128)S(1)} %pad_add_fusion.par, f32[3,64,32,128]{3,2,1,0:T(8,128)} %t_ref.3, s32[32,64]{1,0:T(8,128)} %bitcast.7, s32[32,64]{1,0:T(8,128)} %bitcast.9, f32[32,64]{1,0:T(8,128)} %bitcast.11), custom_call_target="tpu_custom_call" | custom-call | tf_op jit(solution)/shard_map/pallas_call | solution.py:518
  2.7 3.1 %collective-permute-start = (f32[13,32,128]{2,1,0:T(8,128)S(1)}, f32[13,32,128]{2,1,0:T(8,128)S(1)}, u32[]{:S(2)}, u32[]{:S(2)}) collective-permute-start(f32[13,32,128]{2,1,0:T(8,128)S(1)} %get-tuple-element.25), channel_id=1, source_target_pairs={{0,8},{8,0},{16,24},{24,16},{1,9},{9,1},{17,25},{25,17},{2,10},{10... | collective-permute-start | bytes 638984 | tf_op jit(solution)/shard_map/ppermute | solution.py:460
  6.5 2.0 %shard_map.59 = (f32[3,72,32,128]{3,2,1,0:T(8,128)S(1)}, f32[3,32,128]{2,1,0:T(8,128)S(1)}) custom-call(s32[32,64]{1,0:T(8,128)} %bitcast.8, s32[32,64]{1,0:T(8,128)} %bitcast.10, f32[32,64]{1,0:T(8,128)} %bitcast.12), custom_call_target="tpu_custom_call" | custom-call | tf_op jit(solution)/shard_map/pallas_call | solution.py:518
  8.4 2.6 %collective-permute-done.row_a = f32[13,32,128]{2,1,0:T(8,128)S(1)} collective-permute-done((f32[13,32,128]{2,1,0:T(8,128)S(1)}, f32[13,32,128]{2,1,0:T(8,128)S(1)}, u32[]{:S(2)}, u32[]{:S(2)}) %collective-permute-start) | collective-permute-done | bytes 213024 | tf_op jit(solution)/shard_map/ppermute | solution.py:460
  11.0 2.0 %shard_map.61 = (f32[3,72,32,128]{3,2,1,0:T(8,128)S(1)}, f32[3,72,32,128]{3,2,1,0:T(8,128)S(1)}, f32[440,128]{1,0:T(8,128)}, f32[440,128]{1,0:T(8,128)}) custom-call(s32[2]{0:T(128)S(1)} %pad_add_fusion.par, f32[3,64,32,128]{3,2,1,0:T(8,128)S(1)} %copy-done.2, f32[3,72,32,128]{3,2,1,0:T(8,128)S(1)} %get-tuple-element.23.coef_in, ...), custom_call_target="tpu_custom_call", output_to_operand_aliasing={{1}: (2, {})} | custom-call | tf_op jit(solution)/shard_map/pallas_call | solution.py:518
  13.1 1.7 %copy-done = f32[3,72,32,128]{3,2,1,0:T(8,128)} copy-done((f32[3,72,32,128]{3,2,1,0:T(8,128)}, f32[3,72,32,128]{3,2,1,0:T(8,128)S(1)}, u32[]{:S(2)}) %copy-start) | copy-done | bytes 3538968
  14.8 2.7 %collective-permute-start.3 = (f32[440,128]{1,0:T(8,128)}, f32[440,128]{1,0:T(8,128)}, u32[]{:S(2)}, u32[]{:S(2)}) collective-permute-start(f32[440,128]{1,0:T(8,128)} %get-tuple-element.30), channel_id=1, source_target_pairs={{0,7},{1,2},{2,1},{3,4},{4,3},{5,6},{6,5},{7,0},{8,15},{9,10},{10,... | collective-permute-start | bytes 675848 | tf_op jit(solution)/shard_map/ppermute | solution.py:460
  17.7 2.0 %copy-done.1 = f32[3,72,32,128]{3,2,1,0:T(8,128)S(1)} copy-done((f32[3,72,32,128]{3,2,1,0:T(8,128)S(1)}, f32[3,72,32,128]{3,2,1,0:T(8,128)}, u32[]{:S(2)}) %copy-start.1) | copy-done | bytes 3538968
  19.7 2.0 %shard_map.62.t_ref = f32[3,72,32,128]{3,2,1,0:T(8,128)S(1)} custom-call(f32[3,72,32,128]{3,2,1,0:T(8,128)S(1)} %copy-done.1, f32[3,72,32,128]{3,2,1,0:T(8,128)S(1)} %get-tuple-element.28.coef_ref, f32[72,128]{1,0:T(8,128)S(1)} %broadcast_in_dim.4.spin_ref), custom_call_target="tpu_custom_call" | custom-call | tf_op jit(solution)/shard_map/pallas_call | solution.py:518
  21.7 1.9 %shard_map.63.state_in = f32[3,72,32,128]{3,2,1,0:T(8,128)S(1)} custom-call(f32[3,72,32,128]{3,2,1,0:T(8,128)S(1)} %shard_map.62.t_ref, f32[3,72,32,128]{3,2,1,0:T(8,128)S(1)} %get-tuple-element.28.coef_ref, f32[72,128]{1,0:T(8,128)S(1)} %broadcast_in_dim.4.spin_ref), custom_call_target="tpu_custom_call" | custom-call | tf_op jit(solution)/shard_map/pallas_call | solution.py:518
  23.6 4.1 %shard_map.64 = (f32[3,72,32,128]{3,2,1,0:T(8,128)S(1)}, f32[2,3,4,72,128]{4,3,2,1,0:T(8,128)S(1)}, f32[432,128]{1,0:T(8,128)S(1)}, f32[432,128]{1,0:T(8,128)S(1...) custom-call(s32[2]{0:T(128)S(1)} %pad_add_fusion.par, ...), custom_call_target="tpu_custom_call", output_to_operand_aliasing={{0}: (2, {})} | custom-call | tf_op jit(solution)/shard_map/pallas_call | solution.py:518
  27.8 1.2 %collective-permute-done.6 = f32[64,128]{1,0:T(8,128)S(1)} collective-permute-done((f32[64,128]{1,0:T(8,128)S(1)}, f32[64,128]{1,0:T(8,128)S(1)}, u32[]{:S(2)}, u32[]{:S(2)}) %collective-permute-start.6) | collective-permute-done | bytes 32800 | tf_op jit(solution)/shard_map/ppermute | solution.py:464
  29.0 1.4 %collective-permute-start.7 = (f32[64,128]{1,0:T(8,128)S(1)}, f32[64,128]{1,0:T(8,128)S(1)}, u32[]{:S(2)}, u32[]{:S(2)}) collective-permute-start(f32[64,128]{1,0:T(8,128)S(1)} %add.79), channel_id=1, source_target_pairs={{0,2},{1,3},{2,0},{3,1},{4,6},{5,7},{6,4},{7,5},{8,10},{9,11},{10,... | collective-permute-start | bytes 98312 | tf_op jit(solution)/shard_map/ppermute | solution.py:464
  30.9 1.6 %collective-permute-start.9 = (f32[64,128]{1,0:T(8,128)S(1)}, f32[64,128]{1,0:T(8,128)S(1)}, u32[]{:S(2)}, u32[]{:S(2)}) collective-permute-start(f32[64,128]{1,0:T(8,128)S(1)} %add.79), channel_id=1, source_target_pairs={{0,6},{1,7},{2,4},{3,5},{4,2},{5,3},{6,0},{7,1},{8,14},{9,15},{10,... | collective-permute-start | bytes 98312 | tf_op jit(solution)/shard_map/ppermute | solution.py:464
  32.9 1.7 %collective-permute-done.8 = f32[64,128]{1,0:T(8,128)S(1)} collective-permute-done((f32[64,128]{1,0:T(8,128)S(1)}, f32[64,128]{1,0:T(8,128)S(1)}, u32[]{:S(2)}, u32[]{:S(2)}) %collective-permute-start.8) | collective-permute-done | bytes 32800 | tf_op jit(solution)/shard_map/ppermute | solution.py:464
  35.7 4.7 %collective-permute-start.10 = (f32[64,128]{1,0:T(8,128)S(1)}, f32[64,128]{1,0:T(8,128)S(1)}, u32[]{:S(2)}, u32[]{:S(2)}) collective-permute-start(f32[64,128]{1,0:T(8,128)S(1)} %add_add_fusion.3), channel_id=1, source_target_pairs={{0,8},{8,0},{16,24},{24,16},{1,9},{9,1},{17,25},{25,17},{2,10},{10... | collective-permute-start | bytes 98312 | tf_op jit(solution)/shard_map/ppermute | solution.py:464
  40.4 1.2 %collective-permute-start.11 = (f32[64,128]{1,0:T(8,128)S(1)}, f32[64,128]{1,0:T(8,128)S(1)}, u32[]{:S(2)}, u32[]{:S(2)}) collective-permute-start(f32[64,128]{1,0:T(8,128)S(1)} %add_add_fusion.3), channel_id=1, source_target_pairs={{0,16},{8,24},{16,0},{24,8},{1,17},{9,25},{17,1},{25,9},{2,18},{10... | collective-permute-start | bytes 98312 | tf_op jit(solution)/shard_map/ppermute | solution.py:464
  41.6 1.4 %collective-permute-start.12 = (f32[64,128]{1,0:T(8,128)S(1)}, f32[64,128]{1,0:T(8,128)S(1)}, u32[]{:S(2)}, u32[]{:S(2)}) collective-permute-start(f32[64,128]{1,0:T(8,128)S(1)} %add_add_fusion.3), channel_id=1, source_target_pairs={{0,24},{8,16},{16,8},{24,0},{1,25},{9,17},{17,9},{25,1},{2,26},{10... | collective-permute-start | bytes 98312 | tf_op jit(solution)/shard_map/ppermute | solution.py:464
  43.0 1.7 %collective-permute-start.5 = (f32[432,128]{1,0:T(8,128)S(1)}, f32[432,128]{1,0:T(8,128)S(1)}, u32[]{:S(2)}, u32[]{:S(2)}) collective-permute-start(f32[432,128]{1,0:T(8,128)S(1)} %get-tuple-element.34), channel_id=1, source_target_pairs={{0,7},{1,2},{2,1},{3,4},{4,3},{5,6},{6,5},{7,0},{8,15},{9,10},{10,... | collective-permute-start | bytes 663560 | tf_op jit(solution)/shard_map/ppermute | solution.py:460
  45.7 1.7 %collective-permute-done.12 = f32[64,128]{1,0:T(8,128)S(1)} collective-permute-done((f32[64,128]{1,0:T(8,128)S(1)}, f32[64,128]{1,0:T(8,128)S(1)}, u32[]{:S(2)}, u32[]{:S(2)}) %collective-permute-start.12) | collective-permute-done | bytes 32800 | tf_op jit(solution)/shard_map/ppermute | solution.py:464
  47.4 1.9 %shard_map.65.t_ref = f32[3,72,32,128]{3,2,1,0:T(8,128)S(1)} custom-call(f32[3,72,32,128]{3,2,1,0:T(8,128)S(1)} %get-tuple-element.31.t_ref.old, f32[3,72,32,128]{3,2,1,0:T(8,128)S(1)} %get-tuple-element.28.coef_ref, f32[72,128]{1,0:T(8,128)S(1)} %broadcast_in_dim.4.spin_ref), custom_call_target="tpu_custom_call" | custom-call | tf_op jit(solution)/shard_map/pallas_call | solution.py:518
  49.3 1.8 %shard_map.66.state_in = f32[3,72,32,128]{3,2,1,0:T(8,128)S(1)} custom-call(f32[3,72,32,128]{3,2,1,0:T(8,128)S(1)} %shard_map.65.t_ref, f32[3,72,32,128]{3,2,1,0:T(8,128)S(1)} %get-tuple-element.28.coef_ref, f32[72,128]{1,0:T(8,128)S(1)} %broadcast_in_dim.4.spin_ref), custom_call_target="tpu_custom_call" | custom-call | tf_op jit(solution)/shard_map/pallas_call | solution.py:518
  51.2 4.4 %shard_map.67 = (f32[128,128]{1,0:T(8,128)S(1)}, f32[1,128]{1,0:T(1,128)S(1)}) custom-call(s32[2]{0:T(128)S(1)} %pad_add_fusion.par, f32[64,128]{1,0:T(8,128)S(1)} %add_add_fusion.2.mine_ref, f32[64,128]{1,0:T(8,128)S(1)} %collective-permute-done.13.other_ref, f32[1,128]{1,0:T(1,128)S(1)} %broadcast_in_dim.10.prior_ref), custom_call_target="tpu_custom_call" | custom-call | tf_op jit(solution)/shard_map/pallas_call | solution.py:518
  55.6 4.6 %shard_map.68 = (f32[3,72,32,128]{3,2,1,0:T(8,128)S(1)}, f32[12,512,128]{2,1,0:T(8,128)S(1)}, f32[64,128]{1,0:T(8,128)S(1)}, f32[64,128]{1,0:T(8,128)S(1)}) custom-call(s32[2]{0:T(128)S(1)} %pad_add_fusion.par, f32[3,72,32,128]{3,2,1,0:T(8,128)S(1)} %get-tuple-element.31.t_ref.old, ...), custom_call_target="tpu_custom_call", output_to_operand_aliasing={{0}: (2, {})} | custom-call | tf_op jit(solution)/shard_map/pallas_call | solution.py:518
  61.6 1.7 %collective-permute-start.15 = (f32[64,128]{1,0:T(8,128)S(1)}, f32[64,128]{1,0:T(8,128)S(1)}, u32[]{:S(2)}, u32[]{:S(2)}) collective-permute-start(f32[64,128]{1,0:T(8,128)S(1)} %add.86), channel_id=1, source_target_pairs={{0,2},{1,3},{2,0},{3,1},{4,6},{5,7},{6,4},{7,5},{8,10},{9,11},{10,... | collective-permute-start | bytes 98312 | tf_op jit(solution)/shard_map/ppermute | solution.py:464
  63.7 1.3 %collective-permute-start.17 = (f32[64,128]{1,0:T(8,128)S(1)}, f32[64,128]{1,0:T(8,128)S(1)}, u32[]{:S(2)}, u32[]{:S(2)}) collective-permute-start(f32[64,128]{1,0:T(8,128)S(1)} %add.86), channel_id=1, source_target_pairs={{0,6},{1,7},{2,4},{3,5},{4,2},{5,3},{6,0},{7,1},{8,14},{9,15},{10,... | collective-permute-start | bytes 98312 | tf_op jit(solution)/shard_map/ppermute | solution.py:464
  65.5 2.1 %collective-permute-done.16 = f32[64,128]{1,0:T(8,128)S(1)} collective-permute-done((f32[64,128]{1,0:T(8,128)S(1)}, f32[64,128]{1,0:T(8,128)S(1)}, u32[]{:S(2)}, u32[]{:S(2)}) %collective-permute-start.16) | collective-permute-done | bytes 32800 | tf_op jit(solution)/shard_map/ppermute | solution.py:464
  68.8 1.8 %collective-permute-start.19 = (f32[64,128]{1,0:T(8,128)S(1)}, f32[64,128]{1,0:T(8,128)S(1)}, u32[]{:S(2)}, u32[]{:S(2)}) collective-permute-start(f32[64,128]{1,0:T(8,128)S(1)} %add_add_fusion.1), channel_id=1, source_target_pairs={{0,16},{8,24},{16,0},{24,8},{1,17},{9,25},{17,1},{25,9},{2,18},{10... | collective-permute-start | bytes 98312 | tf_op jit(solution)/shard_map/ppermute | solution.py:464
  70.6 2.4 %collective-permute-start.20 = (f32[64,128]{1,0:T(8,128)S(1)}, f32[64,128]{1,0:T(8,128)S(1)}, u32[]{:S(2)}, u32[]{:S(2)}) collective-permute-start(f32[64,128]{1,0:T(8,128)S(1)} %add_add_fusion.1), channel_id=1, source_target_pairs={{0,24},{8,16},{16,8},{24,0},{1,25},{9,17},{17,9},{25,1},{2,26},{10... | collective-permute-start | bytes 98312 | tf_op jit(solution)/shard_map/ppermute | solution.py:464
  73.8 2.4 %collective-permute-done.20 = f32[64,128]{1,0:T(8,128)S(1)} collective-permute-done((f32[64,128]{1,0:T(8,128)S(1)}, f32[64,128]{1,0:T(8,128)S(1)}, u32[]{:S(2)}, u32[]{:S(2)}) %collective-permute-start.20) | collective-permute-done | bytes 32800 | tf_op jit(solution)/shard_map/ppermute | solution.py:464
  76.4 1.2 %collective-permute-done.21.other_ref = f32[64,128]{1,0:T(8,128)S(1)} collective-permute-done((f32[64,128]{1,0:T(8,128)S(1)}, f32[64,128]{1,0:T(8,128)S(1)}, u32[]{:S(2)}, u32[]{:S(2)}) %collective-permute-start.21) | collective-permute-done | bytes 32800 | tf_op jit(solution)/shard_map/ppermute | solution.py:464
  77.6 7.7 %shard_map.69 = (f32[12,512,128]{2,1,0:T(8,128)}, f32[1,128]{1,0:T(1,128)}) custom-call(s32[2]{0:T(128)S(1)} %pad_add_fusion.par, f32[64,128]{1,0:T(8,128)S(1)} %add_add_fusion.mine_ref, f32[64,128]{1,0:T(8,128)S(1)} %collective-permute-done.21.other_ref, f32[1,128]{1,0:T(1,128)S(1)} %get-tuple-element.40.prior_ref, f32[12,512,128]{2,1,0:T(8,128)S(1)} %get-tuple-element.41.t_ref), custom_call_target="tpu_custom_call" | custom-call | tf_op jit(solution)/shard_map/pallas_call | solution.py:518
  (39 shorter events, 8.4 us)
Async XLA Ops:
  0.6 10.4 %copy-start.2 = (f32[3,64,32,128]{3,2,1,0:T(8,128)S(1)}, f32[3,64,32,128]{3,2,1,0:T(8,128)}, u32[]{:S(2)}) copy-start(f32[3,64,32,128]{3,2,1,0:T(8,128)} %t_ref.3) | copy-start | bytes 9437188
  2.7 8.3 %collective-permute-start = (f32[13,32,128]{2,1,0:T(8,128)S(1)}, f32[13,32,128]{2,1,0:T(8,128)S(1)}, u32[]{:S(2)}, u32[]{:S(2)}) collective-permute-start(f32[13,32,128]{2,1,0:T(8,128)S(1)} %get-tuple-element.25), channel_id=1, source_target_pairs={{0,8},{8,0},{16,24},{24,16},{1,9},{9,1},{17,25},{25,17},{2,10},{10... | collective-permute-start | bytes 638984 | tf_op jit(solution)/shard_map/ppermute | solution.py:460
  5.8 5.3 %collective-permute-start.1 = (f32[13,32,128]{2,1,0:T(8,128)S(1)}, f32[13,32,128]{2,1,0:T(8,128)S(1)}, u32[]{:S(2)}, u32[]{:S(2)}) collective-permute-start(f32[13,32,128]{2,1,0:T(8,128)S(1)} %get-tuple-element.26), channel_id=1, source_target_pairs={{8,16},{16,8},{9,17},{17,9},{10,18},{18,10},{11,19},{19,11},{12,20... | collective-permute-start | bytes 638984 | tf_op jit(solution)/shard_map/ppermute | solution.py:460
  13.1 1.8 %copy-start = (f32[3,72,32,128]{3,2,1,0:T(8,128)}, f32[3,72,32,128]{3,2,1,0:T(8,128)S(1)}, u32[]{:S(2)}) copy-start(f32[3,72,32,128]{3,2,1,0:T(8,128)S(1)} %get-tuple-element.27.t_ref.old) | copy-start | bytes 10616836
  14.8 8.8 %collective-permute-start.2 = (f32[440,128]{1,0:T(8,128)}, f32[440,128]{1,0:T(8,128)}, u32[]{:S(2)}, u32[]{:S(2)}) collective-permute-start(f32[440,128]{1,0:T(8,128)} %get-tuple-element.29), channel_id=1, source_target_pairs={{0,1},{1,0},{2,3},{3,2},{4,5},{5,4},{6,7},{7,6},{8,9},{9,8},{10,11... | collective-permute-start | bytes 675848 | tf_op jit(solution)/shard_map/ppermute | solution.py:460
  14.8 8.8 %collective-permute-start.3 = (f32[440,128]{1,0:T(8,128)}, f32[440,128]{1,0:T(8,128)}, u32[]{:S(2)}, u32[]{:S(2)}) collective-permute-start(f32[440,128]{1,0:T(8,128)} %get-tuple-element.30), channel_id=1, source_target_pairs={{0,7},{1,2},{2,1},{3,4},{4,3},{5,6},{6,5},{7,0},{8,15},{9,10},{10,... | collective-permute-start | bytes 675848 | tf_op jit(solution)/shard_map/ppermute | solution.py:460
  17.7 2.0 %copy-start.1 = (f32[3,72,32,128]{3,2,1,0:T(8,128)S(1)}, f32[3,72,32,128]{3,2,1,0:T(8,128)}, u32[]{:S(2)}) copy-start(f32[3,72,32,128]{3,2,1,0:T(8,128)} %copy-done) | copy-start | bytes 10616836
  27.7 1.3 %collective-permute-start.6 = (f32[64,128]{1,0:T(8,128)S(1)}, f32[64,128]{1,0:T(8,128)S(1)}, u32[]{:S(2)}, u32[]{:S(2)}) collective-permute-start(f32[64,128]{1,0:T(8,128)S(1)} %get-tuple-element.36), channel_id=1, source_target_pairs={{0,1},{1,0},{2,3},{3,2},{4,5},{5,4},{6,7},{7,6},{8,9},{9,8},{10,11... | collective-permute-start | bytes 98312 | tf_op jit(solution)/shard_map/ppermute | solution.py:464
  29.0 3.9 %collective-permute-start.7 = (f32[64,128]{1,0:T(8,128)S(1)}, f32[64,128]{1,0:T(8,128)S(1)}, u32[]{:S(2)}, u32[]{:S(2)}) collective-permute-start(f32[64,128]{1,0:T(8,128)S(1)} %add.79), channel_id=1, source_target_pairs={{0,2},{1,3},{2,0},{3,1},{4,6},{5,7},{6,4},{7,5},{8,10},{9,11},{10,... | collective-permute-start | bytes 98312 | tf_op jit(solution)/shard_map/ppermute | solution.py:464
  30.4 4.3 %collective-permute-start.8 = (f32[64,128]{1,0:T(8,128)S(1)}, f32[64,128]{1,0:T(8,128)S(1)}, u32[]{:S(2)}, u32[]{:S(2)}) collective-permute-start(f32[64,128]{1,0:T(8,128)S(1)} %add.79), channel_id=1, source_target_pairs={{0,4},{1,5},{2,6},{3,7},{4,0},{5,1},{6,2},{7,3},{8,12},{9,13},{10,... | collective-permute-start | bytes 98312 | tf_op jit(solution)/shard_map/ppermute | solution.py:464
  30.9 4.8 %collective-permute-start.9 = (f32[64,128]{1,0:T(8,128)S(1)}, f32[64,128]{1,0:T(8,128)S(1)}, u32[]{:S(2)}, u32[]{:S(2)}) collective-permute-start(f32[64,128]{1,0:T(8,128)S(1)} %add.79), channel_id=1, source_target_pairs={{0,6},{1,7},{2,4},{3,5},{4,2},{5,3},{6,0},{7,1},{8,14},{9,15},{10,... | collective-permute-start | bytes 98312 | tf_op jit(solution)/shard_map/ppermute | solution.py:464
  35.7 9.0 %collective-permute-start.10 = (f32[64,128]{1,0:T(8,128)S(1)}, f32[64,128]{1,0:T(8,128)S(1)}, u32[]{:S(2)}, u32[]{:S(2)}) collective-permute-start(f32[64,128]{1,0:T(8,128)S(1)} %add_add_fusion.3), channel_id=1, source_target_pairs={{0,8},{8,0},{16,24},{24,16},{1,9},{9,1},{17,25},{25,17},{2,10},{10... | collective-permute-start | bytes 98312 | tf_op jit(solution)/shard_map/ppermute | solution.py:464
  40.4 5.3 %collective-permute-start.11 = (f32[64,128]{1,0:T(8,128)S(1)}, f32[64,128]{1,0:T(8,128)S(1)}, u32[]{:S(2)}, u32[]{:S(2)}) collective-permute-start(f32[64,128]{1,0:T(8,128)S(1)} %add_add_fusion.3), channel_id=1, source_target_pairs={{0,16},{8,24},{16,0},{24,8},{1,17},{9,25},{17,1},{25,9},{2,18},{10... | collective-permute-start | bytes 98312 | tf_op jit(solution)/shard_map/ppermute | solution.py:464
  41.6 5.7 %collective-permute-start.12 = (f32[64,128]{1,0:T(8,128)S(1)}, f32[64,128]{1,0:T(8,128)S(1)}, u32[]{:S(2)}, u32[]{:S(2)}) collective-permute-start(f32[64,128]{1,0:T(8,128)S(1)} %add_add_fusion.3), channel_id=1, source_target_pairs={{0,24},{8,16},{16,8},{24,0},{1,25},{9,17},{17,9},{25,1},{2,26},{10... | collective-permute-start | bytes 98312 | tf_op jit(solution)/shard_map/ppermute | solution.py:464
  43.0 12.6 %collective-permute-start.4 = (f32[432,128]{1,0:T(8,128)S(1)}, f32[432,128]{1,0:T(8,128)S(1)}, u32[]{:S(2)}, u32[]{:S(2)}) collective-permute-start(f32[432,128]{1,0:T(8,128)S(1)} %get-tuple-element.33), channel_id=1, source_target_pairs={{0,1},{1,0},{2,3},{3,2},{4,5},{5,4},{6,7},{7,6},{8,9},{9,8},{10,11... | collective-permute-start | bytes 663560 | tf_op jit(solution)/shard_map/ppermute | solution.py:460
  43.0 12.6 %collective-permute-start.5 = (f32[432,128]{1,0:T(8,128)S(1)}, f32[432,128]{1,0:T(8,128)S(1)}, u32[]{:S(2)}, u32[]{:S(2)}) collective-permute-start(f32[432,128]{1,0:T(8,128)S(1)} %get-tuple-element.34), channel_id=1, source_target_pairs={{0,7},{1,2},{2,1},{3,4},{4,3},{5,6},{6,5},{7,0},{8,15},{9,10},{10,... | collective-permute-start | bytes 663560 | tf_op jit(solution)/shard_map/ppermute | solution.py:460
  47.4 3.8 %collective-permute-start.13 = (f32[64,128]{1,0:T(8,128)S(1)}, f32[64,128]{1,0:T(8,128)S(1)}, u32[]{:S(2)}, u32[]{:S(2)}) collective-permute-start(f32[64,128]{1,0:T(8,128)S(1)} %add_add_fusion.2.mine_ref), channel_id=1, source_target_pairs={{0,1},{1,0},{2,3},{3,2},{4,5},{5,4},{6,7},{7,6},{8,9},{9,8},{10,11... | collective-permute-start | bytes 98312 | tf_op jit(solution)/shard_map/ppermute | solution.py:464
  60.1 1.4 %collective-permute-start.14 = (f32[64,128]{1,0:T(8,128)S(1)}, f32[64,128]{1,0:T(8,128)S(1)}, u32[]{:S(2)}, u32[]{:S(2)}) collective-permute-start(f32[64,128]{1,0:T(8,128)S(1)} %get-tuple-element.39), channel_id=1, source_target_pairs={{0,1},{1,0},{2,3},{3,2},{4,5},{5,4},{6,7},{7,6},{8,9},{9,8},{10,11... | collective-permute-start | bytes 98312 | tf_op jit(solution)/shard_map/ppermute | solution.py:464
  61.6 3.9 %collective-permute-start.15 = (f32[64,128]{1,0:T(8,128)S(1)}, f32[64,128]{1,0:T(8,128)S(1)}, u32[]{:S(2)}, u32[]{:S(2)}) collective-permute-start(f32[64,128]{1,0:T(8,128)S(1)} %add.86), channel_id=1, source_target_pairs={{0,2},{1,3},{2,0},{3,1},{4,6},{5,7},{6,4},{7,5},{8,10},{9,11},{10,... | collective-permute-start | bytes 98312 | tf_op jit(solution)/shard_map/ppermute | solution.py:464
  63.3 4.3 %collective-permute-start.16 = (f32[64,128]{1,0:T(8,128)S(1)}, f32[64,128]{1,0:T(8,128)S(1)}, u32[]{:S(2)}, u32[]{:S(2)}) collective-permute-start(f32[64,128]{1,0:T(8,128)S(1)} %add.86), channel_id=1, source_target_pairs={{0,4},{1,5},{2,6},{3,7},{4,0},{5,1},{6,2},{7,3},{8,12},{9,13},{10,... | collective-permute-start | bytes 98312 | tf_op jit(solution)/shard_map/ppermute | solution.py:464
  63.7 4.8 %collective-permute-start.17 = (f32[64,128]{1,0:T(8,128)S(1)}, f32[64,128]{1,0:T(8,128)S(1)}, u32[]{:S(2)}, u32[]{:S(2)}) collective-permute-start(f32[64,128]{1,0:T(8,128)S(1)} %add.86), channel_id=1, source_target_pairs={{0,6},{1,7},{2,4},{3,5},{4,2},{5,3},{6,0},{7,1},{8,14},{9,15},{10,... | collective-permute-start | bytes 98312 | tf_op jit(solution)/shard_map/ppermute | solution.py:464
  68.5 4.5 %collective-permute-start.18 = (f32[64,128]{1,0:T(8,128)S(1)}, f32[64,128]{1,0:T(8,128)S(1)}, u32[]{:S(2)}, u32[]{:S(2)}) collective-permute-start(f32[64,128]{1,0:T(8,128)S(1)} %add_add_fusion.1), channel_id=1, source_target_pairs={{0,8},{8,0},{16,24},{24,16},{1,9},{9,1},{17,25},{25,17},{2,10},{10... | collective-permute-start | bytes 98312 | tf_op jit(solution)/shard_map/ppermute | solution.py:464
  68.8 5.1 %collective-permute-start.19 = (f32[64,128]{1,0:T(8,128)S(1)}, f32[64,128]{1,0:T(8,128)S(1)}, u32[]{:S(2)}, u32[]{:S(2)}) collective-permute-start(f32[64,128]{1,0:T(8,128)S(1)} %add_add_fusion.1), channel_id=1, source_target_pairs={{0,16},{8,24},{16,0},{24,8},{1,17},{9,25},{17,1},{25,9},{2,18},{10... | collective-permute-start | bytes 98312 | tf_op jit(solution)/shard_map/ppermute | solution.py:464
  70.6 5.7 %collective-permute-start.20 = (f32[64,128]{1,0:T(8,128)S(1)}, f32[64,128]{1,0:T(8,128)S(1)}, u32[]{:S(2)}, u32[]{:S(2)}) collective-permute-start(f32[64,128]{1,0:T(8,128)S(1)} %add_add_fusion.1), channel_id=1, source_target_pairs={{0,24},{8,16},{16,8},{24,0},{1,25},{9,17},{17,9},{25,1},{2,26},{10... | collective-permute-start | bytes 98312 | tf_op jit(solution)/shard_map/ppermute | solution.py:464
  76.3 1.3 %collective-permute-start.21 = (f32[64,128]{1,0:T(8,128)S(1)}, f32[64,128]{1,0:T(8,128)S(1)}, u32[]{:S(2)}, u32[]{:S(2)}) collective-permute-start(f32[64,128]{1,0:T(8,128)S(1)} %add_add_fusion.mine_ref), channel_id=1, source_target_pairs={{0,1},{1,0},{2,3},{3,2},{4,5},{5,4},{6,7},{7,6},{8,9},{9,8},{10,11... | collective-permute-start | bytes 98312 | tf_op jit(solution)/shard_map/ppermute | solution.py:464

commit v4 on v3

--- a/solution.py
+++ b/solution.py
@@ -98,9 +98,16 @@
     finish_all(copies)
 
 
-def spread_fields(sea_ref, levels_ref, current_ref, coef, wide, sea, levels, current, sems):
+def spread_fields(
+    total_rows, par, sea_ref, levels_ref, current_ref, coef, wide, spin, sea, levels, current, sems
+):
     rows = sea_ref.shape[1]
-    finish_all(fetch((sea_ref, levels_ref, current_ref), (sea, levels, current), sems))
+    copies = fetch((sea_ref, levels_ref, current_ref), (sea, levels, current), sems)
+    line = lax.broadcasted_iota(jnp.int32, spin.shape, 0)
+    latitude = (par[0] * rows - HALO + line).astype(jnp.float32)
+    angle = (-70.0 + 140.0 * (latitude + 0.5) / total_rows) * (jnp.pi / 180.0)
+    spin[...] = rotation * jnp.sin(angle)
+    finish_all(copies)
     wide[...] = jnp.zeros_like(wide)
     for field, value in enumerate(fields_of(sea, levels, current)):
         wide[field, :, pl.ds(0, rows)] = value
@@ -495,10 +502,6 @@
     par = jnp.stack([row_at, col_at]).astype(jnp.int32)
 
     tall = rows + 2 * HALO
-    lat = (row_at * rows - HALO + jnp.arange(tall)).astype(jnp.float32)
-    angle = (-70.0 + 140.0 * (lat + 0.5) / total_rows) * (jnp.pi / 180.0)
-    spin = jnp.broadcast_to((rotation * jnp.sin(angle))[:, None], (tall, LANES))
-
     height = comps * rows * cols // TILES
     block = shape_of(comps, tall, cols, modes)
     columns = (shape_of(comps * SIDE * tall, modes),) * 2
@@ -552,11 +555,16 @@
         ],
     )
     row_halos = swap_pairs(*packed, "row", False)
-    coef, wide = call(
-        spread_fields,
-        (shape_of(FIELDS, tall, cols, LANES), shape_of(FIELDS, cols, LANES)),
+    coef, wide, spin = call(
+        functools.partial(spread_fields, total_rows),
+        (
+            shape_of(FIELDS, tall, cols, LANES),
+            shape_of(FIELDS, cols, LANES),
+            shape_of(tall, LANES),
+        ),
+        par,
         *fields,
-        specs=[HBM] * 3,
+        specs=[SMEM] + [HBM] * 3,
         scratch=upright + [pltpu.SemaphoreType.DMA((FIELDS,))],
     )
     start, coef, *packed = call(

time: 85.7 us -> 82.2 us (0.959)
  local copies, waits for them, and re-layouts: 3.84 us -> 0.01 us
  waiting for transfers between devices: 18.5 us -> 19.8 us
    unnamed x6 -> x2, local copies, waits for them, and re-layouts: 3.76 us -> 0.01 us
    ppermute x3, waiting for transfers between devices: 0.01 us -> 1.33 us  [swap_pairs(): lax.ppermute(far_value, axis, far)]
  transfers between devices with their start and end apart: 22 -> 22, of which waited for: 14 -> 15; matrix products, arithmetic and copies ran while one was open for 0% -> 0% of each run, Pallas kernels for 16% -> 18%
where the time goes in v4:
time: 82.2 us; the launch traced here: 81.9 us
  Pallas kernels  33.5 us (41%)
  starting transfers between devices  27.5 us (33%)
  waiting for transfers between devices  19.8 us (24%)
  between operations  0.97 us (1%)
    pallas_call x11, Pallas kernels, call(): pl.pallas_call(kernel, out_shape=outs, in_specs=specs or [SMEM] + [VMEM]...  33.5 us
    ppermute x16, starting transfers between devices, swapped(): lax.ppermute(value, axis, [(i, i ^ mask) for i in range(lax.axis_size(axi...  19.6 us
    ppermute x16, waiting for transfers between devices, swapped(): lax.ppermute(value, axis, [(i, i ^ mask) for i in range(lax.axis_size(axi...  16.4 us
    ppermute x3, starting transfers between devices, swap_pairs(): lax.ppermute(far_value, axis, far)  4.73 us
    ppermute x3, starting transfers between devices, swap_pairs(): lax.ppermute(near_value, axis, near)  3.16 us
    ppermute x3, waiting for transfers between devices, swap_pairs(): lax.ppermute(near_value, axis, near)  2.08 us
  transfers between devices with their start and end apart: 22, of which 15 were waited for; matrix products, arithmetic and copies ran while one was open for 0% of the time, Pallas kernels for 18%

profile of v4, /device:TPU:0, one launch (start us, length us, event | category | flops | bytes accessed | tf_op | source)
XLA Modules:
  0.0 81.9 jit_solution(9145824272033981391)
XLA Ops:
  0.7 2.0 %shard_map.60 = (f32[13,32,128]{2,1,0:T(8,128)S(1)}, f32[13,32,128]{2,1,0:T(8,128)S(1)}) custom-call(s32[2]{0:T(128)S(1)} %pad_add_fusion.par, f32[3,64,32,128]{3,2,1,0:T(8,128)} %t_ref.3, s32[32,64]{1,0:T(8,128)} %bitcast.7, s32[32,64]{1,0:T(8,128)} %bitcast.9, f32[32,64]{1,0:T(8,128)} %bitcast.11), custom_call_target="tpu_custom_call" | custom-call | tf_op jit(solution)/shard_map/pallas_call | solution.py:521
  2.7 3.1 %collective-permute-start = (f32[13,32,128]{2,1,0:T(8,128)S(1)}, f32[13,32,128]{2,1,0:T(8,128)S(1)}, u32[]{:S(2)}, u32[]{:S(2)}) collective-permute-start(f32[13,32,128]{2,1,0:T(8,128)S(1)} %get-tuple-element.26), channel_id=1, source_target_pairs={{0,8},{8,0},{16,24},{24,16},{1,9},{9,1},{17,25},{25,17},{2,10},{10... | collective-permute-start | bytes 638984 | tf_op jit(solution)/shard_map/ppermute | solution.py:467
  6.5 2.5 %shard_map.59 = (f32[3,72,32,128]{3,2,1,0:T(8,128)S(1)}, f32[3,32,128]{2,1,0:T(8,128)S(1)}, f32[72,128]{1,0:T(8,128)S(1)}) custom-call(s32[2]{0:T(128)S(1)} %pad_add_fusion.par, s32[32,64]{1,0:T(8,128)} %bitcast.8, s32[32,64]{1,0:T(8,128)} %bitcast.10, f32[32,64]{1,0:T(8,128)} %bitcast.12), custom_call_target="tpu_custom_call" | custom-call | tf_op jit(solution)/shard_map/pallas_call | solution.py:521
  9.0 2.1 %collective-permute-done.row_a = f32[13,32,128]{2,1,0:T(8,128)S(1)} collective-permute-done((f32[13,32,128]{2,1,0:T(8,128)S(1)}, f32[13,32,128]{2,1,0:T(8,128)S(1)}, u32[]{:S(2)}, u32[]{:S(2)}) %collective-permute-start) | collective-permute-done | bytes 213024 | tf_op jit(solution)/shard_map/ppermute | solution.py:467
  11.0 1.3 %shard_map.61 = (f32[3,72,32,128]{3,2,1,0:T(8,128)S(1)}, f32[3,72,32,128]{3,2,1,0:T(8,128)S(1)}, f32[440,128]{1,0:T(8,128)S(1)}, f32[440,128]{1,0:T(8,128)S(1)}) custom-call(s32[2]{0:T(128)S(1)} %pad_add_fusion.par, f32[3,64,32,128]{3,2,1,0:T(8,128)S(1)} %copy-done, ...), custom_call_target="tpu_custom_call", output_to_operand_aliasing={{1}: (2, {})} | custom-call | tf_op jit(solution)/shard_map/pallas_call | solution.py:521
  12.4 2.7 %collective-permute-start.3 = (f32[440,128]{1,0:T(8,128)S(1)}, f32[440,128]{1,0:T(8,128)S(1)}, u32[]{:S(2)}, u32[]{:S(2)}) collective-permute-start(f32[440,128]{1,0:T(8,128)S(1)} %get-tuple-element.32), channel_id=1, source_target_pairs={{0,7},{1,2},{2,1},{3,4},{4,3},{5,6},{6,5},{7,0},{8,15},{9,10},{10,... | collective-permute-start | bytes 675848 | tf_op jit(solution)/shard_map/ppermute | solution.py:467
  15.1 2.0 %shard_map.62.t_ref = f32[3,72,32,128]{3,2,1,0:T(8,128)S(1)} custom-call(f32[3,72,32,128]{3,2,1,0:T(8,128)S(1)} %get-tuple-element.28.t_ref.old, f32[3,72,32,128]{3,2,1,0:T(8,128)S(1)} %get-tuple-element.29.coef_ref, f32[72,128]{1,0:T(8,128)S(1)} %get-tuple-element.30.spin_ref), custom_call_target="tpu_custom_call" | custom-call | tf_op jit(solution)/shard_map/pallas_call | solution.py:521
  17.1 1.9 %shard_map.63.state_in = f32[3,72,32,128]{3,2,1,0:T(8,128)S(1)} custom-call(f32[3,72,32,128]{3,2,1,0:T(8,128)S(1)} %shard_map.62.t_ref, f32[3,72,32,128]{3,2,1,0:T(8,128)S(1)} %get-tuple-element.29.coef_ref, f32[72,128]{1,0:T(8,128)S(1)} %get-tuple-element.30.spin_ref), custom_call_target="tpu_custom_call" | custom-call | tf_op jit(solution)/shard_map/pallas_call | solution.py:521
  19.1 1.3 %collective-permute-done.3.b = f32[440,128]{1,0:T(8,128)S(1)} collective-permute-done((f32[440,128]{1,0:T(8,128)S(1)}, f32[440,128]{1,0:T(8,128)S(1)}, u32[]{:S(2)}, u32[]{:S(2)}) %collective-permute-start.3) | collective-permute-done | bytes 225312 | tf_op jit(solution)/shard_map/ppermute | solution.py:467
  20.4 3.5 %shard_map.64 = (f32[3,72,32,128]{3,2,1,0:T(8,128)S(1)}, f32[2,3,4,72,128]{4,3,2,1,0:T(8,128)S(1)}, f32[432,128]{1,0:T(8,128)S(1)}, f32[432,128]{1,0:T(8,128)S(1...) custom-call(s32[2]{0:T(128)S(1)} %pad_add_fusion.par, ...), custom_call_target="tpu_custom_call", output_to_operand_aliasing={{0}: (2, {})} | custom-call | tf_op jit(solution)/shard_map/pallas_call | solution.py:521
  24.1 1.1 %collective-permute-done.6 = f32[64,128]{1,0:T(8,128)S(1)} collective-permute-done((f32[64,128]{1,0:T(8,128)S(1)}, f32[64,128]{1,0:T(8,128)S(1)}, u32[]{:S(2)}, u32[]{:S(2)}) %collective-permute-start.6) | collective-permute-done | bytes 32800 | tf_op jit(solution)/shard_map/ppermute | solution.py:471
  25.2 2.0 %collective-permute-start.7 = (f32[64,128]{1,0:T(8,128)S(1)}, f32[64,128]{1,0:T(8,128)S(1)}, u32[]{:S(2)}, u32[]{:S(2)}) collective-permute-start(f32[64,128]{1,0:T(8,128)S(1)} %add.42), channel_id=1, source_target_pairs={{0,2},{1,3},{2,0},{3,1},{4,6},{5,7},{6,4},{7,5},{8,10},{9,11},{10,... | collective-permute-start | bytes 98312 | tf_op jit(solution)/shard_map/ppermute | solution.py:471
  29.1 2.3 %collective-permute-done.8 = f32[64,128]{1,0:T(8,128)S(1)} collective-permute-done((f32[64,128]{1,0:T(8,128)S(1)}, f32[64,128]{1,0:T(8,128)S(1)}, u32[]{:S(2)}, u32[]{:S(2)}) %collective-permute-start.8) | collective-permute-done | bytes 32800 | tf_op jit(solution)/shard_map/ppermute | solution.py:471
  31.4 1.1 %collective-permute-done.9 = f32[64,128]{1,0:T(8,128)S(1)} collective-permute-done((f32[64,128]{1,0:T(8,128)S(1)}, f32[64,128]{1,0:T(8,128)S(1)}, u32[]{:S(2)}, u32[]{:S(2)}) %collective-permute-start.9) | collective-permute-done | bytes 32800 | tf_op jit(solution)/shard_map/ppermute | solution.py:471
  32.6 4.7 %collective-permute-start.10 = (f32[64,128]{1,0:T(8,128)S(1)}, f32[64,128]{1,0:T(8,128)S(1)}, u32[]{:S(2)}, u32[]{:S(2)}) collective-permute-start(f32[64,128]{1,0:T(8,128)S(1)} %add_add_fusion.3), channel_id=1, source_target_pairs={{0,8},{8,0},{16,24},{24,16},{1,9},{9,1},{17,25},{25,17},{2,10},{10... | collective-permute-start | bytes 98312 | tf_op jit(solution)/shard_map/ppermute | solution.py:471
  37.2 1.2 %collective-permute-start.11 = (f32[64,128]{1,0:T(8,128)S(1)}, f32[64,128]{1,0:T(8,128)S(1)}, u32[]{:S(2)}, u32[]{:S(2)}) collective-permute-start(f32[64,128]{1,0:T(8,128)S(1)} %add_add_fusion.3), channel_id=1, source_target_pairs={{0,16},{8,24},{16,0},{24,8},{1,17},{9,25},{17,1},{25,9},{2,18},{10... | collective-permute-start | bytes 98312 | tf_op jit(solution)/shard_map/ppermute | solution.py:471
  38.5 1.4 %collective-permute-start.12 = (f32[64,128]{1,0:T(8,128)S(1)}, f32[64,128]{1,0:T(8,128)S(1)}, u32[]{:S(2)}, u32[]{:S(2)}) collective-permute-start(f32[64,128]{1,0:T(8,128)S(1)} %add_add_fusion.3), channel_id=1, source_target_pairs={{0,24},{8,16},{16,8},{24,0},{1,25},{9,17},{17,9},{25,1},{2,26},{10... | collective-permute-start | bytes 98312 | tf_op jit(solution)/shard_map/ppermute | solution.py:471
  39.9 1.4 %collective-permute-start.5 = (f32[432,128]{1,0:T(8,128)S(1)}, f32[432,128]{1,0:T(8,128)S(1)}, u32[]{:S(2)}, u32[]{:S(2)}) collective-permute-start(f32[432,128]{1,0:T(8,128)S(1)} %get-tuple-element.36), channel_id=1, source_target_pairs={{0,7},{1,2},{2,1},{3,4},{4,3},{5,6},{6,5},{7,0},{8,15},{9,10},{10,... | collective-permute-start | bytes 663560 | tf_op jit(solution)/shard_map/ppermute | solution.py:467
  41.2 1.2 %collective-permute-done.11 = f32[64,128]{1,0:T(8,128)S(1)} collective-permute-done((f32[64,128]{1,0:T(8,128)S(1)}, f32[64,128]{1,0:T(8,128)S(1)}, u32[]{:S(2)}, u32[]{:S(2)}) %collective-permute-start.11) | collective-permute-done | bytes 32800 | tf_op jit(solution)/shard_map/ppermute | solution.py:471
  42.5 1.8 %collective-permute-done.12 = f32[64,128]{1,0:T(8,128)S(1)} collective-permute-done((f32[64,128]{1,0:T(8,128)S(1)}, f32[64,128]{1,0:T(8,128)S(1)}, u32[]{:S(2)}, u32[]{:S(2)}) %collective-permute-start.12) | collective-permute-done | bytes 32800 | tf_op jit(solution)/shard_map/ppermute | solution.py:471
  44.3 1.9 %shard_map.65.t_ref = f32[3,72,32,128]{3,2,1,0:T(8,128)S(1)} custom-call(f32[3,72,32,128]{3,2,1,0:T(8,128)S(1)} %get-tuple-element.33.t_ref.old, f32[3,72,32,128]{3,2,1,0:T(8,128)S(1)} %get-tuple-element.29.coef_ref, f32[72,128]{1,0:T(8,128)S(1)} %get-tuple-element.30.spin_ref), custom_call_target="tpu_custom_call" | custom-call | tf_op jit(solution)/shard_map/pallas_call | solution.py:521
  46.2 1.8 %shard_map.66.state_in = f32[3,72,32,128]{3,2,1,0:T(8,128)S(1)} custom-call(f32[3,72,32,128]{3,2,1,0:T(8,128)S(1)} %shard_map.65.t_ref, f32[3,72,32,128]{3,2,1,0:T(8,128)S(1)} %get-tuple-element.29.coef_ref, f32[72,128]{1,0:T(8,128)S(1)} %get-tuple-element.30.spin_ref), custom_call_target="tpu_custom_call" | custom-call | tf_op jit(solution)/shard_map/pallas_call | solution.py:521
  48.0 4.4 %shard_map.67 = (f32[128,128]{1,0:T(8,128)S(1)}, f32[1,128]{1,0:T(1,128)S(1)}) custom-call(s32[2]{0:T(128)S(1)} %pad_add_fusion.par, f32[64,128]{1,0:T(8,128)S(1)} %add_add_fusion.2.mine_ref, f32[64,128]{1,0:T(8,128)S(1)} %collective-permute-done.13.other_ref, f32[1,128]{1,0:T(1,128)S(1)} %broadcast_in_dim.3.prior_ref), custom_call_target="tpu_custom_call" | custom-call | tf_op jit(solution)/shard_map/pallas_call | solution.py:521
  52.5 4.5 %shard_map.68 = (f32[3,72,32,128]{3,2,1,0:T(8,128)S(1)}, f32[12,512,128]{2,1,0:T(8,128)S(1)}, f32[64,128]{1,0:T(8,128)S(1)}, f32[64,128]{1,0:T(8,128)S(1)}) custom-call(s32[2]{0:T(128)S(1)} %pad_add_fusion.par, f32[3,72,32,128]{3,2,1,0:T(8,128)S(1)} %get-tuple-element.33.t_ref.old, ...), custom_call_target="tpu_custom_call", output_to_operand_aliasing={{0}: (2, {})} | custom-call | tf_op jit(solution)/shard_map/pallas_call | solution.py:521
  58.4 1.6 %collective-permute-start.15 = (f32[64,128]{1,0:T(8,128)S(1)}, f32[64,128]{1,0:T(8,128)S(1)}, u32[]{:S(2)}, u32[]{:S(2)}) collective-permute-start(f32[64,128]{1,0:T(8,128)S(1)} %add.49), channel_id=1, source_target_pairs={{0,2},{1,3},{2,0},{3,1},{4,6},{5,7},{6,4},{7,5},{8,10},{9,11},{10,... | collective-permute-start | bytes 98312 | tf_op jit(solution)/shard_map/ppermute | solution.py:471
  60.2 1.7 %collective-permute-start.17 = (f32[64,128]{1,0:T(8,128)S(1)}, f32[64,128]{1,0:T(8,128)S(1)}, u32[]{:S(2)}, u32[]{:S(2)}) collective-permute-start(f32[64,128]{1,0:T(8,128)S(1)} %add.49), channel_id=1, source_target_pairs={{0,6},{1,7},{2,4},{3,5},{4,2},{5,3},{6,0},{7,1},{8,14},{9,15},{10,... | collective-permute-start | bytes 98312 | tf_op jit(solution)/shard_map/ppermute | solution.py:471
  62.3 1.9 %collective-permute-done.16 = f32[64,128]{1,0:T(8,128)S(1)} collective-permute-done((f32[64,128]{1,0:T(8,128)S(1)}, f32[64,128]{1,0:T(8,128)S(1)}, u32[]{:S(2)}, u32[]{:S(2)}) %collective-permute-start.16) | collective-permute-done | bytes 32800 | tf_op jit(solution)/shard_map/ppermute | solution.py:471
  65.3 1.8 %collective-permute-start.19 = (f32[64,128]{1,0:T(8,128)S(1)}, f32[64,128]{1,0:T(8,128)S(1)}, u32[]{:S(2)}, u32[]{:S(2)}) collective-permute-start(f32[64,128]{1,0:T(8,128)S(1)} %add_add_fusion.1), channel_id=1, source_target_pairs={{0,16},{8,24},{16,0},{24,8},{1,17},{9,25},{17,1},{25,9},{2,18},{10... | collective-permute-start | bytes 98312 | tf_op jit(solution)/shard_map/ppermute | solution.py:471
  67.1 2.4 %collective-permute-start.20 = (f32[64,128]{1,0:T(8,128)S(1)}, f32[64,128]{1,0:T(8,128)S(1)}, u32[]{:S(2)}, u32[]{:S(2)}) collective-permute-start(f32[64,128]{1,0:T(8,128)S(1)} %add_add_fusion.1), channel_id=1, source_target_pairs={{0,24},{8,16},{16,8},{24,0},{1,25},{9,17},{17,9},{25,1},{2,26},{10... | collective-permute-start | bytes 98312 | tf_op jit(solution)/shard_map/ppermute | solution.py:471
  70.3 2.5 %collective-permute-done.20 = f32[64,128]{1,0:T(8,128)S(1)} collective-permute-done((f32[64,128]{1,0:T(8,128)S(1)}, f32[64,128]{1,0:T(8,128)S(1)}, u32[]{:S(2)}, u32[]{:S(2)}) %collective-permute-start.20) | collective-permute-done | bytes 32800 | tf_op jit(solution)/shard_map/ppermute | solution.py:471
  72.9 1.2 %collective-permute-done.21.other_ref = f32[64,128]{1,0:T(8,128)S(1)} collective-permute-done((f32[64,128]{1,0:T(8,128)S(1)}, f32[64,128]{1,0:T(8,128)S(1)}, u32[]{:S(2)}, u32[]{:S(2)}) %collective-permute-start.21) | collective-permute-done | bytes 32800 | tf_op jit(solution)/shard_map/ppermute | solution.py:471
  74.1 7.7 %shard_map.69 = (f32[12,512,128]{2,1,0:T(8,128)}, f32[1,128]{1,0:T(1,128)}) custom-call(s32[2]{0:T(128)S(1)} %pad_add_fusion.par, f32[64,128]{1,0:T(8,128)S(1)} %add_add_fusion.mine_ref, f32[64,128]{1,0:T(8,128)S(1)} %collective-permute-done.21.other_ref, f32[1,128]{1,0:T(1,128)S(1)} %get-tuple-element.42.prior_ref, f32[12,512,128]{2,1,0:T(8,128)S(1)} %get-tuple-element.43.t_ref), custom_call_target="tpu_custom_call" | custom-call | tf_op jit(solution)/shard_map/pallas_call | solution.py:521
  (33 shorter events, 7.0 us)
Async XLA Ops:
  0.6 10.4 %copy-start = (f32[3,64,32,128]{3,2,1,0:T(8,128)S(1)}, f32[3,64,32,128]{3,2,1,0:T(8,128)}, u32[]{:S(2)}) copy-start(f32[3,64,32,128]{3,2,1,0:T(8,128)} %t_ref.3) | copy-start | bytes 9437188
  2.7 8.3 %collective-permute-start = (f32[13,32,128]{2,1,0:T(8,128)S(1)}, f32[13,32,128]{2,1,0:T(8,128)S(1)}, u32[]{:S(2)}, u32[]{:S(2)}) collective-permute-start(f32[13,32,128]{2,1,0:T(8,128)S(1)} %get-tuple-element.26), channel_id=1, source_target_pairs={{0,8},{8,0},{16,24},{24,16},{1,9},{9,1},{17,25},{25,17},{2,10},{10... | collective-permute-start | bytes 638984 | tf_op jit(solution)/shard_map/ppermute | solution.py:467
  5.8 5.3 %collective-permute-start.1 = (f32[13,32,128]{2,1,0:T(8,128)S(1)}, f32[13,32,128]{2,1,0:T(8,128)S(1)}, u32[]{:S(2)}, u32[]{:S(2)}) collective-permute-start(f32[13,32,128]{2,1,0:T(8,128)S(1)} %get-tuple-element.27), channel_id=1, source_target_pairs={{8,16},{16,8},{9,17},{17,9},{10,18},{18,10},{11,19},{19,11},{12,20... | collective-permute-start | bytes 638984 | tf_op jit(solution)/shard_map/ppermute | solution.py:467
  12.3 6.7 %collective-permute-start.2 = (f32[440,128]{1,0:T(8,128)S(1)}, f32[440,128]{1,0:T(8,128)S(1)}, u32[]{:S(2)}, u32[]{:S(2)}) collective-permute-start(f32[440,128]{1,0:T(8,128)S(1)} %get-tuple-element.31), channel_id=1, source_target_pairs={{0,1},{1,0},{2,3},{3,2},{4,5},{5,4},{6,7},{7,6},{8,9},{9,8},{10,11... | collective-permute-start | bytes 675848 | tf_op jit(solution)/shard_map/ppermute | solution.py:467
  12.4 8.0 %collective-permute-start.3 = (f32[440,128]{1,0:T(8,128)S(1)}, f32[440,128]{1,0:T(8,128)S(1)}, u32[]{:S(2)}, u32[]{:S(2)}) collective-permute-start(f32[440,128]{1,0:T(8,128)S(1)} %get-tuple-element.32), channel_id=1, source_target_pairs={{0,7},{1,2},{2,1},{3,4},{4,3},{5,6},{6,5},{7,0},{8,15},{9,10},{10,... | collective-permute-start | bytes 675848 | tf_op jit(solution)/shard_map/ppermute | solution.py:467
  23.9 1.3 %collective-permute-start.6 = (f32[64,128]{1,0:T(8,128)S(1)}, f32[64,128]{1,0:T(8,128)S(1)}, u32[]{:S(2)}, u32[]{:S(2)}) collective-permute-start(f32[64,128]{1,0:T(8,128)S(1)} %get-tuple-element.38), channel_id=1, source_target_pairs={{0,1},{1,0},{2,3},{3,2},{4,5},{5,4},{6,7},{7,6},{8,9},{9,8},{10,11... | collective-permute-start | bytes 98312 | tf_op jit(solution)/shard_map/ppermute | solution.py:471
  25.2 3.9 %collective-permute-start.7 = (f32[64,128]{1,0:T(8,128)S(1)}, f32[64,128]{1,0:T(8,128)S(1)}, u32[]{:S(2)}, u32[]{:S(2)}) collective-permute-start(f32[64,128]{1,0:T(8,128)S(1)} %add.42), channel_id=1, source_target_pairs={{0,2},{1,3},{2,0},{3,1},{4,6},{5,7},{6,4},{7,5},{8,10},{9,11},{10,... | collective-permute-start | bytes 98312 | tf_op jit(solution)/shard_map/ppermute | solution.py:471
  27.2 4.3 %collective-permute-start.8 = (f32[64,128]{1,0:T(8,128)S(1)}, f32[64,128]{1,0:T(8,128)S(1)}, u32[]{:S(2)}, u32[]{:S(2)}) collective-permute-start(f32[64,128]{1,0:T(8,128)S(1)} %add.42), channel_id=1, source_target_pairs={{0,4},{1,5},{2,6},{3,7},{4,0},{5,1},{6,2},{7,3},{8,12},{9,13},{10,... | collective-permute-start | bytes 98312 | tf_op jit(solution)/shard_map/ppermute | solution.py:471
  27.8 4.8 %collective-permute-start.9 = (f32[64,128]{1,0:T(8,128)S(1)}, f32[64,128]{1,0:T(8,128)S(1)}, u32[]{:S(2)}, u32[]{:S(2)}) collective-permute-start(f32[64,128]{1,0:T(8,128)S(1)} %add.42), channel_id=1, source_target_pairs={{0,6},{1,7},{2,4},{3,5},{4,2},{5,3},{6,0},{7,1},{8,14},{9,15},{10,... | collective-permute-start | bytes 98312 | tf_op jit(solution)/shard_map/ppermute | solution.py:471
  32.6 8.7 %collective-permute-start.10 = (f32[64,128]{1,0:T(8,128)S(1)}, f32[64,128]{1,0:T(8,128)S(1)}, u32[]{:S(2)}, u32[]{:S(2)}) collective-permute-start(f32[64,128]{1,0:T(8,128)S(1)} %add_add_fusion.3), channel_id=1, source_target_pairs={{0,8},{8,0},{16,24},{24,16},{1,9},{9,1},{17,25},{25,17},{2,10},{10... | collective-permute-start | bytes 98312 | tf_op jit(solution)/shard_map/ppermute | solution.py:471
  37.2 5.2 %collective-permute-start.11 = (f32[64,128]{1,0:T(8,128)S(1)}, f32[64,128]{1,0:T(8,128)S(1)}, u32[]{:S(2)}, u32[]{:S(2)}) collective-permute-start(f32[64,128]{1,0:T(8,128)S(1)} %add_add_fusion.3), channel_id=1, source_target_pairs={{0,16},{8,24},{16,0},{24,8},{1,17},{9,25},{17,1},{25,9},{2,18},{10... | collective-permute-start | bytes 98312 | tf_op jit(solution)/shard_map/ppermute | solution.py:471
  38.5 5.7 %collective-permute-start.12 = (f32[64,128]{1,0:T(8,128)S(1)}, f32[64,128]{1,0:T(8,128)S(1)}, u32[]{:S(2)}, u32[]{:S(2)}) collective-permute-start(f32[64,128]{1,0:T(8,128)S(1)} %add_add_fusion.3), channel_id=1, source_target_pairs={{0,24},{8,16},{16,8},{24,0},{1,25},{9,17},{17,9},{25,1},{2,26},{10... | collective-permute-start | bytes 98312 | tf_op jit(solution)/shard_map/ppermute | solution.py:471
  39.9 12.6 %collective-permute-start.4 = (f32[432,128]{1,0:T(8,128)S(1)}, f32[432,128]{1,0:T(8,128)S(1)}, u32[]{:S(2)}, u32[]{:S(2)}) collective-permute-start(f32[432,128]{1,0:T(8,128)S(1)} %get-tuple-element.35), channel_id=1, source_target_pairs={{0,1},{1,0},{2,3},{3,2},{4,5},{5,4},{6,7},{7,6},{8,9},{9,8},{10,11... | collective-permute-start | bytes 663560 | tf_op jit(solution)/shard_map/ppermute | solution.py:467
  39.9 12.6 %collective-permute-start.5 = (f32[432,128]{1,0:T(8,128)S(1)}, f32[432,128]{1,0:T(8,128)S(1)}, u32[]{:S(2)}, u32[]{:S(2)}) collective-permute-start(f32[432,128]{1,0:T(8,128)S(1)} %get-tuple-element.36), channel_id=1, source_target_pairs={{0,7},{1,2},{2,1},{3,4},{4,3},{5,6},{6,5},{7,0},{8,15},{9,10},{10,... | collective-permute-start | bytes 663560 | tf_op jit(solution)/shard_map/ppermute | solution.py:467
  44.2 3.8 %collective-permute-start.13 = (f32[64,128]{1,0:T(8,128)S(1)}, f32[64,128]{1,0:T(8,128)S(1)}, u32[]{:S(2)}, u32[]{:S(2)}) collective-permute-start(f32[64,128]{1,0:T(8,128)S(1)} %add_add_fusion.2.mine_ref), channel_id=1, source_target_pairs={{0,1},{1,0},{2,3},{3,2},{4,5},{5,4},{6,7},{7,6},{8,9},{9,8},{10,11... | collective-permute-start | bytes 98312 | tf_op jit(solution)/shard_map/ppermute | solution.py:471
  57.0 1.4 %collective-permute-start.14 = (f32[64,128]{1,0:T(8,128)S(1)}, f32[64,128]{1,0:T(8,128)S(1)}, u32[]{:S(2)}, u32[]{:S(2)}) collective-permute-start(f32[64,128]{1,0:T(8,128)S(1)} %get-tuple-element.41), channel_id=1, source_target_pairs={{0,1},{1,0},{2,3},{3,2},{4,5},{5,4},{6,7},{7,6},{8,9},{9,8},{10,11... | collective-permute-start | bytes 98312 | tf_op jit(solution)/shard_map/ppermute | solution.py:471
  58.4 3.9 %collective-permute-start.15 = (f32[64,128]{1,0:T(8,128)S(1)}, f32[64,128]{1,0:T(8,128)S(1)}, u32[]{:S(2)}, u32[]{:S(2)}) collective-permute-start(f32[64,128]{1,0:T(8,128)S(1)} %add.49), channel_id=1, source_target_pairs={{0,2},{1,3},{2,0},{3,1},{4,6},{5,7},{6,4},{7,5},{8,10},{9,11},{10,... | collective-permute-start | bytes 98312 | tf_op jit(solution)/shard_map/ppermute | solution.py:471
  60.0 4.3 %collective-permute-start.16 = (f32[64,128]{1,0:T(8,128)S(1)}, f32[64,128]{1,0:T(8,128)S(1)}, u32[]{:S(2)}, u32[]{:S(2)}) collective-permute-start(f32[64,128]{1,0:T(8,128)S(1)} %add.49), channel_id=1, source_target_pairs={{0,4},{1,5},{2,6},{3,7},{4,0},{5,1},{6,2},{7,3},{8,12},{9,13},{10,... | collective-permute-start | bytes 98312 | tf_op jit(solution)/shard_map/ppermute | solution.py:471
  60.2 4.8 %collective-permute-start.17 = (f32[64,128]{1,0:T(8,128)S(1)}, f32[64,128]{1,0:T(8,128)S(1)}, u32[]{:S(2)}, u32[]{:S(2)}) collective-permute-start(f32[64,128]{1,0:T(8,128)S(1)} %add.49), channel_id=1, source_target_pairs={{0,6},{1,7},{2,4},{3,5},{4,2},{5,3},{6,0},{7,1},{8,14},{9,15},{10,... | collective-permute-start | bytes 98312 | tf_op jit(solution)/shard_map/ppermute | solution.py:471
  65.1 4.5 %collective-permute-start.18 = (f32[64,128]{1,0:T(8,128)S(1)}, f32[64,128]{1,0:T(8,128)S(1)}, u32[]{:S(2)}, u32[]{:S(2)}) collective-permute-start(f32[64,128]{1,0:T(8,128)S(1)} %add_add_fusion.1), channel_id=1, source_target_pairs={{0,8},{8,0},{16,24},{24,16},{1,9},{9,1},{17,25},{25,17},{2,10},{10... | collective-permute-start | bytes 98312 | tf_op jit(solution)/shard_map/ppermute | solution.py:471
  65.3 5.1 %collective-permute-start.19 = (f32[64,128]{1,0:T(8,128)S(1)}, f32[64,128]{1,0:T(8,128)S(1)}, u32[]{:S(2)}, u32[]{:S(2)}) collective-permute-start(f32[64,128]{1,0:T(8,128)S(1)} %add_add_fusion.1), channel_id=1, source_target_pairs={{0,16},{8,24},{16,0},{24,8},{1,17},{9,25},{17,1},{25,9},{2,18},{10... | collective-permute-start | bytes 98312 | tf_op jit(solution)/shard_map/ppermute | solution.py:471
  67.1 5.7 %collective-permute-start.20 = (f32[64,128]{1,0:T(8,128)S(1)}, f32[64,128]{1,0:T(8,128)S(1)}, u32[]{:S(2)}, u32[]{:S(2)}) collective-permute-start(f32[64,128]{1,0:T(8,128)S(1)} %add_add_fusion.1), channel_id=1, source_target_pairs={{0,24},{8,16},{16,8},{24,0},{1,25},{9,17},{17,9},{25,1},{2,26},{10... | collective-permute-start | bytes 98312 | tf_op jit(solution)/shard_map/ppermute | solution.py:471
  72.8 1.3 %collective-permute-start.21 = (f32[64,128]{1,0:T(8,128)S(1)}, f32[64,128]{1,0:T(8,128)S(1)}, u32[]{:S(2)}, u32[]{:S(2)}) collective-permute-start(f32[64,128]{1,0:T(8,128)S(1)} %add_add_fusion.mine_ref), channel_id=1, source_target_pairs={{0,1},{1,0},{2,3},{3,2},{4,5},{5,4},{6,7},{7,6},{8,9},{9,8},{10,11... | collective-permute-start | bytes 98312 | tf_op jit(solution)/shard_map/ppermute | solution.py:471

commit v5 on v4

v5 whole, which is shorter than its diff:
```python
import functools

import jax
import jax.numpy as jnp
from jax import lax
from jax.experimental import pallas as pl
from jax.experimental.pallas import tpu as pltpu
from jax.sharding import PartitionSpec as P

STEPS = 2
RENORMS = 2
LEVELS = 50

viscosity = 0.15
gravity = 0.5
rotation = 0.4

SUB = 8
LANES = 128
FIELDS = 3
HALO = STEPS * RENORMS
SIDE = STEPS
TILES = 12
VMEM_LIMIT = 16 * 1024 * 1024

HBM = pl.BlockSpec(memory_space=pltpu.HBM)
VMEM = pl.BlockSpec(memory_space=pltpu.VMEM)
SMEM = pl.BlockSpec(memory_space=pltpu.SMEM)


def params():
    return pltpu.CompilerParams(vmem_limit_bytes=VMEM_LIMIT)


def shape_of(*dims):
    return jax.ShapeDtypeStruct(dims, jnp.float32)


def lane_spread(block, lane):
    return jnp.broadcast_to(block[:, lane : lane + 1], (block.shape[0], LANES))


def fetch(sources, places, sems):
    copies = [
        pltpu.make_async_copy(source, place, sems.at[i])
        for i, (source, place) in enumerate(zip(sources, places))
    ]
    for copy in copies:
        copy.start()
    return copies


def finish_all(copies):
    for copy in copies:
        copy.wait()


def fields_of(sea_ref, levels_ref, current_ref):
    return (
        sea_ref[...].astype(jnp.float32),
        0.5 * current_ref[...],
        0.5 * ((levels_ref[...] + 1).astype(jnp.float32) / LEVELS),
    )


def sides_of(par):
    odd_row, odd_col = par[0] % 2, par[1] % 2
    return (1 - odd_row, odd_row), (1 - odd_col, odd_col)


def pack_rows(
    par, t_ref, sea_ref, levels_ref, current_ref, row_a, row_b, sea, levels, current, wide, sems, field_sems
):
    comps, rows, cols, _ = t_ref.shape
    norths, _ = sides_of(par)
    field_copies = fetch((sea_ref, levels_ref, current_ref), (sea, levels, current), field_sems)
    slots = [(slot, msg, comp) for slot, msg in ((0, row_a), (1, row_b)) for comp in range(comps)]
    copies = fetch(
        [t_ref.at[comp, pl.ds(norths[slot] * (rows - HALO), HALO)] for slot, _, comp in slots],
        [msg.at[pl.ds(comp * HALO, HALO)] for _, msg, comp in slots],
        sems,
    )
    lane = lax.broadcasted_iota(jnp.int32, (cols, LANES), 1)
    wide[...] = jnp.zeros_like(wide)
    packed = [jnp.zeros((cols, LANES), jnp.float32)] * 2
    finish_all(field_copies)
    for field, value in enumerate(fields_of(sea, levels, current)):
        wide[:, pl.ds(0, rows)] = value
        whole = wide[...]
        for north in (0, 1):
            shift = (field * SUB - north * (rows - HALO)) % LANES
            moved = pltpu.roll(whole, shift, 1) if shift else whole
            here = (lane >= field * SUB) & (lane < field * SUB + HALO)
            packed[north] = jnp.where(here, moved, packed[north])
    for slot, msg in ((0, row_a), (1, row_b)):
        msg[comps * HALO] = jnp.where(norths[slot] == 1, packed[1], packed[0])
    finish_all(copies)


def spread_fields(
    total_rows, par, t_ref, sea_ref, levels_ref, current_ref, state, coef, wide, spin, sea, levels, current, sems, field_sems
):
    comps, rows, cols, _ = t_ref.shape
    field_copies = fetch((sea_ref, levels_ref, current_ref), (sea, levels, current), field_sems)
    cells = [(comp, lon) for comp in range(comps) for lon in range(cols)]
    copies = fetch(
        [t_ref.at[comp, :, lon] for comp, lon in cells],
        [state.at[comp, SIDE + lon, pl.ds(0, rows)] for comp, lon in cells],
        sems,
    )
    line = lax.broadcasted_iota(jnp.int32, spin.shape, 0)
    line = jnp.where(line < rows + HALO, line, line - (rows + 2 * HALO))
    latitude = (par[0] * rows + line).astype(jnp.float32)
    angle = (-70.0 + 140.0 * (latitude + 0.5) / total_rows) * (jnp.pi / 180.0)
    spin[...] = rotation * jnp.sin(angle)
    wide[...] = jnp.zeros_like(wide)
    finish_all(field_copies)
    for field, value in enumerate(fields_of(sea, levels, current)):
        wide[field, :, pl.ds(0, rows)] = value
        natural = jnp.transpose(wide[field])[:rows]
        for lon in range(cols):
            coef[field, SIDE + lon, pl.ds(0, rows), :] = lane_spread(natural, lon)
    finish_all(copies)


def column_at(east, cols, depth):
    return SIDE + depth + east * (cols - 1 - 2 * depth)


def send_columns(par, state, cols_sent):
    comps, wide, tall, _ = state.shape
    _, easts = sides_of(par)
    for slot, msg in enumerate(cols_sent):
        for comp in range(comps):
            for j in range(SIDE):
                column = column_at(easts[slot], wide - 2 * SIDE, j)
                msg[pl.ds((comp * SIDE + j) * tall, tall), :] = state[comp, column]


def join_rows(par, state_in, coef_in, wide, row_a, row_b, state, coef, col_a, col_b):
    comps, length, tall, _ = state.shape
    cols, rows = length - 2 * SIDE, tall - 2 * HALO
    norths, easts = sides_of(par)
    flat = state.reshape(comps * length * tall, LANES)
    for slot, msg in ((0, row_a), (1, row_b)):
        line = rows + HALO * (1 - norths[slot])
        for comp in range(comps):
            for h in range(HALO):
                for lon in range(0, cols, SUB):
                    at = (comp * length + SIDE + lon) * tall + line + h
                    flat[pl.ds(at, SUB, stride=tall), :] = msg[comp * HALO + h, pl.ds(lon, SUB), :]
    lane = lax.broadcasted_iota(jnp.int32, (cols, LANES), 1)
    north = jnp.where(norths[0] == 1, row_a[comps * HALO], row_b[comps * HALO])
    south = jnp.where(norths[0] == 1, row_b[comps * HALO], row_a[comps * HALO])
    beyond = jnp.where(lane % SUB < HALO, north, pltpu.roll(south, HALO, 1))
    natural = jnp.transpose(beyond)
    for field in range(FIELDS):
        block = natural[field * SUB : (field + 1) * SUB]
        for lon in range(cols):
            coef[field, SIDE + lon, pl.ds(rows, SUB), :] = lane_spread(block, lon)
    tail = comps * SIDE * tall
    whole = [
        jnp.where(lane < rows, wide[field], pltpu.roll(beyond, rows - field * SUB, 1))
        for field in range(FIELDS)
    ]
    for slot, msg in ((0, col_a), (1, col_b)):
        msg[pl.ds(tail, SUB), :] = jnp.zeros((SUB, LANES), jnp.float32)
        for field in range(FIELDS):
            msg[pl.ds(tail + field, 1), :] = jnp.where(
                easts[slot] == 1, whole[field][cols - 1 :], whole[field][:1]
            )
    send_columns(par, state, (col_a, col_b))


def model(own, x_diff, x_sum, above, below, sea, flow, depth, spin):
    keep, half = 1.0 - 4.0 * viscosity, 0.5 * gravity
    mixed = [
        keep * c + viscosity * (x + (n + s)) - flow * d
        for c, d, x, n, s in zip(own, x_diff, x_sum, above, below)
    ]
    v_y, h_y = above[1] - below[1], above[2] - below[2]
    return (
        sea * (mixed[0] - half * x_diff[2] + spin * own[1]),
        sea * (mixed[1] - half * h_y - spin * own[0]),
        sea * (mixed[2] - depth * (x_diff[0] + v_y)),
    )


def advance_column(source, target, coef_ref, spin_ref, lon):
    comps, length, tall, _ = source.shape
    flat = source.reshape(comps * length * tall, LANES)
    sub = lax.broadcasted_iota(jnp.int32, (SUB, LANES), 0)
    tiles = tall // SUB
    for tile in range(tiles):
        lines = pl.ds(SUB * tile, SUB)
        own, east, west = (
            [source[comp, lon + shift, lines, :] for comp in range(comps)] for shift in (0, 1, -1)
        )
        starts = [(comp * length + lon) * tall + SUB * tile for comp in range(comps)]
        if tile < tiles - 1:
            above = [flat[pl.ds(start + 1, SUB), :] for start in starts]
        else:
            wrap = [source[comp, lon, pl.ds(0, SUB), :] for comp in range(comps)]
            above = [
                jnp.where(sub == SUB - 1, pltpu.roll(w, SUB - 1, 0), pltpu.roll(o, SUB - 1, 0))
                for w, o in zip(wrap, own)
            ]
        if tile > 0:
            below = [flat[pl.ds(start - 1, SUB), :] for start in starts]
        else:
            wrap = [source[comp, lon, pl.ds(tall - SUB, SUB), :] for comp in range(comps)]
            below = [
                jnp.where(sub == 0, pltpu.roll(w, 1, 0), pltpu.roll(o, 1, 0))
                for w, o in zip(wrap, own)
            ]
        new = model(
            own,
            [e - w for e, w in zip(east, west)],
            [e + w for e, w in zip(east, west)],
            above,
            below,
            *(coef_ref[field, lon, lines, :] for field in range(FIELDS)),
            spin_ref[lines, :],
        )
        for comp in range(comps):
            target[comp, lon, lines, :] = new[comp]


def apply_inside(step, source, coef_ref, spin_ref, target):
    first = SIDE + step + 1
    count = source.shape[1] - 2 * first

    @pl.loop(0, count // 2)
    def _(pair):
        advance_column(source, target, coef_ref, spin_ref, first + 2 * pair)
        advance_column(source, target, coef_ref, spin_ref, first + 2 * pair + 1)


def mend_columns(par, states, coef_ref, spin_ref, cols_got):
    comps, length, tall, _ = states[0].shape
    _, easts = sides_of(par)
    for slot, msg in enumerate(cols_got):
        for comp in range(comps):
            for j in range(SIDE):
                column = column_at(easts[slot], length - 2 * SIDE, -1 - j)
                states[0][comp, column] = msg[pl.ds((comp * SIDE + j) * tall, tall), :]
    for step in range(STEPS):
        first = step + 1
        skip = length - 2 * first - 2 * SIDE

        @pl.loop(0, 2 * SIDE)
        def _(i):
            lon = first + i + (i // SIDE) * skip
            advance_column(states[step], states[step + 1], coef_ref, spin_ref, lon)


def join_gram(
    scale, par, start_in, middle_in, state_in, coef_in, spin_ref, a, b, start, middle, state, coef, col_a, col_b, kept, sent, total
):
    _, length, tall, _ = state.shape
    _, easts = sides_of(par)
    for slot, msg in enumerate((a, b)):
        upright = jnp.transpose(msg[pl.ds(msg.shape[0] - SUB, SUB), :])
        for field in range(FIELDS):
            column = column_at(easts[slot], length - 2 * SIDE, -1)
            coef[field, column] = lane_spread(upright[:tall], field)
    mend_columns(par, (start, middle, state), coef, spin_ref, (a, b))
    send_columns(par, state, (col_a, col_b))
    gram = sum(gram_of(*split_halves(cells)) for _, _, cells in tiles_of(state))
    write_halves(par, gram, scale, kept, sent, total)


def tiles_of(state):
    comps, length, tall, _ = state.shape
    rows = tall - 2 * HALO
    for comp in range(comps):
        for lon in range(0, length - 2 * SIDE, SUB):
            cells = state[comp, pl.ds(SIDE + lon, SUB), pl.ds(0, rows), :]
            yield comp, lon, cells.reshape(SUB * rows, LANES)


def split_halves(value):
    high = value.astype(jnp.bfloat16)
    return high, (value - high.astype(jnp.float32)).astype(jnp.bfloat16)


def gram_of(high, low):
    return lax.dot_general(
        high,
        jnp.concatenate([high, low], axis=1),
        (((0,), (0,)), ((), ())),
        preferred_element_type=jnp.float32,
    )


def write_halves(par, gram, scale, kept, sent, total):
    odd = par[1] % 2
    rows = LANES // 2
    mixed = gram[:, LANES:]
    total[...] = scale * (gram[:, :LANES] + (mixed + jnp.transpose(mixed)))
    kept[...] = total[pl.ds(odd * rows, rows), :]
    sent[...] = total[pl.ds((1 - odd) * rows, rows), :]


def invert_factor(gram_ref, work):
    count = LANES // SUB
    lane = lax.broadcasted_iota(jnp.int32, (SUB, LANES), 1)
    sub = lax.broadcasted_iota(jnp.int32, (SUB, LANES), 0)
    rows = [gram_ref[pl.ds(SUB * i, SUB), :] for i in range(count)]
    for block in range(count):
        base = SUB * block
        here = (lane >= base) & (lane < base + SUB)
        spread = [lane_spread(rows[block], base + l) for l in range(SUB)]
        low = [
            [jnp.broadcast_to(spread[l][k : k + 1, :], (SUB, LANES)) for l in range(k + 1)]
            for k in range(SUB)
        ]
        pivot = jnp.where(here, jnp.where(lane - base == sub, 1.0, 0.0), rows[block])
        inv, scaled = [], []
        for k in range(SUB):
            inv.append(lax.rsqrt(low[k][k]))
            for i in range(k + 1, SUB):
                low[i][k] = low[i][k] * inv[k]
            for i in range(k + 1, SUB):
                for m in range(k + 1, i + 1):
                    low[i][m] = low[i][m] - low[i][k] * low[m][k]
            line = jnp.broadcast_to(pivot[k : k + 1, :], (SUB, LANES))
            for l in range(k):
                line = line - low[k][l] * scaled[l]
            scaled.append(line * inv[k])
        merged = scaled[0]
        for k in range(1, SUB):
            merged = jnp.where(sub == k, scaled[k], merged)
        work[pl.ds(base, SUB), :] = merged
        for i in range(block + 1, count):
            weights = []
            rest = jnp.where(here, 0.0, rows[i])
            for l in range(SUB):
                weight = lane_spread(rows[i], base + l)
                for m in range(l):
                    weight = weight - weights[m] * low[l][m]
                weights.append(weight * inv[l])
            for l in range(SUB):
                rest = rest - weights[l] * scaled[l]
            rows[i] = rest


def factorize(par, mine_ref, other_ref, gram, work):
    rows = LANES // 2
    odd = par[1] % 2
    gram[pl.ds(odd * rows, rows), :] = mine_ref[...]
    gram[pl.ds((1 - odd) * rows, rows), :] = other_ref[...]
    invert_factor(gram, work)
    row = lax.broadcasted_iota(jnp.int32, (LANES, LANES), 0)
    col = lax.broadcasted_iota(jnp.int32, (LANES, LANES), 1)
    inverse = jnp.where(row >= col, work[...], 0.0)
    diagonal = jnp.sum(jnp.where(row == col, inverse, 0.0), axis=0, keepdims=True)
    return inverse, diagonal


def paired(inverse):
    high = inverse.astype(jnp.bfloat16)
    low = (inverse - high.astype(jnp.float32)).astype(jnp.bfloat16)
    return jnp.concatenate(
        [jnp.concatenate([high, high], axis=1), jnp.concatenate([low, low], axis=1)], axis=0
    )


def times_factor(cells, factor):
    pair = jnp.concatenate(split_halves(cells), axis=1)
    both = lax.dot_general(
        pair, factor, (((1,), (1,)), ((), ())), preferred_element_type=jnp.float32
    )
    return both[:, :LANES] + both[:, LANES:]


def factor_only(par, mine_ref, other_ref, prior_ref, inverse_ref, logs_ref, gram, work):
    inverse, diagonal = factorize(par, mine_ref, other_ref, gram, work)
    inverse_ref[...] = inverse
    logs_ref[...] = prior_ref[...] - jnp.log(diagonal)


def join_update(
    scale, par, start_in, middle_in, state_in, coef_ref, spin_ref, a, b, inverse_ref, start, middle, state, out_ref, kept, sent, factor, total, fresh, sems
):
    factor[...] = paired(inverse_ref[...])
    mend_columns(par, (start, middle, state), coef_ref, spin_ref, (a, b))
    cols = fresh.shape[1]

    def back_copy(comp, lon):
        return pltpu.make_async_copy(
            fresh.at[comp, lon], out_ref.at[comp, :, lon], sems.at[comp * cols + lon]
        )

    gram = 0.0
    copies = []
    for comp, lon, cells in tiles_of(state):
        new = times_factor(cells, factor[...])
        fresh[comp, pl.ds(lon, SUB)] = new.reshape((SUB,) + fresh.shape[2:])
        for i in range(SUB):
            copies.append(back_copy(comp, lon + i))
            copies[-1].start()
        gram += gram_of(*split_halves(new))
    write_halves(par, gram, scale, kept, sent, total)
    finish_all(copies)


def finish(par, mine_ref, other_ref, prior_ref, t_ref, out_ref, logs_ref, gram, work, factor, fresh, sems):
    inverse, diagonal = factorize(par, mine_ref, other_ref, gram, work)
    logs_ref[...] = prior_ref[...] - jnp.log(diagonal)
    factor[...] = paired(inverse)

    def out_copy(tile):
        return pltpu.make_async_copy(fresh.at[tile], out_ref.at[tile], sems.at[tile])

    for tile in range(TILES):
        fresh[tile] = times_factor(t_ref[tile], factor[...])
        out_copy(tile).start()

    for tile in range(TILES):
        out_copy(tile).wait()


def swap_pairs(near_value, far_value, axis, closed):
    count = lax.axis_size(axis)
    near = [(i, i ^ 1) for i in range(count)]
    far = [(i, (i + 1 if i % 2 else i - 1) % count) for i in range(count)]
    if not closed:
        far = far[1:-1]
    return lax.ppermute(near_value, axis, near), lax.ppermute(far_value, axis, far)


def swapped(value, axis, mask):
    return lax.ppermute(value, axis, [(i, i ^ mask) for i in range(lax.axis_size(axis))])


def sum_over(value, axis, first_bit):
    bits = lax.axis_size(axis).bit_length() - 1
    while first_bit < bits:
        low = 1 << first_bit
        if first_bit + 1 < bits:
            high = low << 1
            one, two, three = (swapped(value, axis, mask) for mask in (low, high, low | high))
            value = (value + one) + (two + three)
            first_bit += 2
        else:
            value = value + swapped(value, axis, low)
            first_bit += 1
    return value


def sum_devices(kept, sent):
    mine = kept + swapped(sent, "col", 1)
    mine = sum_over(mine, "col", 1)
    mine = sum_over(mine, "row", 0)
    return mine, swapped(mine, "col", 1)


def body(tangents, sea_mask, levels, current):
    comps, rows, cols, modes = tangents.shape
    total_rows = rows * lax.axis_size("row")
    total_cells = total_rows * cols * lax.axis_size("col")
    scale = 1.0 / total_cells
    row_at, col_at = lax.axis_index("row"), lax.axis_index("col")
    par = jnp.stack([row_at, col_at]).astype(jnp.int32)

    tall, length = rows + 2 * HALO, cols + 2 * SIDE

    block = shape_of(comps, length, tall, modes)
    coefs = shape_of(FIELDS, length, tall, LANES)
    columns = (shape_of(comps * SIDE * tall, modes),) * 2
    first_columns = (shape_of(comps * SIDE * tall + SUB, modes),) * 2
    rows_sent = (shape_of(comps * HALO + 1, cols, modes),) * 2
    halves = (shape_of(modes // 2, modes),) * 2
    square = pltpu.VMEM((modes, modes), jnp.float32)
    factor = pltpu.VMEM((2 * modes, 2 * modes), jnp.bfloat16)

    def call(
        kernel, outs, *operands, specs=None, out_specs=None, scratch=(), aliases=None, cost=1.0
    ):
        return pl.pallas_call(
            kernel,
            out_shape=outs,
            in_specs=specs or [SMEM] + [VMEM] * (len(operands) - 1),
            out_specs=out_specs or (VMEM,) * len(outs),
            scratch_shapes=scratch,
            input_output_aliases=aliases or {},
            compiler_params=params(),
            cost_estimate=pl.CostEstimate(
                flops=int(cost * 1e9), bytes_accessed=int(cost * 3e6), transcendentals=0
            ),
        )(*operands)

    def inside(step, state):
        kernel = functools.partial(apply_inside, step)
        return call(kernel, (block,), state, coef, spin, specs=[VMEM] * 3, cost=2.0)[0]

    def swap_columns(packed):
        return swap_pairs(*packed, "col", True)

    source, *fields = (
        pltpu.with_memory_space_constraint(x, pltpu.HBM)
        for x in (tangents, sea_mask.T, levels.T, current.T)
    )
    upright = [pltpu.VMEM(x.shape, x.dtype) for x in fields]
    packed = call(
        pack_rows,
        rows_sent,
        par,
        source,
        *fields,
        specs=[SMEM] + [HBM] * 4,
        scratch=upright
        + [
            pltpu.VMEM((cols, LANES), jnp.float32),
            pltpu.SemaphoreType.DMA((2 * comps,)),
            pltpu.SemaphoreType.DMA((FIELDS,)),
        ],
    )
    row_halos = swap_pairs(*packed, "row", False)
    start, coef, wide, spin = call(
        functools.partial(spread_fields, total_rows),
        (block, coefs, shape_of(FIELDS, cols, LANES), shape_of(tall, LANES)),
        par,
        source,
        *fields,
        specs=[SMEM] + [HBM] * 4,
        scratch=upright
        + [pltpu.SemaphoreType.DMA((comps * cols,)), pltpu.SemaphoreType.DMA((FIELDS,))],
        cost=3.0,
    )
    start, coef, *packed = call(
        join_rows,
        (block, coefs) + first_columns,
        par,
        start,
        coef,
        wide,
        *row_halos,
        aliases={1: 0, 2: 1},
    )
    logs = jnp.zeros((1, modes), jnp.float32)

    halos = swap_columns(packed)
    middle = inside(0, start)
    state = inside(1, middle)
    _, _, start, coef, *packed, kept, sent = call(
        functools.partial(join_gram, scale),
        (block, block, block, coefs) + columns + halves,
        par,
        start,
        middle,
        state,
        coef,
        spin,
        *halos,
        scratch=[square],
        aliases={1: 0, 2: 1, 3: 2, 4: 3},
        cost=2.0,
    )
    halos = swap_columns(packed)
    mine, other = sum_devices(kept, sent)
    middle = inside(0, start)
    state = inside(1, middle)
    inverse, logs = call(
        factor_only,
        (shape_of(modes, modes), shape_of(1, modes)),
        par,
        mine,
        other,
        logs,
        scratch=[square, square],
        cost=4.4,
    )
    _, _, _, state, kept, sent = call(
        functools.partial(join_update, scale),
        (block, block, block, shape_of(comps, rows, cols, modes)) + halves,
        par,
        start,
        middle,
        state,
        coef,
        spin,
        *halos,
        inverse,
        scratch=[
            factor,
            square,
            pltpu.VMEM((comps, cols, rows, modes), jnp.float32),
            pltpu.SemaphoreType.DMA((comps * cols,)),
        ],
        aliases={1: 0, 2: 1, 3: 2},
        cost=3.0,
    )
    height = comps * rows * cols // TILES
    tiled = shape_of(TILES, height, modes)
    mine, other = sum_devices(kept, sent)
    out, logs = call(
        finish,
        (tiled, shape_of(1, modes)),
        par,
        mine,
        other,
        logs,
        state.reshape(TILES, height, modes),
        out_specs=(HBM, VMEM),
        scratch=[
            square,
            square,
            factor,
            pltpu.VMEM((TILES, height, modes), jnp.float32),
            pltpu.SemaphoreType.DMA((TILES,)),
        ],
    )
    return out.reshape(tangents.shape), logs.reshape(modes)


def solution(mesh):
    placed = (P(None, "row", "col", None), P("row", "col"), P("row", "col"), P("row", "col"))
    return jax.shard_map(
        body,
        mesh=mesh,
        in_specs=placed,
        out_specs=(P(None, "row", "col", None), P()),
        check_vma=False,
    )
```

time: 82.2 us -> 87.8 us (1.068)
  Pallas kernels: 33.5 us -> 38.4 us
  waiting for transfers between devices: 19.8 us -> 21.2 us
    pallas_call x11, Pallas kernels: 33.5 us -> 38.4 us  [call(): pl.pallas_call(kernel, out_shape=outs, in_specs=specs or [SMEM] + [VMEM]...]
    ppermute x3, waiting for transfers between devices: 1.33 us -> 5.26 us  [swap_pairs(): lax.ppermute(far_value, axis, far)]
    ppermute x3, waiting for transfers between devices: 2.08 us -> 0.01 us  [swap_pairs(): lax.ppermute(near_value, axis, near)]
where the time goes in v5:
time: 87.8 us; the launch traced here: 87.5 us
  Pallas kernels  38.4 us (44%)
  starting transfers between devices  26.8 us (31%)
  waiting for transfers between devices  21.2 us (24%)
  between operations  0.95 us (1%)
    pallas_call x11, Pallas kernels, call(): pl.pallas_call(kernel, out_shape=outs, in_specs=specs or [SMEM] + [VMEM]...  38.4 us
    ppermute x16, starting transfers between devices, swapped(): lax.ppermute(value, axis, [(i, i ^ mask) for i in range(lax.axis_size(axi...  18.9 us
    ppermute x16, waiting for transfers between devices, swapped(): lax.ppermute(value, axis, [(i, i ^ mask) for i in range(lax.axis_size(axi...  15.9 us
    ppermute x3, waiting for transfers between devices, swap_pairs(): lax.ppermute(far_value, axis, far)  5.26 us
    ppermute x3, starting transfers between devices, swap_pairs(): lax.ppermute(far_value, axis, far)  4.14 us
    ppermute x3, starting transfers between devices, swap_pairs(): lax.ppermute(near_value, axis, near)  3.72 us
  transfers between devices with their start and end apart: 22, of which 15 were waited for; matrix products, arithmetic and copies ran while one was open for 0% of the time, Pallas kernels for 18%

profile of v5, /device:TPU:0, one launch (start us, length us, event | category | flops | bytes accessed | tf_op | source)
XLA Modules:
  0.0 87.5 jit_solution(16642254993935532921)
XLA Ops:
  0.7 1.7 %shard_map.60 = (f32[13,32,128]{2,1,0:T(8,128)S(1)}, f32[13,32,128]{2,1,0:T(8,128)S(1)}) custom-call(s32[2]{0:T(128)S(1)} %pad_add_fusion.par, f32[3,64,32,128]{3,2,1,0:T(8,128)} %t_ref.3, s32[32,64]{1,0:T(8,128)} %bitcast.9, s32[32,64]{1,0:T(8,128)} %bitcast.11, f32[32,64]{1,0:T(8,128)} %bitcast.13), custom_call_target="tpu_custom_call" | custom-call | flops 1000000000 | bytes 3000000 | tf_op jit(solution)/shard_map/pallas_call | solution.py:481
  2.4 3.1 %collective-permute-start = (f32[13,32,128]{2,1,0:T(8,128)S(1)}, f32[13,32,128]{2,1,0:T(8,128)S(1)}, u32[]{:S(2)}, u32[]{:S(2)}) collective-permute-start(f32[13,32,128]{2,1,0:T(8,128)S(1)} %get-tuple-element.28), channel_id=1, source_target_pairs={{0,8},{8,0},{16,24},{24,16},{1,9},{9,1},{17,25},{25,17},{2,10},{10... | collective-permute-start | bytes 638984 | tf_op jit(solution)/shard_map/ppermute | solution.py:430
  6.1 4.9 %shard_map.59 = (f32[3,36,72,128]{3,2,1,0:T(8,128)S(1)}, f32[3,36,72,128]{3,2,1,0:T(8,128)S(1)}, f32[3,32,128]{2,1,0:T(8,128)S(1)}, f32[72,128]{1,0:T(8,128)S(1)}) custom-call(s32[2]{0:T(128)S(1)} %pad_add_fusion.par, f32[3,64,32,128]{3,2,1,0:T(8,128)} %t_ref.3, s32[32,64]{1,0:T(8,128)} %bitcast.10, s32[32,64]{1,0:T(8,128)} %bitcast.12, f32[32,64]{1,0:T(8,128)} %bitcast.14), custom_call_target="tpu_custom_call" | custom-call | flops 3000000000 | bytes 9000000 | tf_op jit(solution)/shard_map/pallas_call | solution.py:481
  11.1 1.0 %shard_map.61 = (f32[3,36,72,128]{3,2,1,0:T(8,128)S(1)}, f32[3,36,72,128]{3,2,1,0:T(8,128)S(1)}, f32[440,128]{1,0:T(8,128)S(1)}, f32[440,128]{1,0:T(8,128)S(1)}) custom-call(s32[2]{0:T(128)S(1)} %pad_add_fusion.par, f32[3,36,72,128]{3,2,1,0:T(8,128)S(1)} %get-tuple-element.25.state_in, ...), custom_call_target="tpu_custom_call", output_to_operand_aliasing={{0}: (1, {}), {1}: (2, {})} | custom-call | flops 1000000000 | bytes 3000000 | tf_op jit(solution)/shard_map/pallas_call | solution.py:481
  12.2 2.5 %collective-permute-start.3 = (f32[440,128]{1,0:T(8,128)S(1)}, f32[440,128]{1,0:T(8,128)S(1)}, u32[]{:S(2)}, u32[]{:S(2)}) collective-permute-start(f32[440,128]{1,0:T(8,128)S(1)} %get-tuple-element.34), channel_id=1, source_target_pairs={{0,7},{1,2},{2,1},{3,4},{4,3},{5,6},{6,5},{7,0},{8,15},{9,10},{10,... | collective-permute-start | bytes 675848 | tf_op jit(solution)/shard_map/ppermute | solution.py:430
  14.7 1.7 %shard_map.62.source.middle_in = f32[3,36,72,128]{3,2,1,0:T(8,128)S(1)} custom-call(f32[3,36,72,128]{3,2,1,0:T(8,128)S(1)} %get-tuple-element.30.source.start_in, f32[3,36,72,128]{3,2,1,0:T(8,128)S(1)} %get-tuple-element.31.coef_ref.coef_in, f32[72,128]{1,0:T(8,128)S(1)} %get-tuple-element.32.spin_ref), custom_call_target="tpu_custom_call" | custom-call | flops 2000000000 | bytes 6000000 | tf_op jit(solution)/shard_map/pallas_call | solution.py:481
  16.5 1.6 %shard_map.63.state_in = f32[3,36,72,128]{3,2,1,0:T(8,128)S(1)} custom-call(f32[3,36,72,128]{3,2,1,0:T(8,128)S(1)} %shard_map.62.source.middle_in, f32[3,36,72,128]{3,2,1,0:T(8,128)S(1)} %get-tuple-element.31.coef_ref.coef_in, f32[72,128]{1,0:T(8,128)S(1)} %get-tuple-element.32.spin_ref), custom_call_target="tpu_custom_call" | custom-call | flops 2000000000 | bytes 6000000 | tf_op jit(solution)/shard_map/pallas_call | solution.py:481
  18.1 2.2 %collective-permute-done.3.b = f32[440,128]{1,0:T(8,128)S(1)} collective-permute-done((f32[440,128]{1,0:T(8,128)S(1)}, f32[440,128]{1,0:T(8,128)S(1)}, u32[]{:S(2)}, u32[]{:S(2)}) %collective-permute-start.3) | collective-permute-done | bytes 225312 | tf_op jit(solution)/shard_map/ppermute | solution.py:430
  20.3 2.1 %shard_map.64 = (f32[3,36,72,128]{3,2,1,0:T(8,128)S(1)}, f32[3,36,72,128]{3,2,1,0:T(8,128)S(1)}, f32[3,36,72,128]{3,2,1,0:T(8,128)S(1)}, f32[3,36,72,128]{3,2,1,...) custom-call(s32[2]{0:T(128)S(1)} %pad_add_fusion.par, ...), custom_call_target="tpu_custom_call", output_to_operand_aliasing={{0}: (1, {}), {1}: (2, {}), {2}: (3, {}), {3}: (4, {})} | custom-call | flops 2000000000 | bytes 6000000 | tf_op jit(solution)/shard_map/pallas_call | solution.py:481
  22.6 1.1 %collective-permute-done.6 = f32[64,128]{1,0:T(8,128)S(1)} collective-permute-done((f32[64,128]{1,0:T(8,128)S(1)}, f32[64,128]{1,0:T(8,128)S(1)}, u32[]{:S(2)}, u32[]{:S(2)}) %collective-permute-start.6) | collective-permute-done | bytes 32800 | tf_op jit(solution)/shard_map/ppermute | solution.py:434
  23.7 1.6 %collective-permute-start.7 = (f32[64,128]{1,0:T(8,128)S(1)}, f32[64,128]{1,0:T(8,128)S(1)}, u32[]{:S(2)}, u32[]{:S(2)}) collective-permute-start(f32[64,128]{1,0:T(8,128)S(1)} %add.42), channel_id=1, source_target_pairs={{0,2},{1,3},{2,0},{3,1},{4,6},{5,7},{6,4},{7,5},{8,10},{9,11},{10,... | collective-permute-start | bytes 98312 | tf_op jit(solution)/shard_map/ppermute | solution.py:434
  25.9 1.2 %collective-permute-start.9 = (f32[64,128]{1,0:T(8,128)S(1)}, f32[64,128]{1,0:T(8,128)S(1)}, u32[]{:S(2)}, u32[]{:S(2)}) collective-permute-start(f32[64,128]{1,0:T(8,128)S(1)} %add.42), channel_id=1, source_target_pairs={{0,6},{1,7},{2,4},{3,5},{4,2},{5,3},{6,0},{7,1},{8,14},{9,15},{10,... | collective-permute-start | bytes 98312 | tf_op jit(solution)/shard_map/ppermute | solution.py:434
  27.6 2.0 %collective-permute-done.8 = f32[64,128]{1,0:T(8,128)S(1)} collective-permute-done((f32[64,128]{1,0:T(8,128)S(1)}, f32[64,128]{1,0:T(8,128)S(1)}, u32[]{:S(2)}, u32[]{:S(2)}) %collective-permute-start.8) | collective-permute-done | bytes 32800 | tf_op jit(solution)/shard_map/ppermute | solution.py:434
  29.6 1.2 %collective-permute-done.9 = f32[64,128]{1,0:T(8,128)S(1)} collective-permute-done((f32[64,128]{1,0:T(8,128)S(1)}, f32[64,128]{1,0:T(8,128)S(1)}, u32[]{:S(2)}, u32[]{:S(2)}) %collective-permute-start.9) | collective-permute-done | bytes 32800 | tf_op jit(solution)/shard_map/ppermute | solution.py:434
  30.8 4.5 %collective-permute-start.10 = (f32[64,128]{1,0:T(8,128)S(1)}, f32[64,128]{1,0:T(8,128)S(1)}, u32[]{:S(2)}, u32[]{:S(2)}) collective-permute-start(f32[64,128]{1,0:T(8,128)S(1)} %add_add_fusion.3), channel_id=1, source_target_pairs={{0,8},{8,0},{16,24},{24,16},{1,9},{9,1},{17,25},{25,17},{2,10},{10... | collective-permute-start | bytes 98312 | tf_op jit(solution)/shard_map/ppermute | solution.py:434
  35.2 1.2 %collective-permute-start.11 = (f32[64,128]{1,0:T(8,128)S(1)}, f32[64,128]{1,0:T(8,128)S(1)}, u32[]{:S(2)}, u32[]{:S(2)}) collective-permute-start(f32[64,128]{1,0:T(8,128)S(1)} %add_add_fusion.3), channel_id=1, source_target_pairs={{0,16},{8,24},{16,0},{24,8},{1,17},{9,25},{17,1},{25,9},{2,18},{10... | collective-permute-start | bytes 98312 | tf_op jit(solution)/shard_map/ppermute | solution.py:434
  36.5 1.4 %collective-permute-start.12 = (f32[64,128]{1,0:T(8,128)S(1)}, f32[64,128]{1,0:T(8,128)S(1)}, u32[]{:S(2)}, u32[]{:S(2)}) collective-permute-start(f32[64,128]{1,0:T(8,128)S(1)} %add_add_fusion.3), channel_id=1, source_target_pairs={{0,24},{8,16},{16,8},{24,0},{1,25},{9,17},{17,9},{25,1},{2,26},{10... | collective-permute-start | bytes 98312 | tf_op jit(solution)/shard_map/ppermute | solution.py:434
  37.9 1.7 %shard_map.65.source.middle_in = f32[3,36,72,128]{3,2,1,0:T(8,128)S(1)} custom-call(f32[3,36,72,128]{3,2,1,0:T(8,128)S(1)} %get-tuple-element.35.source.start_in, f32[3,36,72,128]{3,2,1,0:T(8,128)S(1)} %get-tuple-element.36.coef_ref, f32[72,128]{1,0:T(8,128)S(1)} %get-tuple-element.32.spin_ref), custom_call_target="tpu_custom_call" | custom-call | flops 2000000000 | bytes 6000000 | tf_op jit(solution)/shard_map/pallas_call | solution.py:481
  40.5 1.7 %collective-permute-done.12 = f32[64,128]{1,0:T(8,128)S(1)} collective-permute-done((f32[64,128]{1,0:T(8,128)S(1)}, f32[64,128]{1,0:T(8,128)S(1)}, u32[]{:S(2)}, u32[]{:S(2)}) %collective-permute-start.12) | collective-permute-done | bytes 32800 | tf_op jit(solution)/shard_map/ppermute | solution.py:434
  42.3 1.6 %shard_map.66.state_in = f32[3,36,72,128]{3,2,1,0:T(8,128)S(1)} custom-call(f32[3,36,72,128]{3,2,1,0:T(8,128)S(1)} %shard_map.65.source.middle_in, f32[3,36,72,128]{3,2,1,0:T(8,128)S(1)} %get-tuple-element.36.coef_ref, f32[72,128]{1,0:T(8,128)S(1)} %get-tuple-element.32.spin_ref), custom_call_target="tpu_custom_call" | custom-call | flops 2000000000 | bytes 6000000 | tf_op jit(solution)/shard_map/pallas_call | solution.py:481
  44.5 0.9 %collective-permute-start.5 = (f32[432,128]{1,0:T(8,128)S(1)}, f32[432,128]{1,0:T(8,128)S(1)}, u32[]{:S(2)}, u32[]{:S(2)}) collective-permute-start(f32[432,128]{1,0:T(8,128)S(1)} %get-tuple-element.38), channel_id=1, source_target_pairs={{0,7},{1,2},{2,1},{3,4},{4,3},{5,6},{6,5},{7,0},{8,15},{9,10},{10,... | collective-permute-start | bytes 663560 | tf_op jit(solution)/shard_map/ppermute | solution.py:430
  45.4 4.4 %shard_map.67 = (f32[128,128]{1,0:T(8,128)S(1)}, f32[1,128]{1,0:T(1,128)S(1)}) custom-call(s32[2]{0:T(128)S(1)} %pad_add_fusion.par, f32[64,128]{1,0:T(8,128)S(1)} %add_add_fusion.2.mine_ref, f32[64,128]{1,0:T(8,128)S(1)} %collective-permute-done.13.other_ref, f32[1,128]{1,0:T(1,128)S(1)} %broadcast_in_dim.3.prior_ref), custom_call_target="tpu_custom_call" | custom-call | flops 4400000000 | bytes 13200000 | tf_op jit(solution)/shard_map/pallas_call | solution.py:481
  49.8 3.1 %collective-permute-done.5.b = f32[432,128]{1,0:T(8,128)S(1)} collective-permute-done((f32[432,128]{1,0:T(8,128)S(1)}, f32[432,128]{1,0:T(8,128)S(1)}, u32[]{:S(2)}, u32[]{:S(2)}) %collective-permute-start.5) | collective-permute-done | bytes 221216 | tf_op jit(solution)/shard_map/ppermute | solution.py:430
  52.9 9.9 %shard_map.68 = (f32[3,36,72,128]{3,2,1,0:T(8,128)S(1)}, f32[3,36,72,128]{3,2,1,0:T(8,128)S(1)}, f32[3,36,72,128]{3,2,1,0:T(8,128)S(1)}, f32[3,64,32,128]{3,2,1,...) custom-call(s32[2]{0:T(128)S(1)} %pad_add_fusion.par, ...), custom_call_target="tpu_custom_call", output_to_operand_aliasing={{0}: (1, {}), {1}: (2, {}), {2}: (3, {})} | custom-call | flops 3000000000 | bytes 9000000 | tf_op jit(solution)/shard_map/pallas_call | solution.py:481
  62.9 1.2 %collective-permute-done.14 = f32[64,128]{1,0:T(8,128)S(1)} collective-permute-done((f32[64,128]{1,0:T(8,128)S(1)}, f32[64,128]{1,0:T(8,128)S(1)}, u32[]{:S(2)}, u32[]{:S(2)}) %collective-permute-start.14) | collective-permute-done | bytes 32800 | tf_op jit(solution)/shard_map/ppermute | solution.py:434
  65.8 1.8 %collective-permute-start.17 = (f32[64,128]{1,0:T(8,128)S(1)}, f32[64,128]{1,0:T(8,128)S(1)}, u32[]{:S(2)}, u32[]{:S(2)}) collective-permute-start(f32[64,128]{1,0:T(8,128)S(1)} %add.49), channel_id=1, source_target_pairs={{0,6},{1,7},{2,4},{3,5},{4,2},{5,3},{6,0},{7,1},{8,14},{9,15},{10,... | collective-permute-start | bytes 98312 | tf_op jit(solution)/shard_map/ppermute | solution.py:434
  68.8 1.8 %collective-permute-done.17 = f32[64,128]{1,0:T(8,128)S(1)} collective-permute-done((f32[64,128]{1,0:T(8,128)S(1)}, f32[64,128]{1,0:T(8,128)S(1)}, u32[]{:S(2)}, u32[]{:S(2)}) %collective-permute-start.17) | collective-permute-done | bytes 32800 | tf_op jit(solution)/shard_map/ppermute | solution.py:434
  70.8 1.8 %collective-permute-start.19 = (f32[64,128]{1,0:T(8,128)S(1)}, f32[64,128]{1,0:T(8,128)S(1)}, u32[]{:S(2)}, u32[]{:S(2)}) collective-permute-start(f32[64,128]{1,0:T(8,128)S(1)} %add_add_fusion.1), channel_id=1, source_target_pairs={{0,16},{8,24},{16,0},{24,8},{1,17},{9,25},{17,1},{25,9},{2,18},{10... | collective-permute-start | bytes 98312 | tf_op jit(solution)/shard_map/ppermute | solution.py:434
  72.6 2.4 %collective-permute-start.20 = (f32[64,128]{1,0:T(8,128)S(1)}, f32[64,128]{1,0:T(8,128)S(1)}, u32[]{:S(2)}, u32[]{:S(2)}) collective-permute-start(f32[64,128]{1,0:T(8,128)S(1)} %add_add_fusion.1), channel_id=1, source_target_pairs={{0,24},{8,16},{16,8},{24,0},{1,25},{9,17},{17,9},{25,1},{2,26},{10... | collective-permute-start | bytes 98312 | tf_op jit(solution)/shard_map/ppermute | solution.py:434
  75.8 2.5 %collective-permute-done.20 = f32[64,128]{1,0:T(8,128)S(1)} collective-permute-done((f32[64,128]{1,0:T(8,128)S(1)}, f32[64,128]{1,0:T(8,128)S(1)}, u32[]{:S(2)}, u32[]{:S(2)}) %collective-permute-start.20) | collective-permute-done | bytes 32800 | tf_op jit(solution)/shard_map/ppermute | solution.py:434
  78.4 1.2 %collective-permute-done.21.other_ref = f32[64,128]{1,0:T(8,128)S(1)} collective-permute-done((f32[64,128]{1,0:T(8,128)S(1)}, f32[64,128]{1,0:T(8,128)S(1)}, u32[]{:S(2)}, u32[]{:S(2)}) %collective-permute-start.21) | collective-permute-done | bytes 32800 | tf_op jit(solution)/shard_map/ppermute | solution.py:434
  79.6 7.7 %shard_map.69 = (f32[12,512,128]{2,1,0:T(8,128)}, f32[1,128]{1,0:T(1,128)}) custom-call(s32[2]{0:T(128)S(1)} %pad_add_fusion.par, f32[64,128]{1,0:T(8,128)S(1)} %add_add_fusion.mine_ref, f32[64,128]{1,0:T(8,128)S(1)} %collective-permute-done.21.other_ref, f32[1,128]{1,0:T(1,128)S(1)} %get-tuple-element.44.prior_ref, f32[12,512,128]{2,1,0:T(8,128)S(1)} %bitcast.8), custom_call_target="tpu_custom_call" | custom-call | flops 1000000000 | bytes 3000000 | tf_op jit(solution)/shard_map/pallas_call | solution.py:481
  (31 shorter events, 7.6 us)
Async XLA Ops:
  2.4 8.7 %collective-permute-start = (f32[13,32,128]{2,1,0:T(8,128)S(1)}, f32[13,32,128]{2,1,0:T(8,128)S(1)}, u32[]{:S(2)}, u32[]{:S(2)}) collective-permute-start(f32[13,32,128]{2,1,0:T(8,128)S(1)} %get-tuple-element.28), channel_id=1, source_target_pairs={{0,8},{8,0},{16,24},{24,16},{1,9},{9,1},{17,25},{25,17},{2,10},{10... | collective-permute-start | bytes 638984 | tf_op jit(solution)/shard_map/ppermute | solution.py:430
  5.5 5.6 %collective-permute-start.1 = (f32[13,32,128]{2,1,0:T(8,128)S(1)}, f32[13,32,128]{2,1,0:T(8,128)S(1)}, u32[]{:S(2)}, u32[]{:S(2)}) collective-permute-start(f32[13,32,128]{2,1,0:T(8,128)S(1)} %get-tuple-element.29), channel_id=1, source_target_pairs={{8,16},{16,8},{9,17},{17,9},{10,18},{18,10},{11,19},{19,11},{12,20... | collective-permute-start | bytes 638984 | tf_op jit(solution)/shard_map/ppermute | solution.py:430
  12.1 6.0 %collective-permute-start.2 = (f32[440,128]{1,0:T(8,128)S(1)}, f32[440,128]{1,0:T(8,128)S(1)}, u32[]{:S(2)}, u32[]{:S(2)}) collective-permute-start(f32[440,128]{1,0:T(8,128)S(1)} %get-tuple-element.33), channel_id=1, source_target_pairs={{0,1},{1,0},{2,3},{3,2},{4,5},{5,4},{6,7},{7,6},{8,9},{9,8},{10,11... | collective-permute-start | bytes 675848 | tf_op jit(solution)/shard_map/ppermute | solution.py:430
  12.2 8.2 %collective-permute-start.3 = (f32[440,128]{1,0:T(8,128)S(1)}, f32[440,128]{1,0:T(8,128)S(1)}, u32[]{:S(2)}, u32[]{:S(2)}) collective-permute-start(f32[440,128]{1,0:T(8,128)S(1)} %get-tuple-element.34), channel_id=1, source_target_pairs={{0,7},{1,2},{2,1},{3,4},{4,3},{5,6},{6,5},{7,0},{8,15},{9,10},{10,... | collective-permute-start | bytes 675848 | tf_op jit(solution)/shard_map/ppermute | solution.py:430
  22.4 1.3 %collective-permute-start.6 = (f32[64,128]{1,0:T(8,128)S(1)}, f32[64,128]{1,0:T(8,128)S(1)}, u32[]{:S(2)}, u32[]{:S(2)}) collective-permute-start(f32[64,128]{1,0:T(8,128)S(1)} %get-tuple-element.40), channel_id=1, source_target_pairs={{0,1},{1,0},{2,3},{3,2},{4,5},{5,4},{6,7},{7,6},{8,9},{9,8},{10,11... | collective-permute-start | bytes 98312 | tf_op jit(solution)/shard_map/ppermute | solution.py:434
  23.7 3.9 %collective-permute-start.7 = (f32[64,128]{1,0:T(8,128)S(1)}, f32[64,128]{1,0:T(8,128)S(1)}, u32[]{:S(2)}, u32[]{:S(2)}) collective-permute-start(f32[64,128]{1,0:T(8,128)S(1)} %add.42), channel_id=1, source_target_pairs={{0,2},{1,3},{2,0},{3,1},{4,6},{5,7},{6,4},{7,5},{8,10},{9,11},{10,... | collective-permute-start | bytes 98312 | tf_op jit(solution)/shard_map/ppermute | solution.py:434
  25.3 4.3 %collective-permute-start.8 = (f32[64,128]{1,0:T(8,128)S(1)}, f32[64,128]{1,0:T(8,128)S(1)}, u32[]{:S(2)}, u32[]{:S(2)}) collective-permute-start(f32[64,128]{1,0:T(8,128)S(1)} %add.42), channel_id=1, source_target_pairs={{0,4},{1,5},{2,6},{3,7},{4,0},{5,1},{6,2},{7,3},{8,12},{9,13},{10,... | collective-permute-start | bytes 98312 | tf_op jit(solution)/shard_map/ppermute | solution.py:434
  25.9 4.8 %collective-permute-start.9 = (f32[64,128]{1,0:T(8,128)S(1)}, f32[64,128]{1,0:T(8,128)S(1)}, u32[]{:S(2)}, u32[]{:S(2)}) collective-permute-start(f32[64,128]{1,0:T(8,128)S(1)} %add.42), channel_id=1, source_target_pairs={{0,6},{1,7},{2,4},{3,5},{4,2},{5,3},{6,0},{7,1},{8,14},{9,15},{10,... | collective-permute-start | bytes 98312 | tf_op jit(solution)/shard_map/ppermute | solution.py:434
  30.8 8.9 %collective-permute-start.10 = (f32[64,128]{1,0:T(8,128)S(1)}, f32[64,128]{1,0:T(8,128)S(1)}, u32[]{:S(2)}, u32[]{:S(2)}) collective-permute-start(f32[64,128]{1,0:T(8,128)S(1)} %add_add_fusion.3), channel_id=1, source_target_pairs={{0,8},{8,0},{16,24},{24,16},{1,9},{9,1},{17,25},{25,17},{2,10},{10... | collective-permute-start | bytes 98312 | tf_op jit(solution)/shard_map/ppermute | solution.py:434
  35.2 5.2 %collective-permute-start.11 = (f32[64,128]{1,0:T(8,128)S(1)}, f32[64,128]{1,0:T(8,128)S(1)}, u32[]{:S(2)}, u32[]{:S(2)}) collective-permute-start(f32[64,128]{1,0:T(8,128)S(1)} %add_add_fusion.3), channel_id=1, source_target_pairs={{0,16},{8,24},{16,0},{24,8},{1,17},{9,25},{17,1},{25,9},{2,18},{10... | collective-permute-start | bytes 98312 | tf_op jit(solution)/shard_map/ppermute | solution.py:434
  36.5 5.7 %collective-permute-start.12 = (f32[64,128]{1,0:T(8,128)S(1)}, f32[64,128]{1,0:T(8,128)S(1)}, u32[]{:S(2)}, u32[]{:S(2)}) collective-permute-start(f32[64,128]{1,0:T(8,128)S(1)} %add_add_fusion.3), channel_id=1, source_target_pairs={{0,24},{8,16},{16,8},{24,0},{1,25},{9,17},{17,9},{25,1},{2,26},{10... | collective-permute-start | bytes 98312 | tf_op jit(solution)/shard_map/ppermute | solution.py:434
  42.2 3.2 %collective-permute-start.13 = (f32[64,128]{1,0:T(8,128)S(1)}, f32[64,128]{1,0:T(8,128)S(1)}, u32[]{:S(2)}, u32[]{:S(2)}) collective-permute-start(f32[64,128]{1,0:T(8,128)S(1)} %add_add_fusion.2.mine_ref), channel_id=1, source_target_pairs={{0,1},{1,0},{2,3},{3,2},{4,5},{5,4},{6,7},{7,6},{8,9},{9,8},{10,11... | collective-permute-start | bytes 98312 | tf_op jit(solution)/shard_map/ppermute | solution.py:434
  43.9 5.9 %collective-permute-start.4 = (f32[432,128]{1,0:T(8,128)S(1)}, f32[432,128]{1,0:T(8,128)S(1)}, u32[]{:S(2)}, u32[]{:S(2)}) collective-permute-start(f32[432,128]{1,0:T(8,128)S(1)} %get-tuple-element.37), channel_id=1, source_target_pairs={{0,1},{1,0},{2,3},{3,2},{4,5},{5,4},{6,7},{7,6},{8,9},{9,8},{10,11... | collective-permute-start | bytes 663560 | tf_op jit(solution)/shard_map/ppermute | solution.py:430
  44.5 8.4 %collective-permute-start.5 = (f32[432,128]{1,0:T(8,128)S(1)}, f32[432,128]{1,0:T(8,128)S(1)}, u32[]{:S(2)}, u32[]{:S(2)}) collective-permute-start(f32[432,128]{1,0:T(8,128)S(1)} %get-tuple-element.38), channel_id=1, source_target_pairs={{0,7},{1,2},{2,1},{3,4},{4,3},{5,6},{6,5},{7,0},{8,15},{9,10},{10,... | collective-permute-start | bytes 663560 | tf_op jit(solution)/shard_map/ppermute | solution.py:430
  62.8 1.3 %collective-permute-start.14 = (f32[64,128]{1,0:T(8,128)S(1)}, f32[64,128]{1,0:T(8,128)S(1)}, u32[]{:S(2)}, u32[]{:S(2)}) collective-permute-start(f32[64,128]{1,0:T(8,128)S(1)} %get-tuple-element.43), channel_id=1, source_target_pairs={{0,1},{1,0},{2,3},{3,2},{4,5},{5,4},{6,7},{7,6},{8,9},{9,8},{10,11... | collective-permute-start | bytes 98312 | tf_op jit(solution)/shard_map/ppermute | solution.py:434
  64.1 3.9 %collective-permute-start.15 = (f32[64,128]{1,0:T(8,128)S(1)}, f32[64,128]{1,0:T(8,128)S(1)}, u32[]{:S(2)}, u32[]{:S(2)}) collective-permute-start(f32[64,128]{1,0:T(8,128)S(1)} %add.49), channel_id=1, source_target_pairs={{0,2},{1,3},{2,0},{3,1},{4,6},{5,7},{6,4},{7,5},{8,10},{9,11},{10,... | collective-permute-start | bytes 98312 | tf_op jit(solution)/shard_map/ppermute | solution.py:434
  64.9 3.9 %collective-permute-start.16 = (f32[64,128]{1,0:T(8,128)S(1)}, f32[64,128]{1,0:T(8,128)S(1)}, u32[]{:S(2)}, u32[]{:S(2)}) collective-permute-start(f32[64,128]{1,0:T(8,128)S(1)} %add.49), channel_id=1, source_target_pairs={{0,4},{1,5},{2,6},{3,7},{4,0},{5,1},{6,2},{7,3},{8,12},{9,13},{10,... | collective-permute-start | bytes 98312 | tf_op jit(solution)/shard_map/ppermute | solution.py:434
  65.8 4.8 %collective-permute-start.17 = (f32[64,128]{1,0:T(8,128)S(1)}, f32[64,128]{1,0:T(8,128)S(1)}, u32[]{:S(2)}, u32[]{:S(2)}) collective-permute-start(f32[64,128]{1,0:T(8,128)S(1)} %add.49), channel_id=1, source_target_pairs={{0,6},{1,7},{2,4},{3,5},{4,2},{5,3},{6,0},{7,1},{8,14},{9,15},{10,... | collective-permute-start | bytes 98312 | tf_op jit(solution)/shard_map/ppermute | solution.py:434
  70.6 4.5 %collective-permute-start.18 = (f32[64,128]{1,0:T(8,128)S(1)}, f32[64,128]{1,0:T(8,128)S(1)}, u32[]{:S(2)}, u32[]{:S(2)}) collective-permute-start(f32[64,128]{1,0:T(8,128)S(1)} %add_add_fusion.1), channel_id=1, source_target_pairs={{0,8},{8,0},{16,24},{24,16},{1,9},{9,1},{17,25},{25,17},{2,10},{10... | collective-permute-start | bytes 98312 | tf_op jit(solution)/shard_map/ppermute | solution.py:434
  70.8 5.0 %collective-permute-start.19 = (f32[64,128]{1,0:T(8,128)S(1)}, f32[64,128]{1,0:T(8,128)S(1)}, u32[]{:S(2)}, u32[]{:S(2)}) collective-permute-start(f32[64,128]{1,0:T(8,128)S(1)} %add_add_fusion.1), channel_id=1, source_target_pairs={{0,16},{8,24},{16,0},{24,8},{1,17},{9,25},{17,1},{25,9},{2,18},{10... | collective-permute-start | bytes 98312 | tf_op jit(solution)/shard_map/ppermute | solution.py:434
  72.6 5.7 %collective-permute-start.20 = (f32[64,128]{1,0:T(8,128)S(1)}, f32[64,128]{1,0:T(8,128)S(1)}, u32[]{:S(2)}, u32[]{:S(2)}) collective-permute-start(f32[64,128]{1,0:T(8,128)S(1)} %add_add_fusion.1), channel_id=1, source_target_pairs={{0,24},{8,16},{16,8},{24,0},{1,25},{9,17},{17,9},{25,1},{2,26},{10... | collective-permute-start | bytes 98312 | tf_op jit(solution)/shard_map/ppermute | solution.py:434
  78.3 1.3 %collective-permute-start.21 = (f32[64,128]{1,0:T(8,128)S(1)}, f32[64,128]{1,0:T(8,128)S(1)}, u32[]{:S(2)}, u32[]{:S(2)}) collective-permute-start(f32[64,128]{1,0:T(8,128)S(1)} %add_add_fusion.mine_ref), channel_id=1, source_target_pairs={{0,1},{1,0},{2,3},{3,2},{4,5},{5,4},{6,7},{7,6},{8,9},{9,8},{10,11... | collective-permute-start | bytes 98312 | tf_op jit(solution)/shard_map/ppermute | solution.py:434

commit v6 on v5

--- a/solution.py
+++ b/solution.py
@@ -302,7 +302,7 @@
     sent[...] = total[pl.ds((1 - odd) * rows, rows), :]
 
 
-def invert_factor(gram_ref, work):
+def invert_factor(gram_ref, work, board):
     count = LANES // SUB
     lane = lax.broadcasted_iota(jnp.int32, (SUB, LANES), 1)
     sub = lax.broadcasted_iota(jnp.int32, (SUB, LANES), 0)
@@ -310,12 +310,17 @@
     for block in range(count):
         base = SUB * block
         here = (lane >= base) & (lane < base + SUB)
-        spread = [lane_spread(rows[block], base + l) for l in range(SUB)]
+        shelf = 2 * SUB * base
+        for l in range(SUB):
+            board[pl.ds(shelf + SUB * l, SUB), :] = lane_spread(rows[block], base + l)
         low = [
-            [jnp.broadcast_to(spread[l][k : k + 1, :], (SUB, LANES)) for l in range(k + 1)]
+            [board[pl.ds(shelf + SUB * l + k, SUB, stride=0), :] for l in range(k + 1)]
             for k in range(SUB)
         ]
-        pivot = jnp.where(here, jnp.where(lane - base == sub, 1.0, 0.0), rows[block])
+        shelf += SUB * SUB
+        board[pl.ds(shelf, SUB), :] = jnp.where(
+            here, jnp.where(lane - base == sub, 1.0, 0.0), rows[block]
+        )
         inv, scaled = [], []
         for k in range(SUB):
             inv.append(lax.rsqrt(low[k][k]))
@@ -324,7 +329,7 @@
             for i in range(k + 1, SUB):
                 for m in range(k + 1, i + 1):
                     low[i][m] = low[i][m] - low[i][k] * low[m][k]
-            line = jnp.broadcast_to(pivot[k : k + 1, :], (SUB, LANES))
+            line = board[pl.ds(shelf + k, SUB, stride=0), :]
             for l in range(k):
                 line = line - low[k][l] * scaled[l]
             scaled.append(line * inv[k])
@@ -345,12 +350,12 @@
             rows[i] = rest
 
 
-def factorize(par, mine_ref, other_ref, gram, work):
+def factorize(par, mine_ref, other_ref, gram, work, board):
     rows = LANES // 2
     odd = par[1] % 2
     gram[pl.ds(odd * rows, rows), :] = mine_ref[...]
     gram[pl.ds((1 - odd) * rows, rows), :] = other_ref[...]
-    invert_factor(gram, work)
+    invert_factor(gram, work, board)
     row = lax.broadcasted_iota(jnp.int32, (LANES, LANES), 0)
     col = lax.broadcasted_iota(jnp.int32, (LANES, LANES), 1)
     inverse = jnp.where(row >= col, work[...], 0.0)
@@ -374,39 +379,37 @@
     return both[:, :LANES] + both[:, LANES:]
 
 
-def factor_only(par, mine_ref, other_ref, prior_ref, inverse_ref, logs_ref, gram, work):
-    inverse, diagonal = factorize(par, mine_ref, other_ref, gram, work)
+def factor_only(par, mine_ref, other_ref, prior_ref, inverse_ref, logs_ref, gram, work, board):
+    inverse, diagonal = factorize(par, mine_ref, other_ref, gram, work, board)
     inverse_ref[...] = inverse
     logs_ref[...] = prior_ref[...] - jnp.log(diagonal)
 
 
 def join_update(
-    scale, par, start_in, middle_in, state_in, coef_ref, spin_ref, a, b, inverse_ref, start, middle, state, out_ref, kept, sent, factor, total, fresh, sems
+    scale, par, start_in, middle_in, state_in, coef_ref, spin_ref, a, b, inverse_ref, start, middle, state, out_ref, kept, sent, factor, total
 ):
     factor[...] = paired(inverse_ref[...])
     mend_columns(par, (start, middle, state), coef_ref, spin_ref, (a, b))
-    cols = fresh.shape[1]
-
-    def back_copy(comp, lon):
-        return pltpu.make_async_copy(
-            fresh.at[comp, lon], out_ref.at[comp, :, lon], sems.at[comp * cols + lon]
-        )
-
     gram = 0.0
-    copies = []
     for comp, lon, cells in tiles_of(state):
         new = times_factor(cells, factor[...])
-        fresh[comp, pl.ds(lon, SUB)] = new.reshape((SUB,) + fresh.shape[2:])
-        for i in range(SUB):
-            copies.append(back_copy(comp, lon + i))
-            copies[-1].start()
+        out_ref[comp, pl.ds(lon, SUB)] = new.reshape((SUB,) + out_ref.shape[2:])
         gram += gram_of(*split_halves(new))
     write_halves(par, gram, scale, kept, sent, total)
-    finish_all(copies)
-
-
-def finish(par, mine_ref, other_ref, prior_ref, t_ref, out_ref, logs_ref, gram, work, factor, fresh, sems):
-    inverse, diagonal = factorize(par, mine_ref, other_ref, gram, work)
+
+
+def restore_order(turned, out_ref):
+    comps, cols, _, _ = turned.shape
+    for comp in range(comps):
+        for lon in range(0, cols, SUB):
+            cells = turned[comp, pl.ds(lon, SUB)]
+            out_ref[comp, :, pl.ds(lon, SUB), :] = jnp.transpose(cells, (1, 0, 2))
+
+
+def finish(
+    par, mine_ref, other_ref, prior_ref, t_ref, out_ref, logs_ref, gram, work, board, factor, fresh, sems
+):
+    inverse, diagonal = factorize(par, mine_ref, other_ref, gram, work, board)
     logs_ref[...] = prior_ref[...] - jnp.log(diagonal)
     factor[...] = paired(inverse)
 
@@ -415,7 +418,7 @@
 
     for tile in range(TILES):
         fresh[tile] = times_factor(t_ref[tile], factor[...])
-        out_copy(tile).start()
+        out_copy(tile).start(priority=tile % 2)
 
     for tile in range(TILES):
         out_copy(tile).wait()
@@ -473,6 +476,7 @@
     rows_sent = (shape_of(comps * HALO + 1, cols, modes),) * 2
     halves = (shape_of(modes // 2, modes),) * 2
     square = pltpu.VMEM((modes, modes), jnp.float32)
+    board = pltpu.VMEM((2 * SUB * modes, LANES), jnp.float32)
     factor = pltpu.VMEM((2 * modes, 2 * modes), jnp.bfloat16)
 
     def call(
@@ -569,12 +573,12 @@
         mine,
         other,
         logs,
-        scratch=[square, square],
-        cost=4.4,
+        scratch=[square, square, board],
+        cost=0.01,
     )
     _, _, _, state, kept, sent = call(
         functools.partial(join_update, scale),
-        (block, block, block, shape_of(comps, rows, cols, modes)) + halves,
+        (block, block, block, shape_of(comps, cols, rows, modes)) + halves,
         par,
         start,
         middle,
@@ -583,15 +587,13 @@
         spin,
         *halos,
         inverse,
-        scratch=[
-            factor,
-            square,
-            pltpu.VMEM((comps, cols, rows, modes), jnp.float32),
-            pltpu.SemaphoreType.DMA((comps * cols,)),
-        ],
+        scratch=[factor, square],
         aliases={1: 0, 2: 1, 3: 2},
         cost=3.0,
     )
+    state = call(
+        restore_order, (shape_of(comps, rows, cols, modes),), state, specs=[VMEM], cost=2.0
+    )[0]
     height = comps * rows * cols // TILES
     tiled = shape_of(TILES, height, modes)
     mine, other = sum_devices(kept, sent)
@@ -607,6 +609,7 @@
         scratch=[
             square,
             square,
+            board,
             factor,
             pltpu.VMEM((TILES, height, modes), jnp.float32),
             pltpu.SemaphoreType.DMA((TILES,)),

time: 87.8 us -> 75.3 us (0.86)
  Pallas kernels: 38.4 us -> 30.6 us
  waiting for transfers between devices: 21.2 us -> 15.6 us
    pallas_call x11 -> x12, Pallas kernels: 38.4 us -> 30.6 us  [call(): pl.pallas_call(kernel, out_shape=outs, in_specs=specs or [SMEM] + [VMEM]...]
    ppermute x3, waiting for transfers between devices: 5.26 us -> 2.2 us  [swap_pairs(): lax.ppermute(far_value, axis, far)]
    ppermute x16, waiting for transfers between devices: 15.9 us -> 13.4 us  [swapped(): lax.ppermute(value, axis, [(i, i ^ mask) for i in range(lax.axis_size(axi...]
  transfers between devices with their start and end apart: 22 -> 22, of which waited for: 15 -> 13; matrix products, arithmetic and copies ran while one was open for 0% -> 0% of each run, Pallas kernels for 18% -> 21%
where the time goes in v6:
time: 75.3 us; the launch traced here: 75 us
  Pallas kernels  30.6 us (41%)
  starting transfers between devices  27.6 us (37%)
  waiting for transfers between devices  15.6 us (21%)
  between operations  0.97 us (1%)
    pallas_call x12, Pallas kernels, call(): pl.pallas_call(kernel, out_shape=outs, in_specs=specs or [SMEM] + [VMEM]...  30.6 us
    ppermute x16, starting transfers between devices, swapped(): lax.ppermute(value, axis, [(i, i ^ mask) for i in range(lax.axis_size(axi...  19.4 us
    ppermute x16, waiting for transfers between devices, swapped(): lax.ppermute(value, axis, [(i, i ^ mask) for i in range(lax.axis_size(axi...  13.4 us
    ppermute x3, starting transfers between devices, swap_pairs(): lax.ppermute(far_value, axis, far)  5 us
    ppermute x3, starting transfers between devices, swap_pairs(): lax.ppermute(near_value, axis, near)  3.16 us
    ppermute x3, waiting for transfers between devices, swap_pairs(): lax.ppermute(far_value, axis, far)  2.2 us
  transfers between devices with their start and end apart: 22, of which 13 were waited for; matrix products, arithmetic and copies ran while one was open for 0% of the time, Pallas kernels for 21%

profile of v6, /device:TPU:0, one launch (start us, length us, event | category | flops | bytes accessed | tf_op | source)
XLA Modules:
  0.0 75.0 jit_solution(11170457844199552290)
XLA Ops:
  0.7 1.7 %shard_map.60 = (f32[13,32,128]{2,1,0:T(8,128)S(1)}, f32[13,32,128]{2,1,0:T(8,128)S(1)}) custom-call(s32[2]{0:T(128)S(1)} %pad_add_fusion.par, f32[3,64,32,128]{3,2,1,0:T(8,128)} %t_ref.3, s32[32,64]{1,0:T(8,128)} %bitcast.9, s32[32,64]{1,0:T(8,128)} %bitcast.11, f32[32,64]{1,0:T(8,128)} %bitcast.13), custom_call_target="tpu_custom_call" | custom-call | flops 1000000000 | bytes 3000000 | tf_op jit(solution)/shard_map/pallas_call | solution.py:485
  2.4 3.1 %collective-permute-start = (f32[13,32,128]{2,1,0:T(8,128)S(1)}, f32[13,32,128]{2,1,0:T(8,128)S(1)}, u32[]{:S(2)}, u32[]{:S(2)}) collective-permute-start(f32[13,32,128]{2,1,0:T(8,128)S(1)} %get-tuple-element.28), channel_id=1, source_target_pairs={{0,8},{8,0},{16,24},{24,16},{1,9},{9,1},{17,25},{25,17},{2,10},{10... | collective-permute-start | bytes 638984 | tf_op jit(solution)/shard_map/ppermute | solution.py:433
  6.1 4.9 %shard_map.59 = (f32[3,36,72,128]{3,2,1,0:T(8,128)S(1)}, f32[3,36,72,128]{3,2,1,0:T(8,128)S(1)}, f32[3,32,128]{2,1,0:T(8,128)S(1)}, f32[72,128]{1,0:T(8,128)S(1)}) custom-call(s32[2]{0:T(128)S(1)} %pad_add_fusion.par, f32[3,64,32,128]{3,2,1,0:T(8,128)} %t_ref.3, s32[32,64]{1,0:T(8,128)} %bitcast.10, s32[32,64]{1,0:T(8,128)} %bitcast.12, f32[32,64]{1,0:T(8,128)} %bitcast.14), custom_call_target="tpu_custom_call" | custom-call | flops 3000000000 | bytes 9000000 | tf_op jit(solution)/shard_map/pallas_call | solution.py:485
  11.1 1.0 %shard_map.61 = (f32[3,36,72,128]{3,2,1,0:T(8,128)S(1)}, f32[3,36,72,128]{3,2,1,0:T(8,128)S(1)}, f32[440,128]{1,0:T(8,128)S(1)}, f32[440,128]{1,0:T(8,128)S(1)}) custom-call(s32[2]{0:T(128)S(1)} %pad_add_fusion.par, f32[3,36,72,128]{3,2,1,0:T(8,128)S(1)} %get-tuple-element.25.state_in, ...), custom_call_target="tpu_custom_call", output_to_operand_aliasing={{0}: (1, {}), {1}: (2, {})} | custom-call | flops 1000000000 | bytes 3000000 | tf_op jit(solution)/shard_map/pallas_call | solution.py:485
  12.2 2.5 %collective-permute-start.3 = (f32[440,128]{1,0:T(8,128)S(1)}, f32[440,128]{1,0:T(8,128)S(1)}, u32[]{:S(2)}, u32[]{:S(2)}) collective-permute-start(f32[440,128]{1,0:T(8,128)S(1)} %get-tuple-element.34), channel_id=1, source_target_pairs={{0,7},{1,2},{2,1},{3,4},{4,3},{5,6},{6,5},{7,0},{8,15},{9,10},{10,... | collective-permute-start | bytes 675848 | tf_op jit(solution)/shard_map/ppermute | solution.py:433
  14.7 1.7 %shard_map.62.source.middle_in = f32[3,36,72,128]{3,2,1,0:T(8,128)S(1)} custom-call(f32[3,36,72,128]{3,2,1,0:T(8,128)S(1)} %get-tuple-element.30.source.start_in, f32[3,36,72,128]{3,2,1,0:T(8,128)S(1)} %get-tuple-element.31.coef_ref.coef_in, f32[72,128]{1,0:T(8,128)S(1)} %get-tuple-element.32.spin_ref), custom_call_target="tpu_custom_call" | custom-call | flops 2000000000 | bytes 6000000 | tf_op jit(solution)/shard_map/pallas_call | solution.py:485
  16.5 1.6 %shard_map.63.state_in = f32[3,36,72,128]{3,2,1,0:T(8,128)S(1)} custom-call(f32[3,36,72,128]{3,2,1,0:T(8,128)S(1)} %shard_map.62.source.middle_in, f32[3,36,72,128]{3,2,1,0:T(8,128)S(1)} %get-tuple-element.31.coef_ref.coef_in, f32[72,128]{1,0:T(8,128)S(1)} %get-tuple-element.32.spin_ref), custom_call_target="tpu_custom_call" | custom-call | flops 2000000000 | bytes 6000000 | tf_op jit(solution)/shard_map/pallas_call | solution.py:485
  18.1 2.2 %collective-permute-done.3.b = f32[440,128]{1,0:T(8,128)S(1)} collective-permute-done((f32[440,128]{1,0:T(8,128)S(1)}, f32[440,128]{1,0:T(8,128)S(1)}, u32[]{:S(2)}, u32[]{:S(2)}) %collective-permute-start.3) | collective-permute-done | bytes 225312 | tf_op jit(solution)/shard_map/ppermute | solution.py:433
  20.3 2.1 %shard_map.64 = (f32[3,36,72,128]{3,2,1,0:T(8,128)S(1)}, f32[3,36,72,128]{3,2,1,0:T(8,128)S(1)}, f32[3,36,72,128]{3,2,1,0:T(8,128)S(1)}, f32[3,36,72,128]{3,2,1,...) custom-call(s32[2]{0:T(128)S(1)} %pad_add_fusion.par, ...), custom_call_target="tpu_custom_call", output_to_operand_aliasing={{0}: (1, {}), {1}: (2, {}), {2}: (3, {}), {3}: (4, {})} | custom-call | flops 2000000000 | bytes 6000000 | tf_op jit(solution)/shard_map/pallas_call | solution.py:485
  22.6 1.1 %collective-permute-done.6 = f32[64,128]{1,0:T(8,128)S(1)} collective-permute-done((f32[64,128]{1,0:T(8,128)S(1)}, f32[64,128]{1,0:T(8,128)S(1)}, u32[]{:S(2)}, u32[]{:S(2)}) %collective-permute-start.6) | collective-permute-done | bytes 32800 | tf_op jit(solution)/shard_map/ppermute | solution.py:437
  23.7 1.6 %collective-permute-start.7 = (f32[64,128]{1,0:T(8,128)S(1)}, f32[64,128]{1,0:T(8,128)S(1)}, u32[]{:S(2)}, u32[]{:S(2)}) collective-permute-start(f32[64,128]{1,0:T(8,128)S(1)} %add.42), channel_id=1, source_target_pairs={{0,2},{1,3},{2,0},{3,1},{4,6},{5,7},{6,4},{7,5},{8,10},{9,11},{10,... | collective-permute-start | bytes 98312 | tf_op jit(solution)/shard_map/ppermute | solution.py:437
  25.9 1.2 %collective-permute-start.9 = (f32[64,128]{1,0:T(8,128)S(1)}, f32[64,128]{1,0:T(8,128)S(1)}, u32[]{:S(2)}, u32[]{:S(2)}) collective-permute-start(f32[64,128]{1,0:T(8,128)S(1)} %add.42), channel_id=1, source_target_pairs={{0,6},{1,7},{2,4},{3,5},{4,2},{5,3},{6,0},{7,1},{8,14},{9,15},{10,... | collective-permute-start | bytes 98312 | tf_op jit(solution)/shard_map/ppermute | solution.py:437
  27.2 1.8 %collective-permute-start.5 = (f32[432,128]{1,0:T(8,128)S(1)}, f32[432,128]{1,0:T(8,128)S(1)}, u32[]{:S(2)}, u32[]{:S(2)}) collective-permute-start(f32[432,128]{1,0:T(8,128)S(1)} %get-tuple-element.38), channel_id=1, source_target_pairs={{0,7},{1,2},{2,1},{3,4},{4,3},{5,6},{6,5},{7,0},{8,15},{9,10},{10,... | collective-permute-start | bytes 663560 | tf_op jit(solution)/shard_map/ppermute | solution.py:433
  29.6 1.2 %collective-permute-done.9 = f32[64,128]{1,0:T(8,128)S(1)} collective-permute-done((f32[64,128]{1,0:T(8,128)S(1)}, f32[64,128]{1,0:T(8,128)S(1)}, u32[]{:S(2)}, u32[]{:S(2)}) %collective-permute-start.9) | collective-permute-done | bytes 32800 | tf_op jit(solution)/shard_map/ppermute | solution.py:437
  30.8 4.5 %collective-permute-start.10 = (f32[64,128]{1,0:T(8,128)S(1)}, f32[64,128]{1,0:T(8,128)S(1)}, u32[]{:S(2)}, u32[]{:S(2)}) collective-permute-start(f32[64,128]{1,0:T(8,128)S(1)} %add_add_fusion.3), channel_id=1, source_target_pairs={{0,8},{8,0},{16,24},{24,16},{1,9},{9,1},{17,25},{25,17},{2,10},{10... | collective-permute-start | bytes 98312 | tf_op jit(solution)/shard_map/ppermute | solution.py:437
  35.2 1.2 %collective-permute-start.11 = (f32[64,128]{1,0:T(8,128)S(1)}, f32[64,128]{1,0:T(8,128)S(1)}, u32[]{:S(2)}, u32[]{:S(2)}) collective-permute-start(f32[64,128]{1,0:T(8,128)S(1)} %add_add_fusion.3), channel_id=1, source_target_pairs={{0,16},{8,24},{16,0},{24,8},{1,17},{9,25},{17,1},{25,9},{2,18},{10... | collective-permute-start | bytes 98312 | tf_op jit(solution)/shard_map/ppermute | solution.py:437
  36.5 1.4 %collective-permute-start.12 = (f32[64,128]{1,0:T(8,128)S(1)}, f32[64,128]{1,0:T(8,128)S(1)}, u32[]{:S(2)}, u32[]{:S(2)}) collective-permute-start(f32[64,128]{1,0:T(8,128)S(1)} %add_add_fusion.3), channel_id=1, source_target_pairs={{0,24},{8,16},{16,8},{24,0},{1,25},{9,17},{17,9},{25,1},{2,26},{10... | collective-permute-start | bytes 98312 | tf_op jit(solution)/shard_map/ppermute | solution.py:437
  37.9 1.7 %shard_map.65.source.middle_in = f32[3,36,72,128]{3,2,1,0:T(8,128)S(1)} custom-call(f32[3,36,72,128]{3,2,1,0:T(8,128)S(1)} %get-tuple-element.35.source.start_in, f32[3,36,72,128]{3,2,1,0:T(8,128)S(1)} %get-tuple-element.36.coef_ref, f32[72,128]{1,0:T(8,128)S(1)} %get-tuple-element.32.spin_ref), custom_call_target="tpu_custom_call" | custom-call | flops 2000000000 | bytes 6000000 | tf_op jit(solution)/shard_map/pallas_call | solution.py:485
  39.6 0.8 %collective-permute-done.11 = f32[64,128]{1,0:T(8,128)S(1)} collective-permute-done((f32[64,128]{1,0:T(8,128)S(1)}, f32[64,128]{1,0:T(8,128)S(1)}, u32[]{:S(2)}, u32[]{:S(2)}) %collective-permute-start.11) | collective-permute-done | bytes 32800 | tf_op jit(solution)/shard_map/ppermute | solution.py:437
  40.5 1.7 %collective-permute-done.12 = f32[64,128]{1,0:T(8,128)S(1)} collective-permute-done((f32[64,128]{1,0:T(8,128)S(1)}, f32[64,128]{1,0:T(8,128)S(1)}, u32[]{:S(2)}, u32[]{:S(2)}) %collective-permute-start.12) | collective-permute-done | bytes 32800 | tf_op jit(solution)/shard_map/ppermute | solution.py:437
  42.3 1.6 %shard_map.66.state_in = f32[3,36,72,128]{3,2,1,0:T(8,128)S(1)} custom-call(f32[3,36,72,128]{3,2,1,0:T(8,128)S(1)} %shard_map.65.source.middle_in, f32[3,36,72,128]{3,2,1,0:T(8,128)S(1)} %get-tuple-element.36.coef_ref, f32[72,128]{1,0:T(8,128)S(1)} %get-tuple-element.32.spin_ref), custom_call_target="tpu_custom_call" | custom-call | flops 2000000000 | bytes 6000000 | tf_op jit(solution)/shard_map/pallas_call | solution.py:485
  44.0 3.7 %shard_map.67 = (f32[128,128]{1,0:T(8,128)S(1)}, f32[1,128]{1,0:T(1,128)S(1)}) custom-call(s32[2]{0:T(128)S(1)} %pad_add_fusion.par, f32[64,128]{1,0:T(8,128)S(1)} %add_add_fusion.2.mine_ref, f32[64,128]{1,0:T(8,128)S(1)} %collective-permute-done.13.other_ref, f32[1,128]{1,0:T(1,128)S(1)} %broadcast_in_dim.3.prior_ref), custom_call_target="tpu_custom_call" | custom-call | flops 10000000 | bytes 30000 | tf_op jit(solution)/shard_map/pallas_call | solution.py:485
  47.6 3.4 %shard_map.68 = (f32[3,36,72,128]{3,2,1,0:T(8,128)S(1)}, f32[3,36,72,128]{3,2,1,0:T(8,128)S(1)}, f32[3,36,72,128]{3,2,1,0:T(8,128)S(1)}, f32[3,32,64,128]{3,2,1,...) custom-call(s32[2]{0:T(128)S(1)} %pad_add_fusion.par, ...), custom_call_target="tpu_custom_call", output_to_operand_aliasing={{0}: (1, {}), {1}: (2, {}), {2}: (3, {})} | custom-call | flops 3000000000 | bytes 9000000 | tf_op jit(solution)/shard_map/pallas_call | solution.py:485
  51.6 0.9 %collective-permute-done.14 = f32[64,128]{1,0:T(8,128)S(1)} collective-permute-done((f32[64,128]{1,0:T(8,128)S(1)}, f32[64,128]{1,0:T(8,128)S(1)}, u32[]{:S(2)}, u32[]{:S(2)}) %collective-permute-start.14) | collective-permute-done | bytes 32800 | tf_op jit(solution)/shard_map/ppermute | solution.py:437
  52.5 1.9 %collective-permute-start.15 = (f32[64,128]{1,0:T(8,128)S(1)}, f32[64,128]{1,0:T(8,128)S(1)}, u32[]{:S(2)}, u32[]{:S(2)}) collective-permute-start(f32[64,128]{1,0:T(8,128)S(1)} %add.49), channel_id=1, source_target_pairs={{0,2},{1,3},{2,0},{3,1},{4,6},{5,7},{6,4},{7,5},{8,10},{9,11},{10,... | collective-permute-start | bytes 98312 | tf_op jit(solution)/shard_map/ppermute | solution.py:437
  54.4 1.6 %collective-permute-start.17 = (f32[64,128]{1,0:T(8,128)S(1)}, f32[64,128]{1,0:T(8,128)S(1)}, u32[]{:S(2)}, u32[]{:S(2)}) collective-permute-start(f32[64,128]{1,0:T(8,128)S(1)} %add.49), channel_id=1, source_target_pairs={{0,6},{1,7},{2,4},{3,5},{4,2},{5,3},{6,0},{7,1},{8,14},{9,15},{10,... | collective-permute-start | bytes 98312 | tf_op jit(solution)/shard_map/ppermute | solution.py:437
  56.4 2.3 %collective-permute-done.16 = f32[64,128]{1,0:T(8,128)S(1)} collective-permute-done((f32[64,128]{1,0:T(8,128)S(1)}, f32[64,128]{1,0:T(8,128)S(1)}, u32[]{:S(2)}, u32[]{:S(2)}) %collective-permute-start.16) | collective-permute-done | bytes 32800 | tf_op jit(solution)/shard_map/ppermute | solution.py:437
  59.5 1.8 %collective-permute-start.19 = (f32[64,128]{1,0:T(8,128)S(1)}, f32[64,128]{1,0:T(8,128)S(1)}, u32[]{:S(2)}, u32[]{:S(2)}) collective-permute-start(f32[64,128]{1,0:T(8,128)S(1)} %add_add_fusion.1), channel_id=1, source_target_pairs={{0,16},{8,24},{16,0},{24,8},{1,17},{9,25},{17,1},{25,9},{2,18},{10... | collective-permute-start | bytes 98312 | tf_op jit(solution)/shard_map/ppermute | solution.py:437
  61.3 2.4 %collective-permute-start.20 = (f32[64,128]{1,0:T(8,128)S(1)}, f32[64,128]{1,0:T(8,128)S(1)}, u32[]{:S(2)}, u32[]{:S(2)}) collective-permute-start(f32[64,128]{1,0:T(8,128)S(1)} %add_add_fusion.1), channel_id=1, source_target_pairs={{0,24},{8,16},{16,8},{24,0},{1,25},{9,17},{17,9},{25,1},{2,26},{10... | collective-permute-start | bytes 98312 | tf_op jit(solution)/shard_map/ppermute | solution.py:437
  63.7 0.9 %collective-permute-done.19 = f32[64,128]{1,0:T(8,128)S(1)} collective-permute-done((f32[64,128]{1,0:T(8,128)S(1)}, f32[64,128]{1,0:T(8,128)S(1)}, u32[]{:S(2)}, u32[]{:S(2)}) %collective-permute-start.19) | collective-permute-done | bytes 32800 | tf_op jit(solution)/shard_map/ppermute | solution.py:437
  64.6 2.3 %collective-permute-done.20 = f32[64,128]{1,0:T(8,128)S(1)} collective-permute-done((f32[64,128]{1,0:T(8,128)S(1)}, f32[64,128]{1,0:T(8,128)S(1)}, u32[]{:S(2)}, u32[]{:S(2)}) %collective-permute-start.20) | collective-permute-done | bytes 32800 | tf_op jit(solution)/shard_map/ppermute | solution.py:437
  68.3 6.5 %shard_map.70 = (f32[12,512,128]{2,1,0:T(8,128)}, f32[1,128]{1,0:T(1,128)}) custom-call(s32[2]{0:T(128)S(1)} %pad_add_fusion.par, f32[64,128]{1,0:T(8,128)S(1)} %add_add_fusion.mine_ref, f32[64,128]{1,0:T(8,128)S(1)} %collective-permute-done.21.other_ref, f32[1,128]{1,0:T(1,128)S(1)} %get-tuple-element.44.prior_ref, f32[12,512,128]{2,1,0:T(8,128)S(1)} %bitcast.8), custom_call_target="tpu_custom_call" | custom-call | flops 1000000000 | bytes 3000000 | tf_op jit(solution)/shard_map/pallas_call | solution.py:485
  (32 shorter events, 5.4 us)
Async XLA Ops:
  2.4 8.7 %collective-permute-start = (f32[13,32,128]{2,1,0:T(8,128)S(1)}, f32[13,32,128]{2,1,0:T(8,128)S(1)}, u32[]{:S(2)}, u32[]{:S(2)}) collective-permute-start(f32[13,32,128]{2,1,0:T(8,128)S(1)} %get-tuple-element.28), channel_id=1, source_target_pairs={{0,8},{8,0},{16,24},{24,16},{1,9},{9,1},{17,25},{25,17},{2,10},{10... | collective-permute-start | bytes 638984 | tf_op jit(solution)/shard_map/ppermute | solution.py:433
  5.5 5.6 %collective-permute-start.1 = (f32[13,32,128]{2,1,0:T(8,128)S(1)}, f32[13,32,128]{2,1,0:T(8,128)S(1)}, u32[]{:S(2)}, u32[]{:S(2)}) collective-permute-start(f32[13,32,128]{2,1,0:T(8,128)S(1)} %get-tuple-element.29), channel_id=1, source_target_pairs={{8,16},{16,8},{9,17},{17,9},{10,18},{18,10},{11,19},{19,11},{12,20... | collective-permute-start | bytes 638984 | tf_op jit(solution)/shard_map/ppermute | solution.py:433
  12.1 6.0 %collective-permute-start.2 = (f32[440,128]{1,0:T(8,128)S(1)}, f32[440,128]{1,0:T(8,128)S(1)}, u32[]{:S(2)}, u32[]{:S(2)}) collective-permute-start(f32[440,128]{1,0:T(8,128)S(1)} %get-tuple-element.33), channel_id=1, source_target_pairs={{0,1},{1,0},{2,3},{3,2},{4,5},{5,4},{6,7},{7,6},{8,9},{9,8},{10,11... | collective-permute-start | bytes 675848 | tf_op jit(solution)/shard_map/ppermute | solution.py:433
  12.2 8.2 %collective-permute-start.3 = (f32[440,128]{1,0:T(8,128)S(1)}, f32[440,128]{1,0:T(8,128)S(1)}, u32[]{:S(2)}, u32[]{:S(2)}) collective-permute-start(f32[440,128]{1,0:T(8,128)S(1)} %get-tuple-element.34), channel_id=1, source_target_pairs={{0,7},{1,2},{2,1},{3,4},{4,3},{5,6},{6,5},{7,0},{8,15},{9,10},{10,... | collective-permute-start | bytes 675848 | tf_op jit(solution)/shard_map/ppermute | solution.py:433
  22.4 1.3 %collective-permute-start.6 = (f32[64,128]{1,0:T(8,128)S(1)}, f32[64,128]{1,0:T(8,128)S(1)}, u32[]{:S(2)}, u32[]{:S(2)}) collective-permute-start(f32[64,128]{1,0:T(8,128)S(1)} %get-tuple-element.40), channel_id=1, source_target_pairs={{0,1},{1,0},{2,3},{3,2},{4,5},{5,4},{6,7},{7,6},{8,9},{9,8},{10,11... | collective-permute-start | bytes 98312 | tf_op jit(solution)/shard_map/ppermute | solution.py:437
  23.7 5.3 %collective-permute-start.7 = (f32[64,128]{1,0:T(8,128)S(1)}, f32[64,128]{1,0:T(8,128)S(1)}, u32[]{:S(2)}, u32[]{:S(2)}) collective-permute-start(f32[64,128]{1,0:T(8,128)S(1)} %add.42), channel_id=1, source_target_pairs={{0,2},{1,3},{2,0},{3,1},{4,6},{5,7},{6,4},{7,5},{8,10},{9,11},{10,... | collective-permute-start | bytes 98312 | tf_op jit(solution)/shard_map/ppermute | solution.py:437
  25.3 4.3 %collective-permute-start.8 = (f32[64,128]{1,0:T(8,128)S(1)}, f32[64,128]{1,0:T(8,128)S(1)}, u32[]{:S(2)}, u32[]{:S(2)}) collective-permute-start(f32[64,128]{1,0:T(8,128)S(1)} %add.42), channel_id=1, source_target_pairs={{0,4},{1,5},{2,6},{3,7},{4,0},{5,1},{6,2},{7,3},{8,12},{9,13},{10,... | collective-permute-start | bytes 98312 | tf_op jit(solution)/shard_map/ppermute | solution.py:437
  25.9 4.8 %collective-permute-start.9 = (f32[64,128]{1,0:T(8,128)S(1)}, f32[64,128]{1,0:T(8,128)S(1)}, u32[]{:S(2)}, u32[]{:S(2)}) collective-permute-start(f32[64,128]{1,0:T(8,128)S(1)} %add.42), channel_id=1, source_target_pairs={{0,6},{1,7},{2,4},{3,5},{4,2},{5,3},{6,0},{7,1},{8,14},{9,15},{10,... | collective-permute-start | bytes 98312 | tf_op jit(solution)/shard_map/ppermute | solution.py:437
  27.2 20.5 %collective-permute-start.4 = (f32[432,128]{1,0:T(8,128)S(1)}, f32[432,128]{1,0:T(8,128)S(1)}, u32[]{:S(2)}, u32[]{:S(2)}) collective-permute-start(f32[432,128]{1,0:T(8,128)S(1)} %get-tuple-element.37), channel_id=1, source_target_pairs={{0,1},{1,0},{2,3},{3,2},{4,5},{5,4},{6,7},{7,6},{8,9},{9,8},{10,11... | collective-permute-start | bytes 663560 | tf_op jit(solution)/shard_map/ppermute | solution.py:433
  27.2 20.5 %collective-permute-start.5 = (f32[432,128]{1,0:T(8,128)S(1)}, f32[432,128]{1,0:T(8,128)S(1)}, u32[]{:S(2)}, u32[]{:S(2)}) collective-permute-start(f32[432,128]{1,0:T(8,128)S(1)} %get-tuple-element.38), channel_id=1, source_target_pairs={{0,7},{1,2},{2,1},{3,4},{4,3},{5,6},{6,5},{7,0},{8,15},{9,10},{10,... | collective-permute-start | bytes 663560 | tf_op jit(solution)/shard_map/ppermute | solution.py:433
  30.8 8.9 %collective-permute-start.10 = (f32[64,128]{1,0:T(8,128)S(1)}, f32[64,128]{1,0:T(8,128)S(1)}, u32[]{:S(2)}, u32[]{:S(2)}) collective-permute-start(f32[64,128]{1,0:T(8,128)S(1)} %add_add_fusion.3), channel_id=1, source_target_pairs={{0,8},{8,0},{16,24},{24,16},{1,9},{9,1},{17,25},{25,17},{2,10},{10... | collective-permute-start | bytes 98312 | tf_op jit(solution)/shard_map/ppermute | solution.py:437
  35.2 5.2 %collective-permute-start.11 = (f32[64,128]{1,0:T(8,128)S(1)}, f32[64,128]{1,0:T(8,128)S(1)}, u32[]{:S(2)}, u32[]{:S(2)}) collective-permute-start(f32[64,128]{1,0:T(8,128)S(1)} %add_add_fusion.3), channel_id=1, source_target_pairs={{0,16},{8,24},{16,0},{24,8},{1,17},{9,25},{17,1},{25,9},{2,18},{10... | collective-permute-start | bytes 98312 | tf_op jit(solution)/shard_map/ppermute | solution.py:437
  36.5 5.7 %collective-permute-start.12 = (f32[64,128]{1,0:T(8,128)S(1)}, f32[64,128]{1,0:T(8,128)S(1)}, u32[]{:S(2)}, u32[]{:S(2)}) collective-permute-start(f32[64,128]{1,0:T(8,128)S(1)} %add_add_fusion.3), channel_id=1, source_target_pairs={{0,24},{8,16},{16,8},{24,0},{1,25},{9,17},{17,9},{25,1},{2,26},{10... | collective-permute-start | bytes 98312 | tf_op jit(solution)/shard_map/ppermute | solution.py:437
  42.2 1.7 %collective-permute-start.13 = (f32[64,128]{1,0:T(8,128)S(1)}, f32[64,128]{1,0:T(8,128)S(1)}, u32[]{:S(2)}, u32[]{:S(2)}) collective-permute-start(f32[64,128]{1,0:T(8,128)S(1)} %add_add_fusion.2.mine_ref), channel_id=1, source_target_pairs={{0,1},{1,0},{2,3},{3,2},{4,5},{5,4},{6,7},{7,6},{8,9},{9,8},{10,11... | collective-permute-start | bytes 98312 | tf_op jit(solution)/shard_map/ppermute | solution.py:437
  51.1 1.4 %collective-permute-start.14 = (f32[64,128]{1,0:T(8,128)S(1)}, f32[64,128]{1,0:T(8,128)S(1)}, u32[]{:S(2)}, u32[]{:S(2)}) collective-permute-start(f32[64,128]{1,0:T(8,128)S(1)} %get-tuple-element.43), channel_id=1, source_target_pairs={{0,1},{1,0},{2,3},{3,2},{4,5},{5,4},{6,7},{7,6},{8,9},{9,8},{10,11... | collective-permute-start | bytes 98312 | tf_op jit(solution)/shard_map/ppermute | solution.py:437
  52.5 3.9 %collective-permute-start.15 = (f32[64,128]{1,0:T(8,128)S(1)}, f32[64,128]{1,0:T(8,128)S(1)}, u32[]{:S(2)}, u32[]{:S(2)}) collective-permute-start(f32[64,128]{1,0:T(8,128)S(1)} %add.49), channel_id=1, source_target_pairs={{0,2},{1,3},{2,0},{3,1},{4,6},{5,7},{6,4},{7,5},{8,10},{9,11},{10,... | collective-permute-start | bytes 98312 | tf_op jit(solution)/shard_map/ppermute | solution.py:437
  54.4 4.3 %collective-permute-start.16 = (f32[64,128]{1,0:T(8,128)S(1)}, f32[64,128]{1,0:T(8,128)S(1)}, u32[]{:S(2)}, u32[]{:S(2)}) collective-permute-start(f32[64,128]{1,0:T(8,128)S(1)} %add.49), channel_id=1, source_target_pairs={{0,4},{1,5},{2,6},{3,7},{4,0},{5,1},{6,2},{7,3},{8,12},{9,13},{10,... | collective-permute-start | bytes 98312 | tf_op jit(solution)/shard_map/ppermute | solution.py:437
  54.4 4.8 %collective-permute-start.17 = (f32[64,128]{1,0:T(8,128)S(1)}, f32[64,128]{1,0:T(8,128)S(1)}, u32[]{:S(2)}, u32[]{:S(2)}) collective-permute-start(f32[64,128]{1,0:T(8,128)S(1)} %add.49), channel_id=1, source_target_pairs={{0,6},{1,7},{2,4},{3,5},{4,2},{5,3},{6,0},{7,1},{8,14},{9,15},{10,... | collective-permute-start | bytes 98312 | tf_op jit(solution)/shard_map/ppermute | solution.py:437
  59.3 4.5 %collective-permute-start.18 = (f32[64,128]{1,0:T(8,128)S(1)}, f32[64,128]{1,0:T(8,128)S(1)}, u32[]{:S(2)}, u32[]{:S(2)}) collective-permute-start(f32[64,128]{1,0:T(8,128)S(1)} %add_add_fusion.1), channel_id=1, source_target_pairs={{0,8},{8,0},{16,24},{24,16},{1,9},{9,1},{17,25},{25,17},{2,10},{10... | collective-permute-start | bytes 98312 | tf_op jit(solution)/shard_map/ppermute | solution.py:437
  59.5 5.2 %collective-permute-start.19 = (f32[64,128]{1,0:T(8,128)S(1)}, f32[64,128]{1,0:T(8,128)S(1)}, u32[]{:S(2)}, u32[]{:S(2)}) collective-permute-start(f32[64,128]{1,0:T(8,128)S(1)} %add_add_fusion.1), channel_id=1, source_target_pairs={{0,16},{8,24},{16,0},{24,8},{1,17},{9,25},{17,1},{25,9},{2,18},{10... | collective-permute-start | bytes 98312 | tf_op jit(solution)/shard_map/ppermute | solution.py:437
  61.3 5.7 %collective-permute-start.20 = (f32[64,128]{1,0:T(8,128)S(1)}, f32[64,128]{1,0:T(8,128)S(1)}, u32[]{:S(2)}, u32[]{:S(2)}) collective-permute-start(f32[64,128]{1,0:T(8,128)S(1)} %add_add_fusion.1), channel_id=1, source_target_pairs={{0,24},{8,16},{16,8},{24,0},{1,25},{9,17},{17,9},{25,1},{2,26},{10... | collective-permute-start | bytes 98312 | tf_op jit(solution)/shard_map/ppermute | solution.py:437
  67.0 1.3 %collective-permute-start.21 = (f32[64,128]{1,0:T(8,128)S(1)}, f32[64,128]{1,0:T(8,128)S(1)}, u32[]{:S(2)}, u32[]{:S(2)}) collective-permute-start(f32[64,128]{1,0:T(8,128)S(1)} %add_add_fusion.mine_ref), channel_id=1, source_target_pairs={{0,1},{1,0},{2,3},{3,2},{4,5},{5,4},{6,7},{7,6},{8,9},{9,8},{10,11... | collective-permute-start | bytes 98312 | tf_op jit(solution)/shard_map/ppermute | solution.py:437

commit v7 on v6

--- a/solution.py
+++ b/solution.py
@@ -98,15 +98,12 @@
 
 
 def spread_fields(
-    total_rows, par, t_ref, sea_ref, levels_ref, current_ref, state, coef, wide, spin, sea, levels, current, sems, field_sems
+    total_rows, par, t_ref, sea_ref, levels_ref, current_ref, state, coef, wide, spin, block, sea, levels, current, sems, field_sems
 ):
     comps, rows, cols, _ = t_ref.shape
     field_copies = fetch((sea_ref, levels_ref, current_ref), (sea, levels, current), field_sems)
-    cells = [(comp, lon) for comp in range(comps) for lon in range(cols)]
     copies = fetch(
-        [t_ref.at[comp, :, lon] for comp, lon in cells],
-        [state.at[comp, SIDE + lon, pl.ds(0, rows)] for comp, lon in cells],
-        sems,
+        [t_ref.at[comp] for comp in range(comps)], [block.at[comp] for comp in range(comps)], sems
     )
     line = lax.broadcasted_iota(jnp.int32, spin.shape, 0)
     line = jnp.where(line < rows + HALO, line, line - (rows + 2 * HALO))
@@ -120,7 +117,11 @@
         natural = jnp.transpose(wide[field])[:rows]
         for lon in range(cols):
             coef[field, SIDE + lon, pl.ds(0, rows), :] = lane_spread(natural, lon)
-    finish_all(copies)
+    for comp in range(comps):
+        copies[comp].wait()
+        for row in range(0, rows, SUB):
+            cells = block[comp, pl.ds(row, SUB)]
+            state[comp, pl.ds(SIDE, cols), pl.ds(row, SUB), :] = jnp.transpose(cells, (1, 0, 2))
 
 
 def column_at(east, cols, depth):
@@ -294,19 +295,44 @@
 
 
 def write_halves(par, gram, scale, kept, sent, total):
+    half, rows = LANES // 2, kept.shape[0]
+    mixed = gram[:, LANES:]
+    whole = scale * (gram[:, :LANES] + (mixed + jnp.transpose(mixed)))
+    row = lax.broadcasted_iota(jnp.int32, (half, LANES), 0)
+    col = lax.broadcasted_iota(jnp.int32, (half, LANES), 1)
+    total[pl.ds(0, half), :] = jnp.where(
+        (col < half) | (col - half > row), whole[half:], pltpu.roll(whole[:half], half, 1)
+    )
+    row = lax.broadcasted_iota(jnp.int32, (LANES, LANES), 0)
+    col = lax.broadcasted_iota(jnp.int32, (LANES, LANES), 1)
+    total[pl.ds(half, 2 * rows - half), :] = jnp.zeros((2 * rows - half, LANES), jnp.float32)
+    total[pl.ds(half, 1), :] = jnp.sum(jnp.where(row == col, whole, 0.0), axis=0, keepdims=True)
     odd = par[1] % 2
-    rows = LANES // 2
-    mixed = gram[:, LANES:]
-    total[...] = scale * (gram[:, :LANES] + (mixed + jnp.transpose(mixed)))
     kept[...] = total[pl.ds(odd * rows, rows), :]
     sent[...] = total[pl.ds((1 - odd) * rows, rows), :]
 
 
-def invert_factor(gram_ref, work, board):
+def factor_pair(low, p):
+    q, size = p + 1, len(low)
+    a, b, c = low[p][p], low[q][p], low[q][q]
+    root_a, root_det = lax.rsqrt(a), lax.rsqrt(a * c - b * b)
+    both = root_a * root_det
+    turned = [a * low[i][q] - b * low[i][p] for i in range(q + 1, size)]
+    low[q][p] = b * root_a
+    for i, value in zip(range(q + 1, size), turned):
+        low[i][p] = low[i][p] * root_a
+        low[i][q] = value * both
+    for i in range(q + 1, size):
+        for m in range(q + 1, i + 1):
+            low[i][m] = (low[i][m] - low[i][p] * low[m][p]) - low[i][q] * low[m][q]
+    return root_a, a * both
+
+
+def invert_factor(gram, work, board):
     count = LANES // SUB
     lane = lax.broadcasted_iota(jnp.int32, (SUB, LANES), 1)
     sub = lax.broadcasted_iota(jnp.int32, (SUB, LANES), 0)
-    rows = [gram_ref[pl.ds(SUB * i, SUB), :] for i in range(count)]
+    rows = [gram[SUB * i : SUB * (i + 1)] for i in range(count)]
     for block in range(count):
         base = SUB * block
         here = (lane >= base) & (lane < base + SUB)
@@ -321,14 +347,11 @@
         board[pl.ds(shelf, SUB), :] = jnp.where(
             here, jnp.where(lane - base == sub, 1.0, 0.0), rows[block]
         )
-        inv, scaled = [], []
+        inv = []
+        for p in range(0, SUB, 2):
+            inv.extend(factor_pair(low, p))
+        scaled = []
         for k in range(SUB):
-            inv.append(lax.rsqrt(low[k][k]))
-            for i in range(k + 1, SUB):
-                low[i][k] = low[i][k] * inv[k]
-            for i in range(k + 1, SUB):
-                for m in range(k + 1, i + 1):
-                    low[i][m] = low[i][m] - low[i][k] * low[m][k]
             line = board[pl.ds(shelf + k, SUB, stride=0), :]
             for l in range(k):
                 line = line - low[k][l] * scaled[l]
@@ -351,14 +374,26 @@
 
 
 def factorize(par, mine_ref, other_ref, gram, work, board):
-    rows = LANES // 2
+    half, rows = LANES // 2, mine_ref.shape[0]
     odd = par[1] % 2
     gram[pl.ds(odd * rows, rows), :] = mine_ref[...]
     gram[pl.ds((1 - odd) * rows, rows), :] = other_ref[...]
-    invert_factor(gram, work, board)
+    packed, diagonal = gram[pl.ds(0, half), :], gram[pl.ds(half, 1), :]
+    row = lax.broadcasted_iota(jnp.int32, (half, LANES), 0)
+    col = lax.broadcasted_iota(jnp.int32, (half, LANES), 1)
+    triangles = jnp.concatenate(
+        [
+            jnp.where(col < row, pltpu.roll(packed, half, 1), 0.0),
+            jnp.where((col < half) | (col - half > row), packed, 0.0),
+        ],
+        axis=0,
+    )
     row = lax.broadcasted_iota(jnp.int32, (LANES, LANES), 0)
     col = lax.broadcasted_iota(jnp.int32, (LANES, LANES), 1)
-    inverse = jnp.where(row >= col, work[...], 0.0)
+    size = jnp.broadcast_to(lax.rsqrt(diagonal), (LANES, LANES))
+    whole = jnp.where(row == col, diagonal, triangles + jnp.transpose(triangles))
+    invert_factor((whole * size) * jnp.transpose(size), work, board)
+    inverse = jnp.where(row >= col, work[...], 0.0) * size
     diagonal = jnp.sum(jnp.where(row == col, inverse, 0.0), axis=0, keepdims=True)
     return inverse, diagonal
 
@@ -437,26 +472,43 @@
     return lax.ppermute(value, axis, [(i, i ^ mask) for i in range(lax.axis_size(axis))])
 
 
-def sum_over(value, axis, first_bit):
+def add_four(first, second, third, fourth, *rest):
+    out_ref = rest[len(rest) // 2]
+    out_ref[...] = (first[...] + second[...]) + (third[...] + fourth[...])
+
+
+def sum_over(value, axis, first_bit, beside=None, held=()):
     bits = lax.axis_size(axis).bit_length() - 1
     while first_bit < bits:
         low = 1 << first_bit
         if first_bit + 1 < bits:
             high = low << 1
             one, two, three = (swapped(value, axis, mask) for mask in (low, high, low | high))
-            value = (value + one) + (two + three)
+            if beside is None:
+                value = (value + one) + (two + three)
+            else:
+                anywhere = pl.BlockSpec(memory_space=pl.ANY)
+                value, *held = pl.pallas_call(
+                    add_four,
+                    out_shape=[jax.ShapeDtypeStruct(x.shape, x.dtype) for x in (value, *held)],
+                    in_specs=[VMEM] * 4 + [anywhere] * (1 + len(held)),
+                    out_specs=[VMEM] + [anywhere] * len(held),
+                    input_output_aliases={5 + i: 1 + i for i in range(len(held))},
+                    compiler_params=params(),
+                )(value, one, two, three, beside, *held)
+                beside = None
             first_bit += 2
         else:
             value = value + swapped(value, axis, low)
             first_bit += 1
-    return value
-
-
-def sum_devices(kept, sent):
+    return value, held
+
+
+def sum_devices(kept, sent, beside=(None, None), held=()):
     mine = kept + swapped(sent, "col", 1)
-    mine = sum_over(mine, "col", 1)
-    mine = sum_over(mine, "row", 0)
-    return mine, swapped(mine, "col", 1)
+    mine, held = sum_over(mine, "col", 1, beside[0], held)
+    mine, _ = sum_over(mine, "row", 0, beside[1])
+    return mine, swapped(mine, "col", 1), held
 
 
 def body(tangents, sea_mask, levels, current):
@@ -474,7 +526,7 @@
     columns = (shape_of(comps * SIDE * tall, modes),) * 2
     first_columns = (shape_of(comps * SIDE * tall + SUB, modes),) * 2
     rows_sent = (shape_of(comps * HALO + 1, cols, modes),) * 2
-    halves = (shape_of(modes // 2, modes),) * 2
+    halves = (shape_of(modes // 4 + SUB, modes),) * 2
     square = pltpu.VMEM((modes, modes), jnp.float32)
     board = pltpu.VMEM((2 * SUB * modes, LANES), jnp.float32)
     factor = pltpu.VMEM((2 * modes, 2 * modes), jnp.bfloat16)
@@ -529,8 +581,9 @@
         source,
         *fields,
         specs=[SMEM] + [HBM] * 4,
-        scratch=upright
-        + [pltpu.SemaphoreType.DMA((comps * cols,)), pltpu.SemaphoreType.DMA((FIELDS,))],
+        scratch=[pltpu.VMEM(tangents.shape, jnp.float32)]
+        + upright
+        + [pltpu.SemaphoreType.DMA((comps,)), pltpu.SemaphoreType.DMA((FIELDS,))],
         cost=3.0,
     )
     start, coef, *packed = call(
@@ -562,10 +615,10 @@
         aliases={1: 0, 2: 1, 3: 2, 4: 3},
         cost=2.0,
     )
-    halos = swap_columns(packed)
-    mine, other = sum_devices(kept, sent)
     middle = inside(0, start)
     state = inside(1, middle)
+    mine, other, packed = sum_devices(kept, sent, (middle, state), packed)
+    halos = swap_columns(packed)
     inverse, logs = call(
         factor_only,
         (shape_of(modes, modes), shape_of(1, modes)),
@@ -596,7 +649,7 @@
     )[0]
     height = comps * rows * cols // TILES
     tiled = shape_of(TILES, height, modes)
-    mine, other = sum_devices(kept, sent)
+    mine, other, _ = sum_devices(kept, sent)
     out, logs = call(
         finish,
         (tiled, shape_of(1, modes)),

time: 75.3 us -> 75.6 us (level)
  waiting for transfers between devices: 15.6 us -> 17.5 us
  Pallas kernels: 30.6 us -> 29.6 us
    ppermute x16, waiting for transfers between devices: 13.4 us -> 14.9 us  [swapped(): lax.ppermute(value, axis, [(i, i ^ mask) for i in range(lax.axis_size(axi...]
    pallas_call x12, Pallas kernels: 30.6 us -> 29.6 us  [call(): pl.pallas_call(kernel, out_shape=outs, in_specs=specs or [SMEM] + [VMEM]...]
    ppermute x3, waiting for transfers between devices: 0.01 us -> 0.8 us  [swap_pairs(): lax.ppermute(near_value, axis, near)]
  transfers between devices with their start and end apart: 22 -> 22, of which waited for: 13 -> 15; matrix products, arithmetic and copies ran while one was open for 0% -> 0% of each run, Pallas kernels for 21% -> 20%
where the time goes in v7:
time: 75.6 us; the launch traced here: 75.3 us
  Pallas kernels  29.6 us (39%)
  starting transfers between devices  27.2 us (36%)
  waiting for transfers between devices  17.5 us (23%)
  between operations  0.94 us (1%)
    pallas_call x12, Pallas kernels, call(): pl.pallas_call(kernel, out_shape=outs, in_specs=specs or [SMEM] + [VMEM]...  29.6 us
    ppermute x16, starting transfers between devices, swapped(): lax.ppermute(value, axis, [(i, i ^ mask) for i in range(lax.axis_size(axi...  19.5 us
    ppermute x16, waiting for transfers between devices, swapped(): lax.ppermute(value, axis, [(i, i ^ mask) for i in range(lax.axis_size(axi...  14.9 us
    ppermute x3, starting transfers between devices, swap_pairs(): lax.ppermute(far_value, axis, far)  4.4 us
    ppermute x3, starting transfers between devices, swap_pairs(): lax.ppermute(near_value, axis, near)  3.22 us
    ppermute x3, waiting for transfers between devices, swap_pairs(): lax.ppermute(far_value, axis, far)  1.77 us
  transfers between devices with their start and end apart: 22, of which 15 were waited for; matrix products, arithmetic and copies ran while one was open for 0% of the time, Pallas kernels for 20%

profile of v7, /device:TPU:0, one launch (start us, length us, event | category | flops | bytes accessed | tf_op | source)
XLA Modules:
  0.0 75.3 jit_solution(439815095622440448)
XLA Ops:
  0.7 1.7 %shard_map.60 = (f32[13,32,128]{2,1,0:T(8,128)S(1)}, f32[13,32,128]{2,1,0:T(8,128)S(1)}) custom-call(s32[2]{0:T(128)S(1)} %pad_add_fusion.par, f32[3,64,32,128]{3,2,1,0:T(8,128)} %t_ref.3, s32[32,64]{1,0:T(8,128)} %bitcast.9, s32[32,64]{1,0:T(8,128)} %bitcast.11, f32[32,64]{1,0:T(8,128)} %bitcast.13), custom_call_target="tpu_custom_call" | custom-call | flops 1000000000 | bytes 3000000 | tf_op jit(solution)/shard_map/pallas_call | solution.py:537
  2.4 3.1 %collective-permute-start = (f32[13,32,128]{2,1,0:T(8,128)S(1)}, f32[13,32,128]{2,1,0:T(8,128)S(1)}, u32[]{:S(2)}, u32[]{:S(2)}) collective-permute-start(f32[13,32,128]{2,1,0:T(8,128)S(1)} %get-tuple-element.31), channel_id=1, source_target_pairs={{0,8},{8,0},{16,24},{24,16},{1,9},{9,1},{17,25},{25,17},{2,10},{10... | collective-permute-start | bytes 638984 | tf_op jit(solution)/shard_map/ppermute | solution.py:468
  6.1 3.8 %shard_map.59 = (f32[3,36,72,128]{3,2,1,0:T(8,128)S(1)}, f32[3,36,72,128]{3,2,1,0:T(8,128)S(1)}, f32[3,32,128]{2,1,0:T(8,128)S(1)}, f32[72,128]{1,0:T(8,128)S(1)}) custom-call(s32[2]{0:T(128)S(1)} %pad_add_fusion.par, f32[3,64,32,128]{3,2,1,0:T(8,128)} %t_ref.3, s32[32,64]{1,0:T(8,128)} %bitcast.10, s32[32,64]{1,0:T(8,128)} %bitcast.12, f32[32,64]{1,0:T(8,128)} %bitcast.14), custom_call_target="tpu_custom_call" | custom-call | flops 3000000000 | bytes 9000000 | tf_op jit(solution)/shard_map/pallas_call | solution.py:537
  10.7 1.0 %shard_map.61 = (f32[3,36,72,128]{3,2,1,0:T(8,128)S(1)}, f32[3,36,72,128]{3,2,1,0:T(8,128)S(1)}, f32[440,128]{1,0:T(8,128)S(1)}, f32[440,128]{1,0:T(8,128)S(1)}) custom-call(s32[2]{0:T(128)S(1)} %pad_add_fusion.par, f32[3,36,72,128]{3,2,1,0:T(8,128)S(1)} %get-tuple-element.28.state_in, ...), custom_call_target="tpu_custom_call", output_to_operand_aliasing={{0}: (1, {}), {1}: (2, {})} | custom-call | flops 1000000000 | bytes 3000000 | tf_op jit(solution)/shard_map/pallas_call | solution.py:537
  11.8 2.7 %collective-permute-start.3 = (f32[440,128]{1,0:T(8,128)S(1)}, f32[440,128]{1,0:T(8,128)S(1)}, u32[]{:S(2)}, u32[]{:S(2)}) collective-permute-start(f32[440,128]{1,0:T(8,128)S(1)} %get-tuple-element.37), channel_id=1, source_target_pairs={{0,7},{1,2},{2,1},{3,4},{4,3},{5,6},{6,5},{7,0},{8,15},{9,10},{10,... | collective-permute-start | bytes 675848 | tf_op jit(solution)/shard_map/ppermute | solution.py:468
  14.5 1.8 %shard_map.62.source.middle_in = f32[3,36,72,128]{3,2,1,0:T(8,128)S(1)} custom-call(f32[3,36,72,128]{3,2,1,0:T(8,128)S(1)} %get-tuple-element.33.source.start_in, f32[3,36,72,128]{3,2,1,0:T(8,128)S(1)} %get-tuple-element.34.coef_ref.coef_in, f32[72,128]{1,0:T(8,128)S(1)} %get-tuple-element.35.spin_ref), custom_call_target="tpu_custom_call" | custom-call | flops 2000000000 | bytes 6000000 | tf_op jit(solution)/shard_map/pallas_call | solution.py:537
  16.4 1.6 %shard_map.63.state_in = f32[3,36,72,128]{3,2,1,0:T(8,128)S(1)} custom-call(f32[3,36,72,128]{3,2,1,0:T(8,128)S(1)} %shard_map.62.source.middle_in, f32[3,36,72,128]{3,2,1,0:T(8,128)S(1)} %get-tuple-element.34.coef_ref.coef_in, f32[72,128]{1,0:T(8,128)S(1)} %get-tuple-element.35.spin_ref), custom_call_target="tpu_custom_call" | custom-call | flops 2000000000 | bytes 6000000 | tf_op jit(solution)/shard_map/pallas_call | solution.py:537
  18.1 1.8 %collective-permute-done.3.b = f32[440,128]{1,0:T(8,128)S(1)} collective-permute-done((f32[440,128]{1,0:T(8,128)S(1)}, f32[440,128]{1,0:T(8,128)S(1)}, u32[]{:S(2)}, u32[]{:S(2)}) %collective-permute-start.3) | collective-permute-done | bytes 225312 | tf_op jit(solution)/shard_map/ppermute | solution.py:468
  19.8 2.1 %shard_map.64 = (f32[3,36,72,128]{3,2,1,0:T(8,128)S(1)}, f32[3,36,72,128]{3,2,1,0:T(8,128)S(1)}, f32[3,36,72,128]{3,2,1,0:T(8,128)S(1)}, f32[3,36,72,128]{3,2,1,...) custom-call(s32[2]{0:T(128)S(1)} %pad_add_fusion.par, ...), custom_call_target="tpu_custom_call", output_to_operand_aliasing={{0}: (1, {}), {1}: (2, {}), {2}: (3, {}), {3}: (4, {})} | custom-call | flops 2000000000 | bytes 6000000 | tf_op jit(solution)/shard_map/pallas_call | solution.py:537
  22.1 1.1 %collective-permute-done.4 = f32[40,128]{1,0:T(8,128)S(1)} collective-permute-done((f32[40,128]{1,0:T(8,128)S(1)}, f32[40,128]{1,0:T(8,128)S(1)}, u32[]{:S(2)}, u32[]{:S(2)}) %collective-permute-start.4) | collective-permute-done | bytes 20512 | tf_op jit(solution)/shard_map/ppermute | solution.py:472
  23.1 2.0 %collective-permute-start.5 = (f32[40,128]{1,0:T(8,128)S(1)}, f32[40,128]{1,0:T(8,128)S(1)}, u32[]{:S(2)}, u32[]{:S(2)}) collective-permute-start(f32[40,128]{1,0:T(8,128)S(1)} %add.24.first), channel_id=1, source_target_pairs={{0,2},{1,3},{2,0},{3,1},{4,6},{5,7},{6,4},{7,5},{8,10},{9,11},{10,... | collective-permute-start | bytes 61448 | tf_op jit(solution)/shard_map/ppermute | solution.py:472
  25.7 0.9 %collective-permute-start.7 = (f32[40,128]{1,0:T(8,128)S(1)}, f32[40,128]{1,0:T(8,128)S(1)}, u32[]{:S(2)}, u32[]{:S(2)}) collective-permute-start(f32[40,128]{1,0:T(8,128)S(1)} %add.24.first), channel_id=1, source_target_pairs={{0,6},{1,7},{2,4},{3,5},{4,2},{5,3},{6,0},{7,1},{8,14},{9,15},{10,... | collective-permute-start | bytes 61448 | tf_op jit(solution)/shard_map/ppermute | solution.py:472
  26.6 1.8 %shard_map.65.source.rest_0_.middle_in = f32[3,36,72,128]{3,2,1,0:T(8,128)S(1)} custom-call(f32[3,36,72,128]{3,2,1,0:T(8,128)S(1)} %get-tuple-element.38.source.start_in, f32[3,36,72,128]{3,2,1,0:T(8,128)S(1)} %get-tuple-element.39.coef_ref, f32[72,128]{1,0:T(8,128)S(1)} %get-tuple-element.35.spin_ref), custom_call_target="tpu_custom_call" | custom-call | flops 2000000000 | bytes 6000000 | tf_op jit(solution)/shard_map/pallas_call | solution.py:537
  28.9 1.5 %collective-permute-done.7.fourth = f32[40,128]{1,0:T(8,128)S(1)} collective-permute-done((f32[40,128]{1,0:T(8,128)S(1)}, f32[40,128]{1,0:T(8,128)S(1)}, u32[]{:S(2)}, u32[]{:S(2)}) %collective-permute-start.7) | collective-permute-done | bytes 20512 | tf_op jit(solution)/shard_map/ppermute | solution.py:472
  30.5 1.0 %collective-permute-start.9 = (f32[432,128]{1,0:T(8,128)S(1)}, f32[432,128]{1,0:T(8,128)S(1)}, u32[]{:S(2)}, u32[]{:S(2)}) collective-permute-start(f32[432,128]{1,0:T(8,128)S(1)} %get-tuple-element.45), channel_id=1, source_target_pairs={{0,7},{1,2},{2,1},{3,4},{4,3},{5,6},{6,5},{7,0},{8,15},{9,10},{10,... | collective-permute-start | bytes 663560 | tf_op jit(solution)/shard_map/ppermute | solution.py:468
  31.5 4.9 %collective-permute-start.10 = (f32[40,128]{1,0:T(8,128)S(1)}, f32[40,128]{1,0:T(8,128)S(1)}, u32[]{:S(2)}, u32[]{:S(2)}) collective-permute-start(f32[40,128]{1,0:T(8,128)S(1)} %get-tuple-element.46.first), channel_id=1, source_target_pairs={{0,8},{8,0},{16,24},{24,16},{1,9},{9,1},{17,25},{25,17},{2,10},{10... | collective-permute-start | bytes 61448 | tf_op jit(solution)/shard_map/ppermute | solution.py:472
  36.4 1.2 %collective-permute-start.11 = (f32[40,128]{1,0:T(8,128)S(1)}, f32[40,128]{1,0:T(8,128)S(1)}, u32[]{:S(2)}, u32[]{:S(2)}) collective-permute-start(f32[40,128]{1,0:T(8,128)S(1)} %get-tuple-element.46.first), channel_id=1, source_target_pairs={{0,16},{8,24},{16,0},{24,8},{1,17},{9,25},{17,1},{25,9},{2,18},{10... | collective-permute-start | bytes 61448 | tf_op jit(solution)/shard_map/ppermute | solution.py:472
  37.6 1.5 %collective-permute-start.12 = (f32[40,128]{1,0:T(8,128)S(1)}, f32[40,128]{1,0:T(8,128)S(1)}, u32[]{:S(2)}, u32[]{:S(2)}) collective-permute-start(f32[40,128]{1,0:T(8,128)S(1)} %get-tuple-element.46.first), channel_id=1, source_target_pairs={{0,24},{8,16},{16,8},{24,0},{1,25},{9,17},{17,9},{25,1},{2,26},{10... | collective-permute-start | bytes 61448 | tf_op jit(solution)/shard_map/ppermute | solution.py:472
  39.1 1.6 %shard_map.66.rest_0_.state_in = f32[3,36,72,128]{3,2,1,0:T(8,128)S(1)} custom-call(f32[3,36,72,128]{3,2,1,0:T(8,128)S(1)} %shard_map.65.source.rest_0_.middle_in, f32[3,36,72,128]{3,2,1,0:T(8,128)S(1)} %get-tuple-element.39.coef_ref, f32[72,128]{1,0:T(8,128)S(1)} %get-tuple-element.35.spin_ref), custom_call_target="tpu_custom_call" | custom-call | flops 2000000000 | bytes 6000000 | tf_op jit(solution)/shard_map/pallas_call | solution.py:537
  41.3 1.9 %collective-permute-done.12.fourth = f32[40,128]{1,0:T(8,128)S(1)} collective-permute-done((f32[40,128]{1,0:T(8,128)S(1)}, f32[40,128]{1,0:T(8,128)S(1)}, u32[]{:S(2)}, u32[]{:S(2)}) %collective-permute-start.12) | collective-permute-done | bytes 20512 | tf_op jit(solution)/shard_map/ppermute | solution.py:472
  43.3 1.2 %collective-permute-done.13.other_ref = f32[40,128]{1,0:T(8,128)S(1)} collective-permute-done((f32[40,128]{1,0:T(8,128)S(1)}, f32[40,128]{1,0:T(8,128)S(1)}, u32[]{:S(2)}, u32[]{:S(2)}) %collective-permute-start.13) | collective-permute-done | bytes 20512 | tf_op jit(solution)/shard_map/ppermute | solution.py:472
  44.4 3.6 %shard_map.69 = (f32[128,128]{1,0:T(8,128)S(1)}, f32[1,128]{1,0:T(1,128)S(1)}) custom-call(s32[2]{0:T(128)S(1)} %pad_add_fusion.par, f32[40,128]{1,0:T(8,128)S(1)} %shard_map.68.mine_ref, f32[40,128]{1,0:T(8,128)S(1)} %collective-permute-done.13.other_ref, f32[1,128]{1,0:T(1,128)S(1)} %broadcast_in_dim.3.prior_ref), custom_call_target="tpu_custom_call" | custom-call | flops 10000000 | bytes 30000 | tf_op jit(solution)/shard_map/pallas_call | solution.py:537
  48.0 3.5 %shard_map.70 = (f32[3,36,72,128]{3,2,1,0:T(8,128)S(1)}, f32[3,36,72,128]{3,2,1,0:T(8,128)S(1)}, f32[3,36,72,128]{3,2,1,0:T(8,128)S(1)}, f32[3,32,64,128]{3,2,1,...) custom-call(s32[2]{0:T(128)S(1)} %pad_add_fusion.par, ...), custom_call_target="tpu_custom_call", output_to_operand_aliasing={{0}: (1, {}), {1}: (2, {}), {2}: (3, {})} | custom-call | flops 3000000000 | bytes 9000000 | tf_op jit(solution)/shard_map/pallas_call | solution.py:537
  51.7 1.0 %collective-permute-done.14 = f32[40,128]{1,0:T(8,128)S(1)} collective-permute-done((f32[40,128]{1,0:T(8,128)S(1)}, f32[40,128]{1,0:T(8,128)S(1)}, u32[]{:S(2)}, u32[]{:S(2)}) %collective-permute-start.14) | collective-permute-done | bytes 20512 | tf_op jit(solution)/shard_map/ppermute | solution.py:472
  52.8 0.8 %collective-permute-start.15 = (f32[40,128]{1,0:T(8,128)S(1)}, f32[40,128]{1,0:T(8,128)S(1)}, u32[]{:S(2)}, u32[]{:S(2)}) collective-permute-start(f32[40,128]{1,0:T(8,128)S(1)} %add.25), channel_id=1, source_target_pairs={{0,2},{1,3},{2,0},{3,1},{4,6},{5,7},{6,4},{7,5},{8,10},{9,11},{10,... | collective-permute-start | bytes 61448 | tf_op jit(solution)/shard_map/ppermute | solution.py:472
  53.6 1.4 %collective-permute-start.16 = (f32[40,128]{1,0:T(8,128)S(1)}, f32[40,128]{1,0:T(8,128)S(1)}, u32[]{:S(2)}, u32[]{:S(2)}) collective-permute-start(f32[40,128]{1,0:T(8,128)S(1)} %add.25), channel_id=1, source_target_pairs={{0,4},{1,5},{2,6},{3,7},{4,0},{5,1},{6,2},{7,3},{8,12},{9,13},{10,... | collective-permute-start | bytes 61448 | tf_op jit(solution)/shard_map/ppermute | solution.py:472
  55.0 1.3 %collective-permute-start.17 = (f32[40,128]{1,0:T(8,128)S(1)}, f32[40,128]{1,0:T(8,128)S(1)}, u32[]{:S(2)}, u32[]{:S(2)}) collective-permute-start(f32[40,128]{1,0:T(8,128)S(1)} %add.25), channel_id=1, source_target_pairs={{0,6},{1,7},{2,4},{3,5},{4,2},{5,3},{6,0},{7,1},{8,14},{9,15},{10,... | collective-permute-start | bytes 61448 | tf_op jit(solution)/shard_map/ppermute | solution.py:472
  57.4 2.3 %collective-permute-done.17 = f32[40,128]{1,0:T(8,128)S(1)} collective-permute-done((f32[40,128]{1,0:T(8,128)S(1)}, f32[40,128]{1,0:T(8,128)S(1)}, u32[]{:S(2)}, u32[]{:S(2)}) %collective-permute-start.17) | collective-permute-done | bytes 20512 | tf_op jit(solution)/shard_map/ppermute | solution.py:472
  60.0 1.8 %collective-permute-start.19 = (f32[40,128]{1,0:T(8,128)S(1)}, f32[40,128]{1,0:T(8,128)S(1)}, u32[]{:S(2)}, u32[]{:S(2)}) collective-permute-start(f32[40,128]{1,0:T(8,128)S(1)} %add_add_fusion.1), channel_id=1, source_target_pairs={{0,16},{8,24},{16,0},{24,8},{1,17},{9,25},{17,1},{25,9},{2,18},{10... | collective-permute-start | bytes 61448 | tf_op jit(solution)/shard_map/ppermute | solution.py:472
  61.8 2.4 %collective-permute-start.20 = (f32[40,128]{1,0:T(8,128)S(1)}, f32[40,128]{1,0:T(8,128)S(1)}, u32[]{:S(2)}, u32[]{:S(2)}) collective-permute-start(f32[40,128]{1,0:T(8,128)S(1)} %add_add_fusion.1), channel_id=1, source_target_pairs={{0,24},{8,16},{16,8},{24,0},{1,25},{9,17},{17,9},{25,1},{2,26},{10... | collective-permute-start | bytes 61448 | tf_op jit(solution)/shard_map/ppermute | solution.py:472
  64.6 2.7 %collective-permute-done.20 = f32[40,128]{1,0:T(8,128)S(1)} collective-permute-done((f32[40,128]{1,0:T(8,128)S(1)}, f32[40,128]{1,0:T(8,128)S(1)}, u32[]{:S(2)}, u32[]{:S(2)}) %collective-permute-start.20) | collective-permute-done | bytes 20512 | tf_op jit(solution)/shard_map/ppermute | solution.py:472
  68.6 6.5 %shard_map.72 = (f32[12,512,128]{2,1,0:T(8,128)}, f32[1,128]{1,0:T(1,128)}) custom-call(s32[2]{0:T(128)S(1)} %pad_add_fusion.par, f32[40,128]{1,0:T(8,128)S(1)} %add_add_fusion.mine_ref, f32[40,128]{1,0:T(8,128)S(1)} %collective-permute-done.21.other_ref, f32[1,128]{1,0:T(1,128)S(1)} %get-tuple-element.50.prior_ref, f32[12,512,128]{2,1,0:T(8,128)S(1)} %bitcast.8), custom_call_target="tpu_custom_call" | custom-call | flops 1000000000 | bytes 3000000 | tf_op jit(solution)/shard_map/pallas_call | solution.py:537
  (32 shorter events, 7.0 us)
Async XLA Ops:
  2.4 8.3 %collective-permute-start = (f32[13,32,128]{2,1,0:T(8,128)S(1)}, f32[13,32,128]{2,1,0:T(8,128)S(1)}, u32[]{:S(2)}, u32[]{:S(2)}) collective-permute-start(f32[13,32,128]{2,1,0:T(8,128)S(1)} %get-tuple-element.31), channel_id=1, source_target_pairs={{0,8},{8,0},{16,24},{24,16},{1,9},{9,1},{17,25},{25,17},{2,10},{10... | collective-permute-start | bytes 638984 | tf_op jit(solution)/shard_map/ppermute | solution.py:468
  5.5 5.3 %collective-permute-start.1 = (f32[13,32,128]{2,1,0:T(8,128)S(1)}, f32[13,32,128]{2,1,0:T(8,128)S(1)}, u32[]{:S(2)}, u32[]{:S(2)}) collective-permute-start(f32[13,32,128]{2,1,0:T(8,128)S(1)} %get-tuple-element.32), channel_id=1, source_target_pairs={{8,16},{16,8},{9,17},{17,9},{10,18},{18,10},{11,19},{19,11},{12,20... | collective-permute-start | bytes 638984 | tf_op jit(solution)/shard_map/ppermute | solution.py:468
  11.8 6.3 %collective-permute-start.2 = (f32[440,128]{1,0:T(8,128)S(1)}, f32[440,128]{1,0:T(8,128)S(1)}, u32[]{:S(2)}, u32[]{:S(2)}) collective-permute-start(f32[440,128]{1,0:T(8,128)S(1)} %get-tuple-element.36), channel_id=1, source_target_pairs={{0,1},{1,0},{2,3},{3,2},{4,5},{5,4},{6,7},{7,6},{8,9},{9,8},{10,11... | collective-permute-start | bytes 675848 | tf_op jit(solution)/shard_map/ppermute | solution.py:468
  11.8 8.0 %collective-permute-start.3 = (f32[440,128]{1,0:T(8,128)S(1)}, f32[440,128]{1,0:T(8,128)S(1)}, u32[]{:S(2)}, u32[]{:S(2)}) collective-permute-start(f32[440,128]{1,0:T(8,128)S(1)} %get-tuple-element.37), channel_id=1, source_target_pairs={{0,7},{1,2},{2,1},{3,4},{4,3},{5,6},{6,5},{7,0},{8,15},{9,10},{10,... | collective-permute-start | bytes 675848 | tf_op jit(solution)/shard_map/ppermute | solution.py:468
  21.9 1.3 %collective-permute-start.4 = (f32[40,128]{1,0:T(8,128)S(1)}, f32[40,128]{1,0:T(8,128)S(1)}, u32[]{:S(2)}, u32[]{:S(2)}) collective-permute-start(f32[40,128]{1,0:T(8,128)S(1)} %get-tuple-element.41), channel_id=1, source_target_pairs={{0,1},{1,0},{2,3},{3,2},{4,5},{5,4},{6,7},{7,6},{8,9},{9,8},{10,11... | collective-permute-start | bytes 61448 | tf_op jit(solution)/shard_map/ppermute | solution.py:472
  23.1 5.3 %collective-permute-start.5 = (f32[40,128]{1,0:T(8,128)S(1)}, f32[40,128]{1,0:T(8,128)S(1)}, u32[]{:S(2)}, u32[]{:S(2)}) collective-permute-start(f32[40,128]{1,0:T(8,128)S(1)} %add.24.first), channel_id=1, source_target_pairs={{0,2},{1,3},{2,0},{3,1},{4,6},{5,7},{6,4},{7,5},{8,10},{9,11},{10,... | collective-permute-start | bytes 61448 | tf_op jit(solution)/shard_map/ppermute | solution.py:472
  25.1 3.8 %collective-permute-start.6 = (f32[40,128]{1,0:T(8,128)S(1)}, f32[40,128]{1,0:T(8,128)S(1)}, u32[]{:S(2)}, u32[]{:S(2)}) collective-permute-start(f32[40,128]{1,0:T(8,128)S(1)} %add.24.first), channel_id=1, source_target_pairs={{0,4},{1,5},{2,6},{3,7},{4,0},{5,1},{6,2},{7,3},{8,12},{9,13},{10,... | collective-permute-start | bytes 61448 | tf_op jit(solution)/shard_map/ppermute | solution.py:472
  25.7 4.7 %collective-permute-start.7 = (f32[40,128]{1,0:T(8,128)S(1)}, f32[40,128]{1,0:T(8,128)S(1)}, u32[]{:S(2)}, u32[]{:S(2)}) collective-permute-start(f32[40,128]{1,0:T(8,128)S(1)} %add.24.first), channel_id=1, source_target_pairs={{0,6},{1,7},{2,4},{3,5},{4,2},{5,3},{6,0},{7,1},{8,14},{9,15},{10,... | collective-permute-start | bytes 61448 | tf_op jit(solution)/shard_map/ppermute | solution.py:472
  30.4 17.6 %collective-permute-start.8 = (f32[432,128]{1,0:T(8,128)S(1)}, f32[432,128]{1,0:T(8,128)S(1)}, u32[]{:S(2)}, u32[]{:S(2)}) collective-permute-start(f32[432,128]{1,0:T(8,128)S(1)} %get-tuple-element.44), channel_id=1, source_target_pairs={{0,1},{1,0},{2,3},{3,2},{4,5},{5,4},{6,7},{7,6},{8,9},{9,8},{10,11... | collective-permute-start | bytes 663560 | tf_op jit(solution)/shard_map/ppermute | solution.py:468
  30.5 17.6 %collective-permute-start.9 = (f32[432,128]{1,0:T(8,128)S(1)}, f32[432,128]{1,0:T(8,128)S(1)}, u32[]{:S(2)}, u32[]{:S(2)}) collective-permute-start(f32[432,128]{1,0:T(8,128)S(1)} %get-tuple-element.45), channel_id=1, source_target_pairs={{0,7},{1,2},{2,1},{3,4},{4,3},{5,6},{6,5},{7,0},{8,15},{9,10},{10,... | collective-permute-start | bytes 663560 | tf_op jit(solution)/shard_map/ppermute | solution.py:468
  31.5 9.2 %collective-permute-start.10 = (f32[40,128]{1,0:T(8,128)S(1)}, f32[40,128]{1,0:T(8,128)S(1)}, u32[]{:S(2)}, u32[]{:S(2)}) collective-permute-start(f32[40,128]{1,0:T(8,128)S(1)} %get-tuple-element.46.first), channel_id=1, source_target_pairs={{0,8},{8,0},{16,24},{24,16},{1,9},{9,1},{17,25},{25,17},{2,10},{10... | collective-permute-start | bytes 61448 | tf_op jit(solution)/shard_map/ppermute | solution.py:472
  36.4 4.8 %collective-permute-start.11 = (f32[40,128]{1,0:T(8,128)S(1)}, f32[40,128]{1,0:T(8,128)S(1)}, u32[]{:S(2)}, u32[]{:S(2)}) collective-permute-start(f32[40,128]{1,0:T(8,128)S(1)} %get-tuple-element.46.first), channel_id=1, source_target_pairs={{0,16},{8,24},{16,0},{24,8},{1,17},{9,25},{17,1},{25,9},{2,18},{10... | collective-permute-start | bytes 61448 | tf_op jit(solution)/shard_map/ppermute | solution.py:472
  37.6 5.6 %collective-permute-start.12 = (f32[40,128]{1,0:T(8,128)S(1)}, f32[40,128]{1,0:T(8,128)S(1)}, u32[]{:S(2)}, u32[]{:S(2)}) collective-permute-start(f32[40,128]{1,0:T(8,128)S(1)} %get-tuple-element.46.first), channel_id=1, source_target_pairs={{0,24},{8,16},{16,8},{24,0},{1,25},{9,17},{17,9},{25,1},{2,26},{10... | collective-permute-start | bytes 61448 | tf_op jit(solution)/shard_map/ppermute | solution.py:472
  43.2 1.2 %collective-permute-start.13 = (f32[40,128]{1,0:T(8,128)S(1)}, f32[40,128]{1,0:T(8,128)S(1)}, u32[]{:S(2)}, u32[]{:S(2)}) collective-permute-start(f32[40,128]{1,0:T(8,128)S(1)} %shard_map.68.mine_ref), channel_id=1, source_target_pairs={{0,1},{1,0},{2,3},{3,2},{4,5},{5,4},{6,7},{7,6},{8,9},{9,8},{10,11... | collective-permute-start | bytes 61448 | tf_op jit(solution)/shard_map/ppermute | solution.py:472
  51.5 1.3 %collective-permute-start.14 = (f32[40,128]{1,0:T(8,128)S(1)}, f32[40,128]{1,0:T(8,128)S(1)}, u32[]{:S(2)}, u32[]{:S(2)}) collective-permute-start(f32[40,128]{1,0:T(8,128)S(1)} %get-tuple-element.49), channel_id=1, source_target_pairs={{0,1},{1,0},{2,3},{3,2},{4,5},{5,4},{6,7},{7,6},{8,9},{9,8},{10,11... | collective-permute-start | bytes 61448 | tf_op jit(solution)/shard_map/ppermute | solution.py:472
  52.8 3.8 %collective-permute-start.15 = (f32[40,128]{1,0:T(8,128)S(1)}, f32[40,128]{1,0:T(8,128)S(1)}, u32[]{:S(2)}, u32[]{:S(2)}) collective-permute-start(f32[40,128]{1,0:T(8,128)S(1)} %add.25), channel_id=1, source_target_pairs={{0,2},{1,3},{2,0},{3,1},{4,6},{5,7},{6,4},{7,5},{8,10},{9,11},{10,... | collective-permute-start | bytes 61448 | tf_op jit(solution)/shard_map/ppermute | solution.py:472
  53.6 3.8 %collective-permute-start.16 = (f32[40,128]{1,0:T(8,128)S(1)}, f32[40,128]{1,0:T(8,128)S(1)}, u32[]{:S(2)}, u32[]{:S(2)}) collective-permute-start(f32[40,128]{1,0:T(8,128)S(1)} %add.25), channel_id=1, source_target_pairs={{0,4},{1,5},{2,6},{3,7},{4,0},{5,1},{6,2},{7,3},{8,12},{9,13},{10,... | collective-permute-start | bytes 61448 | tf_op jit(solution)/shard_map/ppermute | solution.py:472
  55.0 4.7 %collective-permute-start.17 = (f32[40,128]{1,0:T(8,128)S(1)}, f32[40,128]{1,0:T(8,128)S(1)}, u32[]{:S(2)}, u32[]{:S(2)}) collective-permute-start(f32[40,128]{1,0:T(8,128)S(1)} %add.25), channel_id=1, source_target_pairs={{0,6},{1,7},{2,4},{3,5},{4,2},{5,3},{6,0},{7,1},{8,14},{9,15},{10,... | collective-permute-start | bytes 61448 | tf_op jit(solution)/shard_map/ppermute | solution.py:472
  59.7 4.5 %collective-permute-start.18 = (f32[40,128]{1,0:T(8,128)S(1)}, f32[40,128]{1,0:T(8,128)S(1)}, u32[]{:S(2)}, u32[]{:S(2)}) collective-permute-start(f32[40,128]{1,0:T(8,128)S(1)} %add_add_fusion.1), channel_id=1, source_target_pairs={{0,8},{8,0},{16,24},{24,16},{1,9},{9,1},{17,25},{25,17},{2,10},{10... | collective-permute-start | bytes 61448 | tf_op jit(solution)/shard_map/ppermute | solution.py:472
  60.0 4.7 %collective-permute-start.19 = (f32[40,128]{1,0:T(8,128)S(1)}, f32[40,128]{1,0:T(8,128)S(1)}, u32[]{:S(2)}, u32[]{:S(2)}) collective-permute-start(f32[40,128]{1,0:T(8,128)S(1)} %add_add_fusion.1), channel_id=1, source_target_pairs={{0,16},{8,24},{16,0},{24,8},{1,17},{9,25},{17,1},{25,9},{2,18},{10... | collective-permute-start | bytes 61448 | tf_op jit(solution)/shard_map/ppermute | solution.py:472
  61.8 5.6 %collective-permute-start.20 = (f32[40,128]{1,0:T(8,128)S(1)}, f32[40,128]{1,0:T(8,128)S(1)}, u32[]{:S(2)}, u32[]{:S(2)}) collective-permute-start(f32[40,128]{1,0:T(8,128)S(1)} %add_add_fusion.1), channel_id=1, source_target_pairs={{0,24},{8,16},{16,8},{24,0},{1,25},{9,17},{17,9},{25,1},{2,26},{10... | collective-permute-start | bytes 61448 | tf_op jit(solution)/shard_map/ppermute | solution.py:472
  67.4 1.2 %collective-permute-start.21 = (f32[40,128]{1,0:T(8,128)S(1)}, f32[40,128]{1,0:T(8,128)S(1)}, u32[]{:S(2)}, u32[]{:S(2)}) collective-permute-start(f32[40,128]{1,0:T(8,128)S(1)} %add_add_fusion.mine_ref), channel_id=1, source_target_pairs={{0,1},{1,0},{2,3},{3,2},{4,5},{5,4},{6,7},{7,6},{8,9},{9,8},{10,11... | collective-permute-start | bytes 61448 | tf_op jit(solution)/shard_map/ppermute | solution.py:472

commit v8 on v7

--- a/solution.py
+++ b/solution.py
@@ -360,14 +360,18 @@
         for k in range(1, SUB):
             merged = jnp.where(sub == k, scaled[k], merged)
         work[pl.ds(base, SUB), :] = merged
+        turned = jnp.transpose(merged)
         for i in range(block + 1, count):
-            weights = []
             rest = jnp.where(here, 0.0, rows[i])
-            for l in range(SUB):
-                weight = lane_spread(rows[i], base + l)
-                for m in range(l):
-                    weight = weight - weights[m] * low[l][m]
-                weights.append(weight * inv[l])
+            if i == block + 1:
+                weights = []
+                for l in range(SUB):
+                    weight = lane_spread(rows[i], base + l)
+                    for m in range(l):
+                        weight = weight - weights[m] * low[l][m]
+                    weights.append(weight * inv[l])
+            else:
+                weights = [lane_spread(turned[SUB * i : SUB * (i + 1)], l) for l in range(SUB)]
             for l in range(SUB):
                 rest = rest - weights[l] * scaled[l]
             rows[i] = rest
@@ -406,28 +410,28 @@
     )
 
 
-def times_factor(cells, factor):
-    pair = jnp.concatenate(split_halves(cells), axis=1)
+def times_factor(pair, factor):
     both = lax.dot_general(
         pair, factor, (((1,), (1,)), ((), ())), preferred_element_type=jnp.float32
     )
     return both[:, :LANES] + both[:, LANES:]
 
 
-def factor_only(par, mine_ref, other_ref, prior_ref, inverse_ref, logs_ref, gram, work, board):
+def factor_only(par, mine_ref, other_ref, prior_ref, _, inverse_ref, logs_ref, gram, work, board):
     inverse, diagonal = factorize(par, mine_ref, other_ref, gram, work, board)
     inverse_ref[...] = inverse
     logs_ref[...] = prior_ref[...] - jnp.log(diagonal)
 
 
-def join_update(
-    scale, par, start_in, middle_in, state_in, coef_ref, spin_ref, a, b, inverse_ref, start, middle, state, out_ref, kept, sent, factor, total
-):
+def mend_only(par, start_in, middle_in, state_in, coef_ref, spin_ref, a, b, start, middle, state):
+    mend_columns(par, (start, middle, state), coef_ref, spin_ref, (a, b))
+
+
+def update(scale, par, state, inverse_ref, out_ref, kept, sent, factor, total):
     factor[...] = paired(inverse_ref[...])
-    mend_columns(par, (start, middle, state), coef_ref, spin_ref, (a, b))
     gram = 0.0
     for comp, lon, cells in tiles_of(state):
-        new = times_factor(cells, factor[...])
+        new = times_factor(jnp.concatenate(split_halves(cells), axis=1), factor[...])
         out_ref[comp, pl.ds(lon, SUB)] = new.reshape((SUB,) + out_ref.shape[2:])
         gram += gram_of(*split_halves(new))
     write_halves(par, gram, scale, kept, sent, total)
@@ -436,9 +440,18 @@
 def restore_order(turned, out_ref):
     comps, cols, _, _ = turned.shape
     for comp in range(comps):
-        for lon in range(0, cols, SUB):
-            cells = turned[comp, pl.ds(lon, SUB)]
-            out_ref[comp, :, pl.ds(lon, SUB), :] = jnp.transpose(cells, (1, 0, 2))
+        for lon in range(0, cols, 2 * SUB):
+            cells = jnp.concatenate(
+                [
+                    jnp.transpose(turned[comp, pl.ds(lon + shift, SUB)], (1, 0, 2))
+                    for shift in (0, SUB)
+                ],
+                axis=1,
+            )
+            high = cells.astype(jnp.bfloat16)
+            low = (cells - high.astype(jnp.float32)).astype(jnp.bfloat16)
+            out_ref[comp, :, pl.ds(lon, 2 * SUB), pl.ds(0, LANES)] = high
+            out_ref[comp, :, pl.ds(lon, 2 * SUB), pl.ds(LANES, LANES)] = low
 
 
 def finish(
@@ -474,7 +487,7 @@
 
 def add_four(first, second, third, fourth, *rest):
     out_ref = rest[len(rest) // 2]
-    out_ref[...] = (first[...] + second[...]) + (third[...] + fourth[...])
+    out_ref[...] = (first[...] + fourth[...]) + (third[...] + second[...])
 
 
 def sum_over(value, axis, first_bit, beside=None, held=()):
@@ -483,9 +496,9 @@
         low = 1 << first_bit
         if first_bit + 1 < bits:
             high = low << 1
-            one, two, three = (swapped(value, axis, mask) for mask in (low, high, low | high))
+            three, two, one = (swapped(value, axis, mask) for mask in (low | high, high, low))
             if beside is None:
-                value = (value + one) + (two + three)
+                value = (three + two) + (one + value)
             else:
                 anywhere = pl.BlockSpec(memory_space=pl.ANY)
                 value, *held = pl.pallas_call(
@@ -495,7 +508,7 @@
                     out_specs=[VMEM] + [anywhere] * len(held),
                     input_output_aliases={5 + i: 1 + i for i in range(len(held))},
                     compiler_params=params(),
-                )(value, one, two, three, beside, *held)
+                )(value, three, two, one, beside, *held)
                 beside = None
             first_bit += 2
         else:
@@ -619,6 +632,18 @@
     state = inside(1, middle)
     mine, other, packed = sum_devices(kept, sent, (middle, state), packed)
     halos = swap_columns(packed)
+    _, _, state = call(
+        mend_only,
+        (block,) * 3,
+        par,
+        start,
+        middle,
+        state,
+        coef,
+        spin,
+        *halos,
+        aliases={1: 0, 2: 1, 3: 2},
+    )
     inverse, logs = call(
         factor_only,
         (shape_of(modes, modes), shape_of(1, modes)),
@@ -626,26 +651,26 @@
         mine,
         other,
         logs,
+        state,
+        specs=[SMEM] + [VMEM] * 3 + [pl.BlockSpec(memory_space=pl.ANY)],
         scratch=[square, square, board],
         cost=0.01,
     )
-    _, _, _, state, kept, sent = call(
-        functools.partial(join_update, scale),
-        (block, block, block, shape_of(comps, cols, rows, modes)) + halves,
+    state, kept, sent = call(
+        functools.partial(update, scale),
+        (shape_of(comps, cols, rows, modes),) + halves,
         par,
-        start,
-        middle,
         state,
-        coef,
-        spin,
-        *halos,
         inverse,
         scratch=[factor, square],
-        aliases={1: 0, 2: 1, 3: 2},
-        cost=3.0,
+        cost=2.0,
     )
     state = call(
-        restore_order, (shape_of(comps, rows, cols, modes),), state, specs=[VMEM], cost=2.0
+        restore_order,
+        (jax.ShapeDtypeStruct((comps, rows, cols, 2 * modes), jnp.bfloat16),),
+        state,
+        specs=[VMEM],
+        cost=1.0,
     )[0]
     height = comps * rows * cols // TILES
     tiled = shape_of(TILES, height, modes)
@@ -657,7 +682,7 @@
         mine,
         other,
         logs,
-        state.reshape(TILES, height, modes),
+        state.reshape(TILES, height, 2 * modes),
         out_specs=(HBM, VMEM),
         scratch=[
             square,

time: 75.6 us -> 75.1 us (level)
  waiting for transfers between devices: 17.5 us -> 13.6 us
  Pallas kernels: 29.6 us -> 33.1 us
    ppermute x16, waiting for transfers between devices: 14.9 us -> 11 us  [swapped(): lax.ppermute(value, axis, [(i, i ^ mask) for i in range(lax.axis_size(axi...]
    pallas_call x12 -> x13, Pallas kernels: 29.6 us -> 33.1 us  [call(): pl.pallas_call(kernel, out_shape=outs, in_specs=specs or [SMEM] + [VMEM]...]
  transfers between devices with their start and end apart: 22 -> 22, of which waited for: 15 -> 13; matrix products, arithmetic and copies ran while one was open for 0% -> 0% of each run, Pallas kernels for 20% -> 17%
where the time goes in v8:
time: 75.1 us; the launch traced here: 74.7 us
  Pallas kernels  33.1 us (44%)
  starting transfers between devices  26.9 us (36%)
  waiting for transfers between devices  13.6 us (18%)
  between operations  0.96 us (1%)
    pallas_call x13, Pallas kernels, call(): pl.pallas_call(kernel, out_shape=outs, in_specs=specs or [SMEM] + [VMEM]...  33.1 us
    ppermute x16, starting transfers between devices, swapped(): lax.ppermute(value, axis, [(i, i ^ mask) for i in range(lax.axis_size(axi...  18.8 us
    ppermute x16, waiting for transfers between devices, swapped(): lax.ppermute(value, axis, [(i, i ^ mask) for i in range(lax.axis_size(axi...  11 us
    ppermute x3, starting transfers between devices, swap_pairs(): lax.ppermute(far_value, axis, far)  4.93 us
    ppermute x3, starting transfers between devices, swap_pairs(): lax.ppermute(near_value, axis, near)  3.22 us
    ppermute x3, waiting for transfers between devices, swap_pairs(): lax.ppermute(far_value, axis, far)  1.86 us
  transfers between devices with their start and end apart: 22, of which 13 were waited for; matrix products, arithmetic and copies ran while one was open for 0% of the time, Pallas kernels for 17%

profile of v8, /device:TPU:0, one launch (start us, length us, event | category | flops | bytes accessed | tf_op | source)
XLA Modules:
  0.0 74.7 jit_solution(12765726315543118105)
XLA Ops:
  0.7 1.7 %shard_map.60 = (f32[13,32,128]{2,1,0:T(8,128)S(1)}, f32[13,32,128]{2,1,0:T(8,128)S(1)}) custom-call(s32[2]{0:T(128)S(1)} %pad_add_fusion.par, f32[3,64,32,128]{3,2,1,0:T(8,128)} %t_ref.3, s32[32,64]{1,0:T(8,128)} %bitcast.9, s32[32,64]{1,0:T(8,128)} %bitcast.11, f32[32,64]{1,0:T(8,128)} %bitcast.13), custom_call_target="tpu_custom_call" | custom-call | flops 1000000000 | bytes 3000000 | tf_op jit(solution)/shard_map/pallas_call | solution.py:550
  2.4 3.1 %collective-permute-start = (f32[13,32,128]{2,1,0:T(8,128)S(1)}, f32[13,32,128]{2,1,0:T(8,128)S(1)}, u32[]{:S(2)}, u32[]{:S(2)}) collective-permute-start(f32[13,32,128]{2,1,0:T(8,128)S(1)} %get-tuple-element.32), channel_id=1, source_target_pairs={{0,8},{8,0},{16,24},{24,16},{1,9},{9,1},{17,25},{25,17},{2,10},{10... | collective-permute-start | bytes 638984 | tf_op jit(solution)/shard_map/ppermute | solution.py:481
  6.1 3.8 %shard_map.59 = (f32[3,36,72,128]{3,2,1,0:T(8,128)S(1)}, f32[3,36,72,128]{3,2,1,0:T(8,128)S(1)}, f32[3,32,128]{2,1,0:T(8,128)S(1)}, f32[72,128]{1,0:T(8,128)S(1)}) custom-call(s32[2]{0:T(128)S(1)} %pad_add_fusion.par, f32[3,64,32,128]{3,2,1,0:T(8,128)} %t_ref.3, s32[32,64]{1,0:T(8,128)} %bitcast.10, s32[32,64]{1,0:T(8,128)} %bitcast.12, f32[32,64]{1,0:T(8,128)} %bitcast.14), custom_call_target="tpu_custom_call" | custom-call | flops 3000000000 | bytes 9000000 | tf_op jit(solution)/shard_map/pallas_call | solution.py:550
  10.7 1.0 %shard_map.61 = (f32[3,36,72,128]{3,2,1,0:T(8,128)S(1)}, f32[3,36,72,128]{3,2,1,0:T(8,128)S(1)}, f32[440,128]{1,0:T(8,128)S(1)}, f32[440,128]{1,0:T(8,128)S(1)}) custom-call(s32[2]{0:T(128)S(1)} %pad_add_fusion.par, f32[3,36,72,128]{3,2,1,0:T(8,128)S(1)} %get-tuple-element.29.state_in, ...), custom_call_target="tpu_custom_call", output_to_operand_aliasing={{0}: (1, {}), {1}: (2, {})} | custom-call | flops 1000000000 | bytes 3000000 | tf_op jit(solution)/shard_map/pallas_call | solution.py:550
  11.8 2.7 %collective-permute-start.3 = (f32[440,128]{1,0:T(8,128)S(1)}, f32[440,128]{1,0:T(8,128)S(1)}, u32[]{:S(2)}, u32[]{:S(2)}) collective-permute-start(f32[440,128]{1,0:T(8,128)S(1)} %get-tuple-element.38), channel_id=1, source_target_pairs={{0,7},{1,2},{2,1},{3,4},{4,3},{5,6},{6,5},{7,0},{8,15},{9,10},{10,... | collective-permute-start | bytes 675848 | tf_op jit(solution)/shard_map/ppermute | solution.py:481
  14.5 1.8 %shard_map.62.source.middle_in = f32[3,36,72,128]{3,2,1,0:T(8,128)S(1)} custom-call(f32[3,36,72,128]{3,2,1,0:T(8,128)S(1)} %get-tuple-element.34.source.start_in, f32[3,36,72,128]{3,2,1,0:T(8,128)S(1)} %get-tuple-element.35.coef_ref.coef_in, f32[72,128]{1,0:T(8,128)S(1)} %get-tuple-element.36.spin_ref), custom_call_target="tpu_custom_call" | custom-call | flops 2000000000 | bytes 6000000 | tf_op jit(solution)/shard_map/pallas_call | solution.py:550
  16.3 1.6 %shard_map.63.state_in = f32[3,36,72,128]{3,2,1,0:T(8,128)S(1)} custom-call(f32[3,36,72,128]{3,2,1,0:T(8,128)S(1)} %shard_map.62.source.middle_in, f32[3,36,72,128]{3,2,1,0:T(8,128)S(1)} %get-tuple-element.35.coef_ref.coef_in, f32[72,128]{1,0:T(8,128)S(1)} %get-tuple-element.36.spin_ref), custom_call_target="tpu_custom_call" | custom-call | flops 2000000000 | bytes 6000000 | tf_op jit(solution)/shard_map/pallas_call | solution.py:550
  18.0 1.9 %collective-permute-done.3.b = f32[440,128]{1,0:T(8,128)S(1)} collective-permute-done((f32[440,128]{1,0:T(8,128)S(1)}, f32[440,128]{1,0:T(8,128)S(1)}, u32[]{:S(2)}, u32[]{:S(2)}) %collective-permute-start.3) | collective-permute-done | bytes 225312 | tf_op jit(solution)/shard_map/ppermute | solution.py:481
  19.8 2.1 %shard_map.64 = (f32[3,36,72,128]{3,2,1,0:T(8,128)S(1)}, f32[3,36,72,128]{3,2,1,0:T(8,128)S(1)}, f32[3,36,72,128]{3,2,1,0:T(8,128)S(1)}, f32[3,36,72,128]{3,2,1,...) custom-call(s32[2]{0:T(128)S(1)} %pad_add_fusion.par, ...), custom_call_target="tpu_custom_call", output_to_operand_aliasing={{0}: (1, {}), {1}: (2, {}), {2}: (3, {}), {3}: (4, {})} | custom-call | flops 2000000000 | bytes 6000000 | tf_op jit(solution)/shard_map/pallas_call | solution.py:550
  22.1 1.1 %collective-permute-done.4 = f32[40,128]{1,0:T(8,128)S(1)} collective-permute-done((f32[40,128]{1,0:T(8,128)S(1)}, f32[40,128]{1,0:T(8,128)S(1)}, u32[]{:S(2)}, u32[]{:S(2)}) %collective-permute-start.4) | collective-permute-done | bytes 20512 | tf_op jit(solution)/shard_map/ppermute | solution.py:485
  23.2 2.0 %collective-permute-start.5 = (f32[40,128]{1,0:T(8,128)S(1)}, f32[40,128]{1,0:T(8,128)S(1)}, u32[]{:S(2)}, u32[]{:S(2)}) collective-permute-start(f32[40,128]{1,0:T(8,128)S(1)} %add.24.first), channel_id=1, source_target_pairs={{0,6},{1,7},{2,4},{3,5},{4,2},{5,3},{6,0},{7,1},{8,14},{9,15},{10,... | collective-permute-start | bytes 61448 | tf_op jit(solution)/shard_map/ppermute | solution.py:485
  25.2 1.4 %collective-permute-start.6 = (f32[40,128]{1,0:T(8,128)S(1)}, f32[40,128]{1,0:T(8,128)S(1)}, u32[]{:S(2)}, u32[]{:S(2)}) collective-permute-start(f32[40,128]{1,0:T(8,128)S(1)} %add.24.first), channel_id=1, source_target_pairs={{0,4},{1,5},{2,6},{3,7},{4,0},{5,1},{6,2},{7,3},{8,12},{9,13},{10,... | collective-permute-start | bytes 61448 | tf_op jit(solution)/shard_map/ppermute | solution.py:485
  26.7 1.8 %shard_map.65.source.rest_0_.middle_in = f32[3,36,72,128]{3,2,1,0:T(8,128)S(1)} custom-call(f32[3,36,72,128]{3,2,1,0:T(8,128)S(1)} %get-tuple-element.39.source.start_in, f32[3,36,72,128]{3,2,1,0:T(8,128)S(1)} %get-tuple-element.40.coef_ref, f32[72,128]{1,0:T(8,128)S(1)} %get-tuple-element.36.spin_ref), custom_call_target="tpu_custom_call" | custom-call | flops 2000000000 | bytes 6000000 | tf_op jit(solution)/shard_map/pallas_call | solution.py:550
  29.0 1.4 %collective-permute-done.7.fourth = f32[40,128]{1,0:T(8,128)S(1)} collective-permute-done((f32[40,128]{1,0:T(8,128)S(1)}, f32[40,128]{1,0:T(8,128)S(1)}, u32[]{:S(2)}, u32[]{:S(2)}) %collective-permute-start.7) | collective-permute-done | bytes 20512 | tf_op jit(solution)/shard_map/ppermute | solution.py:485
  30.5 1.6 %collective-permute-start.9 = (f32[432,128]{1,0:T(8,128)S(1)}, f32[432,128]{1,0:T(8,128)S(1)}, u32[]{:S(2)}, u32[]{:S(2)}) collective-permute-start(f32[432,128]{1,0:T(8,128)S(1)} %get-tuple-element.46), channel_id=1, source_target_pairs={{0,7},{1,2},{2,1},{3,4},{4,3},{5,6},{6,5},{7,0},{8,15},{9,10},{10,... | collective-permute-start | bytes 663560 | tf_op jit(solution)/shard_map/ppermute | solution.py:481
  32.1 3.8 %collective-permute-start.10 = (f32[40,128]{1,0:T(8,128)S(1)}, f32[40,128]{1,0:T(8,128)S(1)}, u32[]{:S(2)}, u32[]{:S(2)}) collective-permute-start(f32[40,128]{1,0:T(8,128)S(1)} %get-tuple-element.48.first), channel_id=1, source_target_pairs={{0,24},{8,16},{16,8},{24,0},{1,25},{9,17},{17,9},{25,1},{2,26},{10... | collective-permute-start | bytes 61448 | tf_op jit(solution)/shard_map/ppermute | solution.py:485
  35.8 2.5 %collective-permute-start.11 = (f32[40,128]{1,0:T(8,128)S(1)}, f32[40,128]{1,0:T(8,128)S(1)}, u32[]{:S(2)}, u32[]{:S(2)}) collective-permute-start(f32[40,128]{1,0:T(8,128)S(1)} %get-tuple-element.48.first), channel_id=1, source_target_pairs={{0,16},{8,24},{16,0},{24,8},{1,17},{9,25},{17,1},{25,9},{2,18},{10... | collective-permute-start | bytes 61448 | tf_op jit(solution)/shard_map/ppermute | solution.py:485
  38.6 1.6 %shard_map.66.state_in.rest_0_ = f32[3,36,72,128]{3,2,1,0:T(8,128)S(1)} custom-call(f32[3,36,72,128]{3,2,1,0:T(8,128)S(1)} %shard_map.65.source.rest_0_.middle_in, f32[3,36,72,128]{3,2,1,0:T(8,128)S(1)} %get-tuple-element.40.coef_ref, f32[72,128]{1,0:T(8,128)S(1)} %get-tuple-element.36.spin_ref), custom_call_target="tpu_custom_call" | custom-call | flops 2000000000 | bytes 6000000 | tf_op jit(solution)/shard_map/pallas_call | solution.py:550
  40.5 1.6 %collective-permute-done.12.fourth = f32[40,128]{1,0:T(8,128)S(1)} collective-permute-done((f32[40,128]{1,0:T(8,128)S(1)}, f32[40,128]{1,0:T(8,128)S(1)}, u32[]{:S(2)}, u32[]{:S(2)}) %collective-permute-start.12) | collective-permute-done | bytes 20512 | tf_op jit(solution)/shard_map/ppermute | solution.py:485
  42.2 1.3 %shard_map.68 = (f32[3,36,72,128]{3,2,1,0:T(8,128)S(1)}, f32[3,36,72,128]{3,2,1,0:T(8,128)S(1)}, f32[3,36,72,128]{3,2,1,0:T(8,128)S(1)}) custom-call(s32[2]{0:T(128)S(1)} %pad_add_fusion.par, f32[3,36,72,128]{3,2,1,0:T(8,128)S(1)} %get-tuple-element.39.source.start_in, ...), custom_call_target="tpu_custom_call", output_to_operand_aliasing={{0}: (1, {}), {1}: (2, {}), {2}: (3, {})} | custom-call | flops 1000000000 | bytes 3000000 | tf_op jit(solution)/shard_map/pallas_call | solution.py:550
  43.5 5.3 %shard_map.70 = (f32[128,128]{1,0:T(8,128)S(1)}, f32[1,128]{1,0:T(1,128)S(1)}) custom-call(s32[2]{0:T(128)S(1)} %pad_add_fusion.par, f32[40,128]{1,0:T(8,128)S(1)} %shard_map.69.mine_ref, f32[40,128]{1,0:T(8,128)S(1)} %collective-permute-done.13.other_ref, f32[1,128]{1,0:T(1,128)S(1)} %broadcast_in_dim.3.prior_ref, ...), custom_call_target="tpu_custom_call" | custom-call | flops 10000000 | bytes 30000 | tf_op jit(solution)/shard_map/pallas_call | solution.py:550
  48.8 2.7 %shard_map.71 = (f32[3,32,64,128]{3,2,1,0:T(8,128)S(1)}, f32[40,128]{1,0:T(8,128)S(1)}, f32[40,128]{1,0:T(8,128)S(1)}) custom-call(s32[2]{0:T(128)S(1)} %pad_add_fusion.par, f32[3,36,72,128]{3,2,1,0:T(8,128)S(1)} %get-tuple-element.47._.state, f32[128,128]{1,0:T(8,128)S(1)} %get-tuple-element.49.inverse_ref), custom_call_target="tpu_custom_call" | custom-call | flops 2000000000 | bytes 6000000 | tf_op jit(solution)/shard_map/pallas_call | solution.py:550
  53.3 1.4 %collective-permute-start.16 = (f32[40,128]{1,0:T(8,128)S(1)}, f32[40,128]{1,0:T(8,128)S(1)}, u32[]{:S(2)}, u32[]{:S(2)}) collective-permute-start(f32[40,128]{1,0:T(8,128)S(1)} %add.25), channel_id=1, source_target_pairs={{0,4},{1,5},{2,6},{3,7},{4,0},{5,1},{6,2},{7,3},{8,12},{9,13},{10,... | collective-permute-start | bytes 61448 | tf_op jit(solution)/shard_map/ppermute | solution.py:485
  54.8 1.6 %collective-permute-start.17 = (f32[40,128]{1,0:T(8,128)S(1)}, f32[40,128]{1,0:T(8,128)S(1)}, u32[]{:S(2)}, u32[]{:S(2)}) collective-permute-start(f32[40,128]{1,0:T(8,128)S(1)} %add.25), channel_id=1, source_target_pairs={{0,2},{1,3},{2,0},{3,1},{4,6},{5,7},{6,4},{7,5},{8,10},{9,11},{10,... | collective-permute-start | bytes 61448 | tf_op jit(solution)/shard_map/ppermute | solution.py:485
  56.4 1.3 %collective-permute-done.15 = f32[40,128]{1,0:T(8,128)S(1)} collective-permute-done((f32[40,128]{1,0:T(8,128)S(1)}, f32[40,128]{1,0:T(8,128)S(1)}, u32[]{:S(2)}, u32[]{:S(2)}) %collective-permute-start.15) | collective-permute-done | bytes 20512 | tf_op jit(solution)/shard_map/ppermute | solution.py:485
  57.6 0.9 %collective-permute-done.17 = f32[40,128]{1,0:T(8,128)S(1)} collective-permute-done((f32[40,128]{1,0:T(8,128)S(1)}, f32[40,128]{1,0:T(8,128)S(1)}, u32[]{:S(2)}, u32[]{:S(2)}) %collective-permute-start.17) | collective-permute-done | bytes 20512 | tf_op jit(solution)/shard_map/ppermute | solution.py:485
  58.5 2.7 %collective-permute-start.18 = (f32[40,128]{1,0:T(8,128)S(1)}, f32[40,128]{1,0:T(8,128)S(1)}, u32[]{:S(2)}, u32[]{:S(2)}) collective-permute-start(f32[40,128]{1,0:T(8,128)S(1)} %add_add_fusion.1), channel_id=1, source_target_pairs={{0,24},{8,16},{16,8},{24,0},{1,25},{9,17},{17,9},{25,1},{2,26},{10... | collective-permute-start | bytes 61448 | tf_op jit(solution)/shard_map/ppermute | solution.py:485
  61.3 1.7 %collective-permute-start.20 = (f32[40,128]{1,0:T(8,128)S(1)}, f32[40,128]{1,0:T(8,128)S(1)}, u32[]{:S(2)}, u32[]{:S(2)}) collective-permute-start(f32[40,128]{1,0:T(8,128)S(1)} %add_add_fusion.1), channel_id=1, source_target_pairs={{0,8},{8,0},{16,24},{24,16},{1,9},{9,1},{17,25},{25,17},{2,10},{10... | collective-permute-start | bytes 61448 | tf_op jit(solution)/shard_map/ppermute | solution.py:485
  63.0 1.2 %collective-permute-done.18 = f32[40,128]{1,0:T(8,128)S(1)} collective-permute-done((f32[40,128]{1,0:T(8,128)S(1)}, f32[40,128]{1,0:T(8,128)S(1)}, u32[]{:S(2)}, u32[]{:S(2)}) %collective-permute-start.18) | collective-permute-done | bytes 20512 | tf_op jit(solution)/shard_map/ppermute | solution.py:485
  64.2 1.8 %collective-permute-done.19 = f32[40,128]{1,0:T(8,128)S(1)} collective-permute-done((f32[40,128]{1,0:T(8,128)S(1)}, f32[40,128]{1,0:T(8,128)S(1)}, u32[]{:S(2)}, u32[]{:S(2)}) %collective-permute-start.19) | collective-permute-done | bytes 20512 | tf_op jit(solution)/shard_map/ppermute | solution.py:485
  66.0 1.1 %shard_map.72 = bf16[3,64,32,256]{3,2,1,0:T(8,128)(2,1)S(1)} custom-call(f32[3,32,64,128]{3,2,1,0:T(8,128)S(1)} %get-tuple-element.53.turned), custom_call_target="tpu_custom_call" | custom-call | flops 1000000000 | bytes 3000000 | tf_op jit(solution)/shard_map/pallas_call | solution.py:550
  67.2 7.3 %shard_map.73 = (f32[12,512,128]{2,1,0:T(8,128)}, f32[1,128]{1,0:T(1,128)}) custom-call(s32[2]{0:T(128)S(1)} %pad_add_fusion.par, f32[40,128]{1,0:T(8,128)S(1)} %add_add_fusion.mine_ref, f32[40,128]{1,0:T(8,128)S(1)} %collective-permute-done.21.other_ref, f32[1,128]{1,0:T(1,128)S(1)} %get-tuple-element.52.prior_ref, bf16[12,512,256]{2,1,0:T(8,128)(2,1)S(1)} %bitcast.8), custom_call_target="tpu_custom_call" | custom-call | flops 1000000000 | bytes 3000000 | tf_op jit(solution)/shard_map/pallas_call | solution.py:550
  (33 shorter events, 5.3 us)
Async XLA Ops:
  2.4 8.3 %collective-permute-start = (f32[13,32,128]{2,1,0:T(8,128)S(1)}, f32[13,32,128]{2,1,0:T(8,128)S(1)}, u32[]{:S(2)}, u32[]{:S(2)}) collective-permute-start(f32[13,32,128]{2,1,0:T(8,128)S(1)} %get-tuple-element.32), channel_id=1, source_target_pairs={{0,8},{8,0},{16,24},{24,16},{1,9},{9,1},{17,25},{25,17},{2,10},{10... | collective-permute-start | bytes 638984 | tf_op jit(solution)/shard_map/ppermute | solution.py:481
  5.5 5.3 %collective-permute-start.1 = (f32[13,32,128]{2,1,0:T(8,128)S(1)}, f32[13,32,128]{2,1,0:T(8,128)S(1)}, u32[]{:S(2)}, u32[]{:S(2)}) collective-permute-start(f32[13,32,128]{2,1,0:T(8,128)S(1)} %get-tuple-element.33), channel_id=1, source_target_pairs={{8,16},{16,8},{9,17},{17,9},{10,18},{18,10},{11,19},{19,11},{12,20... | collective-permute-start | bytes 638984 | tf_op jit(solution)/shard_map/ppermute | solution.py:481
  11.8 6.2 %collective-permute-start.2 = (f32[440,128]{1,0:T(8,128)S(1)}, f32[440,128]{1,0:T(8,128)S(1)}, u32[]{:S(2)}, u32[]{:S(2)}) collective-permute-start(f32[440,128]{1,0:T(8,128)S(1)} %get-tuple-element.37), channel_id=1, source_target_pairs={{0,1},{1,0},{2,3},{3,2},{4,5},{5,4},{6,7},{7,6},{8,9},{9,8},{10,11... | collective-permute-start | bytes 675848 | tf_op jit(solution)/shard_map/ppermute | solution.py:481
  11.8 8.0 %collective-permute-start.3 = (f32[440,128]{1,0:T(8,128)S(1)}, f32[440,128]{1,0:T(8,128)S(1)}, u32[]{:S(2)}, u32[]{:S(2)}) collective-permute-start(f32[440,128]{1,0:T(8,128)S(1)} %get-tuple-element.38), channel_id=1, source_target_pairs={{0,7},{1,2},{2,1},{3,4},{4,3},{5,6},{6,5},{7,0},{8,15},{9,10},{10,... | collective-permute-start | bytes 675848 | tf_op jit(solution)/shard_map/ppermute | solution.py:481
  21.9 1.3 %collective-permute-start.4 = (f32[40,128]{1,0:T(8,128)S(1)}, f32[40,128]{1,0:T(8,128)S(1)}, u32[]{:S(2)}, u32[]{:S(2)}) collective-permute-start(f32[40,128]{1,0:T(8,128)S(1)} %get-tuple-element.42), channel_id=1, source_target_pairs={{0,1},{1,0},{2,3},{3,2},{4,5},{5,4},{6,7},{7,6},{8,9},{9,8},{10,11... | collective-permute-start | bytes 61448 | tf_op jit(solution)/shard_map/ppermute | solution.py:485
  23.2 5.2 %collective-permute-start.5 = (f32[40,128]{1,0:T(8,128)S(1)}, f32[40,128]{1,0:T(8,128)S(1)}, u32[]{:S(2)}, u32[]{:S(2)}) collective-permute-start(f32[40,128]{1,0:T(8,128)S(1)} %add.24.first), channel_id=1, source_target_pairs={{0,6},{1,7},{2,4},{3,5},{4,2},{5,3},{6,0},{7,1},{8,14},{9,15},{10,... | collective-permute-start | bytes 61448 | tf_op jit(solution)/shard_map/ppermute | solution.py:485
  25.2 3.8 %collective-permute-start.6 = (f32[40,128]{1,0:T(8,128)S(1)}, f32[40,128]{1,0:T(8,128)S(1)}, u32[]{:S(2)}, u32[]{:S(2)}) collective-permute-start(f32[40,128]{1,0:T(8,128)S(1)} %add.24.first), channel_id=1, source_target_pairs={{0,4},{1,5},{2,6},{3,7},{4,0},{5,1},{6,2},{7,3},{8,12},{9,13},{10,... | collective-permute-start | bytes 61448 | tf_op jit(solution)/shard_map/ppermute | solution.py:485
  26.6 3.8 %collective-permute-start.7 = (f32[40,128]{1,0:T(8,128)S(1)}, f32[40,128]{1,0:T(8,128)S(1)}, u32[]{:S(2)}, u32[]{:S(2)}) collective-permute-start(f32[40,128]{1,0:T(8,128)S(1)} %add.24.first), channel_id=1, source_target_pairs={{0,2},{1,3},{2,0},{3,1},{4,6},{5,7},{6,4},{7,5},{8,10},{9,11},{10,... | collective-permute-start | bytes 61448 | tf_op jit(solution)/shard_map/ppermute | solution.py:485
  30.4 11.7 %collective-permute-start.8 = (f32[432,128]{1,0:T(8,128)S(1)}, f32[432,128]{1,0:T(8,128)S(1)}, u32[]{:S(2)}, u32[]{:S(2)}) collective-permute-start(f32[432,128]{1,0:T(8,128)S(1)} %get-tuple-element.45), channel_id=1, source_target_pairs={{0,1},{1,0},{2,3},{3,2},{4,5},{5,4},{6,7},{7,6},{8,9},{9,8},{10,11... | collective-permute-start | bytes 663560 | tf_op jit(solution)/shard_map/ppermute | solution.py:481
  30.5 11.7 %collective-permute-start.9 = (f32[432,128]{1,0:T(8,128)S(1)}, f32[432,128]{1,0:T(8,128)S(1)}, u32[]{:S(2)}, u32[]{:S(2)}) collective-permute-start(f32[432,128]{1,0:T(8,128)S(1)} %get-tuple-element.46), channel_id=1, source_target_pairs={{0,7},{1,2},{2,1},{3,4},{4,3},{5,6},{6,5},{7,0},{8,15},{9,10},{10,... | collective-permute-start | bytes 663560 | tf_op jit(solution)/shard_map/ppermute | solution.py:481
  32.1 8.1 %collective-permute-start.10 = (f32[40,128]{1,0:T(8,128)S(1)}, f32[40,128]{1,0:T(8,128)S(1)}, u32[]{:S(2)}, u32[]{:S(2)}) collective-permute-start(f32[40,128]{1,0:T(8,128)S(1)} %get-tuple-element.48.first), channel_id=1, source_target_pairs={{0,24},{8,16},{16,8},{24,0},{1,25},{9,17},{17,9},{25,1},{2,26},{10... | collective-permute-start | bytes 61448 | tf_op jit(solution)/shard_map/ppermute | solution.py:485
  35.8 4.7 %collective-permute-start.11 = (f32[40,128]{1,0:T(8,128)S(1)}, f32[40,128]{1,0:T(8,128)S(1)}, u32[]{:S(2)}, u32[]{:S(2)}) collective-permute-start(f32[40,128]{1,0:T(8,128)S(1)} %get-tuple-element.48.first), channel_id=1, source_target_pairs={{0,16},{8,24},{16,0},{24,8},{1,17},{9,25},{17,1},{25,9},{2,18},{10... | collective-permute-start | bytes 61448 | tf_op jit(solution)/shard_map/ppermute | solution.py:485
  38.3 3.8 %collective-permute-start.12 = (f32[40,128]{1,0:T(8,128)S(1)}, f32[40,128]{1,0:T(8,128)S(1)}, u32[]{:S(2)}, u32[]{:S(2)}) collective-permute-start(f32[40,128]{1,0:T(8,128)S(1)} %get-tuple-element.48.first), channel_id=1, source_target_pairs={{0,8},{8,0},{16,24},{24,16},{1,9},{9,1},{17,25},{25,17},{2,10},{10... | collective-permute-start | bytes 61448 | tf_op jit(solution)/shard_map/ppermute | solution.py:485
  42.1 1.4 %collective-permute-start.13 = (f32[40,128]{1,0:T(8,128)S(1)}, f32[40,128]{1,0:T(8,128)S(1)}, u32[]{:S(2)}, u32[]{:S(2)}) collective-permute-start(f32[40,128]{1,0:T(8,128)S(1)} %shard_map.69.mine_ref), channel_id=1, source_target_pairs={{0,1},{1,0},{2,3},{3,2},{4,5},{5,4},{6,7},{7,6},{8,9},{9,8},{10,11... | collective-permute-start | bytes 61448 | tf_op jit(solution)/shard_map/ppermute | solution.py:485
  51.5 1.4 %collective-permute-start.14 = (f32[40,128]{1,0:T(8,128)S(1)}, f32[40,128]{1,0:T(8,128)S(1)}, u32[]{:S(2)}, u32[]{:S(2)}) collective-permute-start(f32[40,128]{1,0:T(8,128)S(1)} %get-tuple-element.51), channel_id=1, source_target_pairs={{0,1},{1,0},{2,3},{3,2},{4,5},{5,4},{6,7},{7,6},{8,9},{9,8},{10,11... | collective-permute-start | bytes 61448 | tf_op jit(solution)/shard_map/ppermute | solution.py:485
  52.9 4.7 %collective-permute-start.15 = (f32[40,128]{1,0:T(8,128)S(1)}, f32[40,128]{1,0:T(8,128)S(1)}, u32[]{:S(2)}, u32[]{:S(2)}) collective-permute-start(f32[40,128]{1,0:T(8,128)S(1)} %add.25), channel_id=1, source_target_pairs={{0,6},{1,7},{2,4},{3,5},{4,2},{5,3},{6,0},{7,1},{8,14},{9,15},{10,... | collective-permute-start | bytes 61448 | tf_op jit(solution)/shard_map/ppermute | solution.py:485
  53.3 4.3 %collective-permute-start.16 = (f32[40,128]{1,0:T(8,128)S(1)}, f32[40,128]{1,0:T(8,128)S(1)}, u32[]{:S(2)}, u32[]{:S(2)}) collective-permute-start(f32[40,128]{1,0:T(8,128)S(1)} %add.25), channel_id=1, source_target_pairs={{0,4},{1,5},{2,6},{3,7},{4,0},{5,1},{6,2},{7,3},{8,12},{9,13},{10,... | collective-permute-start | bytes 61448 | tf_op jit(solution)/shard_map/ppermute | solution.py:485
  54.8 3.8 %collective-permute-start.17 = (f32[40,128]{1,0:T(8,128)S(1)}, f32[40,128]{1,0:T(8,128)S(1)}, u32[]{:S(2)}, u32[]{:S(2)}) collective-permute-start(f32[40,128]{1,0:T(8,128)S(1)} %add.25), channel_id=1, source_target_pairs={{0,2},{1,3},{2,0},{3,1},{4,6},{5,7},{6,4},{7,5},{8,10},{9,11},{10,... | collective-permute-start | bytes 61448 | tf_op jit(solution)/shard_map/ppermute | solution.py:485
  58.5 5.6 %collective-permute-start.18 = (f32[40,128]{1,0:T(8,128)S(1)}, f32[40,128]{1,0:T(8,128)S(1)}, u32[]{:S(2)}, u32[]{:S(2)}) collective-permute-start(f32[40,128]{1,0:T(8,128)S(1)} %add_add_fusion.1), channel_id=1, source_target_pairs={{0,24},{8,16},{16,8},{24,0},{1,25},{9,17},{17,9},{25,1},{2,26},{10... | collective-permute-start | bytes 61448 | tf_op jit(solution)/shard_map/ppermute | solution.py:485
  61.2 4.7 %collective-permute-start.19 = (f32[40,128]{1,0:T(8,128)S(1)}, f32[40,128]{1,0:T(8,128)S(1)}, u32[]{:S(2)}, u32[]{:S(2)}) collective-permute-start(f32[40,128]{1,0:T(8,128)S(1)} %add_add_fusion.1), channel_id=1, source_target_pairs={{0,16},{8,24},{16,0},{24,8},{1,17},{9,25},{17,1},{25,9},{2,18},{10... | collective-permute-start | bytes 61448 | tf_op jit(solution)/shard_map/ppermute | solution.py:485
  61.3 4.6 %collective-permute-start.20 = (f32[40,128]{1,0:T(8,128)S(1)}, f32[40,128]{1,0:T(8,128)S(1)}, u32[]{:S(2)}, u32[]{:S(2)}) collective-permute-start(f32[40,128]{1,0:T(8,128)S(1)} %add_add_fusion.1), channel_id=1, source_target_pairs={{0,8},{8,0},{16,24},{24,16},{1,9},{9,1},{17,25},{25,17},{2,10},{10... | collective-permute-start | bytes 61448 | tf_op jit(solution)/shard_map/ppermute | solution.py:485
  66.0 1.3 %collective-permute-start.21 = (f32[40,128]{1,0:T(8,128)S(1)}, f32[40,128]{1,0:T(8,128)S(1)}, u32[]{:S(2)}, u32[]{:S(2)}) collective-permute-start(f32[40,128]{1,0:T(8,128)S(1)} %add_add_fusion.mine_ref), channel_id=1, source_target_pairs={{0,1},{1,0},{2,3},{3,2},{4,5},{5,4},{6,7},{7,6},{8,9},{9,8},{10,11... | collective-permute-start | bytes 61448 | tf_op jit(solution)/shard_map/ppermute | solution.py:485

commit v9 on v8

--- a/solution.py
+++ b/solution.py
@@ -98,7 +98,7 @@
 
 
 def spread_fields(
-    total_rows, par, t_ref, sea_ref, levels_ref, current_ref, state, coef, wide, spin, block, sea, levels, current, sems, field_sems
+    total_rows, par, t_ref, sea_ref, levels_ref, current_ref, state, coef, spin, col_a, col_b, wide, block, sea, levels, current, sems, field_sems
 ):
     comps, rows, cols, _ = t_ref.shape
     field_copies = fetch((sea_ref, levels_ref, current_ref), (sea, levels, current), field_sems)
@@ -122,23 +122,32 @@
         for row in range(0, rows, SUB):
             cells = block[comp, pl.ds(row, SUB)]
             state[comp, pl.ds(SIDE, cols), pl.ds(row, SUB), :] = jnp.transpose(cells, (1, 0, 2))
+    send_columns(par, state, (col_a, col_b), 0, rows)
+    tail = comps * SIDE * rows
+    _, easts = sides_of(par)
+    for slot, msg in enumerate((col_a, col_b)):
+        msg[pl.ds(tail, SUB), :] = jnp.zeros((SUB, LANES), jnp.float32)
+        for field in range(FIELDS):
+            msg[pl.ds(tail + field, 1), :] = wide[field, pl.ds(easts[slot] * (cols - 1), 1), :]
 
 
 def column_at(east, cols, depth):
     return SIDE + depth + east * (cols - 1 - 2 * depth)
 
 
-def send_columns(par, state, cols_sent):
-    comps, wide, tall, _ = state.shape
+def send_columns(par, state, cols_sent, first, count):
+    comps, length, _, _ = state.shape
     _, easts = sides_of(par)
     for slot, msg in enumerate(cols_sent):
         for comp in range(comps):
             for j in range(SIDE):
-                column = column_at(easts[slot], wide - 2 * SIDE, j)
-                msg[pl.ds((comp * SIDE + j) * tall, tall), :] = state[comp, column]
-
-
-def join_rows(par, state_in, coef_in, wide, row_a, row_b, state, coef, col_a, col_b):
+                column = column_at(easts[slot], length - 2 * SIDE, j)
+                msg[pl.ds((comp * SIDE + j) * count, count), :] = state[
+                    comp, column, pl.ds(first, count), :
+                ]
+
+
+def join_rows(par, state_in, coef_in, row_a, row_b, state, coef, col_a, col_b):
     comps, length, tall, _ = state.shape
     cols, rows = length - 2 * SIDE, tall - 2 * HALO
     norths, easts = sides_of(par)
@@ -159,18 +168,11 @@
         block = natural[field * SUB : (field + 1) * SUB]
         for lon in range(cols):
             coef[field, SIDE + lon, pl.ds(rows, SUB), :] = lane_spread(block, lon)
-    tail = comps * SIDE * tall
-    whole = [
-        jnp.where(lane < rows, wide[field], pltpu.roll(beyond, rows - field * SUB, 1))
-        for field in range(FIELDS)
-    ]
+    send_columns(par, state, (col_a, col_b), rows, SUB)
+    tail = comps * SIDE * SUB
     for slot, msg in ((0, col_a), (1, col_b)):
         msg[pl.ds(tail, SUB), :] = jnp.zeros((SUB, LANES), jnp.float32)
-        for field in range(FIELDS):
-            msg[pl.ds(tail + field, 1), :] = jnp.where(
-                easts[slot] == 1, whole[field][cols - 1 :], whole[field][:1]
-            )
-    send_columns(par, state, (col_a, col_b))
+        msg[pl.ds(tail, 1), :] = jnp.where(easts[slot] == 1, beyond[cols - 1 :], beyond[:1])
 
 
 def model(own, x_diff, x_sum, above, below, sea, flow, depth, spin):
@@ -237,14 +239,17 @@
         advance_column(source, target, coef_ref, spin_ref, first + 2 * pair + 1)
 
 
-def mend_columns(par, states, coef_ref, spin_ref, cols_got):
-    comps, length, tall, _ = states[0].shape
+def mend_columns(par, states, coef_ref, spin_ref, pieces):
+    comps, length, _, _ = states[0].shape
     _, easts = sides_of(par)
-    for slot, msg in enumerate(cols_got):
-        for comp in range(comps):
-            for j in range(SIDE):
-                column = column_at(easts[slot], length - 2 * SIDE, -1 - j)
-                states[0][comp, column] = msg[pl.ds((comp * SIDE + j) * tall, tall), :]
+    for first, count, cols_got in pieces:
+        for slot, msg in enumerate(cols_got):
+            for comp in range(comps):
+                for j in range(SIDE):
+                    column = column_at(easts[slot], length - 2 * SIDE, -1 - j)
+                    states[0][comp, column, pl.ds(first, count), :] = msg[
+                        pl.ds((comp * SIDE + j) * count, count), :
+                    ]
     for step in range(STEPS):
         first = step + 1
         skip = length - 2 * first - 2 * SIDE
@@ -256,17 +261,23 @@
 
 
 def join_gram(
-    scale, par, start_in, middle_in, state_in, coef_in, spin_ref, a, b, start, middle, state, coef, col_a, col_b, kept, sent, total
+    scale, par, start_in, middle_in, state_in, coef_in, spin_ref, a, b, c, d, start, middle, state, coef, col_a, col_b, kept, sent, total
 ):
     _, length, tall, _ = state.shape
+    rows = tall - 2 * HALO
     _, easts = sides_of(par)
-    for slot, msg in enumerate((a, b)):
-        upright = jnp.transpose(msg[pl.ds(msg.shape[0] - SUB, SUB), :])
+    for slot, (own, beyond) in enumerate(((a, c), (b, d))):
+        own, beyond = (jnp.transpose(x[pl.ds(x.shape[0] - SUB, SUB), :]) for x in (own, beyond))
+        column = column_at(easts[slot], length - 2 * SIDE, -1)
         for field in range(FIELDS):
-            column = column_at(easts[slot], length - 2 * SIDE, -1)
-            coef[field, column] = lane_spread(upright[:tall], field)
-    mend_columns(par, (start, middle, state), coef, spin_ref, (a, b))
-    send_columns(par, state, (col_a, col_b))
+            coef[field, column, pl.ds(0, rows), :] = lane_spread(own[:rows], field)
+            coef[field, column, pl.ds(rows, SUB), :] = lane_spread(
+                beyond[field * SUB : (field + 1) * SUB], 0
+            )
+    mend_columns(
+        par, (start, middle, state), coef, spin_ref, ((0, rows, (a, b)), (rows, SUB, (c, d)))
+    )
+    send_columns(par, state, (col_a, col_b), 0, tall)
     gram = sum(gram_of(*split_halves(cells)) for _, _, cells in tiles_of(state))
     write_halves(par, gram, scale, kept, sent, total)
 
@@ -360,18 +371,14 @@
         for k in range(1, SUB):
             merged = jnp.where(sub == k, scaled[k], merged)
         work[pl.ds(base, SUB), :] = merged
-        turned = jnp.transpose(merged)
         for i in range(block + 1, count):
+            weights = []
             rest = jnp.where(here, 0.0, rows[i])
-            if i == block + 1:
-                weights = []
-                for l in range(SUB):
-                    weight = lane_spread(rows[i], base + l)
-                    for m in range(l):
-                        weight = weight - weights[m] * low[l][m]
-                    weights.append(weight * inv[l])
-            else:
-                weights = [lane_spread(turned[SUB * i : SUB * (i + 1)], l) for l in range(SUB)]
+            for l in range(SUB):
+                weight = lane_spread(rows[i], base + l)
+                for m in range(l):
+                    weight = weight - weights[m] * low[l][m]
+                weights.append(weight * inv[l])
             for l in range(SUB):
                 rest = rest - weights[l] * scaled[l]
             rows[i] = rest
@@ -424,7 +431,8 @@
 
 
 def mend_only(par, start_in, middle_in, state_in, coef_ref, spin_ref, a, b, start, middle, state):
-    mend_columns(par, (start, middle, state), coef_ref, spin_ref, (a, b))
+    tall = state.shape[2]
+    mend_columns(par, (start, middle, state), coef_ref, spin_ref, ((0, tall, (a, b)),))
 
 
 def update(scale, par, state, inverse_ref, out_ref, kept, sent, factor, total):
@@ -537,7 +545,8 @@
     block = shape_of(comps, length, tall, modes)
     coefs = shape_of(FIELDS, length, tall, LANES)
     columns = (shape_of(comps * SIDE * tall, modes),) * 2
-    first_columns = (shape_of(comps * SIDE * tall + SUB, modes),) * 2
+    own_columns = (shape_of(comps * SIDE * rows + SUB, modes),) * 2
+    corners = (shape_of(comps * SIDE * SUB + SUB, modes),) * 2
     rows_sent = (shape_of(comps * HALO + 1, cols, modes),) * 2
     halves = (shape_of(modes // 4 + SUB, modes),) * 2
     square = pltpu.VMEM((modes, modes), jnp.float32)
@@ -587,31 +596,34 @@
         ],
     )
     row_halos = swap_pairs(*packed, "row", False)
-    start, coef, wide, spin = call(
+    start, coef, spin, *packed = call(
         functools.partial(spread_fields, total_rows),
-        (block, coefs, shape_of(FIELDS, cols, LANES), shape_of(tall, LANES)),
+        (block, coefs, shape_of(tall, LANES)) + own_columns,
         par,
         source,
         *fields,
         specs=[SMEM] + [HBM] * 4,
-        scratch=[pltpu.VMEM(tangents.shape, jnp.float32)]
+        scratch=[
+            pltpu.VMEM((FIELDS, cols, LANES), jnp.float32),
+            pltpu.VMEM(tangents.shape, jnp.float32),
+        ]
         + upright
         + [pltpu.SemaphoreType.DMA((comps,)), pltpu.SemaphoreType.DMA((FIELDS,))],
         cost=3.0,
     )
+    halos = swap_columns(packed)
     start, coef, *packed = call(
         join_rows,
-        (block, coefs) + first_columns,
+        (block, coefs) + corners,
         par,
         start,
         coef,
-        wide,
         *row_halos,
         aliases={1: 0, 2: 1},
     )
+    halos += swap_columns(packed)
     logs = jnp.zeros((1, modes), jnp.float32)
 
-    halos = swap_columns(packed)
     middle = inside(0, start)
     state = inside(1, middle)
     _, _, start, coef, *packed, kept, sent = call(

time: 75.1 us -> 69.6 us (0.927)
  waiting for transfers between devices: 13.6 us -> 10.3 us
  Pallas kernels: 33.1 us -> 30.7 us
    pallas_call x13, Pallas kernels: 33.1 us -> 30.7 us  [call(): pl.pallas_call(kernel, out_shape=outs, in_specs=specs or [SMEM] + [VMEM]...]
    ppermute x3 -> x4, waiting for transfers between devices: 1.86 us -> 0.26 us  [swap_pairs(): lax.ppermute(far_value, axis, far)]
    ppermute x16, waiting for transfers between devices: 11 us -> 9.99 us  [swapped(): lax.ppermute(value, axis, [(i, i ^ mask) for i in range(lax.axis_size(axi...]
    ppermute x3 -> x4, starting transfers between devices: 4.93 us -> 5.77 us  [swap_pairs(): lax.ppermute(far_value, axis, far)]
    ppermute x3 -> x4, waiting for transfers between devices: 0.8 us -> 0.01 us  [swap_pairs(): lax.ppermute(near_value, axis, near)]
    ppermute x3 -> x4, starting transfers between devices: 3.22 us -> 3.29 us  [swap_pairs(): lax.ppermute(near_value, axis, near)]
  transfers between devices with their start and end apart: 22 -> 24, of which waited for: 13 -> 13; matrix products, arithmetic and copies ran while one was open for 0% -> 0% of each run, Pallas kernels for 17% -> 20%
where the time goes in v9:
time: 69.6 us; the launch traced here: 69.2 us
  Pallas kernels  30.7 us (44%)
  starting transfers between devices  27.2 us (39%)
  waiting for transfers between devices  10.3 us (15%)
  between operations  0.99 us (1%)
    pallas_call x13, Pallas kernels, call(): pl.pallas_call(kernel, out_shape=outs, in_specs=specs or [SMEM] + [VMEM]...  30.7 us
    ppermute x16, starting transfers between devices, swapped(): lax.ppermute(value, axis, [(i, i ^ mask) for i in range(lax.axis_size(axi...  18.1 us
    ppermute x16, waiting for transfers between devices, swapped(): lax.ppermute(value, axis, [(i, i ^ mask) for i in range(lax.axis_size(axi...  9.99 us
    ppermute x4, starting transfers between devices, swap_pairs(): lax.ppermute(far_value, axis, far)  5.77 us
    ppermute x4, starting transfers between devices, swap_pairs(): lax.ppermute(near_value, axis, near)  3.29 us
  transfers between devices with their start and end apart: 24, of which 13 were waited for; matrix products, arithmetic and copies ran while one was open for 0% of the time, Pallas kernels for 20%

profile of v9, /device:TPU:0, one launch (start us, length us, event | category | flops | bytes accessed | tf_op | source)
XLA Modules:
  0.0 69.2 jit_solution(13565834874860122109)
XLA Ops:
  0.7 1.7 %shard_map.60 = (f32[13,32,128]{2,1,0:T(8,128)S(1)}, f32[13,32,128]{2,1,0:T(8,128)S(1)}) custom-call(s32[2]{0:T(128)S(1)} %pad_add_fusion.par, f32[3,64,32,128]{3,2,1,0:T(8,128)} %t_ref.3, s32[32,64]{1,0:T(8,128)} %bitcast.9, s32[32,64]{1,0:T(8,128)} %bitcast.11, f32[32,64]{1,0:T(8,128)} %bitcast.13), custom_call_target="tpu_custom_call" | custom-call | flops 1000000000 | bytes 3000000 | tf_op jit(solution)/shard_map/pallas_call | solution.py:559
  2.4 3.1 %collective-permute-start = (f32[13,32,128]{2,1,0:T(8,128)S(1)}, f32[13,32,128]{2,1,0:T(8,128)S(1)}, u32[]{:S(2)}, u32[]{:S(2)}) collective-permute-start(f32[13,32,128]{2,1,0:T(8,128)S(1)} %get-tuple-element.32), channel_id=1, source_target_pairs={{0,8},{8,0},{16,24},{24,16},{1,9},{9,1},{17,25},{25,17},{2,10},{10... | collective-permute-start | bytes 638984 | tf_op jit(solution)/shard_map/ppermute | solution.py:489
  6.1 3.8 %shard_map.59 = (f32[3,36,72,128]{3,2,1,0:T(8,128)S(1)}, f32[3,36,72,128]{3,2,1,0:T(8,128)S(1)}, f32[72,128]{1,0:T(8,128)S(1)}, f32[392,128]{1,0:T(8,128)S(1)}, f32[392,128]{1,0:T(8,128)S(1)}) custom-call(s32[2]{0:T(128)S(1)} %pad_add_fusion.par, f32[3,64,32,128]{3,2,1,0:T(8,128)} %t_ref.3, s32[32,64]{1,0:T(8,128)} %bitcast.10, s32[32,64]{1,0:T(8,128)} %bitcast.12, ...), custom_call_target="tpu_custom_call" | custom-call | flops 3000000000 | bytes 9000000 | tf_op jit(solution)/shard_map/pallas_call | solution.py:559
  10.0 2.5 %collective-permute-start.3 = (f32[392,128]{1,0:T(8,128)S(1)}, f32[392,128]{1,0:T(8,128)S(1)}, u32[]{:S(2)}, u32[]{:S(2)}) collective-permute-start(f32[392,128]{1,0:T(8,128)S(1)} %get-tuple-element.38), channel_id=1, source_target_pairs={{0,7},{1,2},{2,1},{3,4},{4,3},{5,6},{6,5},{7,0},{8,15},{9,10},{10,... | collective-permute-start | bytes 602120 | tf_op jit(solution)/shard_map/ppermute | solution.py:489
  12.6 1.0 %shard_map.61 = (f32[3,36,72,128]{3,2,1,0:T(8,128)S(1)}, f32[3,36,72,128]{3,2,1,0:T(8,128)S(1)}, f32[56,128]{1,0:T(8,128)S(1)}, f32[56,128]{1,0:T(8,128)S(1)}) custom-call(s32[2]{0:T(128)S(1)} %pad_add_fusion.par, f32[3,36,72,128]{3,2,1,0:T(8,128)S(1)} %get-tuple-element.30.state_in, ...), custom_call_target="tpu_custom_call", output_to_operand_aliasing={{0}: (1, {}), {1}: (2, {})} | custom-call | flops 1000000000 | bytes 3000000 | tf_op jit(solution)/shard_map/pallas_call | solution.py:559
  14.5 1.8 %shard_map.62.source.middle_in = f32[3,36,72,128]{3,2,1,0:T(8,128)S(1)} custom-call(f32[3,36,72,128]{3,2,1,0:T(8,128)S(1)} %get-tuple-element.34.source.start_in, f32[3,36,72,128]{3,2,1,0:T(8,128)S(1)} %get-tuple-element.35.coef_ref.coef_in, f32[72,128]{1,0:T(8,128)S(1)} %get-tuple-element.36.spin_ref), custom_call_target="tpu_custom_call" | custom-call | flops 2000000000 | bytes 6000000 | tf_op jit(solution)/shard_map/pallas_call | solution.py:559
  16.4 1.6 %shard_map.63.state_in = f32[3,36,72,128]{3,2,1,0:T(8,128)S(1)} custom-call(f32[3,36,72,128]{3,2,1,0:T(8,128)S(1)} %shard_map.62.source.middle_in, f32[3,36,72,128]{3,2,1,0:T(8,128)S(1)} %get-tuple-element.35.coef_ref.coef_in, f32[72,128]{1,0:T(8,128)S(1)} %get-tuple-element.36.spin_ref), custom_call_target="tpu_custom_call" | custom-call | flops 2000000000 | bytes 6000000 | tf_op jit(solution)/shard_map/pallas_call | solution.py:559
  18.3 2.1 %shard_map.64 = (f32[3,36,72,128]{3,2,1,0:T(8,128)S(1)}, f32[3,36,72,128]{3,2,1,0:T(8,128)S(1)}, f32[3,36,72,128]{3,2,1,0:T(8,128)S(1)}, f32[3,36,72,128]{3,2,1,...) custom-call(s32[2]{0:T(128)S(1)} %pad_add_fusion.par, ...), custom_call_target="tpu_custom_call", output_to_operand_aliasing={{0}: (1, {}), {1}: (2, {}), {2}: (3, {}), {3}: (4, {})} | custom-call | flops 2000000000 | bytes 6000000 | tf_op jit(solution)/shard_map/pallas_call | solution.py:559
  20.6 1.1 %collective-permute-done.6 = f32[40,128]{1,0:T(8,128)S(1)} collective-permute-done((f32[40,128]{1,0:T(8,128)S(1)}, f32[40,128]{1,0:T(8,128)S(1)}, u32[]{:S(2)}, u32[]{:S(2)}) %collective-permute-start.6) | collective-permute-done | bytes 20512 | tf_op jit(solution)/shard_map/ppermute | solution.py:493
  21.7 1.7 %collective-permute-start.7 = (f32[40,128]{1,0:T(8,128)S(1)}, f32[40,128]{1,0:T(8,128)S(1)}, u32[]{:S(2)}, u32[]{:S(2)}) collective-permute-start(f32[40,128]{1,0:T(8,128)S(1)} %add.24.first), channel_id=1, source_target_pairs={{0,6},{1,7},{2,4},{3,5},{4,2},{5,3},{6,0},{7,1},{8,14},{9,15},{10,... | collective-permute-start | bytes 61448 | tf_op jit(solution)/shard_map/ppermute | solution.py:493
  23.4 1.4 %collective-permute-start.8 = (f32[40,128]{1,0:T(8,128)S(1)}, f32[40,128]{1,0:T(8,128)S(1)}, u32[]{:S(2)}, u32[]{:S(2)}) collective-permute-start(f32[40,128]{1,0:T(8,128)S(1)} %add.24.first), channel_id=1, source_target_pairs={{0,4},{1,5},{2,6},{3,7},{4,0},{5,1},{6,2},{7,3},{8,12},{9,13},{10,... | collective-permute-start | bytes 61448 | tf_op jit(solution)/shard_map/ppermute | solution.py:493
  25.2 1.7 %shard_map.65.source.rest_0_.middle_in = f32[3,36,72,128]{3,2,1,0:T(8,128)S(1)} custom-call(f32[3,36,72,128]{3,2,1,0:T(8,128)S(1)} %get-tuple-element.41.source.start_in, f32[3,36,72,128]{3,2,1,0:T(8,128)S(1)} %get-tuple-element.42.coef_ref, f32[72,128]{1,0:T(8,128)S(1)} %get-tuple-element.36.spin_ref), custom_call_target="tpu_custom_call" | custom-call | flops 2000000000 | bytes 6000000 | tf_op jit(solution)/shard_map/pallas_call | solution.py:559
  27.1 1.4 %collective-permute-done.9.fourth = f32[40,128]{1,0:T(8,128)S(1)} collective-permute-done((f32[40,128]{1,0:T(8,128)S(1)}, f32[40,128]{1,0:T(8,128)S(1)}, u32[]{:S(2)}, u32[]{:S(2)}) %collective-permute-start.9) | collective-permute-done | bytes 20512 | tf_op jit(solution)/shard_map/ppermute | solution.py:493
  28.6 1.7 %collective-permute-start.11 = (f32[432,128]{1,0:T(8,128)S(1)}, f32[432,128]{1,0:T(8,128)S(1)}, u32[]{:S(2)}, u32[]{:S(2)}) collective-permute-start(f32[432,128]{1,0:T(8,128)S(1)} %get-tuple-element.48), channel_id=1, source_target_pairs={{0,7},{1,2},{2,1},{3,4},{4,3},{5,6},{6,5},{7,0},{8,15},{9,10},{10,... | collective-permute-start | bytes 663560 | tf_op jit(solution)/shard_map/ppermute | solution.py:489
  30.3 2.5 %collective-permute-start.12 = (f32[40,128]{1,0:T(8,128)S(1)}, f32[40,128]{1,0:T(8,128)S(1)}, u32[]{:S(2)}, u32[]{:S(2)}) collective-permute-start(f32[40,128]{1,0:T(8,128)S(1)} %get-tuple-element.50.first), channel_id=1, source_target_pairs={{0,24},{8,16},{16,8},{24,0},{1,25},{9,17},{17,9},{25,1},{2,26},{10... | collective-permute-start | bytes 61448 | tf_op jit(solution)/shard_map/ppermute | solution.py:493
  32.8 3.4 %collective-permute-start.13 = (f32[40,128]{1,0:T(8,128)S(1)}, f32[40,128]{1,0:T(8,128)S(1)}, u32[]{:S(2)}, u32[]{:S(2)}) collective-permute-start(f32[40,128]{1,0:T(8,128)S(1)} %get-tuple-element.50.first), channel_id=1, source_target_pairs={{0,16},{8,24},{16,0},{24,8},{1,17},{9,25},{17,1},{25,9},{2,18},{10... | collective-permute-start | bytes 61448 | tf_op jit(solution)/shard_map/ppermute | solution.py:493
  36.2 1.7 %shard_map.66.state_in.rest_0_ = f32[3,36,72,128]{3,2,1,0:T(8,128)S(1)} custom-call(f32[3,36,72,128]{3,2,1,0:T(8,128)S(1)} %shard_map.65.source.rest_0_.middle_in, f32[3,36,72,128]{3,2,1,0:T(8,128)S(1)} %get-tuple-element.42.coef_ref, f32[72,128]{1,0:T(8,128)S(1)} %get-tuple-element.36.spin_ref), custom_call_target="tpu_custom_call" | custom-call | flops 2000000000 | bytes 6000000 | tf_op jit(solution)/shard_map/pallas_call | solution.py:559
  38.4 1.6 %collective-permute-done.14.fourth = f32[40,128]{1,0:T(8,128)S(1)} collective-permute-done((f32[40,128]{1,0:T(8,128)S(1)}, f32[40,128]{1,0:T(8,128)S(1)}, u32[]{:S(2)}, u32[]{:S(2)}) %collective-permute-start.14) | collective-permute-done | bytes 20512 | tf_op jit(solution)/shard_map/ppermute | solution.py:493
  40.1 1.3 %shard_map.68 = (f32[3,36,72,128]{3,2,1,0:T(8,128)S(1)}, f32[3,36,72,128]{3,2,1,0:T(8,128)S(1)}, f32[3,36,72,128]{3,2,1,0:T(8,128)S(1)}) custom-call(s32[2]{0:T(128)S(1)} %pad_add_fusion.par, f32[3,36,72,128]{3,2,1,0:T(8,128)S(1)} %get-tuple-element.41.source.start_in, ...), custom_call_target="tpu_custom_call", output_to_operand_aliasing={{0}: (1, {}), {1}: (2, {}), {2}: (3, {})} | custom-call | flops 1000000000 | bytes 3000000 | tf_op jit(solution)/shard_map/pallas_call | solution.py:559
  41.4 3.6 %shard_map.70 = (f32[128,128]{1,0:T(8,128)S(1)}, f32[1,128]{1,0:T(1,128)S(1)}) custom-call(s32[2]{0:T(128)S(1)} %pad_add_fusion.par, f32[40,128]{1,0:T(8,128)S(1)} %shard_map.69.mine_ref, f32[40,128]{1,0:T(8,128)S(1)} %collective-permute-done.15.other_ref, f32[1,128]{1,0:T(1,128)S(1)} %broadcast_in_dim.3.prior_ref, ...), custom_call_target="tpu_custom_call" | custom-call | flops 10000000 | bytes 30000 | tf_op jit(solution)/shard_map/pallas_call | solution.py:559
  45.0 2.7 %shard_map.71 = (f32[3,32,64,128]{3,2,1,0:T(8,128)S(1)}, f32[40,128]{1,0:T(8,128)S(1)}, f32[40,128]{1,0:T(8,128)S(1)}) custom-call(s32[2]{0:T(128)S(1)} %pad_add_fusion.par, f32[3,36,72,128]{3,2,1,0:T(8,128)S(1)} %get-tuple-element.49._.state, f32[128,128]{1,0:T(8,128)S(1)} %get-tuple-element.51.inverse_ref), custom_call_target="tpu_custom_call" | custom-call | flops 2000000000 | bytes 6000000 | tf_op jit(solution)/shard_map/pallas_call | solution.py:559
  48.3 0.8 %collective-permute-done.16 = f32[40,128]{1,0:T(8,128)S(1)} collective-permute-done((f32[40,128]{1,0:T(8,128)S(1)}, f32[40,128]{1,0:T(8,128)S(1)}, u32[]{:S(2)}, u32[]{:S(2)}) %collective-permute-start.16) | collective-permute-done | bytes 20512 | tf_op jit(solution)/shard_map/ppermute | solution.py:493
  49.6 1.4 %collective-permute-start.18 = (f32[40,128]{1,0:T(8,128)S(1)}, f32[40,128]{1,0:T(8,128)S(1)}, u32[]{:S(2)}, u32[]{:S(2)}) collective-permute-start(f32[40,128]{1,0:T(8,128)S(1)} %add.25), channel_id=1, source_target_pairs={{0,4},{1,5},{2,6},{3,7},{4,0},{5,1},{6,2},{7,3},{8,12},{9,13},{10,... | collective-permute-start | bytes 61448 | tf_op jit(solution)/shard_map/ppermute | solution.py:493
  51.0 1.6 %collective-permute-start.19 = (f32[40,128]{1,0:T(8,128)S(1)}, f32[40,128]{1,0:T(8,128)S(1)}, u32[]{:S(2)}, u32[]{:S(2)}) collective-permute-start(f32[40,128]{1,0:T(8,128)S(1)} %add.25), channel_id=1, source_target_pairs={{0,2},{1,3},{2,0},{3,1},{4,6},{5,7},{6,4},{7,5},{8,10},{9,11},{10,... | collective-permute-start | bytes 61448 | tf_op jit(solution)/shard_map/ppermute | solution.py:493
  52.6 1.3 %collective-permute-done.17 = f32[40,128]{1,0:T(8,128)S(1)} collective-permute-done((f32[40,128]{1,0:T(8,128)S(1)}, f32[40,128]{1,0:T(8,128)S(1)}, u32[]{:S(2)}, u32[]{:S(2)}) %collective-permute-start.17) | collective-permute-done | bytes 20512 | tf_op jit(solution)/shard_map/ppermute | solution.py:493
  53.9 0.9 %collective-permute-done.19 = f32[40,128]{1,0:T(8,128)S(1)} collective-permute-done((f32[40,128]{1,0:T(8,128)S(1)}, f32[40,128]{1,0:T(8,128)S(1)}, u32[]{:S(2)}, u32[]{:S(2)}) %collective-permute-start.19) | collective-permute-done | bytes 20512 | tf_op jit(solution)/shard_map/ppermute | solution.py:493
  54.8 1.3 %collective-permute-start.20 = (f32[40,128]{1,0:T(8,128)S(1)}, f32[40,128]{1,0:T(8,128)S(1)}, u32[]{:S(2)}, u32[]{:S(2)}) collective-permute-start(f32[40,128]{1,0:T(8,128)S(1)} %add_add_fusion.1), channel_id=1, source_target_pairs={{0,24},{8,16},{16,8},{24,0},{1,25},{9,17},{17,9},{25,1},{2,26},{10... | collective-permute-start | bytes 61448 | tf_op jit(solution)/shard_map/ppermute | solution.py:493
  56.1 1.5 %collective-permute-start.21 = (f32[40,128]{1,0:T(8,128)S(1)}, f32[40,128]{1,0:T(8,128)S(1)}, u32[]{:S(2)}, u32[]{:S(2)}) collective-permute-start(f32[40,128]{1,0:T(8,128)S(1)} %add_add_fusion.1), channel_id=1, source_target_pairs={{0,16},{8,24},{16,0},{24,8},{1,17},{9,25},{17,1},{25,9},{2,18},{10... | collective-permute-start | bytes 61448 | tf_op jit(solution)/shard_map/ppermute | solution.py:493
  57.6 1.7 %collective-permute-start.22 = (f32[40,128]{1,0:T(8,128)S(1)}, f32[40,128]{1,0:T(8,128)S(1)}, u32[]{:S(2)}, u32[]{:S(2)}) collective-permute-start(f32[40,128]{1,0:T(8,128)S(1)} %add_add_fusion.1), channel_id=1, source_target_pairs={{0,8},{8,0},{16,24},{24,16},{1,9},{9,1},{17,25},{25,17},{2,10},{10... | collective-permute-start | bytes 61448 | tf_op jit(solution)/shard_map/ppermute | solution.py:493
  59.2 1.2 %collective-permute-done.20 = f32[40,128]{1,0:T(8,128)S(1)} collective-permute-done((f32[40,128]{1,0:T(8,128)S(1)}, f32[40,128]{1,0:T(8,128)S(1)}, u32[]{:S(2)}, u32[]{:S(2)}) %collective-permute-start.20) | collective-permute-done | bytes 20512 | tf_op jit(solution)/shard_map/ppermute | solution.py:493
  61.4 1.1 %shard_map.72 = bf16[3,64,32,256]{3,2,1,0:T(8,128)(2,1)S(1)} custom-call(f32[3,32,64,128]{3,2,1,0:T(8,128)S(1)} %get-tuple-element.55.turned), custom_call_target="tpu_custom_call" | custom-call | flops 1000000000 | bytes 3000000 | tf_op jit(solution)/shard_map/pallas_call | solution.py:559
  62.6 6.5 %shard_map.73 = (f32[12,512,128]{2,1,0:T(8,128)}, f32[1,128]{1,0:T(1,128)}) custom-call(s32[2]{0:T(128)S(1)} %pad_add_fusion.par, f32[40,128]{1,0:T(8,128)S(1)} %add_add_fusion.mine_ref, f32[40,128]{1,0:T(8,128)S(1)} %collective-permute-done.23.other_ref, f32[1,128]{1,0:T(1,128)S(1)} %get-tuple-element.54.prior_ref, bf16[12,512,256]{2,1,0:T(8,128)(2,1)S(1)} %bitcast.8), custom_call_target="tpu_custom_call" | custom-call | flops 1000000000 | bytes 3000000 | tf_op jit(solution)/shard_map/pallas_call | solution.py:559
  (37 shorter events, 5.5 us)
Async XLA Ops:
  2.4 10.2 %collective-permute-start = (f32[13,32,128]{2,1,0:T(8,128)S(1)}, f32[13,32,128]{2,1,0:T(8,128)S(1)}, u32[]{:S(2)}, u32[]{:S(2)}) collective-permute-start(f32[13,32,128]{2,1,0:T(8,128)S(1)} %get-tuple-element.32), channel_id=1, source_target_pairs={{0,8},{8,0},{16,24},{24,16},{1,9},{9,1},{17,25},{25,17},{2,10},{10... | collective-permute-start | bytes 638984 | tf_op jit(solution)/shard_map/ppermute | solution.py:489
  5.5 7.1 %collective-permute-start.1 = (f32[13,32,128]{2,1,0:T(8,128)S(1)}, f32[13,32,128]{2,1,0:T(8,128)S(1)}, u32[]{:S(2)}, u32[]{:S(2)}) collective-permute-start(f32[13,32,128]{2,1,0:T(8,128)S(1)} %get-tuple-element.33), channel_id=1, source_target_pairs={{8,16},{16,8},{9,17},{17,9},{10,18},{18,10},{11,19},{19,11},{12,20... | collective-permute-start | bytes 638984 | tf_op jit(solution)/shard_map/ppermute | solution.py:489
  10.0 8.1 %collective-permute-start.2 = (f32[392,128]{1,0:T(8,128)S(1)}, f32[392,128]{1,0:T(8,128)S(1)}, u32[]{:S(2)}, u32[]{:S(2)}) collective-permute-start(f32[392,128]{1,0:T(8,128)S(1)} %get-tuple-element.37), channel_id=1, source_target_pairs={{0,1},{1,0},{2,3},{3,2},{4,5},{5,4},{6,7},{7,6},{8,9},{9,8},{10,11... | collective-permute-start | bytes 602120 | tf_op jit(solution)/shard_map/ppermute | solution.py:489
  10.0 8.0 %collective-permute-start.3 = (f32[392,128]{1,0:T(8,128)S(1)}, f32[392,128]{1,0:T(8,128)S(1)}, u32[]{:S(2)}, u32[]{:S(2)}) collective-permute-start(f32[392,128]{1,0:T(8,128)S(1)} %get-tuple-element.38), channel_id=1, source_target_pairs={{0,7},{1,2},{2,1},{3,4},{4,3},{5,6},{6,5},{7,0},{8,15},{9,10},{10,... | collective-permute-start | bytes 602120 | tf_op jit(solution)/shard_map/ppermute | solution.py:489
  13.6 4.4 %collective-permute-start.4 = (f32[56,128]{1,0:T(8,128)S(1)}, f32[56,128]{1,0:T(8,128)S(1)}, u32[]{:S(2)}, u32[]{:S(2)}) collective-permute-start(f32[56,128]{1,0:T(8,128)S(1)} %get-tuple-element.39), channel_id=1, source_target_pairs={{0,1},{1,0},{2,3},{3,2},{4,5},{5,4},{6,7},{7,6},{8,9},{9,8},{10,11... | collective-permute-start | bytes 86024 | tf_op jit(solution)/shard_map/ppermute | solution.py:489
  13.7 4.6 %collective-permute-start.5 = (f32[56,128]{1,0:T(8,128)S(1)}, f32[56,128]{1,0:T(8,128)S(1)}, u32[]{:S(2)}, u32[]{:S(2)}) collective-permute-start(f32[56,128]{1,0:T(8,128)S(1)} %get-tuple-element.40), channel_id=1, source_target_pairs={{0,7},{1,2},{2,1},{3,4},{4,3},{5,6},{6,5},{7,0},{8,15},{9,10},{10,... | collective-permute-start | bytes 86024 | tf_op jit(solution)/shard_map/ppermute | solution.py:489
  20.4 1.3 %collective-permute-start.6 = (f32[40,128]{1,0:T(8,128)S(1)}, f32[40,128]{1,0:T(8,128)S(1)}, u32[]{:S(2)}, u32[]{:S(2)}) collective-permute-start(f32[40,128]{1,0:T(8,128)S(1)} %get-tuple-element.44), channel_id=1, source_target_pairs={{0,1},{1,0},{2,3},{3,2},{4,5},{5,4},{6,7},{7,6},{8,9},{9,8},{10,11... | collective-permute-start | bytes 61448 | tf_op jit(solution)/shard_map/ppermute | solution.py:493
  21.7 5.2 %collective-permute-start.7 = (f32[40,128]{1,0:T(8,128)S(1)}, f32[40,128]{1,0:T(8,128)S(1)}, u32[]{:S(2)}, u32[]{:S(2)}) collective-permute-start(f32[40,128]{1,0:T(8,128)S(1)} %add.24.first), channel_id=1, source_target_pairs={{0,6},{1,7},{2,4},{3,5},{4,2},{5,3},{6,0},{7,1},{8,14},{9,15},{10,... | collective-permute-start | bytes 61448 | tf_op jit(solution)/shard_map/ppermute | solution.py:493
  23.4 3.8 %collective-permute-start.8 = (f32[40,128]{1,0:T(8,128)S(1)}, f32[40,128]{1,0:T(8,128)S(1)}, u32[]{:S(2)}, u32[]{:S(2)}) collective-permute-start(f32[40,128]{1,0:T(8,128)S(1)} %add.24.first), channel_id=1, source_target_pairs={{0,4},{1,5},{2,6},{3,7},{4,0},{5,1},{6,2},{7,3},{8,12},{9,13},{10,... | collective-permute-start | bytes 61448 | tf_op jit(solution)/shard_map/ppermute | solution.py:493
  24.8 3.8 %collective-permute-start.9 = (f32[40,128]{1,0:T(8,128)S(1)}, f32[40,128]{1,0:T(8,128)S(1)}, u32[]{:S(2)}, u32[]{:S(2)}) collective-permute-start(f32[40,128]{1,0:T(8,128)S(1)} %add.24.first), channel_id=1, source_target_pairs={{0,2},{1,3},{2,0},{3,1},{4,6},{5,7},{6,4},{7,5},{8,10},{9,11},{10,... | collective-permute-start | bytes 61448 | tf_op jit(solution)/shard_map/ppermute | solution.py:493
  28.6 11.5 %collective-permute-start.10 = (f32[432,128]{1,0:T(8,128)S(1)}, f32[432,128]{1,0:T(8,128)S(1)}, u32[]{:S(2)}, u32[]{:S(2)}) collective-permute-start(f32[432,128]{1,0:T(8,128)S(1)} %get-tuple-element.47), channel_id=1, source_target_pairs={{0,1},{1,0},{2,3},{3,2},{4,5},{5,4},{6,7},{7,6},{8,9},{9,8},{10,11... | collective-permute-start | bytes 663560 | tf_op jit(solution)/shard_map/ppermute | solution.py:489
  28.6 11.4 %collective-permute-start.11 = (f32[432,128]{1,0:T(8,128)S(1)}, f32[432,128]{1,0:T(8,128)S(1)}, u32[]{:S(2)}, u32[]{:S(2)}) collective-permute-start(f32[432,128]{1,0:T(8,128)S(1)} %get-tuple-element.48), channel_id=1, source_target_pairs={{0,7},{1,2},{2,1},{3,4},{4,3},{5,6},{6,5},{7,0},{8,15},{9,10},{10,... | collective-permute-start | bytes 663560 | tf_op jit(solution)/shard_map/ppermute | solution.py:489
  30.3 7.6 %collective-permute-start.12 = (f32[40,128]{1,0:T(8,128)S(1)}, f32[40,128]{1,0:T(8,128)S(1)}, u32[]{:S(2)}, u32[]{:S(2)}) collective-permute-start(f32[40,128]{1,0:T(8,128)S(1)} %get-tuple-element.50.first), channel_id=1, source_target_pairs={{0,24},{8,16},{16,8},{24,0},{1,25},{9,17},{17,9},{25,1},{2,26},{10... | collective-permute-start | bytes 61448 | tf_op jit(solution)/shard_map/ppermute | solution.py:493
  32.8 5.6 %collective-permute-start.13 = (f32[40,128]{1,0:T(8,128)S(1)}, f32[40,128]{1,0:T(8,128)S(1)}, u32[]{:S(2)}, u32[]{:S(2)}) collective-permute-start(f32[40,128]{1,0:T(8,128)S(1)} %get-tuple-element.50.first), channel_id=1, source_target_pairs={{0,16},{8,24},{16,0},{24,8},{1,17},{9,25},{17,1},{25,9},{2,18},{10... | collective-permute-start | bytes 61448 | tf_op jit(solution)/shard_map/ppermute | solution.py:493
  36.2 3.8 %collective-permute-start.14 = (f32[40,128]{1,0:T(8,128)S(1)}, f32[40,128]{1,0:T(8,128)S(1)}, u32[]{:S(2)}, u32[]{:S(2)}) collective-permute-start(f32[40,128]{1,0:T(8,128)S(1)} %get-tuple-element.50.first), channel_id=1, source_target_pairs={{0,8},{8,0},{16,24},{24,16},{1,9},{9,1},{17,25},{25,17},{2,10},{10... | collective-permute-start | bytes 61448 | tf_op jit(solution)/shard_map/ppermute | solution.py:493
  40.0 1.4 %collective-permute-start.15 = (f32[40,128]{1,0:T(8,128)S(1)}, f32[40,128]{1,0:T(8,128)S(1)}, u32[]{:S(2)}, u32[]{:S(2)}) collective-permute-start(f32[40,128]{1,0:T(8,128)S(1)} %shard_map.69.mine_ref), channel_id=1, source_target_pairs={{0,1},{1,0},{2,3},{3,2},{4,5},{5,4},{6,7},{7,6},{8,9},{9,8},{10,11... | collective-permute-start | bytes 61448 | tf_op jit(solution)/shard_map/ppermute | solution.py:493
  47.7 1.4 %collective-permute-start.16 = (f32[40,128]{1,0:T(8,128)S(1)}, f32[40,128]{1,0:T(8,128)S(1)}, u32[]{:S(2)}, u32[]{:S(2)}) collective-permute-start(f32[40,128]{1,0:T(8,128)S(1)} %get-tuple-element.53), channel_id=1, source_target_pairs={{0,1},{1,0},{2,3},{3,2},{4,5},{5,4},{6,7},{7,6},{8,9},{9,8},{10,11... | collective-permute-start | bytes 61448 | tf_op jit(solution)/shard_map/ppermute | solution.py:493
  49.1 4.8 %collective-permute-start.17 = (f32[40,128]{1,0:T(8,128)S(1)}, f32[40,128]{1,0:T(8,128)S(1)}, u32[]{:S(2)}, u32[]{:S(2)}) collective-permute-start(f32[40,128]{1,0:T(8,128)S(1)} %add.25), channel_id=1, source_target_pairs={{0,6},{1,7},{2,4},{3,5},{4,2},{5,3},{6,0},{7,1},{8,14},{9,15},{10,... | collective-permute-start | bytes 61448 | tf_op jit(solution)/shard_map/ppermute | solution.py:493
  49.6 4.3 %collective-permute-start.18 = (f32[40,128]{1,0:T(8,128)S(1)}, f32[40,128]{1,0:T(8,128)S(1)}, u32[]{:S(2)}, u32[]{:S(2)}) collective-permute-start(f32[40,128]{1,0:T(8,128)S(1)} %add.25), channel_id=1, source_target_pairs={{0,4},{1,5},{2,6},{3,7},{4,0},{5,1},{6,2},{7,3},{8,12},{9,13},{10,... | collective-permute-start | bytes 61448 | tf_op jit(solution)/shard_map/ppermute | solution.py:493
  51.0 3.8 %collective-permute-start.19 = (f32[40,128]{1,0:T(8,128)S(1)}, f32[40,128]{1,0:T(8,128)S(1)}, u32[]{:S(2)}, u32[]{:S(2)}) collective-permute-start(f32[40,128]{1,0:T(8,128)S(1)} %add.25), channel_id=1, source_target_pairs={{0,2},{1,3},{2,0},{3,1},{4,6},{5,7},{6,4},{7,5},{8,10},{9,11},{10,... | collective-permute-start | bytes 61448 | tf_op jit(solution)/shard_map/ppermute | solution.py:493
  54.8 5.6 %collective-permute-start.20 = (f32[40,128]{1,0:T(8,128)S(1)}, f32[40,128]{1,0:T(8,128)S(1)}, u32[]{:S(2)}, u32[]{:S(2)}) collective-permute-start(f32[40,128]{1,0:T(8,128)S(1)} %add_add_fusion.1), channel_id=1, source_target_pairs={{0,24},{8,16},{16,8},{24,0},{1,25},{9,17},{17,9},{25,1},{2,26},{10... | collective-permute-start | bytes 61448 | tf_op jit(solution)/shard_map/ppermute | solution.py:493
  56.1 4.9 %collective-permute-start.21 = (f32[40,128]{1,0:T(8,128)S(1)}, f32[40,128]{1,0:T(8,128)S(1)}, u32[]{:S(2)}, u32[]{:S(2)}) collective-permute-start(f32[40,128]{1,0:T(8,128)S(1)} %add_add_fusion.1), channel_id=1, source_target_pairs={{0,16},{8,24},{16,0},{24,8},{1,17},{9,25},{17,1},{25,9},{2,18},{10... | collective-permute-start | bytes 61448 | tf_op jit(solution)/shard_map/ppermute | solution.py:493
  57.6 3.8 %collective-permute-start.22 = (f32[40,128]{1,0:T(8,128)S(1)}, f32[40,128]{1,0:T(8,128)S(1)}, u32[]{:S(2)}, u32[]{:S(2)}) collective-permute-start(f32[40,128]{1,0:T(8,128)S(1)} %add_add_fusion.1), channel_id=1, source_target_pairs={{0,8},{8,0},{16,24},{24,16},{1,9},{9,1},{17,25},{25,17},{2,10},{10... | collective-permute-start | bytes 61448 | tf_op jit(solution)/shard_map/ppermute | solution.py:493
  61.4 1.2 %collective-permute-start.23 = (f32[40,128]{1,0:T(8,128)S(1)}, f32[40,128]{1,0:T(8,128)S(1)}, u32[]{:S(2)}, u32[]{:S(2)}) collective-permute-start(f32[40,128]{1,0:T(8,128)S(1)} %add_add_fusion.mine_ref), channel_id=1, source_target_pairs={{0,1},{1,0},{2,3},{3,2},{4,5},{5,4},{6,7},{7,6},{8,9},{9,8},{10,11... | collective-permute-start | bytes 61448 | tf_op jit(solution)/shard_map/ppermute | solution.py:493

commit v10 on v9

--- a/solution.py
+++ b/solution.py
@@ -147,7 +147,7 @@
                 ]
 
 
-def join_rows(par, state_in, coef_in, row_a, row_b, state, coef, col_a, col_b):
+def join_rows(par, state_in, coef_in, row_a, row_b, _, state, coef, col_a, col_b):
     comps, length, tall, _ = state.shape
     cols, rows = length - 2 * SIDE, tall - 2 * HALO
     norths, easts = sides_of(par)
@@ -189,12 +189,12 @@
     )
 
 
-def advance_column(source, target, coef_ref, spin_ref, lon):
+def advance_column(source, target, coef_ref, spin_ref, lon, chosen=None):
     comps, length, tall, _ = source.shape
     flat = source.reshape(comps * length * tall, LANES)
     sub = lax.broadcasted_iota(jnp.int32, (SUB, LANES), 0)
     tiles = tall // SUB
-    for tile in range(tiles):
+    for tile in chosen or range(tiles):
         lines = pl.ds(SUB * tile, SUB)
         own, east, west = (
             [source[comp, lon + shift, lines, :] for comp in range(comps)] for shift in (0, 1, -1)
@@ -229,14 +229,15 @@
             target[comp, lon, lines, :] = new[comp]
 
 
-def apply_inside(step, source, coef_ref, spin_ref, target):
+def apply_inside(step, chosen, source, coef_ref, spin_ref, *refs):
     first = SIDE + step + 1
     count = source.shape[1] - 2 * first
+    target = refs[-1]
 
     @pl.loop(0, count // 2)
     def _(pair):
-        advance_column(source, target, coef_ref, spin_ref, first + 2 * pair)
-        advance_column(source, target, coef_ref, spin_ref, first + 2 * pair + 1)
+        for lon in (first + 2 * pair, first + 2 * pair + 1):
+            advance_column(source, target, coef_ref, spin_ref, lon, chosen)
 
 
 def mend_columns(par, states, coef_ref, spin_ref, pieces):
@@ -493,43 +494,49 @@
     return lax.ppermute(value, axis, [(i, i ^ mask) for i in range(lax.axis_size(axis))])
 
 
-def add_four(first, second, third, fourth, *rest):
-    out_ref = rest[len(rest) // 2]
-    out_ref[...] = (first[...] + fourth[...]) + (third[...] + second[...])
-
-
-def sum_over(value, axis, first_bit, beside=None, held=()):
+def add_two(first, second, _, out_ref):
+    out_ref[...] = first[...] + second[...]
+
+
+def add_beside(value, other, beside):
+    return pl.pallas_call(
+        add_two,
+        out_shape=jax.ShapeDtypeStruct(value.shape, value.dtype),
+        in_specs=[VMEM] * 2 + [pl.BlockSpec(memory_space=pl.ANY)],
+        out_specs=VMEM,
+        compiler_params=params(),
+    )(value, other, beside)
+
+
+def sum_over(value, axis, first_bit):
     bits = lax.axis_size(axis).bit_length() - 1
     while first_bit < bits:
         low = 1 << first_bit
         if first_bit + 1 < bits:
             high = low << 1
             three, two, one = (swapped(value, axis, mask) for mask in (low | high, high, low))
-            if beside is None:
-                value = (three + two) + (one + value)
-            else:
-                anywhere = pl.BlockSpec(memory_space=pl.ANY)
-                value, *held = pl.pallas_call(
-                    add_four,
-                    out_shape=[jax.ShapeDtypeStruct(x.shape, x.dtype) for x in (value, *held)],
-                    in_specs=[VMEM] * 4 + [anywhere] * (1 + len(held)),
-                    out_specs=[VMEM] + [anywhere] * len(held),
-                    input_output_aliases={5 + i: 1 + i for i in range(len(held))},
-                    compiler_params=params(),
-                )(value, three, two, one, beside, *held)
-                beside = None
+            value = (three + two) + (one + value)
             first_bit += 2
         else:
             value = value + swapped(value, axis, low)
             first_bit += 1
-    return value, held
-
-
-def sum_devices(kept, sent, beside=(None, None), held=()):
+    return value
+
+
+def sum_devices(kept, sent):
     mine = kept + swapped(sent, "col", 1)
-    mine, held = sum_over(mine, "col", 1, beside[0], held)
-    mine, _ = sum_over(mine, "row", 0, beside[1])
-    return mine, swapped(mine, "col", 1), held
+    mine = sum_over(mine, "col", 1)
+    mine = sum_over(mine, "row", 0)
+    return mine, swapped(mine, "col", 1)
+
+
+def sum_devices_beside(kept, sent, work):
+    mine = kept + swapped(sent, "col", 1)
+    for axis, first_bit in (("row", 0), ("col", 1)):
+        for bit in range(first_bit, lax.axis_size(axis).bit_length() - 1):
+            other = swapped(mine, axis, 1 << bit)
+            mine = add_beside(mine, other, work.pop(0)) if work else mine + other
+    return mine, swapped(mine, "col", 1)
 
 
 def body(tangents, sea_mask, levels, current):
@@ -569,9 +576,18 @@
             ),
         )(*operands)
 
-    def inside(step, state):
-        kernel = functools.partial(apply_inside, step)
-        return call(kernel, (block,), state, coef, spin, specs=[VMEM] * 3, cost=2.0)[0]
+    def inside(step, state, chosen=None, partly=()):
+        return call(
+            functools.partial(apply_inside, step, chosen),
+            (block,),
+            state,
+            coef,
+            spin,
+            *partly,
+            specs=[VMEM] * (3 + len(partly)),
+            aliases={3: 0} if partly else None,
+            cost=2.0,
+        )[0]
 
     def swap_columns(packed):
         return swap_pairs(*packed, "col", True)
@@ -612,6 +628,9 @@
         cost=3.0,
     )
     halos = swap_columns(packed)
+    middle_tiles = tuple(range(1, rows // SUB - 1))
+    outer_tiles = (0,) + tuple(range(rows // SUB - 1, tall // SUB))
+    middle = inside(0, start, middle_tiles)
     start, coef, *packed = call(
         join_rows,
         (block, coefs) + corners,
@@ -619,12 +638,14 @@
         start,
         coef,
         *row_halos,
+        middle,
+        specs=[SMEM] + [VMEM] * 4 + [pl.BlockSpec(memory_space=pl.ANY)],
         aliases={1: 0, 2: 1},
     )
     halos += swap_columns(packed)
     logs = jnp.zeros((1, modes), jnp.float32)
 
-    middle = inside(0, start)
+    middle = inside(0, start, outer_tiles, (middle,))
     state = inside(1, middle)
     _, _, start, coef, *packed, kept, sent = call(
         functools.partial(join_gram, scale),
@@ -642,9 +663,9 @@
     )
     middle = inside(0, start)
     state = inside(1, middle)
-    mine, other, packed = sum_devices(kept, sent, (middle, state), packed)
+
     halos = swap_columns(packed)
-    _, _, state = call(
+    _, _, mended = call(
         mend_only,
         (block,) * 3,
         par,
@@ -656,6 +677,8 @@
         *halos,
         aliases={1: 0, 2: 1, 3: 2},
     )
+    mine, other = sum_devices_beside(kept, sent, [middle, state, mended])
+    state = mended
     inverse, logs = call(
         factor_only,
         (shape_of(modes, modes), shape_of(1, modes)),
@@ -686,7 +709,7 @@
     )[0]
     height = comps * rows * cols // TILES
     tiled = shape_of(TILES, height, modes)
-    mine, other, _ = sum_devices(kept, sent)
+    mine, other = sum_devices(kept, sent)
     out, logs = call(
         finish,
         (tiled, shape_of(1, modes)),

time: 69.6 us -> 71.6 us (1.029)
  waiting for transfers between devices: 10.3 us -> 13.6 us
  starting transfers between devices: 27.2 us -> 25.7 us
    ppermute x16 -> x14, waiting for transfers between devices: 9.99 us -> 12.3 us  [swapped(): lax.ppermute(value, axis, [(i, i ^ mask) for i in range(lax.axis_size(axi...]
    ppermute x4, starting transfers between devices: 5.77 us -> 4.7 us  [swap_pairs(): lax.ppermute(far_value, axis, far)]
    ppermute x4, waiting for transfers between devices: 0.26 us -> 1.25 us  [swap_pairs(): lax.ppermute(far_value, axis, far)]
    ppermute x16 -> x14, starting transfers between devices: 18.1 us -> 17.3 us  [swapped(): lax.ppermute(value, axis, [(i, i ^ mask) for i in range(lax.axis_size(axi...]
    pallas_call x13 -> x14, Pallas kernels: 30.7 us -> 30.8 us  [call(): pl.pallas_call(kernel, out_shape=outs, in_specs=specs or [SMEM] + [VMEM]...]
  transfers between devices with their start and end apart: 24 -> 22, of which waited for: 13 -> 13; matrix products, arithmetic and copies ran while one was open for 0% -> 0% of each run, Pallas kernels for 20% -> 20%
where the time goes in v10:
time: 71.6 us; the launch traced here: 71.2 us
  Pallas kernels  30.9 us (43%)
  starting transfers between devices  25.7 us (36%)
  waiting for transfers between devices  13.6 us (19%)
  between operations  0.97 us (1%)
    pallas_call x14, Pallas kernels, call(): pl.pallas_call(kernel, out_shape=outs, in_specs=specs or [SMEM] + [VMEM]...  30.8 us
    ppermute x14, starting transfers between devices, swapped(): lax.ppermute(value, axis, [(i, i ^ mask) for i in range(lax.axis_size(axi...  17.3 us
    ppermute x14, waiting for transfers between devices, swapped(): lax.ppermute(value, axis, [(i, i ^ mask) for i in range(lax.axis_size(axi...  12.3 us
    ppermute x4, starting transfers between devices, swap_pairs(): lax.ppermute(far_value, axis, far)  4.7 us
    ppermute x4, starting transfers between devices, swap_pairs(): lax.ppermute(near_value, axis, near)  3.72 us
  transfers between devices with their start and end apart: 22, of which 13 were waited for; matrix products, arithmetic and copies ran while one was open for 0% of the time, Pallas kernels for 20%

profile of v10, /device:TPU:0, one launch (start us, length us, event | category | flops | bytes accessed | tf_op | source)
XLA Modules:
  0.0 71.2 jit_solution(10396396164538368339)
XLA Ops:
  0.7 1.7 %shard_map.60 = (f32[13,32,128]{2,1,0:T(8,128)S(1)}, f32[13,32,128]{2,1,0:T(8,128)S(1)}) custom-call(s32[2]{0:T(128)S(1)} %pad_add_fusion.par, f32[3,64,32,128]{3,2,1,0:T(8,128)} %t_ref.3, s32[32,64]{1,0:T(8,128)} %bitcast.9, s32[32,64]{1,0:T(8,128)} %bitcast.11, f32[32,64]{1,0:T(8,128)} %bitcast.13), custom_call_target="tpu_custom_call" | custom-call | flops 1000000000 | bytes 3000000 | tf_op jit(solution)/shard_map/pallas_call | solution.py:566
  2.4 3.1 %collective-permute-start = (f32[13,32,128]{2,1,0:T(8,128)S(1)}, f32[13,32,128]{2,1,0:T(8,128)S(1)}, u32[]{:S(2)}, u32[]{:S(2)}) collective-permute-start(f32[13,32,128]{2,1,0:T(8,128)S(1)} %get-tuple-element.29), channel_id=1, source_target_pairs={{0,8},{8,0},{16,24},{24,16},{1,9},{9,1},{17,25},{25,17},{2,10},{10... | collective-permute-start | bytes 638984 | tf_op jit(solution)/shard_map/ppermute | solution.py:490
  6.1 3.8 %shard_map.59 = (f32[3,36,72,128]{3,2,1,0:T(8,128)S(1)}, f32[3,36,72,128]{3,2,1,0:T(8,128)S(1)}, f32[72,128]{1,0:T(8,128)S(1)}, f32[392,128]{1,0:T(8,128)S(1)}, f32[392,128]{1,0:T(8,128)S(1)}) custom-call(s32[2]{0:T(128)S(1)} %pad_add_fusion.par, f32[3,64,32,128]{3,2,1,0:T(8,128)} %t_ref.3, s32[32,64]{1,0:T(8,128)} %bitcast.10, s32[32,64]{1,0:T(8,128)} %bitcast.12, ...), custom_call_target="tpu_custom_call" | custom-call | flops 3000000000 | bytes 9000000 | tf_op jit(solution)/shard_map/pallas_call | solution.py:566
  10.0 2.5 %collective-permute-start.3 = (f32[392,128]{1,0:T(8,128)S(1)}, f32[392,128]{1,0:T(8,128)S(1)}, u32[]{:S(2)}, u32[]{:S(2)}) collective-permute-start(f32[392,128]{1,0:T(8,128)S(1)} %get-tuple-element.35), channel_id=1, source_target_pairs={{0,7},{1,2},{2,1},{3,4},{4,3},{5,6},{6,5},{7,0},{8,15},{9,10},{10,... | collective-permute-start | bytes 602120 | tf_op jit(solution)/shard_map/ppermute | solution.py:490
  12.6 1.2 %shard_map.61._.refs_0_ = f32[3,36,72,128]{3,2,1,0:T(8,128)S(1)} custom-call(f32[3,36,72,128]{3,2,1,0:T(8,128)S(1)} %get-tuple-element.27.source.state_in, f32[3,36,72,128]{3,2,1,0:T(8,128)S(1)} %get-tuple-element.28.coef_ref.coef_in, f32[72,128]{1,0:T(8,128)S(1)} %get-tuple-element.31.spin_ref), custom_call_target="tpu_custom_call" | custom-call | flops 2000000000 | bytes 6000000 | tf_op jit(solution)/shard_map/pallas_call | solution.py:566
  13.8 1.0 %shard_map.62 = (f32[3,36,72,128]{3,2,1,0:T(8,128)S(1)}, f32[3,36,72,128]{3,2,1,0:T(8,128)S(1)}, f32[56,128]{1,0:T(8,128)S(1)}, f32[56,128]{1,0:T(8,128)S(1)}) custom-call(s32[2]{0:T(128)S(1)} %pad_add_fusion.par, f32[3,36,72,128]{3,2,1,0:T(8,128)S(1)} %get-tuple-element.27.source.state_in, ...), custom_call_target="tpu_custom_call", output_to_operand_aliasing={{0}: (1, {}), {1}: (2, {})} | custom-call | flops 1000000000 | bytes 3000000 | tf_op jit(solution)/shard_map/pallas_call | solution.py:566
  16.2 1.6 %shard_map.64.state_in = f32[3,36,72,128]{3,2,1,0:T(8,128)S(1)} custom-call(f32[3,36,72,128]{3,2,1,0:T(8,128)S(1)} %shard_map.63.source.middle_in, f32[3,36,72,128]{3,2,1,0:T(8,128)S(1)} %get-tuple-element.33.coef_ref.coef_in, f32[72,128]{1,0:T(8,128)S(1)} %get-tuple-element.31.spin_ref), custom_call_target="tpu_custom_call" | custom-call | flops 2000000000 | bytes 6000000 | tf_op jit(solution)/shard_map/pallas_call | solution.py:566
  17.9 1.2 %collective-permute-done.5.d = f32[56,128]{1,0:T(8,128)S(1)} collective-permute-done((f32[56,128]{1,0:T(8,128)S(1)}, f32[56,128]{1,0:T(8,128)S(1)}, u32[]{:S(2)}, u32[]{:S(2)}) %collective-permute-start.5) | collective-permute-done | bytes 28704 | tf_op jit(solution)/shard_map/ppermute | solution.py:490
  19.1 2.2 %shard_map.65 = (f32[3,36,72,128]{3,2,1,0:T(8,128)S(1)}, f32[3,36,72,128]{3,2,1,0:T(8,128)S(1)}, f32[3,36,72,128]{3,2,1,0:T(8,128)S(1)}, f32[3,36,72,128]{3,2,1,...) custom-call(s32[2]{0:T(128)S(1)} %pad_add_fusion.par, ...), custom_call_target="tpu_custom_call", output_to_operand_aliasing={{0}: (1, {}), {1}: (2, {}), {2}: (3, {}), {3}: (4, {})} | custom-call | flops 2000000000 | bytes 6000000 | tf_op jit(solution)/shard_map/pallas_call | solution.py:566
  22.7 4.4 %collective-permute-start.9 = (f32[40,128]{1,0:T(8,128)S(1)}, f32[40,128]{1,0:T(8,128)S(1)}, u32[]{:S(2)}, u32[]{:S(2)}) collective-permute-start(f32[40,128]{1,0:T(8,128)S(1)} %add.27.first), channel_id=1, source_target_pairs={{0,8},{8,0},{16,24},{24,16},{1,9},{9,1},{17,25},{25,17},{2,10},{10... | collective-permute-start | bytes 61448 | tf_op jit(solution)/shard_map/ppermute | solution.py:494
  27.1 1.8 %shard_map.66.source.middle_in._ = f32[3,36,72,128]{3,2,1,0:T(8,128)S(1)} custom-call(f32[3,36,72,128]{3,2,1,0:T(8,128)S(1)} %get-tuple-element.38.source.start_in, f32[3,36,72,128]{3,2,1,0:T(8,128)S(1)} %get-tuple-element.39.coef_ref, f32[72,128]{1,0:T(8,128)S(1)} %get-tuple-element.31.spin_ref), custom_call_target="tpu_custom_call" | custom-call | flops 2000000000 | bytes 6000000 | tf_op jit(solution)/shard_map/pallas_call | solution.py:566
  29.0 2.0 %collective-permute-start.10 = (f32[40,128]{1,0:T(8,128)S(1)}, f32[40,128]{1,0:T(8,128)S(1)}, u32[]{:S(2)}, u32[]{:S(2)}) collective-permute-start(f32[40,128]{1,0:T(8,128)S(1)} %shard_map.69.first), channel_id=1, source_target_pairs={{0,16},{8,24},{16,0},{24,8},{1,17},{9,25},{17,1},{25,9},{2,18},{10... | collective-permute-start | bytes 61448 | tf_op jit(solution)/shard_map/ppermute | solution.py:494
  31.1 1.7 %shard_map.67.state_in._ = f32[3,36,72,128]{3,2,1,0:T(8,128)S(1)} custom-call(f32[3,36,72,128]{3,2,1,0:T(8,128)S(1)} %shard_map.66.source.middle_in._, f32[3,36,72,128]{3,2,1,0:T(8,128)S(1)} %get-tuple-element.39.coef_ref, f32[72,128]{1,0:T(8,128)S(1)} %get-tuple-element.31.spin_ref), custom_call_target="tpu_custom_call" | custom-call | flops 2000000000 | bytes 6000000 | tf_op jit(solution)/shard_map/pallas_call | solution.py:566
  33.8 1.1 %collective-permute-start.11 = (f32[40,128]{1,0:T(8,128)S(1)}, f32[40,128]{1,0:T(8,128)S(1)}, u32[]{:S(2)}, u32[]{:S(2)}) collective-permute-start(f32[40,128]{1,0:T(8,128)S(1)} %shard_map.70.first), channel_id=1, source_target_pairs={{0,2},{1,3},{2,0},{3,1},{4,6},{5,7},{6,4},{7,5},{8,10},{9,11},{10,... | collective-permute-start | bytes 61448 | tf_op jit(solution)/shard_map/ppermute | solution.py:494
  34.9 1.3 %shard_map.68 = (f32[3,36,72,128]{3,2,1,0:T(8,128)S(1)}, f32[3,36,72,128]{3,2,1,0:T(8,128)S(1)}, f32[3,36,72,128]{3,2,1,0:T(8,128)S(1)}) custom-call(s32[2]{0:T(128)S(1)} %pad_add_fusion.par, f32[3,36,72,128]{3,2,1,0:T(8,128)S(1)} %get-tuple-element.38.source.start_in, ...), custom_call_target="tpu_custom_call", output_to_operand_aliasing={{0}: (1, {}), {1}: (2, {}), {2}: (3, {})} | custom-call | flops 1000000000 | bytes 3000000 | tf_op jit(solution)/shard_map/pallas_call | solution.py:566
  36.2 1.4 %collective-permute-done.11.second = f32[40,128]{1,0:T(8,128)S(1)} collective-permute-done((f32[40,128]{1,0:T(8,128)S(1)}, f32[40,128]{1,0:T(8,128)S(1)}, u32[]{:S(2)}, u32[]{:S(2)}) %collective-permute-start.11) | collective-permute-done | bytes 20512 | tf_op jit(solution)/shard_map/ppermute | solution.py:494
  37.6 1.4 %collective-permute-start.12 = (f32[40,128]{1,0:T(8,128)S(1)}, f32[40,128]{1,0:T(8,128)S(1)}, u32[]{:S(2)}, u32[]{:S(2)}) collective-permute-start(f32[40,128]{1,0:T(8,128)S(1)} %shard_map.71), channel_id=1, source_target_pairs={{0,4},{1,5},{2,6},{3,7},{4,0},{5,1},{6,2},{7,3},{8,12},{9,13},{10,... | collective-permute-start | bytes 61448 | tf_op jit(solution)/shard_map/ppermute | solution.py:494
  39.0 2.4 %collective-permute-done.12 = f32[40,128]{1,0:T(8,128)S(1)} collective-permute-done((f32[40,128]{1,0:T(8,128)S(1)}, f32[40,128]{1,0:T(8,128)S(1)}, u32[]{:S(2)}, u32[]{:S(2)}) %collective-permute-start.12) | collective-permute-done | bytes 20512 | tf_op jit(solution)/shard_map/ppermute | solution.py:494
  41.3 1.2 %collective-permute-done.13.other_ref = f32[40,128]{1,0:T(8,128)S(1)} collective-permute-done((f32[40,128]{1,0:T(8,128)S(1)}, f32[40,128]{1,0:T(8,128)S(1)}, u32[]{:S(2)}, u32[]{:S(2)}) %collective-permute-start.13) | collective-permute-done | bytes 20512 | tf_op jit(solution)/shard_map/ppermute | solution.py:494
  42.5 3.6 %shard_map.72 = (f32[128,128]{1,0:T(8,128)S(1)}, f32[1,128]{1,0:T(1,128)S(1)}) custom-call(s32[2]{0:T(128)S(1)} %pad_add_fusion.par, f32[40,128]{1,0:T(8,128)S(1)} %add.28.mine_ref, f32[40,128]{1,0:T(8,128)S(1)} %collective-permute-done.13.other_ref, f32[1,128]{1,0:T(1,128)S(1)} %broadcast_in_dim.3.prior_ref, f32[3,36,72,128]{3,2,1,0:T(8,128)S(1)} %get-tuple-element.42._.state), custom_call_target="tpu_custom_call" | custom-call | flops 10000000 | bytes 30000 | tf_op jit(solution)/shard_map/pallas_call | solution.py:566
  46.1 2.7 %shard_map.73 = (f32[3,32,64,128]{3,2,1,0:T(8,128)S(1)}, f32[40,128]{1,0:T(8,128)S(1)}, f32[40,128]{1,0:T(8,128)S(1)}) custom-call(s32[2]{0:T(128)S(1)} %pad_add_fusion.par, f32[3,36,72,128]{3,2,1,0:T(8,128)S(1)} %get-tuple-element.42._.state, f32[128,128]{1,0:T(8,128)S(1)} %get-tuple-element.45.inverse_ref), custom_call_target="tpu_custom_call" | custom-call | flops 2000000000 | bytes 6000000 | tf_op jit(solution)/shard_map/pallas_call | solution.py:566
  49.0 1.0 %collective-permute-done.14 = f32[40,128]{1,0:T(8,128)S(1)} collective-permute-done((f32[40,128]{1,0:T(8,128)S(1)}, f32[40,128]{1,0:T(8,128)S(1)}, u32[]{:S(2)}, u32[]{:S(2)}) %collective-permute-start.14) | collective-permute-done | bytes 20512 | tf_op jit(solution)/shard_map/ppermute | solution.py:494
  50.1 1.2 %collective-permute-start.15 = (f32[40,128]{1,0:T(8,128)S(1)}, f32[40,128]{1,0:T(8,128)S(1)}, u32[]{:S(2)}, u32[]{:S(2)}) collective-permute-start(f32[40,128]{1,0:T(8,128)S(1)} %add.29), channel_id=1, source_target_pairs={{0,6},{1,7},{2,4},{3,5},{4,2},{5,3},{6,0},{7,1},{8,14},{9,15},{10,... | collective-permute-start | bytes 61448 | tf_op jit(solution)/shard_map/ppermute | solution.py:494
  51.2 1.4 %collective-permute-start.16 = (f32[40,128]{1,0:T(8,128)S(1)}, f32[40,128]{1,0:T(8,128)S(1)}, u32[]{:S(2)}, u32[]{:S(2)}) collective-permute-start(f32[40,128]{1,0:T(8,128)S(1)} %add.29), channel_id=1, source_target_pairs={{0,4},{1,5},{2,6},{3,7},{4,0},{5,1},{6,2},{7,3},{8,12},{9,13},{10,... | collective-permute-start | bytes 61448 | tf_op jit(solution)/shard_map/ppermute | solution.py:494
  53.6 1.2 %collective-permute-done.15 = f32[40,128]{1,0:T(8,128)S(1)} collective-permute-done((f32[40,128]{1,0:T(8,128)S(1)}, f32[40,128]{1,0:T(8,128)S(1)}, u32[]{:S(2)}, u32[]{:S(2)}) %collective-permute-start.15) | collective-permute-done | bytes 20512 | tf_op jit(solution)/shard_map/ppermute | solution.py:494
  55.0 1.4 %collective-permute-done.17 = f32[40,128]{1,0:T(8,128)S(1)} collective-permute-done((f32[40,128]{1,0:T(8,128)S(1)}, f32[40,128]{1,0:T(8,128)S(1)}, u32[]{:S(2)}, u32[]{:S(2)}) %collective-permute-start.17) | collective-permute-done | bytes 20512 | tf_op jit(solution)/shard_map/ppermute | solution.py:494
  56.4 1.2 %collective-permute-start.18 = (f32[40,128]{1,0:T(8,128)S(1)}, f32[40,128]{1,0:T(8,128)S(1)}, u32[]{:S(2)}, u32[]{:S(2)}) collective-permute-start(f32[40,128]{1,0:T(8,128)S(1)} %add_add_fusion.1), channel_id=1, source_target_pairs={{0,24},{8,16},{16,8},{24,0},{1,25},{9,17},{17,9},{25,1},{2,26},{10... | collective-permute-start | bytes 61448 | tf_op jit(solution)/shard_map/ppermute | solution.py:494
  57.6 2.0 %collective-permute-start.19 = (f32[40,128]{1,0:T(8,128)S(1)}, f32[40,128]{1,0:T(8,128)S(1)}, u32[]{:S(2)}, u32[]{:S(2)}) collective-permute-start(f32[40,128]{1,0:T(8,128)S(1)} %add_add_fusion.1), channel_id=1, source_target_pairs={{0,16},{8,24},{16,0},{24,8},{1,17},{9,25},{17,1},{25,9},{2,18},{10... | collective-permute-start | bytes 61448 | tf_op jit(solution)/shard_map/ppermute | solution.py:494
  59.6 1.3 %collective-permute-start.20 = (f32[40,128]{1,0:T(8,128)S(1)}, f32[40,128]{1,0:T(8,128)S(1)}, u32[]{:S(2)}, u32[]{:S(2)}) collective-permute-start(f32[40,128]{1,0:T(8,128)S(1)} %add_add_fusion.1), channel_id=1, source_target_pairs={{0,8},{8,0},{16,24},{24,16},{1,9},{9,1},{17,25},{25,17},{2,10},{10... | collective-permute-start | bytes 61448 | tf_op jit(solution)/shard_map/ppermute | solution.py:494
  60.9 1.2 %collective-permute-done.18 = f32[40,128]{1,0:T(8,128)S(1)} collective-permute-done((f32[40,128]{1,0:T(8,128)S(1)}, f32[40,128]{1,0:T(8,128)S(1)}, u32[]{:S(2)}, u32[]{:S(2)}) %collective-permute-start.18) | collective-permute-done | bytes 20512 | tf_op jit(solution)/shard_map/ppermute | solution.py:494
  63.4 1.1 %shard_map.74 = bf16[3,64,32,256]{3,2,1,0:T(8,128)(2,1)S(1)} custom-call(f32[3,32,64,128]{3,2,1,0:T(8,128)S(1)} %get-tuple-element.49.turned), custom_call_target="tpu_custom_call" | custom-call | flops 1000000000 | bytes 3000000 | tf_op jit(solution)/shard_map/pallas_call | solution.py:566
  64.6 6.5 %shard_map.75 = (f32[12,512,128]{2,1,0:T(8,128)}, f32[1,128]{1,0:T(1,128)}) custom-call(s32[2]{0:T(128)S(1)} %pad_add_fusion.par, f32[40,128]{1,0:T(8,128)S(1)} %add_add_fusion.mine_ref, f32[40,128]{1,0:T(8,128)S(1)} %collective-permute-done.21.other_ref, f32[1,128]{1,0:T(1,128)S(1)} %get-tuple-element.48.prior_ref, bf16[12,512,256]{2,1,0:T(8,128)(2,1)S(1)} %bitcast.8), custom_call_target="tpu_custom_call" | custom-call | flops 1000000000 | bytes 3000000 | tf_op jit(solution)/shard_map/pallas_call | solution.py:566
  (36 shorter events, 7.5 us)
Async XLA Ops:
  2.4 11.4 %collective-permute-start = (f32[13,32,128]{2,1,0:T(8,128)S(1)}, f32[13,32,128]{2,1,0:T(8,128)S(1)}, u32[]{:S(2)}, u32[]{:S(2)}) collective-permute-start(f32[13,32,128]{2,1,0:T(8,128)S(1)} %get-tuple-element.29), channel_id=1, source_target_pairs={{0,8},{8,0},{16,24},{24,16},{1,9},{9,1},{17,25},{25,17},{2,10},{10... | collective-permute-start | bytes 638984 | tf_op jit(solution)/shard_map/ppermute | solution.py:490
  5.5 8.3 %collective-permute-start.1 = (f32[13,32,128]{2,1,0:T(8,128)S(1)}, f32[13,32,128]{2,1,0:T(8,128)S(1)}, u32[]{:S(2)}, u32[]{:S(2)}) collective-permute-start(f32[13,32,128]{2,1,0:T(8,128)S(1)} %get-tuple-element.30), channel_id=1, source_target_pairs={{8,16},{16,8},{9,17},{17,9},{10,18},{18,10},{11,19},{19,11},{12,20... | collective-permute-start | bytes 638984 | tf_op jit(solution)/shard_map/ppermute | solution.py:490
  10.0 7.9 %collective-permute-start.2 = (f32[392,128]{1,0:T(8,128)S(1)}, f32[392,128]{1,0:T(8,128)S(1)}, u32[]{:S(2)}, u32[]{:S(2)}) collective-permute-start(f32[392,128]{1,0:T(8,128)S(1)} %get-tuple-element.34), channel_id=1, source_target_pairs={{0,1},{1,0},{2,3},{3,2},{4,5},{5,4},{6,7},{7,6},{8,9},{9,8},{10,11... | collective-permute-start | bytes 602120 | tf_op jit(solution)/shard_map/ppermute | solution.py:490
  10.0 7.8 %collective-permute-start.3 = (f32[392,128]{1,0:T(8,128)S(1)}, f32[392,128]{1,0:T(8,128)S(1)}, u32[]{:S(2)}, u32[]{:S(2)}) collective-permute-start(f32[392,128]{1,0:T(8,128)S(1)} %get-tuple-element.35), channel_id=1, source_target_pairs={{0,7},{1,2},{2,1},{3,4},{4,3},{5,6},{6,5},{7,0},{8,15},{9,10},{10,... | collective-permute-start | bytes 602120 | tf_op jit(solution)/shard_map/ppermute | solution.py:490
  14.8 3.1 %collective-permute-start.4 = (f32[56,128]{1,0:T(8,128)S(1)}, f32[56,128]{1,0:T(8,128)S(1)}, u32[]{:S(2)}, u32[]{:S(2)}) collective-permute-start(f32[56,128]{1,0:T(8,128)S(1)} %get-tuple-element.36), channel_id=1, source_target_pairs={{0,1},{1,0},{2,3},{3,2},{4,5},{5,4},{6,7},{7,6},{8,9},{9,8},{10,11... | collective-permute-start | bytes 86024 | tf_op jit(solution)/shard_map/ppermute | solution.py:490
  14.8 4.3 %collective-permute-start.5 = (f32[56,128]{1,0:T(8,128)S(1)}, f32[56,128]{1,0:T(8,128)S(1)}, u32[]{:S(2)}, u32[]{:S(2)}) collective-permute-start(f32[56,128]{1,0:T(8,128)S(1)} %get-tuple-element.37), channel_id=1, source_target_pairs={{0,7},{1,2},{2,1},{3,4},{4,3},{5,6},{6,5},{7,0},{8,15},{9,10},{10,... | collective-permute-start | bytes 86024 | tf_op jit(solution)/shard_map/ppermute | solution.py:490
  21.3 1.4 %collective-permute-start.8 = (f32[40,128]{1,0:T(8,128)S(1)}, f32[40,128]{1,0:T(8,128)S(1)}, u32[]{:S(2)}, u32[]{:S(2)}) collective-permute-start(f32[40,128]{1,0:T(8,128)S(1)} %get-tuple-element.44), channel_id=1, source_target_pairs={{0,1},{1,0},{2,3},{3,2},{4,5},{5,4},{6,7},{7,6},{8,9},{9,8},{10,11... | collective-permute-start | bytes 61448 | tf_op jit(solution)/shard_map/ppermute | solution.py:494
  21.3 13.5 %collective-permute-start.6 = (f32[432,128]{1,0:T(8,128)S(1)}, f32[432,128]{1,0:T(8,128)S(1)}, u32[]{:S(2)}, u32[]{:S(2)}) collective-permute-start(f32[432,128]{1,0:T(8,128)S(1)} %get-tuple-element.40), channel_id=1, source_target_pairs={{0,1},{1,0},{2,3},{3,2},{4,5},{5,4},{6,7},{7,6},{8,9},{9,8},{10,11... | collective-permute-start | bytes 663560 | tf_op jit(solution)/shard_map/ppermute | solution.py:490
  21.8 13.0 %collective-permute-start.7 = (f32[432,128]{1,0:T(8,128)S(1)}, f32[432,128]{1,0:T(8,128)S(1)}, u32[]{:S(2)}, u32[]{:S(2)}) collective-permute-start(f32[432,128]{1,0:T(8,128)S(1)} %get-tuple-element.41), channel_id=1, source_target_pairs={{0,7},{1,2},{2,1},{3,4},{4,3},{5,6},{6,5},{7,0},{8,15},{9,10},{10,... | collective-permute-start | bytes 663560 | tf_op jit(solution)/shard_map/ppermute | solution.py:490
  22.7 6.3 %collective-permute-start.9 = (f32[40,128]{1,0:T(8,128)S(1)}, f32[40,128]{1,0:T(8,128)S(1)}, u32[]{:S(2)}, u32[]{:S(2)}) collective-permute-start(f32[40,128]{1,0:T(8,128)S(1)} %add.27.first), channel_id=1, source_target_pairs={{0,8},{8,0},{16,24},{24,16},{1,9},{9,1},{17,25},{25,17},{2,10},{10... | collective-permute-start | bytes 61448 | tf_op jit(solution)/shard_map/ppermute | solution.py:494
  29.0 4.7 %collective-permute-start.10 = (f32[40,128]{1,0:T(8,128)S(1)}, f32[40,128]{1,0:T(8,128)S(1)}, u32[]{:S(2)}, u32[]{:S(2)}) collective-permute-start(f32[40,128]{1,0:T(8,128)S(1)} %shard_map.69.first), channel_id=1, source_target_pairs={{0,16},{8,24},{16,0},{24,8},{1,17},{9,25},{17,1},{25,9},{2,18},{10... | collective-permute-start | bytes 61448 | tf_op jit(solution)/shard_map/ppermute | solution.py:494
  33.8 3.8 %collective-permute-start.11 = (f32[40,128]{1,0:T(8,128)S(1)}, f32[40,128]{1,0:T(8,128)S(1)}, u32[]{:S(2)}, u32[]{:S(2)}) collective-permute-start(f32[40,128]{1,0:T(8,128)S(1)} %shard_map.70.first), channel_id=1, source_target_pairs={{0,2},{1,3},{2,0},{3,1},{4,6},{5,7},{6,4},{7,5},{8,10},{9,11},{10,... | collective-permute-start | bytes 61448 | tf_op jit(solution)/shard_map/ppermute | solution.py:494
  37.6 3.8 %collective-permute-start.12 = (f32[40,128]{1,0:T(8,128)S(1)}, f32[40,128]{1,0:T(8,128)S(1)}, u32[]{:S(2)}, u32[]{:S(2)}) collective-permute-start(f32[40,128]{1,0:T(8,128)S(1)} %shard_map.71), channel_id=1, source_target_pairs={{0,4},{1,5},{2,6},{3,7},{4,0},{5,1},{6,2},{7,3},{8,12},{9,13},{10,... | collective-permute-start | bytes 61448 | tf_op jit(solution)/shard_map/ppermute | solution.py:494
  41.3 1.2 %collective-permute-start.13 = (f32[40,128]{1,0:T(8,128)S(1)}, f32[40,128]{1,0:T(8,128)S(1)}, u32[]{:S(2)}, u32[]{:S(2)}) collective-permute-start(f32[40,128]{1,0:T(8,128)S(1)} %add.28.mine_ref), channel_id=1, source_target_pairs={{0,1},{1,0},{2,3},{3,2},{4,5},{5,4},{6,7},{7,6},{8,9},{9,8},{10,11... | collective-permute-start | bytes 61448 | tf_op jit(solution)/shard_map/ppermute | solution.py:494
  48.8 1.3 %collective-permute-start.14 = (f32[40,128]{1,0:T(8,128)S(1)}, f32[40,128]{1,0:T(8,128)S(1)}, u32[]{:S(2)}, u32[]{:S(2)}) collective-permute-start(f32[40,128]{1,0:T(8,128)S(1)} %get-tuple-element.47), channel_id=1, source_target_pairs={{0,1},{1,0},{2,3},{3,2},{4,5},{5,4},{6,7},{7,6},{8,9},{9,8},{10,11... | collective-permute-start | bytes 61448 | tf_op jit(solution)/shard_map/ppermute | solution.py:494
  50.1 4.7 %collective-permute-start.15 = (f32[40,128]{1,0:T(8,128)S(1)}, f32[40,128]{1,0:T(8,128)S(1)}, u32[]{:S(2)}, u32[]{:S(2)}) collective-permute-start(f32[40,128]{1,0:T(8,128)S(1)} %add.29), channel_id=1, source_target_pairs={{0,6},{1,7},{2,4},{3,5},{4,2},{5,3},{6,0},{7,1},{8,14},{9,15},{10,... | collective-permute-start | bytes 61448 | tf_op jit(solution)/shard_map/ppermute | solution.py:494
  51.2 3.8 %collective-permute-start.16 = (f32[40,128]{1,0:T(8,128)S(1)}, f32[40,128]{1,0:T(8,128)S(1)}, u32[]{:S(2)}, u32[]{:S(2)}) collective-permute-start(f32[40,128]{1,0:T(8,128)S(1)} %add.29), channel_id=1, source_target_pairs={{0,4},{1,5},{2,6},{3,7},{4,0},{5,1},{6,2},{7,3},{8,12},{9,13},{10,... | collective-permute-start | bytes 61448 | tf_op jit(solution)/shard_map/ppermute | solution.py:494
  52.6 3.8 %collective-permute-start.17 = (f32[40,128]{1,0:T(8,128)S(1)}, f32[40,128]{1,0:T(8,128)S(1)}, u32[]{:S(2)}, u32[]{:S(2)}) collective-permute-start(f32[40,128]{1,0:T(8,128)S(1)} %add.29), channel_id=1, source_target_pairs={{0,2},{1,3},{2,0},{3,1},{4,6},{5,7},{6,4},{7,5},{8,10},{9,11},{10,... | collective-permute-start | bytes 61448 | tf_op jit(solution)/shard_map/ppermute | solution.py:494
  56.4 5.6 %collective-permute-start.18 = (f32[40,128]{1,0:T(8,128)S(1)}, f32[40,128]{1,0:T(8,128)S(1)}, u32[]{:S(2)}, u32[]{:S(2)}) collective-permute-start(f32[40,128]{1,0:T(8,128)S(1)} %add_add_fusion.1), channel_id=1, source_target_pairs={{0,24},{8,16},{16,8},{24,0},{1,25},{9,17},{17,9},{25,1},{2,26},{10... | collective-permute-start | bytes 61448 | tf_op jit(solution)/shard_map/ppermute | solution.py:494
  57.6 4.9 %collective-permute-start.19 = (f32[40,128]{1,0:T(8,128)S(1)}, f32[40,128]{1,0:T(8,128)S(1)}, u32[]{:S(2)}, u32[]{:S(2)}) collective-permute-start(f32[40,128]{1,0:T(8,128)S(1)} %add_add_fusion.1), channel_id=1, source_target_pairs={{0,16},{8,24},{16,0},{24,8},{1,17},{9,25},{17,1},{25,9},{2,18},{10... | collective-permute-start | bytes 61448 | tf_op jit(solution)/shard_map/ppermute | solution.py:494
  59.6 3.8 %collective-permute-start.20 = (f32[40,128]{1,0:T(8,128)S(1)}, f32[40,128]{1,0:T(8,128)S(1)}, u32[]{:S(2)}, u32[]{:S(2)}) collective-permute-start(f32[40,128]{1,0:T(8,128)S(1)} %add_add_fusion.1), channel_id=1, source_target_pairs={{0,8},{8,0},{16,24},{24,16},{1,9},{9,1},{17,25},{25,17},{2,10},{10... | collective-permute-start | bytes 61448 | tf_op jit(solution)/shard_map/ppermute | solution.py:494
  63.4 1.2 %collective-permute-start.21 = (f32[40,128]{1,0:T(8,128)S(1)}, f32[40,128]{1,0:T(8,128)S(1)}, u32[]{:S(2)}, u32[]{:S(2)}) collective-permute-start(f32[40,128]{1,0:T(8,128)S(1)} %add_add_fusion.mine_ref), channel_id=1, source_target_pairs={{0,1},{1,0},{2,3},{3,2},{4,5},{5,4},{6,7},{7,6},{8,9},{9,8},{10,11... | collective-permute-start | bytes 61448 | tf_op jit(solution)/shard_map/ppermute | solution.py:494

commit v11 on v9

--- a/solution.py
+++ b/solution.py
@@ -20,7 +20,8 @@
 FIELDS = 3
 HALO = STEPS * RENORMS
 SIDE = STEPS
-TILES = 12
+TILES = 24
+BATCH = 16
 VMEM_LIMIT = 16 * 1024 * 1024
 
 HBM = pl.BlockSpec(memory_space=pltpu.HBM)
@@ -98,13 +99,10 @@
 
 
 def spread_fields(
-    total_rows, par, t_ref, sea_ref, levels_ref, current_ref, state, coef, spin, col_a, col_b, wide, block, sea, levels, current, sems, field_sems
+    total_rows, par, t_ref, sea_ref, levels_ref, current_ref, state, coef, spin, col_a, col_b, wide, sea, levels, current, field_sems
 ):
     comps, rows, cols, _ = t_ref.shape
     field_copies = fetch((sea_ref, levels_ref, current_ref), (sea, levels, current), field_sems)
-    copies = fetch(
-        [t_ref.at[comp] for comp in range(comps)], [block.at[comp] for comp in range(comps)], sems
-    )
     line = lax.broadcasted_iota(jnp.int32, spin.shape, 0)
     line = jnp.where(line < rows + HALO, line, line - (rows + 2 * HALO))
     latitude = (par[0] * rows + line).astype(jnp.float32)
@@ -118,9 +116,8 @@
         for lon in range(cols):
             coef[field, SIDE + lon, pl.ds(0, rows), :] = lane_spread(natural, lon)
     for comp in range(comps):
-        copies[comp].wait()
         for row in range(0, rows, SUB):
-            cells = block[comp, pl.ds(row, SUB)]
+            cells = t_ref[comp, pl.ds(row, SUB)]
             state[comp, pl.ds(SIDE, cols), pl.ds(row, SUB), :] = jnp.transpose(cells, (1, 0, 2))
     send_columns(par, state, (col_a, col_b), 0, rows)
     tail = comps * SIDE * rows
@@ -147,7 +144,7 @@
                 ]
 
 
-def join_rows(par, state_in, coef_in, row_a, row_b, state, coef, col_a, col_b):
+def join_rows(par, state_in, coef_in, row_a, row_b, _, state, coef, col_a, col_b):
     comps, length, tall, _ = state.shape
     cols, rows = length - 2 * SIDE, tall - 2 * HALO
     norths, easts = sides_of(par)
@@ -189,12 +186,12 @@
     )
 
 
-def advance_column(source, target, coef_ref, spin_ref, lon):
+def advance_column(source, target, coef_ref, spin_ref, lon, chosen=None):
     comps, length, tall, _ = source.shape
     flat = source.reshape(comps * length * tall, LANES)
     sub = lax.broadcasted_iota(jnp.int32, (SUB, LANES), 0)
     tiles = tall // SUB
-    for tile in range(tiles):
+    for tile in chosen or range(tiles):
         lines = pl.ds(SUB * tile, SUB)
         own, east, west = (
             [source[comp, lon + shift, lines, :] for comp in range(comps)] for shift in (0, 1, -1)
@@ -229,14 +226,15 @@
             target[comp, lon, lines, :] = new[comp]
 
 
-def apply_inside(step, source, coef_ref, spin_ref, target):
+def apply_inside(step, chosen, source, coef_ref, spin_ref, *refs):
     first = SIDE + step + 1
     count = source.shape[1] - 2 * first
+    target = refs[-1]
 
     @pl.loop(0, count // 2)
     def _(pair):
-        advance_column(source, target, coef_ref, spin_ref, first + 2 * pair)
-        advance_column(source, target, coef_ref, spin_ref, first + 2 * pair + 1)
+        for lon in (first + 2 * pair, first + 2 * pair + 1):
+            advance_column(source, target, coef_ref, spin_ref, lon, chosen)
 
 
 def mend_columns(par, states, coef_ref, spin_ref, pieces):
@@ -286,9 +284,9 @@
     comps, length, tall, _ = state.shape
     rows = tall - 2 * HALO
     for comp in range(comps):
-        for lon in range(0, length - 2 * SIDE, SUB):
-            cells = state[comp, pl.ds(SIDE + lon, SUB), pl.ds(0, rows), :]
-            yield comp, lon, cells.reshape(SUB * rows, LANES)
+        for lon in range(0, length - 2 * SIDE, BATCH):
+            cells = state[comp, pl.ds(SIDE + lon, BATCH), pl.ds(0, rows), :]
+            yield comp, lon, cells.reshape(BATCH * rows, LANES)
 
 
 def split_halves(value):
@@ -344,12 +342,13 @@
     lane = lax.broadcasted_iota(jnp.int32, (SUB, LANES), 1)
     sub = lax.broadcasted_iota(jnp.int32, (SUB, LANES), 0)
     rows = [gram[SUB * i : SUB * (i + 1)] for i in range(count)]
+    columns = [lane_spread(rows[0], l) for l in range(SUB)]
     for block in range(count):
         base = SUB * block
         here = (lane >= base) & (lane < base + SUB)
-        shelf = 2 * SUB * base
+        shelf = 3 * SUB * base
         for l in range(SUB):
-            board[pl.ds(shelf + SUB * l, SUB), :] = lane_spread(rows[block], base + l)
+            board[pl.ds(shelf + SUB * l, SUB), :] = columns[l]
         low = [
             [board[pl.ds(shelf + SUB * l + k, SUB, stride=0), :] for l in range(k + 1)]
             for k in range(SUB)
@@ -371,14 +370,22 @@
         for k in range(1, SUB):
             merged = jnp.where(sub == k, scaled[k], merged)
         work[pl.ds(base, SUB), :] = merged
+        shelf += SUB
         for i in range(block + 1, count):
             weights = []
-            rest = jnp.where(here, 0.0, rows[i])
             for l in range(SUB):
                 weight = lane_spread(rows[i], base + l)
                 for m in range(l):
                     weight = weight - weights[m] * low[l][m]
                 weights.append(weight * inv[l])
+            if i == block + 1:
+                columns = [lane_spread(rows[i], base + SUB + l) for l in range(SUB)]
+                for l in range(SUB):
+                    board[pl.ds(shelf + SUB * l, SUB), :] = weights[l]
+                    for k in range(SUB):
+                        across = board[pl.ds(shelf + SUB * l + k, SUB, stride=0), :]
+                        columns[k] = columns[k] - weights[l] * across
+            rest = jnp.where(here, 0.0, rows[i])
             for l in range(SUB):
                 rest = rest - weights[l] * scaled[l]
             rows[i] = rest
@@ -440,7 +447,7 @@
     gram = 0.0
     for comp, lon, cells in tiles_of(state):
         new = times_factor(jnp.concatenate(split_halves(cells), axis=1), factor[...])
-        out_ref[comp, pl.ds(lon, SUB)] = new.reshape((SUB,) + out_ref.shape[2:])
+        out_ref[comp, pl.ds(lon, BATCH)] = new.reshape((BATCH,) + out_ref.shape[2:])
         gram += gram_of(*split_halves(new))
     write_halves(par, gram, scale, kept, sent, total)
 
@@ -466,7 +473,6 @@
     par, mine_ref, other_ref, prior_ref, t_ref, out_ref, logs_ref, gram, work, board, factor, fresh, sems
 ):
     inverse, diagonal = factorize(par, mine_ref, other_ref, gram, work, board)
-    logs_ref[...] = prior_ref[...] - jnp.log(diagonal)
     factor[...] = paired(inverse)
 
     def out_copy(tile):
@@ -475,6 +481,7 @@
     for tile in range(TILES):
         fresh[tile] = times_factor(t_ref[tile], factor[...])
         out_copy(tile).start(priority=tile % 2)
+    logs_ref[...] = prior_ref[...] - jnp.log(diagonal)
 
     for tile in range(TILES):
         out_copy(tile).wait()
@@ -550,7 +557,7 @@
     rows_sent = (shape_of(comps * HALO + 1, cols, modes),) * 2
     halves = (shape_of(modes // 4 + SUB, modes),) * 2
     square = pltpu.VMEM((modes, modes), jnp.float32)
-    board = pltpu.VMEM((2 * SUB * modes, LANES), jnp.float32)
+    board = pltpu.VMEM((3 * SUB * modes, LANES), jnp.float32)
     factor = pltpu.VMEM((2 * modes, 2 * modes), jnp.bfloat16)
 
     def call(
@@ -569,9 +576,18 @@
             ),
         )(*operands)
 
-    def inside(step, state):
-        kernel = functools.partial(apply_inside, step)
-        return call(kernel, (block,), state, coef, spin, specs=[VMEM] * 3, cost=2.0)[0]
+    def inside(step, state, chosen=None, partly=()):
+        return call(
+            functools.partial(apply_inside, step, chosen),
+            (block,),
+            state,
+            coef,
+            spin,
+            *partly,
+            specs=[VMEM] * (3 + len(partly)),
+            aliases={3: 0} if partly else None,
+            cost=2.0,
+        )[0]
 
     def swap_columns(packed):
         return swap_pairs(*packed, "col", True)
@@ -594,24 +610,25 @@
             pltpu.SemaphoreType.DMA((2 * comps,)),
             pltpu.SemaphoreType.DMA((FIELDS,)),
         ],
+        cost=5.0,
     )
     row_halos = swap_pairs(*packed, "row", False)
     start, coef, spin, *packed = call(
         functools.partial(spread_fields, total_rows),
         (block, coefs, shape_of(tall, LANES)) + own_columns,
         par,
-        source,
+        tangents,
         *fields,
-        specs=[SMEM] + [HBM] * 4,
-        scratch=[
-            pltpu.VMEM((FIELDS, cols, LANES), jnp.float32),
-            pltpu.VMEM(tangents.shape, jnp.float32),
-        ]
+        specs=[SMEM, VMEM] + [HBM] * 3,
+        scratch=[pltpu.VMEM((FIELDS, cols, LANES), jnp.float32)]
         + upright
-        + [pltpu.SemaphoreType.DMA((comps,)), pltpu.SemaphoreType.DMA((FIELDS,))],
+        + [pltpu.SemaphoreType.DMA((FIELDS,))],
         cost=3.0,
     )
     halos = swap_columns(packed)
+    middle_tiles = tuple(range(1, rows // SUB - 1))
+    outer_tiles = (0,) + tuple(range(rows // SUB - 1, tall // SUB))
+    middle = inside(0, start, middle_tiles)
     start, coef, *packed = call(
         join_rows,
         (block, coefs) + corners,
@@ -619,12 +636,14 @@
         start,
         coef,
         *row_halos,
+        middle,
+        specs=[SMEM] + [VMEM] * 4 + [pl.BlockSpec(memory_space=pl.ANY)],
         aliases={1: 0, 2: 1},
     )
     halos += swap_columns(packed)
     logs = jnp.zeros((1, modes), jnp.float32)
 
-    middle = inside(0, start)
+    middle = inside(0, start, outer_tiles, (middle,))
     state = inside(1, middle)
     _, _, start, coef, *packed, kept, sent = call(
         functools.partial(join_gram, scale),
@@ -642,6 +661,7 @@
     )
     middle = inside(0, start)
     state = inside(1, middle)
+
     mine, other, packed = sum_devices(kept, sent, (middle, state), packed)
     halos = swap_columns(packed)
     _, _, state = call(

time: 69.6 us -> 69.1 us (level)
    ppermute x4, waiting for transfers between devices: 0.26 us -> 1.25 us  [swap_pairs(): lax.ppermute(far_value, axis, far)]
    pallas_call x13 -> x14, Pallas kernels: 30.7 us -> 30.5 us  [call(): pl.pallas_call(kernel, out_shape=outs, in_specs=specs or [SMEM] + [VMEM]...]
  transfers between devices with their start and end apart: 24 -> 24, of which waited for: 13 -> 12; matrix products, arithmetic and copies ran while one was open for 0% -> 0% of each run, Pallas kernels for 20% -> 20%
where the time goes in v11:
time: 69.1 us; the launch traced here: 68.8 us
  Pallas kernels  30.6 us (44%)
  starting transfers between devices  26.6 us (38%)
  waiting for transfers between devices  10.6 us (15%)
  between operations  1.03 us (1%)
    pallas_call x14, Pallas kernels, call(): pl.pallas_call(kernel, out_shape=outs, in_specs=specs or [SMEM] + [VMEM]...  30.5 us
    ppermute x16, starting transfers between devices, swapped(): lax.ppermute(value, axis, [(i, i ^ mask) for i in range(lax.axis_size(axi...  18 us
    ppermute x16, waiting for transfers between devices, swapped(): lax.ppermute(value, axis, [(i, i ^ mask) for i in range(lax.axis_size(axi...  9.31 us
    ppermute x4, starting transfers between devices, swap_pairs(): lax.ppermute(far_value, axis, far)  5.26 us
    ppermute x4, starting transfers between devices, swap_pairs(): lax.ppermute(near_value, axis, near)  3.29 us
  transfers between devices with their start and end apart: 24, of which 12 were waited for; matrix products, arithmetic and copies ran while one was open for 0% of the time, Pallas kernels for 20%

profile of v11, /device:TPU:0, one launch (start us, length us, event | category | flops | bytes accessed | tf_op | source)
XLA Modules:
  0.0 68.8 jit_solution(5613749982059277149)
XLA Ops:
  0.7 1.9 %shard_map.60 = (f32[13,32,128]{2,1,0:T(8,128)S(1)}, f32[13,32,128]{2,1,0:T(8,128)S(1)}) custom-call(s32[2]{0:T(128)S(1)} %pad_add_fusion.par, f32[3,64,32,128]{3,2,1,0:T(8,128)} %t_ref.3, s32[32,64]{1,0:T(8,128)} %bitcast.9, s32[32,64]{1,0:T(8,128)} %bitcast.11, f32[32,64]{1,0:T(8,128)} %bitcast.13), custom_call_target="tpu_custom_call" | custom-call | flops 5000000000 | bytes 15000000 | tf_op jit(solution)/shard_map/pallas_call | solution.py:566
  2.6 3.1 %collective-permute-start = (f32[13,32,128]{2,1,0:T(8,128)S(1)}, f32[13,32,128]{2,1,0:T(8,128)S(1)}, u32[]{:S(2)}, u32[]{:S(2)}) collective-permute-start(f32[13,32,128]{2,1,0:T(8,128)S(1)} %get-tuple-element.32), channel_id=1, source_target_pairs={{0,8},{8,0},{16,24},{24,16},{1,9},{9,1},{17,25},{25,17},{2,10},{10... | collective-permute-start | bytes 638984 | tf_op jit(solution)/shard_map/ppermute | solution.py:496
  6.4 3.1 %shard_map.59 = (f32[3,36,72,128]{3,2,1,0:T(8,128)S(1)}, f32[3,36,72,128]{3,2,1,0:T(8,128)S(1)}, f32[72,128]{1,0:T(8,128)S(1)}, f32[392,128]{1,0:T(8,128)S(1)}, f32[392,128]{1,0:T(8,128)S(1)}) custom-call(s32[2]{0:T(128)S(1)} %pad_add_fusion.par, f32[3,64,32,128]{3,2,1,0:T(8,128)S(1)} %copy-done, s32[32,64]{1,0:T(8,128)} %bitcast.10, s32[32,64]{1,0:T(8,128)} %bitcast.12, ...), custom_call_target="tpu_custom_call" | custom-call | flops 3000000000 | bytes 9000000 | tf_op jit(solution)/shard_map/pallas_call | solution.py:566
  9.6 2.5 %collective-permute-start.3 = (f32[392,128]{1,0:T(8,128)S(1)}, f32[392,128]{1,0:T(8,128)S(1)}, u32[]{:S(2)}, u32[]{:S(2)}) collective-permute-start(f32[392,128]{1,0:T(8,128)S(1)} %get-tuple-element.38), channel_id=1, source_target_pairs={{0,7},{1,2},{2,1},{3,4},{4,3},{5,6},{6,5},{7,0},{8,15},{9,10},{10,... | collective-permute-start | bytes 602120 | tf_op jit(solution)/shard_map/ppermute | solution.py:496
  12.1 1.2 %shard_map.61._.refs_0_ = f32[3,36,72,128]{3,2,1,0:T(8,128)S(1)} custom-call(f32[3,36,72,128]{3,2,1,0:T(8,128)S(1)} %get-tuple-element.30.source.state_in, f32[3,36,72,128]{3,2,1,0:T(8,128)S(1)} %get-tuple-element.31.coef_ref.coef_in, f32[72,128]{1,0:T(8,128)S(1)} %get-tuple-element.34.spin_ref), custom_call_target="tpu_custom_call" | custom-call | flops 2000000000 | bytes 6000000 | tf_op jit(solution)/shard_map/pallas_call | solution.py:566
  13.3 1.0 %shard_map.62 = (f32[3,36,72,128]{3,2,1,0:T(8,128)S(1)}, f32[3,36,72,128]{3,2,1,0:T(8,128)S(1)}, f32[56,128]{1,0:T(8,128)S(1)}, f32[56,128]{1,0:T(8,128)S(1)}) custom-call(s32[2]{0:T(128)S(1)} %pad_add_fusion.par, f32[3,36,72,128]{3,2,1,0:T(8,128)S(1)} %get-tuple-element.30.source.state_in, ...), custom_call_target="tpu_custom_call", output_to_operand_aliasing={{0}: (1, {}), {1}: (2, {})} | custom-call | flops 1000000000 | bytes 3000000 | tf_op jit(solution)/shard_map/pallas_call | solution.py:566
  15.7 1.6 %shard_map.64.state_in = f32[3,36,72,128]{3,2,1,0:T(8,128)S(1)} custom-call(f32[3,36,72,128]{3,2,1,0:T(8,128)S(1)} %shard_map.63.source.middle_in, f32[3,36,72,128]{3,2,1,0:T(8,128)S(1)} %get-tuple-element.36.coef_ref.coef_in, f32[72,128]{1,0:T(8,128)S(1)} %get-tuple-element.34.spin_ref), custom_call_target="tpu_custom_call" | custom-call | flops 2000000000 | bytes 6000000 | tf_op jit(solution)/shard_map/pallas_call | solution.py:566
  17.4 1.2 %collective-permute-done.5.d = f32[56,128]{1,0:T(8,128)S(1)} collective-permute-done((f32[56,128]{1,0:T(8,128)S(1)}, f32[56,128]{1,0:T(8,128)S(1)}, u32[]{:S(2)}, u32[]{:S(2)}) %collective-permute-start.5) | collective-permute-done | bytes 28704 | tf_op jit(solution)/shard_map/ppermute | solution.py:496
  18.6 2.2 %shard_map.65 = (f32[3,36,72,128]{3,2,1,0:T(8,128)S(1)}, f32[3,36,72,128]{3,2,1,0:T(8,128)S(1)}, f32[3,36,72,128]{3,2,1,0:T(8,128)S(1)}, f32[3,36,72,128]{3,2,1,...) custom-call(s32[2]{0:T(128)S(1)} %pad_add_fusion.par, ...), custom_call_target="tpu_custom_call", output_to_operand_aliasing={{0}: (1, {}), {1}: (2, {}), {2}: (3, {}), {3}: (4, {})} | custom-call | flops 2000000000 | bytes 6000000 | tf_op jit(solution)/shard_map/pallas_call | solution.py:566
  20.9 1.2 %collective-permute-done.6 = f32[40,128]{1,0:T(8,128)S(1)} collective-permute-done((f32[40,128]{1,0:T(8,128)S(1)}, f32[40,128]{1,0:T(8,128)S(1)}, u32[]{:S(2)}, u32[]{:S(2)}) %collective-permute-start.6) | collective-permute-done | bytes 20512 | tf_op jit(solution)/shard_map/ppermute | solution.py:500
  22.0 0.9 %collective-permute-start.7 = (f32[40,128]{1,0:T(8,128)S(1)}, f32[40,128]{1,0:T(8,128)S(1)}, u32[]{:S(2)}, u32[]{:S(2)}) collective-permute-start(f32[40,128]{1,0:T(8,128)S(1)} %add.24.first), channel_id=1, source_target_pairs={{0,6},{1,7},{2,4},{3,5},{4,2},{5,3},{6,0},{7,1},{8,14},{9,15},{10,... | collective-permute-start | bytes 61448 | tf_op jit(solution)/shard_map/ppermute | solution.py:500
  22.9 1.4 %collective-permute-start.8 = (f32[40,128]{1,0:T(8,128)S(1)}, f32[40,128]{1,0:T(8,128)S(1)}, u32[]{:S(2)}, u32[]{:S(2)}) collective-permute-start(f32[40,128]{1,0:T(8,128)S(1)} %add.24.first), channel_id=1, source_target_pairs={{0,4},{1,5},{2,6},{3,7},{4,0},{5,1},{6,2},{7,3},{8,12},{9,13},{10,... | collective-permute-start | bytes 61448 | tf_op jit(solution)/shard_map/ppermute | solution.py:500
  24.3 1.2 %collective-permute-start.9 = (f32[40,128]{1,0:T(8,128)S(1)}, f32[40,128]{1,0:T(8,128)S(1)}, u32[]{:S(2)}, u32[]{:S(2)}) collective-permute-start(f32[40,128]{1,0:T(8,128)S(1)} %add.24.first), channel_id=1, source_target_pairs={{0,2},{1,3},{2,0},{3,1},{4,6},{5,7},{6,4},{7,5},{8,10},{9,11},{10,... | collective-permute-start | bytes 61448 | tf_op jit(solution)/shard_map/ppermute | solution.py:500
  25.5 1.8 %shard_map.66.source.rest_0_.middle_in = f32[3,36,72,128]{3,2,1,0:T(8,128)S(1)} custom-call(f32[3,36,72,128]{3,2,1,0:T(8,128)S(1)} %get-tuple-element.41.source.start_in, f32[3,36,72,128]{3,2,1,0:T(8,128)S(1)} %get-tuple-element.42.coef_ref, f32[72,128]{1,0:T(8,128)S(1)} %get-tuple-element.34.spin_ref), custom_call_target="tpu_custom_call" | custom-call | flops 2000000000 | bytes 6000000 | tf_op jit(solution)/shard_map/pallas_call | solution.py:566
  28.2 1.4 %collective-permute-start.11 = (f32[432,128]{1,0:T(8,128)S(1)}, f32[432,128]{1,0:T(8,128)S(1)}, u32[]{:S(2)}, u32[]{:S(2)}) collective-permute-start(f32[432,128]{1,0:T(8,128)S(1)} %get-tuple-element.48), channel_id=1, source_target_pairs={{0,7},{1,2},{2,1},{3,4},{4,3},{5,6},{6,5},{7,0},{8,15},{9,10},{10,... | collective-permute-start | bytes 663560 | tf_op jit(solution)/shard_map/ppermute | solution.py:496
  29.6 2.5 %collective-permute-start.12 = (f32[40,128]{1,0:T(8,128)S(1)}, f32[40,128]{1,0:T(8,128)S(1)}, u32[]{:S(2)}, u32[]{:S(2)}) collective-permute-start(f32[40,128]{1,0:T(8,128)S(1)} %get-tuple-element.50.first), channel_id=1, source_target_pairs={{0,24},{8,16},{16,8},{24,0},{1,25},{9,17},{17,9},{25,1},{2,26},{10... | collective-permute-start | bytes 61448 | tf_op jit(solution)/shard_map/ppermute | solution.py:500
  32.1 3.4 %collective-permute-start.13 = (f32[40,128]{1,0:T(8,128)S(1)}, f32[40,128]{1,0:T(8,128)S(1)}, u32[]{:S(2)}, u32[]{:S(2)}) collective-permute-start(f32[40,128]{1,0:T(8,128)S(1)} %get-tuple-element.50.first), channel_id=1, source_target_pairs={{0,16},{8,24},{16,0},{24,8},{1,17},{9,25},{17,1},{25,9},{2,18},{10... | collective-permute-start | bytes 61448 | tf_op jit(solution)/shard_map/ppermute | solution.py:500
  35.5 1.7 %shard_map.67.state_in.rest_0_ = f32[3,36,72,128]{3,2,1,0:T(8,128)S(1)} custom-call(f32[3,36,72,128]{3,2,1,0:T(8,128)S(1)} %shard_map.66.source.rest_0_.middle_in, f32[3,36,72,128]{3,2,1,0:T(8,128)S(1)} %get-tuple-element.42.coef_ref, f32[72,128]{1,0:T(8,128)S(1)} %get-tuple-element.34.spin_ref), custom_call_target="tpu_custom_call" | custom-call | flops 2000000000 | bytes 6000000 | tf_op jit(solution)/shard_map/pallas_call | solution.py:566
  37.7 1.6 %collective-permute-done.14.fourth = f32[40,128]{1,0:T(8,128)S(1)} collective-permute-done((f32[40,128]{1,0:T(8,128)S(1)}, f32[40,128]{1,0:T(8,128)S(1)}, u32[]{:S(2)}, u32[]{:S(2)}) %collective-permute-start.14) | collective-permute-done | bytes 20512 | tf_op jit(solution)/shard_map/ppermute | solution.py:500
  39.4 1.3 %shard_map.69 = (f32[3,36,72,128]{3,2,1,0:T(8,128)S(1)}, f32[3,36,72,128]{3,2,1,0:T(8,128)S(1)}, f32[3,36,72,128]{3,2,1,0:T(8,128)S(1)}) custom-call(s32[2]{0:T(128)S(1)} %pad_add_fusion.par, f32[3,36,72,128]{3,2,1,0:T(8,128)S(1)} %get-tuple-element.41.source.start_in, ...), custom_call_target="tpu_custom_call", output_to_operand_aliasing={{0}: (1, {}), {1}: (2, {}), {2}: (3, {})} | custom-call | flops 1000000000 | bytes 3000000 | tf_op jit(solution)/shard_map/pallas_call | solution.py:566
  40.7 3.7 %shard_map.71 = (f32[128,128]{1,0:T(8,128)S(1)}, f32[1,128]{1,0:T(1,128)S(1)}) custom-call(s32[2]{0:T(128)S(1)} %pad_add_fusion.par, f32[40,128]{1,0:T(8,128)S(1)} %shard_map.70.mine_ref, f32[40,128]{1,0:T(8,128)S(1)} %collective-permute-done.15.other_ref, f32[1,128]{1,0:T(1,128)S(1)} %broadcast_in_dim.3.prior_ref, ...), custom_call_target="tpu_custom_call" | custom-call | flops 10000000 | bytes 30000 | tf_op jit(solution)/shard_map/pallas_call | solution.py:566
  44.4 2.8 %shard_map.72 = (f32[3,32,64,128]{3,2,1,0:T(8,128)S(1)}, f32[40,128]{1,0:T(8,128)S(1)}, f32[40,128]{1,0:T(8,128)S(1)}) custom-call(s32[2]{0:T(128)S(1)} %pad_add_fusion.par, f32[3,36,72,128]{3,2,1,0:T(8,128)S(1)} %get-tuple-element.49._.state, f32[128,128]{1,0:T(8,128)S(1)} %get-tuple-element.51.inverse_ref), custom_call_target="tpu_custom_call" | custom-call | flops 2000000000 | bytes 6000000 | tf_op jit(solution)/shard_map/pallas_call | solution.py:566
  49.5 1.4 %collective-permute-start.18 = (f32[40,128]{1,0:T(8,128)S(1)}, f32[40,128]{1,0:T(8,128)S(1)}, u32[]{:S(2)}, u32[]{:S(2)}) collective-permute-start(f32[40,128]{1,0:T(8,128)S(1)} %add.25), channel_id=1, source_target_pairs={{0,4},{1,5},{2,6},{3,7},{4,0},{5,1},{6,2},{7,3},{8,12},{9,13},{10,... | collective-permute-start | bytes 61448 | tf_op jit(solution)/shard_map/ppermute | solution.py:500
  50.8 1.3 %collective-permute-start.19 = (f32[40,128]{1,0:T(8,128)S(1)}, f32[40,128]{1,0:T(8,128)S(1)}, u32[]{:S(2)}, u32[]{:S(2)}) collective-permute-start(f32[40,128]{1,0:T(8,128)S(1)} %add.25), channel_id=1, source_target_pairs={{0,2},{1,3},{2,0},{3,1},{4,6},{5,7},{6,4},{7,5},{8,10},{9,11},{10,... | collective-permute-start | bytes 61448 | tf_op jit(solution)/shard_map/ppermute | solution.py:500
  52.1 1.3 %collective-permute-done.17 = f32[40,128]{1,0:T(8,128)S(1)} collective-permute-done((f32[40,128]{1,0:T(8,128)S(1)}, f32[40,128]{1,0:T(8,128)S(1)}, u32[]{:S(2)}, u32[]{:S(2)}) %collective-permute-start.17) | collective-permute-done | bytes 20512 | tf_op jit(solution)/shard_map/ppermute | solution.py:500
  53.5 1.2 %collective-permute-done.19 = f32[40,128]{1,0:T(8,128)S(1)} collective-permute-done((f32[40,128]{1,0:T(8,128)S(1)}, f32[40,128]{1,0:T(8,128)S(1)}, u32[]{:S(2)}, u32[]{:S(2)}) %collective-permute-start.19) | collective-permute-done | bytes 20512 | tf_op jit(solution)/shard_map/ppermute | solution.py:500
  54.6 1.5 %collective-permute-start.20 = (f32[40,128]{1,0:T(8,128)S(1)}, f32[40,128]{1,0:T(8,128)S(1)}, u32[]{:S(2)}, u32[]{:S(2)}) collective-permute-start(f32[40,128]{1,0:T(8,128)S(1)} %add_add_fusion.1), channel_id=1, source_target_pairs={{0,24},{8,16},{16,8},{24,0},{1,25},{9,17},{17,9},{25,1},{2,26},{10... | collective-permute-start | bytes 61448 | tf_op jit(solution)/shard_map/ppermute | solution.py:500
  56.1 1.0 %collective-permute-start.21 = (f32[40,128]{1,0:T(8,128)S(1)}, f32[40,128]{1,0:T(8,128)S(1)}, u32[]{:S(2)}, u32[]{:S(2)}) collective-permute-start(f32[40,128]{1,0:T(8,128)S(1)} %add_add_fusion.1), channel_id=1, source_target_pairs={{0,16},{8,24},{16,0},{24,8},{1,17},{9,25},{17,1},{25,9},{2,18},{10... | collective-permute-start | bytes 61448 | tf_op jit(solution)/shard_map/ppermute | solution.py:500
  57.1 2.0 %collective-permute-start.22 = (f32[40,128]{1,0:T(8,128)S(1)}, f32[40,128]{1,0:T(8,128)S(1)}, u32[]{:S(2)}, u32[]{:S(2)}) collective-permute-start(f32[40,128]{1,0:T(8,128)S(1)} %add_add_fusion.1), channel_id=1, source_target_pairs={{0,8},{8,0},{16,24},{24,16},{1,9},{9,1},{17,25},{25,17},{2,10},{10... | collective-permute-start | bytes 61448 | tf_op jit(solution)/shard_map/ppermute | solution.py:500
  59.1 1.2 %collective-permute-done.20 = f32[40,128]{1,0:T(8,128)S(1)} collective-permute-done((f32[40,128]{1,0:T(8,128)S(1)}, f32[40,128]{1,0:T(8,128)S(1)}, u32[]{:S(2)}, u32[]{:S(2)}) %collective-permute-start.20) | collective-permute-done | bytes 20512 | tf_op jit(solution)/shard_map/ppermute | solution.py:500
  61.1 1.1 %shard_map.73 = bf16[3,64,32,256]{3,2,1,0:T(8,128)(2,1)S(1)} custom-call(f32[3,32,64,128]{3,2,1,0:T(8,128)S(1)} %get-tuple-element.55.turned), custom_call_target="tpu_custom_call" | custom-call | flops 1000000000 | bytes 3000000 | tf_op jit(solution)/shard_map/pallas_call | solution.py:566
  62.3 6.4 %shard_map.74 = (f32[24,256,128]{2,1,0:T(8,128)}, f32[1,128]{1,0:T(1,128)}) custom-call(s32[2]{0:T(128)S(1)} %pad_add_fusion.par, f32[40,128]{1,0:T(8,128)S(1)} %add_add_fusion.mine_ref, f32[40,128]{1,0:T(8,128)S(1)} %collective-permute-done.23.other_ref, f32[1,128]{1,0:T(1,128)S(1)} %get-tuple-element.54.prior_ref, bf16[24,256,256]{2,1,0:T(8,128)(2,1)S(1)} %bitcast.8), custom_call_target="tpu_custom_call" | custom-call | flops 1000000000 | bytes 3000000 | tf_op jit(solution)/shard_map/pallas_call | solution.py:566
  (40 shorter events, 6.8 us)
Async XLA Ops:
  0.7 5.7 %copy-start = (f32[3,64,32,128]{3,2,1,0:T(8,128)S(1)}, f32[3,64,32,128]{3,2,1,0:T(8,128)}, u32[]{:S(2)}) copy-start(f32[3,64,32,128]{3,2,1,0:T(8,128)} %t_ref.3) | copy-start | bytes 9437188
  2.6 10.6 %collective-permute-start = (f32[13,32,128]{2,1,0:T(8,128)S(1)}, f32[13,32,128]{2,1,0:T(8,128)S(1)}, u32[]{:S(2)}, u32[]{:S(2)}) collective-permute-start(f32[13,32,128]{2,1,0:T(8,128)S(1)} %get-tuple-element.32), channel_id=1, source_target_pairs={{0,8},{8,0},{16,24},{24,16},{1,9},{9,1},{17,25},{25,17},{2,10},{10... | collective-permute-start | bytes 638984 | tf_op jit(solution)/shard_map/ppermute | solution.py:496
  5.7 7.6 %collective-permute-start.1 = (f32[13,32,128]{2,1,0:T(8,128)S(1)}, f32[13,32,128]{2,1,0:T(8,128)S(1)}, u32[]{:S(2)}, u32[]{:S(2)}) collective-permute-start(f32[13,32,128]{2,1,0:T(8,128)S(1)} %get-tuple-element.33), channel_id=1, source_target_pairs={{8,16},{16,8},{9,17},{17,9},{10,18},{18,10},{11,19},{19,11},{12,20... | collective-permute-start | bytes 638984 | tf_op jit(solution)/shard_map/ppermute | solution.py:496
  9.5 7.9 %collective-permute-start.2 = (f32[392,128]{1,0:T(8,128)S(1)}, f32[392,128]{1,0:T(8,128)S(1)}, u32[]{:S(2)}, u32[]{:S(2)}) collective-permute-start(f32[392,128]{1,0:T(8,128)S(1)} %get-tuple-element.37), channel_id=1, source_target_pairs={{0,1},{1,0},{2,3},{3,2},{4,5},{5,4},{6,7},{7,6},{8,9},{9,8},{10,11... | collective-permute-start | bytes 602120 | tf_op jit(solution)/shard_map/ppermute | solution.py:496
  9.6 7.8 %collective-permute-start.3 = (f32[392,128]{1,0:T(8,128)S(1)}, f32[392,128]{1,0:T(8,128)S(1)}, u32[]{:S(2)}, u32[]{:S(2)}) collective-permute-start(f32[392,128]{1,0:T(8,128)S(1)} %get-tuple-element.38), channel_id=1, source_target_pairs={{0,7},{1,2},{2,1},{3,4},{4,3},{5,6},{6,5},{7,0},{8,15},{9,10},{10,... | collective-permute-start | bytes 602120 | tf_op jit(solution)/shard_map/ppermute | solution.py:496
  14.3 3.1 %collective-permute-start.4 = (f32[56,128]{1,0:T(8,128)S(1)}, f32[56,128]{1,0:T(8,128)S(1)}, u32[]{:S(2)}, u32[]{:S(2)}) collective-permute-start(f32[56,128]{1,0:T(8,128)S(1)} %get-tuple-element.39), channel_id=1, source_target_pairs={{0,1},{1,0},{2,3},{3,2},{4,5},{5,4},{6,7},{7,6},{8,9},{9,8},{10,11... | collective-permute-start | bytes 86024 | tf_op jit(solution)/shard_map/ppermute | solution.py:496
  14.4 4.3 %collective-permute-start.5 = (f32[56,128]{1,0:T(8,128)S(1)}, f32[56,128]{1,0:T(8,128)S(1)}, u32[]{:S(2)}, u32[]{:S(2)}) collective-permute-start(f32[56,128]{1,0:T(8,128)S(1)} %get-tuple-element.40), channel_id=1, source_target_pairs={{0,7},{1,2},{2,1},{3,4},{4,3},{5,6},{6,5},{7,0},{8,15},{9,10},{10,... | collective-permute-start | bytes 86024 | tf_op jit(solution)/shard_map/ppermute | solution.py:496
  20.8 1.3 %collective-permute-start.6 = (f32[40,128]{1,0:T(8,128)S(1)}, f32[40,128]{1,0:T(8,128)S(1)}, u32[]{:S(2)}, u32[]{:S(2)}) collective-permute-start(f32[40,128]{1,0:T(8,128)S(1)} %get-tuple-element.44), channel_id=1, source_target_pairs={{0,1},{1,0},{2,3},{3,2},{4,5},{5,4},{6,7},{7,6},{8,9},{9,8},{10,11... | collective-permute-start | bytes 61448 | tf_op jit(solution)/shard_map/ppermute | solution.py:500
  22.0 5.3 %collective-permute-start.7 = (f32[40,128]{1,0:T(8,128)S(1)}, f32[40,128]{1,0:T(8,128)S(1)}, u32[]{:S(2)}, u32[]{:S(2)}) collective-permute-start(f32[40,128]{1,0:T(8,128)S(1)} %add.24.first), channel_id=1, source_target_pairs={{0,6},{1,7},{2,4},{3,5},{4,2},{5,3},{6,0},{7,1},{8,14},{9,15},{10,... | collective-permute-start | bytes 61448 | tf_op jit(solution)/shard_map/ppermute | solution.py:500
  22.9 4.5 %collective-permute-start.8 = (f32[40,128]{1,0:T(8,128)S(1)}, f32[40,128]{1,0:T(8,128)S(1)}, u32[]{:S(2)}, u32[]{:S(2)}) collective-permute-start(f32[40,128]{1,0:T(8,128)S(1)} %add.24.first), channel_id=1, source_target_pairs={{0,4},{1,5},{2,6},{3,7},{4,0},{5,1},{6,2},{7,3},{8,12},{9,13},{10,... | collective-permute-start | bytes 61448 | tf_op jit(solution)/shard_map/ppermute | solution.py:500
  24.3 3.8 %collective-permute-start.9 = (f32[40,128]{1,0:T(8,128)S(1)}, f32[40,128]{1,0:T(8,128)S(1)}, u32[]{:S(2)}, u32[]{:S(2)}) collective-permute-start(f32[40,128]{1,0:T(8,128)S(1)} %add.24.first), channel_id=1, source_target_pairs={{0,2},{1,3},{2,0},{3,1},{4,6},{5,7},{6,4},{7,5},{8,10},{9,11},{10,... | collective-permute-start | bytes 61448 | tf_op jit(solution)/shard_map/ppermute | solution.py:500
  28.1 11.2 %collective-permute-start.10 = (f32[432,128]{1,0:T(8,128)S(1)}, f32[432,128]{1,0:T(8,128)S(1)}, u32[]{:S(2)}, u32[]{:S(2)}) collective-permute-start(f32[432,128]{1,0:T(8,128)S(1)} %get-tuple-element.47), channel_id=1, source_target_pairs={{0,1},{1,0},{2,3},{3,2},{4,5},{5,4},{6,7},{7,6},{8,9},{9,8},{10,11... | collective-permute-start | bytes 663560 | tf_op jit(solution)/shard_map/ppermute | solution.py:496
  28.2 11.1 %collective-permute-start.11 = (f32[432,128]{1,0:T(8,128)S(1)}, f32[432,128]{1,0:T(8,128)S(1)}, u32[]{:S(2)}, u32[]{:S(2)}) collective-permute-start(f32[432,128]{1,0:T(8,128)S(1)} %get-tuple-element.48), channel_id=1, source_target_pairs={{0,7},{1,2},{2,1},{3,4},{4,3},{5,6},{6,5},{7,0},{8,15},{9,10},{10,... | collective-permute-start | bytes 663560 | tf_op jit(solution)/shard_map/ppermute | solution.py:496
  29.6 7.6 %collective-permute-start.12 = (f32[40,128]{1,0:T(8,128)S(1)}, f32[40,128]{1,0:T(8,128)S(1)}, u32[]{:S(2)}, u32[]{:S(2)}) collective-permute-start(f32[40,128]{1,0:T(8,128)S(1)} %get-tuple-element.50.first), channel_id=1, source_target_pairs={{0,24},{8,16},{16,8},{24,0},{1,25},{9,17},{17,9},{25,1},{2,26},{10... | collective-permute-start | bytes 61448 | tf_op jit(solution)/shard_map/ppermute | solution.py:500
  32.1 5.6 %collective-permute-start.13 = (f32[40,128]{1,0:T(8,128)S(1)}, f32[40,128]{1,0:T(8,128)S(1)}, u32[]{:S(2)}, u32[]{:S(2)}) collective-permute-start(f32[40,128]{1,0:T(8,128)S(1)} %get-tuple-element.50.first), channel_id=1, source_target_pairs={{0,16},{8,24},{16,0},{24,8},{1,17},{9,25},{17,1},{25,9},{2,18},{10... | collective-permute-start | bytes 61448 | tf_op jit(solution)/shard_map/ppermute | solution.py:500
  35.5 3.8 %collective-permute-start.14 = (f32[40,128]{1,0:T(8,128)S(1)}, f32[40,128]{1,0:T(8,128)S(1)}, u32[]{:S(2)}, u32[]{:S(2)}) collective-permute-start(f32[40,128]{1,0:T(8,128)S(1)} %get-tuple-element.50.first), channel_id=1, source_target_pairs={{0,8},{8,0},{16,24},{24,16},{1,9},{9,1},{17,25},{25,17},{2,10},{10... | collective-permute-start | bytes 61448 | tf_op jit(solution)/shard_map/ppermute | solution.py:500
  39.3 1.4 %collective-permute-start.15 = (f32[40,128]{1,0:T(8,128)S(1)}, f32[40,128]{1,0:T(8,128)S(1)}, u32[]{:S(2)}, u32[]{:S(2)}) collective-permute-start(f32[40,128]{1,0:T(8,128)S(1)} %shard_map.70.mine_ref), channel_id=1, source_target_pairs={{0,1},{1,0},{2,3},{3,2},{4,5},{5,4},{6,7},{7,6},{8,9},{9,8},{10,11... | collective-permute-start | bytes 61448 | tf_op jit(solution)/shard_map/ppermute | solution.py:500
  47.3 1.4 %collective-permute-start.16 = (f32[40,128]{1,0:T(8,128)S(1)}, f32[40,128]{1,0:T(8,128)S(1)}, u32[]{:S(2)}, u32[]{:S(2)}) collective-permute-start(f32[40,128]{1,0:T(8,128)S(1)} %get-tuple-element.53), channel_id=1, source_target_pairs={{0,1},{1,0},{2,3},{3,2},{4,5},{5,4},{6,7},{7,6},{8,9},{9,8},{10,11... | collective-permute-start | bytes 61448 | tf_op jit(solution)/shard_map/ppermute | solution.py:500
  48.7 4.8 %collective-permute-start.17 = (f32[40,128]{1,0:T(8,128)S(1)}, f32[40,128]{1,0:T(8,128)S(1)}, u32[]{:S(2)}, u32[]{:S(2)}) collective-permute-start(f32[40,128]{1,0:T(8,128)S(1)} %add.25), channel_id=1, source_target_pairs={{0,6},{1,7},{2,4},{3,5},{4,2},{5,3},{6,0},{7,1},{8,14},{9,15},{10,... | collective-permute-start | bytes 61448 | tf_op jit(solution)/shard_map/ppermute | solution.py:500
  49.5 4.0 %collective-permute-start.18 = (f32[40,128]{1,0:T(8,128)S(1)}, f32[40,128]{1,0:T(8,128)S(1)}, u32[]{:S(2)}, u32[]{:S(2)}) collective-permute-start(f32[40,128]{1,0:T(8,128)S(1)} %add.25), channel_id=1, source_target_pairs={{0,4},{1,5},{2,6},{3,7},{4,0},{5,1},{6,2},{7,3},{8,12},{9,13},{10,... | collective-permute-start | bytes 61448 | tf_op jit(solution)/shard_map/ppermute | solution.py:500
  50.8 3.8 %collective-permute-start.19 = (f32[40,128]{1,0:T(8,128)S(1)}, f32[40,128]{1,0:T(8,128)S(1)}, u32[]{:S(2)}, u32[]{:S(2)}) collective-permute-start(f32[40,128]{1,0:T(8,128)S(1)} %add.25), channel_id=1, source_target_pairs={{0,2},{1,3},{2,0},{3,1},{4,6},{5,7},{6,4},{7,5},{8,10},{9,11},{10,... | collective-permute-start | bytes 61448 | tf_op jit(solution)/shard_map/ppermute | solution.py:500
  54.6 5.6 %collective-permute-start.20 = (f32[40,128]{1,0:T(8,128)S(1)}, f32[40,128]{1,0:T(8,128)S(1)}, u32[]{:S(2)}, u32[]{:S(2)}) collective-permute-start(f32[40,128]{1,0:T(8,128)S(1)} %add_add_fusion.1), channel_id=1, source_target_pairs={{0,24},{8,16},{16,8},{24,0},{1,25},{9,17},{17,9},{25,1},{2,26},{10... | collective-permute-start | bytes 61448 | tf_op jit(solution)/shard_map/ppermute | solution.py:500
  56.1 4.7 %collective-permute-start.21 = (f32[40,128]{1,0:T(8,128)S(1)}, f32[40,128]{1,0:T(8,128)S(1)}, u32[]{:S(2)}, u32[]{:S(2)}) collective-permute-start(f32[40,128]{1,0:T(8,128)S(1)} %add_add_fusion.1), channel_id=1, source_target_pairs={{0,16},{8,24},{16,0},{24,8},{1,17},{9,25},{17,1},{25,9},{2,18},{10... | collective-permute-start | bytes 61448 | tf_op jit(solution)/shard_map/ppermute | solution.py:500
  57.1 3.9 %collective-permute-start.22 = (f32[40,128]{1,0:T(8,128)S(1)}, f32[40,128]{1,0:T(8,128)S(1)}, u32[]{:S(2)}, u32[]{:S(2)}) collective-permute-start(f32[40,128]{1,0:T(8,128)S(1)} %add_add_fusion.1), channel_id=1, source_target_pairs={{0,8},{8,0},{16,24},{24,16},{1,9},{9,1},{17,25},{25,17},{2,10},{10... | collective-permute-start | bytes 61448 | tf_op jit(solution)/shard_map/ppermute | solution.py:500
  61.0 1.2 %collective-permute-start.23 = (f32[40,128]{1,0:T(8,128)S(1)}, f32[40,128]{1,0:T(8,128)S(1)}, u32[]{:S(2)}, u32[]{:S(2)}) collective-permute-start(f32[40,128]{1,0:T(8,128)S(1)} %add_add_fusion.mine_ref), channel_id=1, source_target_pairs={{0,1},{1,0},{2,3},{3,2},{4,5},{5,4},{6,7},{7,6},{8,9},{9,8},{10,11... | collective-permute-start | bytes 61448 | tf_op jit(solution)/shard_map/ppermute | solution.py:500

commit v12 on v11

--- a/solution.py
+++ b/solution.py
@@ -21,7 +21,8 @@
 HALO = STEPS * RENORMS
 SIDE = STEPS
 TILES = 24
-BATCH = 16
+BATCH = 8
+GROUP = 4
 VMEM_LIMIT = 16 * 1024 * 1024
 
 HBM = pl.BlockSpec(memory_space=pltpu.HBM)
@@ -337,18 +338,30 @@
     return root_a, a * both
 
 
+def square_of(pivots):
+    high = pivots.astype(jnp.bfloat16)
+    rest = pivots - high.astype(jnp.float32)
+    middle = rest.astype(jnp.bfloat16)
+    low = (rest - middle.astype(jnp.float32)).astype(jnp.bfloat16)
+    return lax.dot_general(
+        jnp.concatenate([high, high, middle, middle, high, low], axis=0),
+        jnp.concatenate([high, middle, high, middle, low, high], axis=0),
+        (((0,), (0,)), ((), ())),
+        preferred_element_type=jnp.float32,
+    )
+
+
 def invert_factor(gram, work, board):
     count = LANES // SUB
     lane = lax.broadcasted_iota(jnp.int32, (SUB, LANES), 1)
     sub = lax.broadcasted_iota(jnp.int32, (SUB, LANES), 0)
     rows = [gram[SUB * i : SUB * (i + 1)] for i in range(count)]
-    columns = [lane_spread(rows[0], l) for l in range(SUB)]
     for block in range(count):
         base = SUB * block
         here = (lane >= base) & (lane < base + SUB)
-        shelf = 3 * SUB * base
+        shelf = 2 * SUB * base
         for l in range(SUB):
-            board[pl.ds(shelf + SUB * l, SUB), :] = columns[l]
+            board[pl.ds(shelf + SUB * l, SUB), :] = lane_spread(rows[block], base + l)
         low = [
             [board[pl.ds(shelf + SUB * l + k, SUB, stride=0), :] for l in range(k + 1)]
             for k in range(SUB)
@@ -370,25 +383,27 @@
         for k in range(1, SUB):
             merged = jnp.where(sub == k, scaled[k], merged)
         work[pl.ds(base, SUB), :] = merged
-        shelf += SUB
-        for i in range(block + 1, count):
+        for i in range(block + 1, (block // GROUP + 1) * GROUP):
             weights = []
+            rest = jnp.where(here, 0.0, rows[i])
             for l in range(SUB):
                 weight = lane_spread(rows[i], base + l)
                 for m in range(l):
                     weight = weight - weights[m] * low[l][m]
                 weights.append(weight * inv[l])
-            if i == block + 1:
-                columns = [lane_spread(rows[i], base + SUB + l) for l in range(SUB)]
-                for l in range(SUB):
-                    board[pl.ds(shelf + SUB * l, SUB), :] = weights[l]
-                    for k in range(SUB):
-                        across = board[pl.ds(shelf + SUB * l + k, SUB, stride=0), :]
-                        columns[k] = columns[k] - weights[l] * across
-            rest = jnp.where(here, 0.0, rows[i])
             for l in range(SUB):
                 rest = rest - weights[l] * scaled[l]
             rows[i] = rest
+        if block % GROUP == GROUP - 1 and block + 1 < count:
+            first = SUB * (block + 1 - GROUP)
+            tall = (SUB * GROUP, LANES)
+            to_lane = lax.broadcasted_iota(jnp.int32, tall, 1) // SUB - first // SUB
+            to_row = lax.broadcasted_iota(jnp.int32, tall, 0) // SUB
+            pivots = work[pl.ds(first, SUB * GROUP), :]
+            update = square_of(jnp.where((to_lane > to_row) & (to_lane < GROUP), 0.0, pivots))
+            here = (lane >= first) & (lane < base + SUB)
+            for i in range(block + 1, count):
+                rows[i] = jnp.where(here, 0.0, rows[i]) - update[SUB * i : SUB * (i + 1)]
 
 
 def factorize(par, mine_ref, other_ref, gram, work, board):
@@ -557,7 +572,7 @@
     rows_sent = (shape_of(comps * HALO + 1, cols, modes),) * 2
     halves = (shape_of(modes // 4 + SUB, modes),) * 2
     square = pltpu.VMEM((modes, modes), jnp.float32)
-    board = pltpu.VMEM((3 * SUB * modes, LANES), jnp.float32)
+    board = pltpu.VMEM((2 * SUB * modes, LANES), jnp.float32)
     factor = pltpu.VMEM((2 * modes, 2 * modes), jnp.bfloat16)
 
     def call(

time: 69.1 us -> 68 us (0.984)
  Pallas kernels: 30.6 us -> 29.6 us
    pallas_call x14, Pallas kernels: 30.5 us -> 29.6 us  [call(): pl.pallas_call(kernel, out_shape=outs, in_specs=specs or [SMEM] + [VMEM]...]
where the time goes in v12:
time: 68 us; the launch traced here: 67.8 us
  Pallas kernels  29.6 us (44%)
  starting transfers between devices  26.6 us (39%)
  waiting for transfers between devices  10.6 us (16%)
  between operations  0.86 us (1%)
    pallas_call x14, Pallas kernels, call(): pl.pallas_call(kernel, out_shape=outs, in_specs=specs or [SMEM] + [VMEM]...  29.6 us
    ppermute x16, starting transfers between devices, swapped(): lax.ppermute(value, axis, [(i, i ^ mask) for i in range(lax.axis_size(axi...  18 us
    ppermute x16, waiting for transfers between devices, swapped(): lax.ppermute(value, axis, [(i, i ^ mask) for i in range(lax.axis_size(axi...  9.31 us
    ppermute x4, starting transfers between devices, swap_pairs(): lax.ppermute(far_value, axis, far)  5.25 us
    ppermute x4, starting transfers between devices, swap_pairs(): lax.ppermute(near_value, axis, near)  3.29 us
  transfers between devices with their start and end apart: 24, of which 12 were waited for; matrix products, arithmetic and copies ran while one was open for 0% of the time, Pallas kernels for 20%

profile of v12, /device:TPU:0, one launch (start us, length us, event | category | flops | bytes accessed | tf_op | source)
XLA Modules:
  0.0 67.8 jit_solution(5347620392354367113)
XLA Ops:
  0.7 1.9 %shard_map.60 = (f32[13,32,128]{2,1,0:T(8,128)S(1)}, f32[13,32,128]{2,1,0:T(8,128)S(1)}) custom-call(s32[2]{0:T(128)S(1)} %pad_add_fusion.par, f32[3,64,32,128]{3,2,1,0:T(8,128)} %t_ref.3, s32[32,64]{1,0:T(8,128)} %bitcast.9, s32[32,64]{1,0:T(8,128)} %bitcast.11, f32[32,64]{1,0:T(8,128)} %bitcast.13), custom_call_target="tpu_custom_call" | custom-call | flops 5000000000 | bytes 15000000 | tf_op jit(solution)/shard_map/pallas_call | solution.py:581
  2.6 3.1 %collective-permute-start = (f32[13,32,128]{2,1,0:T(8,128)S(1)}, f32[13,32,128]{2,1,0:T(8,128)S(1)}, u32[]{:S(2)}, u32[]{:S(2)}) collective-permute-start(f32[13,32,128]{2,1,0:T(8,128)S(1)} %get-tuple-element.32), channel_id=1, source_target_pairs={{0,8},{8,0},{16,24},{24,16},{1,9},{9,1},{17,25},{25,17},{2,10},{10... | collective-permute-start | bytes 638984 | tf_op jit(solution)/shard_map/ppermute | solution.py:511
  6.4 3.1 %shard_map.59 = (f32[3,36,72,128]{3,2,1,0:T(8,128)S(1)}, f32[3,36,72,128]{3,2,1,0:T(8,128)S(1)}, f32[72,128]{1,0:T(8,128)S(1)}, f32[392,128]{1,0:T(8,128)S(1)}, f32[392,128]{1,0:T(8,128)S(1)}) custom-call(s32[2]{0:T(128)S(1)} %pad_add_fusion.par, f32[3,64,32,128]{3,2,1,0:T(8,128)S(1)} %copy-done, s32[32,64]{1,0:T(8,128)} %bitcast.10, s32[32,64]{1,0:T(8,128)} %bitcast.12, ...), custom_call_target="tpu_custom_call" | custom-call | flops 3000000000 | bytes 9000000 | tf_op jit(solution)/shard_map/pallas_call | solution.py:581
  9.6 2.5 %collective-permute-start.3 = (f32[392,128]{1,0:T(8,128)S(1)}, f32[392,128]{1,0:T(8,128)S(1)}, u32[]{:S(2)}, u32[]{:S(2)}) collective-permute-start(f32[392,128]{1,0:T(8,128)S(1)} %get-tuple-element.38), channel_id=1, source_target_pairs={{0,7},{1,2},{2,1},{3,4},{4,3},{5,6},{6,5},{7,0},{8,15},{9,10},{10,... | collective-permute-start | bytes 602120 | tf_op jit(solution)/shard_map/ppermute | solution.py:511
  12.1 1.2 %shard_map.61._.refs_0_ = f32[3,36,72,128]{3,2,1,0:T(8,128)S(1)} custom-call(f32[3,36,72,128]{3,2,1,0:T(8,128)S(1)} %get-tuple-element.30.source.state_in, f32[3,36,72,128]{3,2,1,0:T(8,128)S(1)} %get-tuple-element.31.coef_ref.coef_in, f32[72,128]{1,0:T(8,128)S(1)} %get-tuple-element.34.spin_ref), custom_call_target="tpu_custom_call" | custom-call | flops 2000000000 | bytes 6000000 | tf_op jit(solution)/shard_map/pallas_call | solution.py:581
  13.3 1.0 %shard_map.62 = (f32[3,36,72,128]{3,2,1,0:T(8,128)S(1)}, f32[3,36,72,128]{3,2,1,0:T(8,128)S(1)}, f32[56,128]{1,0:T(8,128)S(1)}, f32[56,128]{1,0:T(8,128)S(1)}) custom-call(s32[2]{0:T(128)S(1)} %pad_add_fusion.par, f32[3,36,72,128]{3,2,1,0:T(8,128)S(1)} %get-tuple-element.30.source.state_in, ...), custom_call_target="tpu_custom_call", output_to_operand_aliasing={{0}: (1, {}), {1}: (2, {})} | custom-call | flops 1000000000 | bytes 3000000 | tf_op jit(solution)/shard_map/pallas_call | solution.py:581
  15.7 1.6 %shard_map.64.state_in = f32[3,36,72,128]{3,2,1,0:T(8,128)S(1)} custom-call(f32[3,36,72,128]{3,2,1,0:T(8,128)S(1)} %shard_map.63.source.middle_in, f32[3,36,72,128]{3,2,1,0:T(8,128)S(1)} %get-tuple-element.36.coef_ref.coef_in, f32[72,128]{1,0:T(8,128)S(1)} %get-tuple-element.34.spin_ref), custom_call_target="tpu_custom_call" | custom-call | flops 2000000000 | bytes 6000000 | tf_op jit(solution)/shard_map/pallas_call | solution.py:581
  17.4 1.2 %collective-permute-done.5.d = f32[56,128]{1,0:T(8,128)S(1)} collective-permute-done((f32[56,128]{1,0:T(8,128)S(1)}, f32[56,128]{1,0:T(8,128)S(1)}, u32[]{:S(2)}, u32[]{:S(2)}) %collective-permute-start.5) | collective-permute-done | bytes 28704 | tf_op jit(solution)/shard_map/ppermute | solution.py:511
  18.6 2.2 %shard_map.65 = (f32[3,36,72,128]{3,2,1,0:T(8,128)S(1)}, f32[3,36,72,128]{3,2,1,0:T(8,128)S(1)}, f32[3,36,72,128]{3,2,1,0:T(8,128)S(1)}, f32[3,36,72,128]{3,2,1,...) custom-call(s32[2]{0:T(128)S(1)} %pad_add_fusion.par, ...), custom_call_target="tpu_custom_call", output_to_operand_aliasing={{0}: (1, {}), {1}: (2, {}), {2}: (3, {}), {3}: (4, {})} | custom-call | flops 2000000000 | bytes 6000000 | tf_op jit(solution)/shard_map/pallas_call | solution.py:581
  20.9 1.2 %collective-permute-done.6 = f32[40,128]{1,0:T(8,128)S(1)} collective-permute-done((f32[40,128]{1,0:T(8,128)S(1)}, f32[40,128]{1,0:T(8,128)S(1)}, u32[]{:S(2)}, u32[]{:S(2)}) %collective-permute-start.6) | collective-permute-done | bytes 20512 | tf_op jit(solution)/shard_map/ppermute | solution.py:515
  22.0 0.9 %collective-permute-start.7 = (f32[40,128]{1,0:T(8,128)S(1)}, f32[40,128]{1,0:T(8,128)S(1)}, u32[]{:S(2)}, u32[]{:S(2)}) collective-permute-start(f32[40,128]{1,0:T(8,128)S(1)} %add.24.first), channel_id=1, source_target_pairs={{0,6},{1,7},{2,4},{3,5},{4,2},{5,3},{6,0},{7,1},{8,14},{9,15},{10,... | collective-permute-start | bytes 61448 | tf_op jit(solution)/shard_map/ppermute | solution.py:515
  22.9 1.4 %collective-permute-start.8 = (f32[40,128]{1,0:T(8,128)S(1)}, f32[40,128]{1,0:T(8,128)S(1)}, u32[]{:S(2)}, u32[]{:S(2)}) collective-permute-start(f32[40,128]{1,0:T(8,128)S(1)} %add.24.first), channel_id=1, source_target_pairs={{0,4},{1,5},{2,6},{3,7},{4,0},{5,1},{6,2},{7,3},{8,12},{9,13},{10,... | collective-permute-start | bytes 61448 | tf_op jit(solution)/shard_map/ppermute | solution.py:515
  24.3 1.2 %collective-permute-start.9 = (f32[40,128]{1,0:T(8,128)S(1)}, f32[40,128]{1,0:T(8,128)S(1)}, u32[]{:S(2)}, u32[]{:S(2)}) collective-permute-start(f32[40,128]{1,0:T(8,128)S(1)} %add.24.first), channel_id=1, source_target_pairs={{0,2},{1,3},{2,0},{3,1},{4,6},{5,7},{6,4},{7,5},{8,10},{9,11},{10,... | collective-permute-start | bytes 61448 | tf_op jit(solution)/shard_map/ppermute | solution.py:515
  25.5 1.8 %shard_map.66.source.rest_0_.middle_in = f32[3,36,72,128]{3,2,1,0:T(8,128)S(1)} custom-call(f32[3,36,72,128]{3,2,1,0:T(8,128)S(1)} %get-tuple-element.41.source.start_in, f32[3,36,72,128]{3,2,1,0:T(8,128)S(1)} %get-tuple-element.42.coef_ref, f32[72,128]{1,0:T(8,128)S(1)} %get-tuple-element.34.spin_ref), custom_call_target="tpu_custom_call" | custom-call | flops 2000000000 | bytes 6000000 | tf_op jit(solution)/shard_map/pallas_call | solution.py:581
  28.2 1.4 %collective-permute-start.11 = (f32[432,128]{1,0:T(8,128)S(1)}, f32[432,128]{1,0:T(8,128)S(1)}, u32[]{:S(2)}, u32[]{:S(2)}) collective-permute-start(f32[432,128]{1,0:T(8,128)S(1)} %get-tuple-element.48), channel_id=1, source_target_pairs={{0,7},{1,2},{2,1},{3,4},{4,3},{5,6},{6,5},{7,0},{8,15},{9,10},{10,... | collective-permute-start | bytes 663560 | tf_op jit(solution)/shard_map/ppermute | solution.py:511
  29.6 2.5 %collective-permute-start.12 = (f32[40,128]{1,0:T(8,128)S(1)}, f32[40,128]{1,0:T(8,128)S(1)}, u32[]{:S(2)}, u32[]{:S(2)}) collective-permute-start(f32[40,128]{1,0:T(8,128)S(1)} %get-tuple-element.50.first), channel_id=1, source_target_pairs={{0,24},{8,16},{16,8},{24,0},{1,25},{9,17},{17,9},{25,1},{2,26},{10... | collective-permute-start | bytes 61448 | tf_op jit(solution)/shard_map/ppermute | solution.py:515
  32.1 3.4 %collective-permute-start.13 = (f32[40,128]{1,0:T(8,128)S(1)}, f32[40,128]{1,0:T(8,128)S(1)}, u32[]{:S(2)}, u32[]{:S(2)}) collective-permute-start(f32[40,128]{1,0:T(8,128)S(1)} %get-tuple-element.50.first), channel_id=1, source_target_pairs={{0,16},{8,24},{16,0},{24,8},{1,17},{9,25},{17,1},{25,9},{2,18},{10... | collective-permute-start | bytes 61448 | tf_op jit(solution)/shard_map/ppermute | solution.py:515
  35.5 1.7 %shard_map.67.state_in.rest_0_ = f32[3,36,72,128]{3,2,1,0:T(8,128)S(1)} custom-call(f32[3,36,72,128]{3,2,1,0:T(8,128)S(1)} %shard_map.66.source.rest_0_.middle_in, f32[3,36,72,128]{3,2,1,0:T(8,128)S(1)} %get-tuple-element.42.coef_ref, f32[72,128]{1,0:T(8,128)S(1)} %get-tuple-element.34.spin_ref), custom_call_target="tpu_custom_call" | custom-call | flops 2000000000 | bytes 6000000 | tf_op jit(solution)/shard_map/pallas_call | solution.py:581
  37.7 1.6 %collective-permute-done.14.fourth = f32[40,128]{1,0:T(8,128)S(1)} collective-permute-done((f32[40,128]{1,0:T(8,128)S(1)}, f32[40,128]{1,0:T(8,128)S(1)}, u32[]{:S(2)}, u32[]{:S(2)}) %collective-permute-start.14) | collective-permute-done | bytes 20512 | tf_op jit(solution)/shard_map/ppermute | solution.py:515
  39.4 1.1 %shard_map.69 = (f32[3,36,72,128]{3,2,1,0:T(8,128)S(1)}, f32[3,36,72,128]{3,2,1,0:T(8,128)S(1)}, f32[3,36,72,128]{3,2,1,0:T(8,128)S(1)}) custom-call(s32[2]{0:T(128)S(1)} %pad_add_fusion.par, f32[3,36,72,128]{3,2,1,0:T(8,128)S(1)} %get-tuple-element.41.source.start_in, ...), custom_call_target="tpu_custom_call", output_to_operand_aliasing={{0}: (1, {}), {1}: (2, {}), {2}: (3, {})} | custom-call | flops 1000000000 | bytes 3000000 | tf_op jit(solution)/shard_map/pallas_call | solution.py:581
  40.5 3.5 %shard_map.71 = (f32[128,128]{1,0:T(8,128)S(1)}, f32[1,128]{1,0:T(1,128)S(1)}) custom-call(s32[2]{0:T(128)S(1)} %pad_add_fusion.par, f32[40,128]{1,0:T(8,128)S(1)} %shard_map.70.mine_ref, f32[40,128]{1,0:T(8,128)S(1)} %collective-permute-done.15.other_ref, f32[1,128]{1,0:T(1,128)S(1)} %broadcast_in_dim.3.prior_ref, ...), custom_call_target="tpu_custom_call" | custom-call | flops 10000000 | bytes 30000 | tf_op jit(solution)/shard_map/pallas_call | solution.py:581
  44.0 2.7 %shard_map.72 = (f32[3,32,64,128]{3,2,1,0:T(8,128)S(1)}, f32[40,128]{1,0:T(8,128)S(1)}, f32[40,128]{1,0:T(8,128)S(1)}) custom-call(s32[2]{0:T(128)S(1)} %pad_add_fusion.par, f32[3,36,72,128]{3,2,1,0:T(8,128)S(1)} %get-tuple-element.49._.state, f32[128,128]{1,0:T(8,128)S(1)} %get-tuple-element.51.inverse_ref), custom_call_target="tpu_custom_call" | custom-call | flops 2000000000 | bytes 6000000 | tf_op jit(solution)/shard_map/pallas_call | solution.py:581
  48.9 1.4 %collective-permute-start.18 = (f32[40,128]{1,0:T(8,128)S(1)}, f32[40,128]{1,0:T(8,128)S(1)}, u32[]{:S(2)}, u32[]{:S(2)}) collective-permute-start(f32[40,128]{1,0:T(8,128)S(1)} %add.25), channel_id=1, source_target_pairs={{0,4},{1,5},{2,6},{3,7},{4,0},{5,1},{6,2},{7,3},{8,12},{9,13},{10,... | collective-permute-start | bytes 61448 | tf_op jit(solution)/shard_map/ppermute | solution.py:515
  50.3 1.3 %collective-permute-start.19 = (f32[40,128]{1,0:T(8,128)S(1)}, f32[40,128]{1,0:T(8,128)S(1)}, u32[]{:S(2)}, u32[]{:S(2)}) collective-permute-start(f32[40,128]{1,0:T(8,128)S(1)} %add.25), channel_id=1, source_target_pairs={{0,2},{1,3},{2,0},{3,1},{4,6},{5,7},{6,4},{7,5},{8,10},{9,11},{10,... | collective-permute-start | bytes 61448 | tf_op jit(solution)/shard_map/ppermute | solution.py:515
  51.6 1.3 %collective-permute-done.17 = f32[40,128]{1,0:T(8,128)S(1)} collective-permute-done((f32[40,128]{1,0:T(8,128)S(1)}, f32[40,128]{1,0:T(8,128)S(1)}, u32[]{:S(2)}, u32[]{:S(2)}) %collective-permute-start.17) | collective-permute-done | bytes 20512 | tf_op jit(solution)/shard_map/ppermute | solution.py:515
  52.9 1.2 %collective-permute-done.19 = f32[40,128]{1,0:T(8,128)S(1)} collective-permute-done((f32[40,128]{1,0:T(8,128)S(1)}, f32[40,128]{1,0:T(8,128)S(1)}, u32[]{:S(2)}, u32[]{:S(2)}) %collective-permute-start.19) | collective-permute-done | bytes 20512 | tf_op jit(solution)/shard_map/ppermute | solution.py:515
  54.1 1.5 %collective-permute-start.20 = (f32[40,128]{1,0:T(8,128)S(1)}, f32[40,128]{1,0:T(8,128)S(1)}, u32[]{:S(2)}, u32[]{:S(2)}) collective-permute-start(f32[40,128]{1,0:T(8,128)S(1)} %add_add_fusion.1), channel_id=1, source_target_pairs={{0,24},{8,16},{16,8},{24,0},{1,25},{9,17},{17,9},{25,1},{2,26},{10... | collective-permute-start | bytes 61448 | tf_op jit(solution)/shard_map/ppermute | solution.py:515
  55.6 1.0 %collective-permute-start.21 = (f32[40,128]{1,0:T(8,128)S(1)}, f32[40,128]{1,0:T(8,128)S(1)}, u32[]{:S(2)}, u32[]{:S(2)}) collective-permute-start(f32[40,128]{1,0:T(8,128)S(1)} %add_add_fusion.1), channel_id=1, source_target_pairs={{0,16},{8,24},{16,0},{24,8},{1,17},{9,25},{17,1},{25,9},{2,18},{10... | collective-permute-start | bytes 61448 | tf_op jit(solution)/shard_map/ppermute | solution.py:515
  56.5 2.0 %collective-permute-start.22 = (f32[40,128]{1,0:T(8,128)S(1)}, f32[40,128]{1,0:T(8,128)S(1)}, u32[]{:S(2)}, u32[]{:S(2)}) collective-permute-start(f32[40,128]{1,0:T(8,128)S(1)} %add_add_fusion.1), channel_id=1, source_target_pairs={{0,8},{8,0},{16,24},{24,16},{1,9},{9,1},{17,25},{25,17},{2,10},{10... | collective-permute-start | bytes 61448 | tf_op jit(solution)/shard_map/ppermute | solution.py:515
  58.5 1.2 %collective-permute-done.20 = f32[40,128]{1,0:T(8,128)S(1)} collective-permute-done((f32[40,128]{1,0:T(8,128)S(1)}, f32[40,128]{1,0:T(8,128)S(1)}, u32[]{:S(2)}, u32[]{:S(2)}) %collective-permute-start.20) | collective-permute-done | bytes 20512 | tf_op jit(solution)/shard_map/ppermute | solution.py:515
  60.5 1.1 %shard_map.73 = bf16[3,64,32,256]{3,2,1,0:T(8,128)(2,1)S(1)} custom-call(f32[3,32,64,128]{3,2,1,0:T(8,128)S(1)} %get-tuple-element.55.turned), custom_call_target="tpu_custom_call" | custom-call | flops 1000000000 | bytes 3000000 | tf_op jit(solution)/shard_map/pallas_call | solution.py:581
  61.7 6.0 %shard_map.74 = (f32[24,256,128]{2,1,0:T(8,128)}, f32[1,128]{1,0:T(1,128)}) custom-call(s32[2]{0:T(128)S(1)} %pad_add_fusion.par, f32[40,128]{1,0:T(8,128)S(1)} %add_add_fusion.mine_ref, f32[40,128]{1,0:T(8,128)S(1)} %collective-permute-done.23.other_ref, f32[1,128]{1,0:T(1,128)S(1)} %get-tuple-element.54.prior_ref, bf16[24,256,256]{2,1,0:T(8,128)(2,1)S(1)} %bitcast.8), custom_call_target="tpu_custom_call" | custom-call | flops 1000000000 | bytes 3000000 | tf_op jit(solution)/shard_map/pallas_call | solution.py:581
  (40 shorter events, 6.8 us)
Async XLA Ops:
  0.7 5.7 %copy-start = (f32[3,64,32,128]{3,2,1,0:T(8,128)S(1)}, f32[3,64,32,128]{3,2,1,0:T(8,128)}, u32[]{:S(2)}) copy-start(f32[3,64,32,128]{3,2,1,0:T(8,128)} %t_ref.3) | copy-start | bytes 9437188
  2.6 10.6 %collective-permute-start = (f32[13,32,128]{2,1,0:T(8,128)S(1)}, f32[13,32,128]{2,1,0:T(8,128)S(1)}, u32[]{:S(2)}, u32[]{:S(2)}) collective-permute-start(f32[13,32,128]{2,1,0:T(8,128)S(1)} %get-tuple-element.32), channel_id=1, source_target_pairs={{0,8},{8,0},{16,24},{24,16},{1,9},{9,1},{17,25},{25,17},{2,10},{10... | collective-permute-start | bytes 638984 | tf_op jit(solution)/shard_map/ppermute | solution.py:511
  5.7 7.6 %collective-permute-start.1 = (f32[13,32,128]{2,1,0:T(8,128)S(1)}, f32[13,32,128]{2,1,0:T(8,128)S(1)}, u32[]{:S(2)}, u32[]{:S(2)}) collective-permute-start(f32[13,32,128]{2,1,0:T(8,128)S(1)} %get-tuple-element.33), channel_id=1, source_target_pairs={{8,16},{16,8},{9,17},{17,9},{10,18},{18,10},{11,19},{19,11},{12,20... | collective-permute-start | bytes 638984 | tf_op jit(solution)/shard_map/ppermute | solution.py:511
  9.5 7.9 %collective-permute-start.2 = (f32[392,128]{1,0:T(8,128)S(1)}, f32[392,128]{1,0:T(8,128)S(1)}, u32[]{:S(2)}, u32[]{:S(2)}) collective-permute-start(f32[392,128]{1,0:T(8,128)S(1)} %get-tuple-element.37), channel_id=1, source_target_pairs={{0,1},{1,0},{2,3},{3,2},{4,5},{5,4},{6,7},{7,6},{8,9},{9,8},{10,11... | collective-permute-start | bytes 602120 | tf_op jit(solution)/shard_map/ppermute | solution.py:511
  9.6 7.8 %collective-permute-start.3 = (f32[392,128]{1,0:T(8,128)S(1)}, f32[392,128]{1,0:T(8,128)S(1)}, u32[]{:S(2)}, u32[]{:S(2)}) collective-permute-start(f32[392,128]{1,0:T(8,128)S(1)} %get-tuple-element.38), channel_id=1, source_target_pairs={{0,7},{1,2},{2,1},{3,4},{4,3},{5,6},{6,5},{7,0},{8,15},{9,10},{10,... | collective-permute-start | bytes 602120 | tf_op jit(solution)/shard_map/ppermute | solution.py:511
  14.3 3.1 %collective-permute-start.4 = (f32[56,128]{1,0:T(8,128)S(1)}, f32[56,128]{1,0:T(8,128)S(1)}, u32[]{:S(2)}, u32[]{:S(2)}) collective-permute-start(f32[56,128]{1,0:T(8,128)S(1)} %get-tuple-element.39), channel_id=1, source_target_pairs={{0,1},{1,0},{2,3},{3,2},{4,5},{5,4},{6,7},{7,6},{8,9},{9,8},{10,11... | collective-permute-start | bytes 86024 | tf_op jit(solution)/shard_map/ppermute | solution.py:511
  14.4 4.3 %collective-permute-start.5 = (f32[56,128]{1,0:T(8,128)S(1)}, f32[56,128]{1,0:T(8,128)S(1)}, u32[]{:S(2)}, u32[]{:S(2)}) collective-permute-start(f32[56,128]{1,0:T(8,128)S(1)} %get-tuple-element.40), channel_id=1, source_target_pairs={{0,7},{1,2},{2,1},{3,4},{4,3},{5,6},{6,5},{7,0},{8,15},{9,10},{10,... | collective-permute-start | bytes 86024 | tf_op jit(solution)/shard_map/ppermute | solution.py:511
  20.8 1.3 %collective-permute-start.6 = (f32[40,128]{1,0:T(8,128)S(1)}, f32[40,128]{1,0:T(8,128)S(1)}, u32[]{:S(2)}, u32[]{:S(2)}) collective-permute-start(f32[40,128]{1,0:T(8,128)S(1)} %get-tuple-element.44), channel_id=1, source_target_pairs={{0,1},{1,0},{2,3},{3,2},{4,5},{5,4},{6,7},{7,6},{8,9},{9,8},{10,11... | collective-permute-start | bytes 61448 | tf_op jit(solution)/shard_map/ppermute | solution.py:515
  22.0 5.3 %collective-permute-start.7 = (f32[40,128]{1,0:T(8,128)S(1)}, f32[40,128]{1,0:T(8,128)S(1)}, u32[]{:S(2)}, u32[]{:S(2)}) collective-permute-start(f32[40,128]{1,0:T(8,128)S(1)} %add.24.first), channel_id=1, source_target_pairs={{0,6},{1,7},{2,4},{3,5},{4,2},{5,3},{6,0},{7,1},{8,14},{9,15},{10,... | collective-permute-start | bytes 61448 | tf_op jit(solution)/shard_map/ppermute | solution.py:515
  22.9 4.5 %collective-permute-start.8 = (f32[40,128]{1,0:T(8,128)S(1)}, f32[40,128]{1,0:T(8,128)S(1)}, u32[]{:S(2)}, u32[]{:S(2)}) collective-permute-start(f32[40,128]{1,0:T(8,128)S(1)} %add.24.first), channel_id=1, source_target_pairs={{0,4},{1,5},{2,6},{3,7},{4,0},{5,1},{6,2},{7,3},{8,12},{9,13},{10,... | collective-permute-start | bytes 61448 | tf_op jit(solution)/shard_map/ppermute | solution.py:515
  24.3 3.8 %collective-permute-start.9 = (f32[40,128]{1,0:T(8,128)S(1)}, f32[40,128]{1,0:T(8,128)S(1)}, u32[]{:S(2)}, u32[]{:S(2)}) collective-permute-start(f32[40,128]{1,0:T(8,128)S(1)} %add.24.first), channel_id=1, source_target_pairs={{0,2},{1,3},{2,0},{3,1},{4,6},{5,7},{6,4},{7,5},{8,10},{9,11},{10,... | collective-permute-start | bytes 61448 | tf_op jit(solution)/shard_map/ppermute | solution.py:515
  28.1 11.2 %collective-permute-start.10 = (f32[432,128]{1,0:T(8,128)S(1)}, f32[432,128]{1,0:T(8,128)S(1)}, u32[]{:S(2)}, u32[]{:S(2)}) collective-permute-start(f32[432,128]{1,0:T(8,128)S(1)} %get-tuple-element.47), channel_id=1, source_target_pairs={{0,1},{1,0},{2,3},{3,2},{4,5},{5,4},{6,7},{7,6},{8,9},{9,8},{10,11... | collective-permute-start | bytes 663560 | tf_op jit(solution)/shard_map/ppermute | solution.py:511
  28.2 11.1 %collective-permute-start.11 = (f32[432,128]{1,0:T(8,128)S(1)}, f32[432,128]{1,0:T(8,128)S(1)}, u32[]{:S(2)}, u32[]{:S(2)}) collective-permute-start(f32[432,128]{1,0:T(8,128)S(1)} %get-tuple-element.48), channel_id=1, source_target_pairs={{0,7},{1,2},{2,1},{3,4},{4,3},{5,6},{6,5},{7,0},{8,15},{9,10},{10,... | collective-permute-start | bytes 663560 | tf_op jit(solution)/shard_map/ppermute | solution.py:511
  29.6 7.6 %collective-permute-start.12 = (f32[40,128]{1,0:T(8,128)S(1)}, f32[40,128]{1,0:T(8,128)S(1)}, u32[]{:S(2)}, u32[]{:S(2)}) collective-permute-start(f32[40,128]{1,0:T(8,128)S(1)} %get-tuple-element.50.first), channel_id=1, source_target_pairs={{0,24},{8,16},{16,8},{24,0},{1,25},{9,17},{17,9},{25,1},{2,26},{10... | collective-permute-start | bytes 61448 | tf_op jit(solution)/shard_map/ppermute | solution.py:515
  32.1 5.6 %collective-permute-start.13 = (f32[40,128]{1,0:T(8,128)S(1)}, f32[40,128]{1,0:T(8,128)S(1)}, u32[]{:S(2)}, u32[]{:S(2)}) collective-permute-start(f32[40,128]{1,0:T(8,128)S(1)} %get-tuple-element.50.first), channel_id=1, source_target_pairs={{0,16},{8,24},{16,0},{24,8},{1,17},{9,25},{17,1},{25,9},{2,18},{10... | collective-permute-start | bytes 61448 | tf_op jit(solution)/shard_map/ppermute | solution.py:515
  35.5 3.8 %collective-permute-start.14 = (f32[40,128]{1,0:T(8,128)S(1)}, f32[40,128]{1,0:T(8,128)S(1)}, u32[]{:S(2)}, u32[]{:S(2)}) collective-permute-start(f32[40,128]{1,0:T(8,128)S(1)} %get-tuple-element.50.first), channel_id=1, source_target_pairs={{0,8},{8,0},{16,24},{24,16},{1,9},{9,1},{17,25},{25,17},{2,10},{10... | collective-permute-start | bytes 61448 | tf_op jit(solution)/shard_map/ppermute | solution.py:515
  39.3 1.2 %collective-permute-start.15 = (f32[40,128]{1,0:T(8,128)S(1)}, f32[40,128]{1,0:T(8,128)S(1)}, u32[]{:S(2)}, u32[]{:S(2)}) collective-permute-start(f32[40,128]{1,0:T(8,128)S(1)} %shard_map.70.mine_ref), channel_id=1, source_target_pairs={{0,1},{1,0},{2,3},{3,2},{4,5},{5,4},{6,7},{7,6},{8,9},{9,8},{10,11... | collective-permute-start | bytes 61448 | tf_op jit(solution)/shard_map/ppermute | solution.py:515
  46.7 1.4 %collective-permute-start.16 = (f32[40,128]{1,0:T(8,128)S(1)}, f32[40,128]{1,0:T(8,128)S(1)}, u32[]{:S(2)}, u32[]{:S(2)}) collective-permute-start(f32[40,128]{1,0:T(8,128)S(1)} %get-tuple-element.53), channel_id=1, source_target_pairs={{0,1},{1,0},{2,3},{3,2},{4,5},{5,4},{6,7},{7,6},{8,9},{9,8},{10,11... | collective-permute-start | bytes 61448 | tf_op jit(solution)/shard_map/ppermute | solution.py:515
  48.1 4.8 %collective-permute-start.17 = (f32[40,128]{1,0:T(8,128)S(1)}, f32[40,128]{1,0:T(8,128)S(1)}, u32[]{:S(2)}, u32[]{:S(2)}) collective-permute-start(f32[40,128]{1,0:T(8,128)S(1)} %add.25), channel_id=1, source_target_pairs={{0,6},{1,7},{2,4},{3,5},{4,2},{5,3},{6,0},{7,1},{8,14},{9,15},{10,... | collective-permute-start | bytes 61448 | tf_op jit(solution)/shard_map/ppermute | solution.py:515
  48.9 4.0 %collective-permute-start.18 = (f32[40,128]{1,0:T(8,128)S(1)}, f32[40,128]{1,0:T(8,128)S(1)}, u32[]{:S(2)}, u32[]{:S(2)}) collective-permute-start(f32[40,128]{1,0:T(8,128)S(1)} %add.25), channel_id=1, source_target_pairs={{0,4},{1,5},{2,6},{3,7},{4,0},{5,1},{6,2},{7,3},{8,12},{9,13},{10,... | collective-permute-start | bytes 61448 | tf_op jit(solution)/shard_map/ppermute | solution.py:515
  50.3 3.8 %collective-permute-start.19 = (f32[40,128]{1,0:T(8,128)S(1)}, f32[40,128]{1,0:T(8,128)S(1)}, u32[]{:S(2)}, u32[]{:S(2)}) collective-permute-start(f32[40,128]{1,0:T(8,128)S(1)} %add.25), channel_id=1, source_target_pairs={{0,2},{1,3},{2,0},{3,1},{4,6},{5,7},{6,4},{7,5},{8,10},{9,11},{10,... | collective-permute-start | bytes 61448 | tf_op jit(solution)/shard_map/ppermute | solution.py:515
  54.1 5.6 %collective-permute-start.20 = (f32[40,128]{1,0:T(8,128)S(1)}, f32[40,128]{1,0:T(8,128)S(1)}, u32[]{:S(2)}, u32[]{:S(2)}) collective-permute-start(f32[40,128]{1,0:T(8,128)S(1)} %add_add_fusion.1), channel_id=1, source_target_pairs={{0,24},{8,16},{16,8},{24,0},{1,25},{9,17},{17,9},{25,1},{2,26},{10... | collective-permute-start | bytes 61448 | tf_op jit(solution)/shard_map/ppermute | solution.py:515
  55.6 4.7 %collective-permute-start.21 = (f32[40,128]{1,0:T(8,128)S(1)}, f32[40,128]{1,0:T(8,128)S(1)}, u32[]{:S(2)}, u32[]{:S(2)}) collective-permute-start(f32[40,128]{1,0:T(8,128)S(1)} %add_add_fusion.1), channel_id=1, source_target_pairs={{0,16},{8,24},{16,0},{24,8},{1,17},{9,25},{17,1},{25,9},{2,18},{10... | collective-permute-start | bytes 61448 | tf_op jit(solution)/shard_map/ppermute | solution.py:515
  56.5 3.9 %collective-permute-start.22 = (f32[40,128]{1,0:T(8,128)S(1)}, f32[40,128]{1,0:T(8,128)S(1)}, u32[]{:S(2)}, u32[]{:S(2)}) collective-permute-start(f32[40,128]{1,0:T(8,128)S(1)} %add_add_fusion.1), channel_id=1, source_target_pairs={{0,8},{8,0},{16,24},{24,16},{1,9},{9,1},{17,25},{25,17},{2,10},{10... | collective-permute-start | bytes 61448 | tf_op jit(solution)/shard_map/ppermute | solution.py:515
  60.5 1.2 %collective-permute-start.23 = (f32[40,128]{1,0:T(8,128)S(1)}, f32[40,128]{1,0:T(8,128)S(1)}, u32[]{:S(2)}, u32[]{:S(2)}) collective-permute-start(f32[40,128]{1,0:T(8,128)S(1)} %add_add_fusion.mine_ref), channel_id=1, source_target_pairs={{0,1},{1,0},{2,3},{3,2},{4,5},{5,4},{6,7},{7,6},{8,9},{9,8},{10,11... | collective-permute-start | bytes 61448 | tf_op jit(solution)/shard_map/ppermute | solution.py:515

commit v13 on v12

--- a/solution.py
+++ b/solution.py
@@ -356,12 +356,13 @@
     lane = lax.broadcasted_iota(jnp.int32, (SUB, LANES), 1)
     sub = lax.broadcasted_iota(jnp.int32, (SUB, LANES), 0)
     rows = [gram[SUB * i : SUB * (i + 1)] for i in range(count)]
+    columns = [lane_spread(rows[0], l) for l in range(SUB)]
     for block in range(count):
         base = SUB * block
         here = (lane >= base) & (lane < base + SUB)
-        shelf = 2 * SUB * base
+        shelf = 3 * SUB * base
         for l in range(SUB):
-            board[pl.ds(shelf + SUB * l, SUB), :] = lane_spread(rows[block], base + l)
+            board[pl.ds(shelf + SUB * l, SUB), :] = columns[l]
         low = [
             [board[pl.ds(shelf + SUB * l + k, SUB, stride=0), :] for l in range(k + 1)]
             for k in range(SUB)
@@ -383,6 +384,7 @@
         for k in range(1, SUB):
             merged = jnp.where(sub == k, scaled[k], merged)
         work[pl.ds(base, SUB), :] = merged
+        shelf += SUB
         for i in range(block + 1, (block // GROUP + 1) * GROUP):
             weights = []
             rest = jnp.where(here, 0.0, rows[i])
@@ -391,6 +393,13 @@
                 for m in range(l):
                     weight = weight - weights[m] * low[l][m]
                 weights.append(weight * inv[l])
+            if i == block + 1:
+                columns = [lane_spread(rows[i], base + SUB + l) for l in range(SUB)]
+                for l in range(SUB):
+                    board[pl.ds(shelf + SUB * l, SUB), :] = weights[l]
+                    for k in range(SUB):
+                        across = board[pl.ds(shelf + SUB * l + k, SUB, stride=0), :]
+                        columns[k] = columns[k] - weights[l] * across
             for l in range(SUB):
                 rest = rest - weights[l] * scaled[l]
             rows[i] = rest
@@ -404,6 +413,7 @@
             here = (lane >= first) & (lane < base + SUB)
             for i in range(block + 1, count):
                 rows[i] = jnp.where(here, 0.0, rows[i]) - update[SUB * i : SUB * (i + 1)]
+            columns = [lane_spread(rows[block + 1], base + SUB + l) for l in range(SUB)]
 
 
 def factorize(par, mine_ref, other_ref, gram, work, board):
@@ -515,12 +525,11 @@
     return lax.ppermute(value, axis, [(i, i ^ mask) for i in range(lax.axis_size(axis))])
 
 
-def add_four(first, second, third, fourth, *rest):
-    out_ref = rest[len(rest) // 2]
+def add_four(first, second, third, fourth, _, out_ref):
     out_ref[...] = (first[...] + fourth[...]) + (third[...] + second[...])
 
 
-def sum_over(value, axis, first_bit, beside=None, held=()):
+def sum_over(value, axis, first_bit, beside=None):
     bits = lax.axis_size(axis).bit_length() - 1
     while first_bit < bits:
         low = 1 << first_bit
@@ -530,28 +539,26 @@
             if beside is None:
                 value = (three + two) + (one + value)
             else:
-                anywhere = pl.BlockSpec(memory_space=pl.ANY)
-                value, *held = pl.pallas_call(
+                value = pl.pallas_call(
                     add_four,
-                    out_shape=[jax.ShapeDtypeStruct(x.shape, x.dtype) for x in (value, *held)],
-                    in_specs=[VMEM] * 4 + [anywhere] * (1 + len(held)),
-                    out_specs=[VMEM] + [anywhere] * len(held),
-                    input_output_aliases={5 + i: 1 + i for i in range(len(held))},
+                    out_shape=jax.ShapeDtypeStruct(value.shape, value.dtype),
+                    in_specs=[VMEM] * 4 + [pl.BlockSpec(memory_space=pl.ANY)],
+                    out_specs=VMEM,
                     compiler_params=params(),
-                )(value, three, two, one, beside, *held)
+                )(value, three, two, one, beside)
                 beside = None
             first_bit += 2
         else:
             value = value + swapped(value, axis, low)
             first_bit += 1
-    return value, held
-
-
-def sum_devices(kept, sent, beside=(None, None), held=()):
+    return value
+
+
+def sum_devices(kept, sent, beside=(None, None)):
     mine = kept + swapped(sent, "col", 1)
-    mine, held = sum_over(mine, "col", 1, beside[0], held)
-    mine, _ = sum_over(mine, "row", 0, beside[1])
-    return mine, swapped(mine, "col", 1), held
+    mine = sum_over(mine, "row", 0, beside[0])
+    mine = sum_over(mine, "col", 1, beside[1])
+    return mine, swapped(mine, "col", 1)
 
 
 def body(tangents, sea_mask, levels, current):
@@ -572,7 +579,7 @@
     rows_sent = (shape_of(comps * HALO + 1, cols, modes),) * 2
     halves = (shape_of(modes // 4 + SUB, modes),) * 2
     square = pltpu.VMEM((modes, modes), jnp.float32)
-    board = pltpu.VMEM((2 * SUB * modes, LANES), jnp.float32)
+    board = pltpu.VMEM((3 * SUB * modes, LANES), jnp.float32)
     factor = pltpu.VMEM((2 * modes, 2 * modes), jnp.bfloat16)
 
     def call(
@@ -677,8 +684,8 @@
     middle = inside(0, start)
     state = inside(1, middle)
 
-    mine, other, packed = sum_devices(kept, sent, (middle, state), packed)
     halos = swap_columns(packed)
+    mine, other = sum_devices(kept, sent, (middle, state))
     _, _, state = call(
         mend_only,
         (block,) * 3,
@@ -721,7 +728,7 @@
     )[0]
     height = comps * rows * cols // TILES
     tiled = shape_of(TILES, height, modes)
-    mine, other, _ = sum_devices(kept, sent)
+    mine, other = sum_devices(kept, sent)
     out, logs = call(
         finish,
         (tiled, shape_of(1, modes)),

time: 68 us -> 67.7 us (level)
  starting transfers between devices: 26.6 us -> 27.5 us
  Pallas kernels: 29.6 us -> 28.8 us
    ppermute x16, starting transfers between devices: 18 us -> 19.1 us  [swapped(): lax.ppermute(value, axis, [(i, i ^ mask) for i in range(lax.axis_size(axi...]
    pallas_call x14, Pallas kernels: 29.6 us -> 28.8 us  [call(): pl.pallas_call(kernel, out_shape=outs, in_specs=specs or [SMEM] + [VMEM]...]
  transfers between devices with their start and end apart: 24 -> 24, of which waited for: 12 -> 11; matrix products, arithmetic and copies ran while one was open for 0% -> 0% of each run, Pallas kernels for 20% -> 20%
where the time goes in v13:
time: 67.7 us; the launch traced here: 67.5 us
  Pallas kernels  28.8 us (43%)
  starting transfers between devices  27.5 us (41%)
  waiting for transfers between devices  10.2 us (15%)
  between operations  0.85 us (1%)
    pallas_call x14, Pallas kernels, call(): pl.pallas_call(kernel, out_shape=outs, in_specs=specs or [SMEM] + [VMEM]...  28.8 us
    ppermute x16, starting transfers between devices, swapped(): lax.ppermute(value, axis, [(i, i ^ mask) for i in range(lax.axis_size(axi...  19.1 us
    ppermute x16, waiting for transfers between devices, swapped(): lax.ppermute(value, axis, [(i, i ^ mask) for i in range(lax.axis_size(axi...  8.89 us
    ppermute x4, starting transfers between devices, swap_pairs(): lax.ppermute(far_value, axis, far)  4.69 us
    ppermute x4, starting transfers between devices, swap_pairs(): lax.ppermute(near_value, axis, near)  3.72 us
  transfers between devices with their start and end apart: 24, of which 11 were waited for; matrix products, arithmetic and copies ran while one was open for 0% of the time, Pallas kernels for 20%

profile of v13, /device:TPU:0, one launch (start us, length us, event | category | flops | bytes accessed | tf_op | source)
XLA Modules:
  0.0 67.5 jit_solution(3720736425642401505)
XLA Ops:
  0.7 1.9 %shard_map.60 = (f32[13,32,128]{2,1,0:T(8,128)S(1)}, f32[13,32,128]{2,1,0:T(8,128)S(1)}) custom-call(s32[2]{0:T(128)S(1)} %pad_add_fusion.par, f32[3,64,32,128]{3,2,1,0:T(8,128)} %t_ref.3, s32[32,64]{1,0:T(8,128)} %bitcast.9, s32[32,64]{1,0:T(8,128)} %bitcast.11, f32[32,64]{1,0:T(8,128)} %bitcast.13), custom_call_target="tpu_custom_call" | custom-call | flops 5000000000 | bytes 15000000 | tf_op jit(solution)/shard_map/pallas_call | solution.py:588
  2.6 3.1 %collective-permute-start = (f32[13,32,128]{2,1,0:T(8,128)S(1)}, f32[13,32,128]{2,1,0:T(8,128)S(1)}, u32[]{:S(2)}, u32[]{:S(2)}) collective-permute-start(f32[13,32,128]{2,1,0:T(8,128)S(1)} %get-tuple-element.29), channel_id=1, source_target_pairs={{0,8},{8,0},{16,24},{24,16},{1,9},{9,1},{17,25},{25,17},{2,10},{10... | collective-permute-start | bytes 638984 | tf_op jit(solution)/shard_map/ppermute | solution.py:521
  6.4 3.1 %shard_map.59 = (f32[3,36,72,128]{3,2,1,0:T(8,128)S(1)}, f32[3,36,72,128]{3,2,1,0:T(8,128)S(1)}, f32[72,128]{1,0:T(8,128)S(1)}, f32[392,128]{1,0:T(8,128)S(1)}, f32[392,128]{1,0:T(8,128)S(1)}) custom-call(s32[2]{0:T(128)S(1)} %pad_add_fusion.par, f32[3,64,32,128]{3,2,1,0:T(8,128)S(1)} %copy-done, s32[32,64]{1,0:T(8,128)} %bitcast.10, s32[32,64]{1,0:T(8,128)} %bitcast.12, ...), custom_call_target="tpu_custom_call" | custom-call | flops 3000000000 | bytes 9000000 | tf_op jit(solution)/shard_map/pallas_call | solution.py:588
  9.6 2.5 %collective-permute-start.3 = (f32[392,128]{1,0:T(8,128)S(1)}, f32[392,128]{1,0:T(8,128)S(1)}, u32[]{:S(2)}, u32[]{:S(2)}) collective-permute-start(f32[392,128]{1,0:T(8,128)S(1)} %get-tuple-element.35), channel_id=1, source_target_pairs={{0,7},{1,2},{2,1},{3,4},{4,3},{5,6},{6,5},{7,0},{8,15},{9,10},{10,... | collective-permute-start | bytes 602120 | tf_op jit(solution)/shard_map/ppermute | solution.py:521
  12.1 1.2 %shard_map.61._.refs_0_ = f32[3,36,72,128]{3,2,1,0:T(8,128)S(1)} custom-call(f32[3,36,72,128]{3,2,1,0:T(8,128)S(1)} %get-tuple-element.27.source.state_in, f32[3,36,72,128]{3,2,1,0:T(8,128)S(1)} %get-tuple-element.28.coef_ref.coef_in, f32[72,128]{1,0:T(8,128)S(1)} %get-tuple-element.31.spin_ref), custom_call_target="tpu_custom_call" | custom-call | flops 2000000000 | bytes 6000000 | tf_op jit(solution)/shard_map/pallas_call | solution.py:588
  13.3 1.0 %shard_map.62 = (f32[3,36,72,128]{3,2,1,0:T(8,128)S(1)}, f32[3,36,72,128]{3,2,1,0:T(8,128)S(1)}, f32[56,128]{1,0:T(8,128)S(1)}, f32[56,128]{1,0:T(8,128)S(1)}) custom-call(s32[2]{0:T(128)S(1)} %pad_add_fusion.par, f32[3,36,72,128]{3,2,1,0:T(8,128)S(1)} %get-tuple-element.27.source.state_in, ...), custom_call_target="tpu_custom_call", output_to_operand_aliasing={{0}: (1, {}), {1}: (2, {})} | custom-call | flops 1000000000 | bytes 3000000 | tf_op jit(solution)/shard_map/pallas_call | solution.py:588
  15.7 1.6 %shard_map.64.state_in = f32[3,36,72,128]{3,2,1,0:T(8,128)S(1)} custom-call(f32[3,36,72,128]{3,2,1,0:T(8,128)S(1)} %shard_map.63.source.middle_in, f32[3,36,72,128]{3,2,1,0:T(8,128)S(1)} %get-tuple-element.33.coef_ref.coef_in, f32[72,128]{1,0:T(8,128)S(1)} %get-tuple-element.31.spin_ref), custom_call_target="tpu_custom_call" | custom-call | flops 2000000000 | bytes 6000000 | tf_op jit(solution)/shard_map/pallas_call | solution.py:588
  17.4 1.2 %collective-permute-done.5.d = f32[56,128]{1,0:T(8,128)S(1)} collective-permute-done((f32[56,128]{1,0:T(8,128)S(1)}, f32[56,128]{1,0:T(8,128)S(1)}, u32[]{:S(2)}, u32[]{:S(2)}) %collective-permute-start.5) | collective-permute-done | bytes 28704 | tf_op jit(solution)/shard_map/ppermute | solution.py:521
  18.6 2.2 %shard_map.65 = (f32[3,36,72,128]{3,2,1,0:T(8,128)S(1)}, f32[3,36,72,128]{3,2,1,0:T(8,128)S(1)}, f32[3,36,72,128]{3,2,1,0:T(8,128)S(1)}, f32[3,36,72,128]{3,2,1,...) custom-call(s32[2]{0:T(128)S(1)} %pad_add_fusion.par, ...), custom_call_target="tpu_custom_call", output_to_operand_aliasing={{0}: (1, {}), {1}: (2, {}), {2}: (3, {}), {3}: (4, {})} | custom-call | flops 2000000000 | bytes 6000000 | tf_op jit(solution)/shard_map/pallas_call | solution.py:588
  21.4 0.8 %collective-permute-start.7 = (f32[432,128]{1,0:T(8,128)S(1)}, f32[432,128]{1,0:T(8,128)S(1)}, u32[]{:S(2)}, u32[]{:S(2)}) collective-permute-start(f32[432,128]{1,0:T(8,128)S(1)} %get-tuple-element.41), channel_id=1, source_target_pairs={{0,7},{1,2},{2,1},{3,4},{4,3},{5,6},{6,5},{7,0},{8,15},{9,10},{10,... | collective-permute-start | bytes 663560 | tf_op jit(solution)/shard_map/ppermute | solution.py:521
  22.2 5.3 %collective-permute-start.10 = (f32[40,128]{1,0:T(8,128)S(1)}, f32[40,128]{1,0:T(8,128)S(1)}, u32[]{:S(2)}, u32[]{:S(2)}) collective-permute-start(f32[40,128]{1,0:T(8,128)S(1)} %add.24.first), channel_id=1, source_target_pairs={{0,16},{8,24},{16,0},{24,8},{1,17},{9,25},{17,1},{25,9},{2,18},{10... | collective-permute-start | bytes 61448 | tf_op jit(solution)/shard_map/ppermute | solution.py:525
  27.5 1.5 %collective-permute-start.9 = (f32[40,128]{1,0:T(8,128)S(1)}, f32[40,128]{1,0:T(8,128)S(1)}, u32[]{:S(2)}, u32[]{:S(2)}) collective-permute-start(f32[40,128]{1,0:T(8,128)S(1)} %add.24.first), channel_id=1, source_target_pairs={{0,24},{8,16},{16,8},{24,0},{1,25},{9,17},{17,9},{25,1},{2,26},{10... | collective-permute-start | bytes 61448 | tf_op jit(solution)/shard_map/ppermute | solution.py:525
  29.1 1.8 %shard_map.66.source.middle_in._ = f32[3,36,72,128]{3,2,1,0:T(8,128)S(1)} custom-call(f32[3,36,72,128]{3,2,1,0:T(8,128)S(1)} %get-tuple-element.38.source.start_in, f32[3,36,72,128]{3,2,1,0:T(8,128)S(1)} %get-tuple-element.39.coef_ref, f32[72,128]{1,0:T(8,128)S(1)} %get-tuple-element.31.spin_ref), custom_call_target="tpu_custom_call" | custom-call | flops 2000000000 | bytes 6000000 | tf_op jit(solution)/shard_map/pallas_call | solution.py:588
  31.4 1.7 %collective-permute-done.9.second = f32[40,128]{1,0:T(8,128)S(1)} collective-permute-done((f32[40,128]{1,0:T(8,128)S(1)}, f32[40,128]{1,0:T(8,128)S(1)}, u32[]{:S(2)}, u32[]{:S(2)}) %collective-permute-start.9) | collective-permute-done | bytes 20512 | tf_op jit(solution)/shard_map/ppermute | solution.py:525
  33.9 0.9 %collective-permute-start.13 = (f32[40,128]{1,0:T(8,128)S(1)}, f32[40,128]{1,0:T(8,128)S(1)}, u32[]{:S(2)}, u32[]{:S(2)}) collective-permute-start(f32[40,128]{1,0:T(8,128)S(1)} %shard_map.69.first), channel_id=1, source_target_pairs={{0,4},{1,5},{2,6},{3,7},{4,0},{5,1},{6,2},{7,3},{8,12},{9,13},{10,... | collective-permute-start | bytes 61448 | tf_op jit(solution)/shard_map/ppermute | solution.py:525
  34.7 2.0 %collective-permute-start.14 = (f32[40,128]{1,0:T(8,128)S(1)}, f32[40,128]{1,0:T(8,128)S(1)}, u32[]{:S(2)}, u32[]{:S(2)}) collective-permute-start(f32[40,128]{1,0:T(8,128)S(1)} %shard_map.69.first), channel_id=1, source_target_pairs={{0,2},{1,3},{2,0},{3,1},{4,6},{5,7},{6,4},{7,5},{8,10},{9,11},{10,... | collective-permute-start | bytes 61448 | tf_op jit(solution)/shard_map/ppermute | solution.py:525
  36.7 1.7 %shard_map.67.state_in._ = f32[3,36,72,128]{3,2,1,0:T(8,128)S(1)} custom-call(f32[3,36,72,128]{3,2,1,0:T(8,128)S(1)} %shard_map.66.source.middle_in._, f32[3,36,72,128]{3,2,1,0:T(8,128)S(1)} %get-tuple-element.39.coef_ref, f32[72,128]{1,0:T(8,128)S(1)} %get-tuple-element.31.spin_ref), custom_call_target="tpu_custom_call" | custom-call | flops 2000000000 | bytes 6000000 | tf_op jit(solution)/shard_map/pallas_call | solution.py:588
  38.6 1.1 %shard_map.68 = (f32[3,36,72,128]{3,2,1,0:T(8,128)S(1)}, f32[3,36,72,128]{3,2,1,0:T(8,128)S(1)}, f32[3,36,72,128]{3,2,1,0:T(8,128)S(1)}) custom-call(s32[2]{0:T(128)S(1)} %pad_add_fusion.par, f32[3,36,72,128]{3,2,1,0:T(8,128)S(1)} %get-tuple-element.38.source.start_in, ...), custom_call_target="tpu_custom_call", output_to_operand_aliasing={{0}: (1, {}), {1}: (2, {}), {2}: (3, {})} | custom-call | flops 1000000000 | bytes 3000000 | tf_op jit(solution)/shard_map/pallas_call | solution.py:588
  39.8 3.1 %shard_map.71 = (f32[128,128]{1,0:T(8,128)S(1)}, f32[1,128]{1,0:T(1,128)S(1)}) custom-call(s32[2]{0:T(128)S(1)} %pad_add_fusion.par, f32[40,128]{1,0:T(8,128)S(1)} %shard_map.70.mine_ref, f32[40,128]{1,0:T(8,128)S(1)} %collective-permute-done.15.other_ref, f32[1,128]{1,0:T(1,128)S(1)} %broadcast_in_dim.3.prior_ref, ...), custom_call_target="tpu_custom_call" | custom-call | flops 10000000 | bytes 30000 | tf_op jit(solution)/shard_map/pallas_call | solution.py:588
  42.8 2.7 %shard_map.72 = (f32[3,32,64,128]{3,2,1,0:T(8,128)S(1)}, f32[40,128]{1,0:T(8,128)S(1)}, f32[40,128]{1,0:T(8,128)S(1)}) custom-call(s32[2]{0:T(128)S(1)} %pad_add_fusion.par, f32[3,36,72,128]{3,2,1,0:T(8,128)S(1)} %get-tuple-element.42._.state, f32[128,128]{1,0:T(8,128)S(1)} %get-tuple-element.45.inverse_ref), custom_call_target="tpu_custom_call" | custom-call | flops 2000000000 | bytes 6000000 | tf_op jit(solution)/shard_map/pallas_call | solution.py:588
  46.1 0.8 %collective-permute-done.16 = f32[40,128]{1,0:T(8,128)S(1)} collective-permute-done((f32[40,128]{1,0:T(8,128)S(1)}, f32[40,128]{1,0:T(8,128)S(1)}, u32[]{:S(2)}, u32[]{:S(2)}) %collective-permute-start.16) | collective-permute-done | bytes 20512 | tf_op jit(solution)/shard_map/ppermute | solution.py:525
  46.9 2.3 %collective-permute-start.17 = (f32[40,128]{1,0:T(8,128)S(1)}, f32[40,128]{1,0:T(8,128)S(1)}, u32[]{:S(2)}, u32[]{:S(2)}) collective-permute-start(f32[40,128]{1,0:T(8,128)S(1)} %add.25), channel_id=1, source_target_pairs={{0,24},{8,16},{16,8},{24,0},{1,25},{9,17},{17,9},{25,1},{2,26},{10... | collective-permute-start | bytes 61448 | tf_op jit(solution)/shard_map/ppermute | solution.py:525
  49.2 2.1 %collective-permute-start.19 = (f32[40,128]{1,0:T(8,128)S(1)}, f32[40,128]{1,0:T(8,128)S(1)}, u32[]{:S(2)}, u32[]{:S(2)}) collective-permute-start(f32[40,128]{1,0:T(8,128)S(1)} %add.25), channel_id=1, source_target_pairs={{0,8},{8,0},{16,24},{24,16},{1,9},{9,1},{17,25},{25,17},{2,10},{10... | collective-permute-start | bytes 61448 | tf_op jit(solution)/shard_map/ppermute | solution.py:525
  51.3 1.2 %collective-permute-done.17 = f32[40,128]{1,0:T(8,128)S(1)} collective-permute-done((f32[40,128]{1,0:T(8,128)S(1)}, f32[40,128]{1,0:T(8,128)S(1)}, u32[]{:S(2)}, u32[]{:S(2)}) %collective-permute-start.17) | collective-permute-done | bytes 20512 | tf_op jit(solution)/shard_map/ppermute | solution.py:525
  52.5 1.4 %collective-permute-done.18 = f32[40,128]{1,0:T(8,128)S(1)} collective-permute-done((f32[40,128]{1,0:T(8,128)S(1)}, f32[40,128]{1,0:T(8,128)S(1)}, u32[]{:S(2)}, u32[]{:S(2)}) %collective-permute-start.18) | collective-permute-done | bytes 20512 | tf_op jit(solution)/shard_map/ppermute | solution.py:525
  53.9 2.1 %collective-permute-start.20 = (f32[40,128]{1,0:T(8,128)S(1)}, f32[40,128]{1,0:T(8,128)S(1)}, u32[]{:S(2)}, u32[]{:S(2)}) collective-permute-start(f32[40,128]{1,0:T(8,128)S(1)} %add_add_fusion.1), channel_id=1, source_target_pairs={{0,6},{1,7},{2,4},{3,5},{4,2},{5,3},{6,0},{7,1},{8,14},{9,15},{10,... | collective-permute-start | bytes 61448 | tf_op jit(solution)/shard_map/ppermute | solution.py:525
  56.0 0.8 %collective-permute-start.21 = (f32[40,128]{1,0:T(8,128)S(1)}, f32[40,128]{1,0:T(8,128)S(1)}, u32[]{:S(2)}, u32[]{:S(2)}) collective-permute-start(f32[40,128]{1,0:T(8,128)S(1)} %add_add_fusion.1), channel_id=1, source_target_pairs={{0,4},{1,5},{2,6},{3,7},{4,0},{5,1},{6,2},{7,3},{8,12},{9,13},{10,... | collective-permute-start | bytes 61448 | tf_op jit(solution)/shard_map/ppermute | solution.py:525
  57.5 1.4 %collective-permute-done.20 = f32[40,128]{1,0:T(8,128)S(1)} collective-permute-done((f32[40,128]{1,0:T(8,128)S(1)}, f32[40,128]{1,0:T(8,128)S(1)}, u32[]{:S(2)}, u32[]{:S(2)}) %collective-permute-start.20) | collective-permute-done | bytes 20512 | tf_op jit(solution)/shard_map/ppermute | solution.py:525
  58.8 0.9 %collective-permute-done.21 = f32[40,128]{1,0:T(8,128)S(1)} collective-permute-done((f32[40,128]{1,0:T(8,128)S(1)}, f32[40,128]{1,0:T(8,128)S(1)}, u32[]{:S(2)}, u32[]{:S(2)}) %collective-permute-start.21) | collective-permute-done | bytes 20512 | tf_op jit(solution)/shard_map/ppermute | solution.py:525
  59.8 0.8 %collective-permute-done.22 = f32[40,128]{1,0:T(8,128)S(1)} collective-permute-done((f32[40,128]{1,0:T(8,128)S(1)}, f32[40,128]{1,0:T(8,128)S(1)}, u32[]{:S(2)}, u32[]{:S(2)}) %collective-permute-start.22) | collective-permute-done | bytes 20512 | tf_op jit(solution)/shard_map/ppermute | solution.py:525
  60.6 1.1 %shard_map.73 = bf16[3,64,32,256]{3,2,1,0:T(8,128)(2,1)S(1)} custom-call(f32[3,32,64,128]{3,2,1,0:T(8,128)S(1)} %get-tuple-element.49.turned), custom_call_target="tpu_custom_call" | custom-call | flops 1000000000 | bytes 3000000 | tf_op jit(solution)/shard_map/pallas_call | solution.py:588
  61.8 5.6 %shard_map.74 = (f32[24,256,128]{2,1,0:T(8,128)}, f32[1,128]{1,0:T(1,128)}) custom-call(s32[2]{0:T(128)S(1)} %pad_add_fusion.par, f32[40,128]{1,0:T(8,128)S(1)} %add_add_fusion.mine_ref, f32[40,128]{1,0:T(8,128)S(1)} %collective-permute-done.23.other_ref, f32[1,128]{1,0:T(1,128)S(1)} %get-tuple-element.48.prior_ref, bf16[24,256,256]{2,1,0:T(8,128)(2,1)S(1)} %bitcast.8), custom_call_target="tpu_custom_call" | custom-call | flops 1000000000 | bytes 3000000 | tf_op jit(solution)/shard_map/pallas_call | solution.py:588
  (40 shorter events, 5.6 us)
Async XLA Ops:
  0.7 5.7 %copy-start = (f32[3,64,32,128]{3,2,1,0:T(8,128)S(1)}, f32[3,64,32,128]{3,2,1,0:T(8,128)}, u32[]{:S(2)}) copy-start(f32[3,64,32,128]{3,2,1,0:T(8,128)} %t_ref.3) | copy-start | bytes 9437188
  2.6 10.6 %collective-permute-start = (f32[13,32,128]{2,1,0:T(8,128)S(1)}, f32[13,32,128]{2,1,0:T(8,128)S(1)}, u32[]{:S(2)}, u32[]{:S(2)}) collective-permute-start(f32[13,32,128]{2,1,0:T(8,128)S(1)} %get-tuple-element.29), channel_id=1, source_target_pairs={{0,8},{8,0},{16,24},{24,16},{1,9},{9,1},{17,25},{25,17},{2,10},{10... | collective-permute-start | bytes 638984 | tf_op jit(solution)/shard_map/ppermute | solution.py:521
  5.7 7.6 %collective-permute-start.1 = (f32[13,32,128]{2,1,0:T(8,128)S(1)}, f32[13,32,128]{2,1,0:T(8,128)S(1)}, u32[]{:S(2)}, u32[]{:S(2)}) collective-permute-start(f32[13,32,128]{2,1,0:T(8,128)S(1)} %get-tuple-element.30), channel_id=1, source_target_pairs={{8,16},{16,8},{9,17},{17,9},{10,18},{18,10},{11,19},{19,11},{12,20... | collective-permute-start | bytes 638984 | tf_op jit(solution)/shard_map/ppermute | solution.py:521
  9.5 7.9 %collective-permute-start.2 = (f32[392,128]{1,0:T(8,128)S(1)}, f32[392,128]{1,0:T(8,128)S(1)}, u32[]{:S(2)}, u32[]{:S(2)}) collective-permute-start(f32[392,128]{1,0:T(8,128)S(1)} %get-tuple-element.34), channel_id=1, source_target_pairs={{0,1},{1,0},{2,3},{3,2},{4,5},{5,4},{6,7},{7,6},{8,9},{9,8},{10,11... | collective-permute-start | bytes 602120 | tf_op jit(solution)/shard_map/ppermute | solution.py:521
  9.6 7.8 %collective-permute-start.3 = (f32[392,128]{1,0:T(8,128)S(1)}, f32[392,128]{1,0:T(8,128)S(1)}, u32[]{:S(2)}, u32[]{:S(2)}) collective-permute-start(f32[392,128]{1,0:T(8,128)S(1)} %get-tuple-element.35), channel_id=1, source_target_pairs={{0,7},{1,2},{2,1},{3,4},{4,3},{5,6},{6,5},{7,0},{8,15},{9,10},{10,... | collective-permute-start | bytes 602120 | tf_op jit(solution)/shard_map/ppermute | solution.py:521
  14.3 3.1 %collective-permute-start.4 = (f32[56,128]{1,0:T(8,128)S(1)}, f32[56,128]{1,0:T(8,128)S(1)}, u32[]{:S(2)}, u32[]{:S(2)}) collective-permute-start(f32[56,128]{1,0:T(8,128)S(1)} %get-tuple-element.36), channel_id=1, source_target_pairs={{0,1},{1,0},{2,3},{3,2},{4,5},{5,4},{6,7},{7,6},{8,9},{9,8},{10,11... | collective-permute-start | bytes 86024 | tf_op jit(solution)/shard_map/ppermute | solution.py:521
  14.4 4.3 %collective-permute-start.5 = (f32[56,128]{1,0:T(8,128)S(1)}, f32[56,128]{1,0:T(8,128)S(1)}, u32[]{:S(2)}, u32[]{:S(2)}) collective-permute-start(f32[56,128]{1,0:T(8,128)S(1)} %get-tuple-element.37), channel_id=1, source_target_pairs={{0,7},{1,2},{2,1},{3,4},{4,3},{5,6},{6,5},{7,0},{8,15},{9,10},{10,... | collective-permute-start | bytes 86024 | tf_op jit(solution)/shard_map/ppermute | solution.py:521
  20.8 1.4 %collective-permute-start.8 = (f32[40,128]{1,0:T(8,128)S(1)}, f32[40,128]{1,0:T(8,128)S(1)}, u32[]{:S(2)}, u32[]{:S(2)}) collective-permute-start(f32[40,128]{1,0:T(8,128)S(1)} %get-tuple-element.44), channel_id=1, source_target_pairs={{0,1},{1,0},{2,3},{3,2},{4,5},{5,4},{6,7},{7,6},{8,9},{9,8},{10,11... | collective-permute-start | bytes 61448 | tf_op jit(solution)/shard_map/ppermute | solution.py:525
  20.9 17.7 %collective-permute-start.6 = (f32[432,128]{1,0:T(8,128)S(1)}, f32[432,128]{1,0:T(8,128)S(1)}, u32[]{:S(2)}, u32[]{:S(2)}) collective-permute-start(f32[432,128]{1,0:T(8,128)S(1)} %get-tuple-element.40), channel_id=1, source_target_pairs={{0,1},{1,0},{2,3},{3,2},{4,5},{5,4},{6,7},{7,6},{8,9},{9,8},{10,11... | collective-permute-start | bytes 663560 | tf_op jit(solution)/shard_map/ppermute | solution.py:521
  21.4 17.2 %collective-permute-start.7 = (f32[432,128]{1,0:T(8,128)S(1)}, f32[432,128]{1,0:T(8,128)S(1)}, u32[]{:S(2)}, u32[]{:S(2)}) collective-permute-start(f32[432,128]{1,0:T(8,128)S(1)} %get-tuple-element.41), channel_id=1, source_target_pairs={{0,7},{1,2},{2,1},{3,4},{4,3},{5,6},{6,5},{7,0},{8,15},{9,10},{10,... | collective-permute-start | bytes 663560 | tf_op jit(solution)/shard_map/ppermute | solution.py:521
  22.2 8.7 %collective-permute-start.10 = (f32[40,128]{1,0:T(8,128)S(1)}, f32[40,128]{1,0:T(8,128)S(1)}, u32[]{:S(2)}, u32[]{:S(2)}) collective-permute-start(f32[40,128]{1,0:T(8,128)S(1)} %add.24.first), channel_id=1, source_target_pairs={{0,16},{8,24},{16,0},{24,8},{1,17},{9,25},{17,1},{25,9},{2,18},{10... | collective-permute-start | bytes 61448 | tf_op jit(solution)/shard_map/ppermute | solution.py:525
  27.5 3.9 %collective-permute-start.11 = (f32[40,128]{1,0:T(8,128)S(1)}, f32[40,128]{1,0:T(8,128)S(1)}, u32[]{:S(2)}, u32[]{:S(2)}) collective-permute-start(f32[40,128]{1,0:T(8,128)S(1)} %add.24.first), channel_id=1, source_target_pairs={{0,8},{8,0},{16,24},{24,16},{1,9},{9,1},{17,25},{25,17},{2,10},{10... | collective-permute-start | bytes 61448 | tf_op jit(solution)/shard_map/ppermute | solution.py:525
  27.5 5.6 %collective-permute-start.9 = (f32[40,128]{1,0:T(8,128)S(1)}, f32[40,128]{1,0:T(8,128)S(1)}, u32[]{:S(2)}, u32[]{:S(2)}) collective-permute-start(f32[40,128]{1,0:T(8,128)S(1)} %add.24.first), channel_id=1, source_target_pairs={{0,24},{8,16},{16,8},{24,0},{1,25},{9,17},{17,9},{25,1},{2,26},{10... | collective-permute-start | bytes 61448 | tf_op jit(solution)/shard_map/ppermute | solution.py:525
  33.1 5.3 %collective-permute-start.12 = (f32[40,128]{1,0:T(8,128)S(1)}, f32[40,128]{1,0:T(8,128)S(1)}, u32[]{:S(2)}, u32[]{:S(2)}) collective-permute-start(f32[40,128]{1,0:T(8,128)S(1)} %shard_map.69.first), channel_id=1, source_target_pairs={{0,6},{1,7},{2,4},{3,5},{4,2},{5,3},{6,0},{7,1},{8,14},{9,15},{10,... | collective-permute-start | bytes 61448 | tf_op jit(solution)/shard_map/ppermute | solution.py:525
  33.9 4.6 %collective-permute-start.13 = (f32[40,128]{1,0:T(8,128)S(1)}, f32[40,128]{1,0:T(8,128)S(1)}, u32[]{:S(2)}, u32[]{:S(2)}) collective-permute-start(f32[40,128]{1,0:T(8,128)S(1)} %shard_map.69.first), channel_id=1, source_target_pairs={{0,4},{1,5},{2,6},{3,7},{4,0},{5,1},{6,2},{7,3},{8,12},{9,13},{10,... | collective-permute-start | bytes 61448 | tf_op jit(solution)/shard_map/ppermute | solution.py:525
  34.7 3.8 %collective-permute-start.14 = (f32[40,128]{1,0:T(8,128)S(1)}, f32[40,128]{1,0:T(8,128)S(1)}, u32[]{:S(2)}, u32[]{:S(2)}) collective-permute-start(f32[40,128]{1,0:T(8,128)S(1)} %shard_map.69.first), channel_id=1, source_target_pairs={{0,2},{1,3},{2,0},{3,1},{4,6},{5,7},{6,4},{7,5},{8,10},{9,11},{10,... | collective-permute-start | bytes 61448 | tf_op jit(solution)/shard_map/ppermute | solution.py:525
  38.5 1.2 %collective-permute-start.15 = (f32[40,128]{1,0:T(8,128)S(1)}, f32[40,128]{1,0:T(8,128)S(1)}, u32[]{:S(2)}, u32[]{:S(2)}) collective-permute-start(f32[40,128]{1,0:T(8,128)S(1)} %shard_map.70.mine_ref), channel_id=1, source_target_pairs={{0,1},{1,0},{2,3},{3,2},{4,5},{5,4},{6,7},{7,6},{8,9},{9,8},{10,11... | collective-permute-start | bytes 61448 | tf_op jit(solution)/shard_map/ppermute | solution.py:525
  45.5 1.4 %collective-permute-start.16 = (f32[40,128]{1,0:T(8,128)S(1)}, f32[40,128]{1,0:T(8,128)S(1)}, u32[]{:S(2)}, u32[]{:S(2)}) collective-permute-start(f32[40,128]{1,0:T(8,128)S(1)} %get-tuple-element.47), channel_id=1, source_target_pairs={{0,1},{1,0},{2,3},{3,2},{4,5},{5,4},{6,7},{7,6},{8,9},{9,8},{10,11... | collective-permute-start | bytes 61448 | tf_op jit(solution)/shard_map/ppermute | solution.py:525
  46.9 5.6 %collective-permute-start.17 = (f32[40,128]{1,0:T(8,128)S(1)}, f32[40,128]{1,0:T(8,128)S(1)}, u32[]{:S(2)}, u32[]{:S(2)}) collective-permute-start(f32[40,128]{1,0:T(8,128)S(1)} %add.25), channel_id=1, source_target_pairs={{0,24},{8,16},{16,8},{24,0},{1,25},{9,17},{17,9},{25,1},{2,26},{10... | collective-permute-start | bytes 61448 | tf_op jit(solution)/shard_map/ppermute | solution.py:525
  49.2 4.7 %collective-permute-start.18 = (f32[40,128]{1,0:T(8,128)S(1)}, f32[40,128]{1,0:T(8,128)S(1)}, u32[]{:S(2)}, u32[]{:S(2)}) collective-permute-start(f32[40,128]{1,0:T(8,128)S(1)} %add.25), channel_id=1, source_target_pairs={{0,16},{8,24},{16,0},{24,8},{1,17},{9,25},{17,1},{25,9},{2,18},{10... | collective-permute-start | bytes 61448 | tf_op jit(solution)/shard_map/ppermute | solution.py:525
  49.2 4.7 %collective-permute-start.19 = (f32[40,128]{1,0:T(8,128)S(1)}, f32[40,128]{1,0:T(8,128)S(1)}, u32[]{:S(2)}, u32[]{:S(2)}) collective-permute-start(f32[40,128]{1,0:T(8,128)S(1)} %add.25), channel_id=1, source_target_pairs={{0,8},{8,0},{16,24},{24,16},{1,9},{9,1},{17,25},{25,17},{2,10},{10... | collective-permute-start | bytes 61448 | tf_op jit(solution)/shard_map/ppermute | solution.py:525
  53.9 4.9 %collective-permute-start.20 = (f32[40,128]{1,0:T(8,128)S(1)}, f32[40,128]{1,0:T(8,128)S(1)}, u32[]{:S(2)}, u32[]{:S(2)}) collective-permute-start(f32[40,128]{1,0:T(8,128)S(1)} %add_add_fusion.1), channel_id=1, source_target_pairs={{0,6},{1,7},{2,4},{3,5},{4,2},{5,3},{6,0},{7,1},{8,14},{9,15},{10,... | collective-permute-start | bytes 61448 | tf_op jit(solution)/shard_map/ppermute | solution.py:525
  56.0 3.8 %collective-permute-start.21 = (f32[40,128]{1,0:T(8,128)S(1)}, f32[40,128]{1,0:T(8,128)S(1)}, u32[]{:S(2)}, u32[]{:S(2)}) collective-permute-start(f32[40,128]{1,0:T(8,128)S(1)} %add_add_fusion.1), channel_id=1, source_target_pairs={{0,4},{1,5},{2,6},{3,7},{4,0},{5,1},{6,2},{7,3},{8,12},{9,13},{10,... | collective-permute-start | bytes 61448 | tf_op jit(solution)/shard_map/ppermute | solution.py:525
  56.8 3.8 %collective-permute-start.22 = (f32[40,128]{1,0:T(8,128)S(1)}, f32[40,128]{1,0:T(8,128)S(1)}, u32[]{:S(2)}, u32[]{:S(2)}) collective-permute-start(f32[40,128]{1,0:T(8,128)S(1)} %add_add_fusion.1), channel_id=1, source_target_pairs={{0,2},{1,3},{2,0},{3,1},{4,6},{5,7},{6,4},{7,5},{8,10},{9,11},{10,... | collective-permute-start | bytes 61448 | tf_op jit(solution)/shard_map/ppermute | solution.py:525
  60.6 1.2 %collective-permute-start.23 = (f32[40,128]{1,0:T(8,128)S(1)}, f32[40,128]{1,0:T(8,128)S(1)}, u32[]{:S(2)}, u32[]{:S(2)}) collective-permute-start(f32[40,128]{1,0:T(8,128)S(1)} %add_add_fusion.mine_ref), channel_id=1, source_target_pairs={{0,1},{1,0},{2,3},{3,2},{4,5},{5,4},{6,7},{7,6},{8,9},{9,8},{10,11... | collective-permute-start | bytes 61448 | tf_op jit(solution)/shard_map/ppermute | solution.py:525

commit v14 on v13

--- a/solution.py
+++ b/solution.py
@@ -22,7 +22,7 @@
 SIDE = STEPS
 TILES = 24
 BATCH = 8
-GROUP = 4
+GROUP = 8
 VMEM_LIMIT = 16 * 1024 * 1024
 
 HBM = pl.BlockSpec(memory_space=pltpu.HBM)
@@ -42,13 +42,13 @@
     return jnp.broadcast_to(block[:, lane : lane + 1], (block.shape[0], LANES))
 
 
-def fetch(sources, places, sems):
+def fetch(sources, places, sems, priority=0):
     copies = [
         pltpu.make_async_copy(source, place, sems.at[i])
         for i, (source, place) in enumerate(zip(sources, places))
     ]
     for copy in copies:
-        copy.start()
+        copy.start(priority=priority)
     return copies
 
 
@@ -81,6 +81,7 @@
         [t_ref.at[comp, pl.ds(norths[slot] * (rows - HALO), HALO)] for slot, _, comp in slots],
         [msg.at[pl.ds(comp * HALO, HALO)] for _, msg, comp in slots],
         sems,
+        1,
     )
     lane = lax.broadcasted_iota(jnp.int32, (cols, LANES), 1)
     wide[...] = jnp.zeros_like(wide)
@@ -554,10 +555,10 @@
     return value
 
 
-def sum_devices(kept, sent, beside=(None, None)):
+def sum_devices(kept, sent, order, beside=(None, None)):
     mine = kept + swapped(sent, "col", 1)
-    mine = sum_over(mine, "row", 0, beside[0])
-    mine = sum_over(mine, "col", 1, beside[1])
+    for axis, work in zip(order, beside):
+        mine = sum_over(mine, axis, 1 if axis == "col" else 0, work)
     return mine, swapped(mine, "col", 1)
 
 
@@ -685,7 +686,7 @@
     state = inside(1, middle)
 
     halos = swap_columns(packed)
-    mine, other = sum_devices(kept, sent, (middle, state))
+    mine, other = sum_devices(kept, sent, ("row", "col"), (middle, state))
     _, _, state = call(
         mend_only,
         (block,) * 3,
@@ -728,7 +729,7 @@
     )[0]
     height = comps * rows * cols // TILES
     tiled = shape_of(TILES, height, modes)
-    mine, other = sum_devices(kept, sent)
+    mine, other = sum_devices(kept, sent, ("col", "row"))
     out, logs = call(
         finish,
         (tiled, shape_of(1, modes)),

time: 67.7 us -> 67.7 us (level)
  no operation moved by 1% of the time
where the time goes in v14:
time: 67.7 us; the launch traced here: 67.5 us
  Pallas kernels  28.9 us (43%)
  starting transfers between devices  27.5 us (41%)
  waiting for transfers between devices  10.2 us (15%)
  between operations  0.85 us (1%)
    pallas_call x14, Pallas kernels, call(): pl.pallas_call(kernel, out_shape=outs, in_specs=specs or [SMEM] + [VMEM]...  28.8 us
    ppermute x16, starting transfers between devices, swapped(): lax.ppermute(value, axis, [(i, i ^ mask) for i in range(lax.axis_size(axi...  19.1 us
    ppermute x16, waiting for transfers between devices, swapped(): lax.ppermute(value, axis, [(i, i ^ mask) for i in range(lax.axis_size(axi...  8.9 us
    ppermute x4, starting transfers between devices, swap_pairs(): lax.ppermute(far_value, axis, far)  4.69 us
    ppermute x4, starting transfers between devices, swap_pairs(): lax.ppermute(near_value, axis, near)  3.72 us
  transfers between devices with their start and end apart: 24, of which 11 were waited for; matrix products, arithmetic and copies ran while one was open for 0% of the time, Pallas kernels for 20%

profile of v14, /device:TPU:0, one launch (start us, length us, event | category | flops | bytes accessed | tf_op | source)
XLA Modules:
  0.0 67.5 jit_solution(9236459964216017656)
XLA Ops:
  0.7 1.9 %shard_map.60 = (f32[13,32,128]{2,1,0:T(8,128)S(1)}, f32[13,32,128]{2,1,0:T(8,128)S(1)}) custom-call(s32[2]{0:T(128)S(1)} %pad_add_fusion.par, f32[3,64,32,128]{3,2,1,0:T(8,128)} %t_ref.3, s32[32,64]{1,0:T(8,128)} %bitcast.9, s32[32,64]{1,0:T(8,128)} %bitcast.11, f32[32,64]{1,0:T(8,128)} %bitcast.13), custom_call_target="tpu_custom_call" | custom-call | flops 5000000000 | bytes 15000000 | tf_op jit(solution)/shard_map/pallas_call | solution.py:589
  2.6 3.1 %collective-permute-start = (f32[13,32,128]{2,1,0:T(8,128)S(1)}, f32[13,32,128]{2,1,0:T(8,128)S(1)}, u32[]{:S(2)}, u32[]{:S(2)}) collective-permute-start(f32[13,32,128]{2,1,0:T(8,128)S(1)} %get-tuple-element.29), channel_id=1, source_target_pairs={{0,8},{8,0},{16,24},{24,16},{1,9},{9,1},{17,25},{25,17},{2,10},{10... | collective-permute-start | bytes 638984 | tf_op jit(solution)/shard_map/ppermute | solution.py:522
  6.4 3.1 %shard_map.59 = (f32[3,36,72,128]{3,2,1,0:T(8,128)S(1)}, f32[3,36,72,128]{3,2,1,0:T(8,128)S(1)}, f32[72,128]{1,0:T(8,128)S(1)}, f32[392,128]{1,0:T(8,128)S(1)}, f32[392,128]{1,0:T(8,128)S(1)}) custom-call(s32[2]{0:T(128)S(1)} %pad_add_fusion.par, f32[3,64,32,128]{3,2,1,0:T(8,128)S(1)} %copy-done, s32[32,64]{1,0:T(8,128)} %bitcast.10, s32[32,64]{1,0:T(8,128)} %bitcast.12, ...), custom_call_target="tpu_custom_call" | custom-call | flops 3000000000 | bytes 9000000 | tf_op jit(solution)/shard_map/pallas_call | solution.py:589
  9.6 2.5 %collective-permute-start.3 = (f32[392,128]{1,0:T(8,128)S(1)}, f32[392,128]{1,0:T(8,128)S(1)}, u32[]{:S(2)}, u32[]{:S(2)}) collective-permute-start(f32[392,128]{1,0:T(8,128)S(1)} %get-tuple-element.35), channel_id=1, source_target_pairs={{0,7},{1,2},{2,1},{3,4},{4,3},{5,6},{6,5},{7,0},{8,15},{9,10},{10,... | collective-permute-start | bytes 602120 | tf_op jit(solution)/shard_map/ppermute | solution.py:522
  12.1 1.2 %shard_map.61._.refs_0_ = f32[3,36,72,128]{3,2,1,0:T(8,128)S(1)} custom-call(f32[3,36,72,128]{3,2,1,0:T(8,128)S(1)} %get-tuple-element.27.source.state_in, f32[3,36,72,128]{3,2,1,0:T(8,128)S(1)} %get-tuple-element.28.coef_ref.coef_in, f32[72,128]{1,0:T(8,128)S(1)} %get-tuple-element.31.spin_ref), custom_call_target="tpu_custom_call" | custom-call | flops 2000000000 | bytes 6000000 | tf_op jit(solution)/shard_map/pallas_call | solution.py:589
  13.3 1.0 %shard_map.62 = (f32[3,36,72,128]{3,2,1,0:T(8,128)S(1)}, f32[3,36,72,128]{3,2,1,0:T(8,128)S(1)}, f32[56,128]{1,0:T(8,128)S(1)}, f32[56,128]{1,0:T(8,128)S(1)}) custom-call(s32[2]{0:T(128)S(1)} %pad_add_fusion.par, f32[3,36,72,128]{3,2,1,0:T(8,128)S(1)} %get-tuple-element.27.source.state_in, ...), custom_call_target="tpu_custom_call", output_to_operand_aliasing={{0}: (1, {}), {1}: (2, {})} | custom-call | flops 1000000000 | bytes 3000000 | tf_op jit(solution)/shard_map/pallas_call | solution.py:589
  15.7 1.6 %shard_map.64.state_in = f32[3,36,72,128]{3,2,1,0:T(8,128)S(1)} custom-call(f32[3,36,72,128]{3,2,1,0:T(8,128)S(1)} %shard_map.63.source.middle_in, f32[3,36,72,128]{3,2,1,0:T(8,128)S(1)} %get-tuple-element.33.coef_ref.coef_in, f32[72,128]{1,0:T(8,128)S(1)} %get-tuple-element.31.spin_ref), custom_call_target="tpu_custom_call" | custom-call | flops 2000000000 | bytes 6000000 | tf_op jit(solution)/shard_map/pallas_call | solution.py:589
  17.4 1.2 %collective-permute-done.5.d = f32[56,128]{1,0:T(8,128)S(1)} collective-permute-done((f32[56,128]{1,0:T(8,128)S(1)}, f32[56,128]{1,0:T(8,128)S(1)}, u32[]{:S(2)}, u32[]{:S(2)}) %collective-permute-start.5) | collective-permute-done | bytes 28704 | tf_op jit(solution)/shard_map/ppermute | solution.py:522
  18.6 2.2 %shard_map.65 = (f32[3,36,72,128]{3,2,1,0:T(8,128)S(1)}, f32[3,36,72,128]{3,2,1,0:T(8,128)S(1)}, f32[3,36,72,128]{3,2,1,0:T(8,128)S(1)}, f32[3,36,72,128]{3,2,1,...) custom-call(s32[2]{0:T(128)S(1)} %pad_add_fusion.par, ...), custom_call_target="tpu_custom_call", output_to_operand_aliasing={{0}: (1, {}), {1}: (2, {}), {2}: (3, {}), {3}: (4, {})} | custom-call | flops 2000000000 | bytes 6000000 | tf_op jit(solution)/shard_map/pallas_call | solution.py:589
  21.4 0.8 %collective-permute-start.7 = (f32[432,128]{1,0:T(8,128)S(1)}, f32[432,128]{1,0:T(8,128)S(1)}, u32[]{:S(2)}, u32[]{:S(2)}) collective-permute-start(f32[432,128]{1,0:T(8,128)S(1)} %get-tuple-element.41), channel_id=1, source_target_pairs={{0,7},{1,2},{2,1},{3,4},{4,3},{5,6},{6,5},{7,0},{8,15},{9,10},{10,... | collective-permute-start | bytes 663560 | tf_op jit(solution)/shard_map/ppermute | solution.py:522
  22.2 5.3 %collective-permute-start.10 = (f32[40,128]{1,0:T(8,128)S(1)}, f32[40,128]{1,0:T(8,128)S(1)}, u32[]{:S(2)}, u32[]{:S(2)}) collective-permute-start(f32[40,128]{1,0:T(8,128)S(1)} %add.24.first), channel_id=1, source_target_pairs={{0,16},{8,24},{16,0},{24,8},{1,17},{9,25},{17,1},{25,9},{2,18},{10... | collective-permute-start | bytes 61448 | tf_op jit(solution)/shard_map/ppermute | solution.py:526
  27.5 1.5 %collective-permute-start.9 = (f32[40,128]{1,0:T(8,128)S(1)}, f32[40,128]{1,0:T(8,128)S(1)}, u32[]{:S(2)}, u32[]{:S(2)}) collective-permute-start(f32[40,128]{1,0:T(8,128)S(1)} %add.24.first), channel_id=1, source_target_pairs={{0,24},{8,16},{16,8},{24,0},{1,25},{9,17},{17,9},{25,1},{2,26},{10... | collective-permute-start | bytes 61448 | tf_op jit(solution)/shard_map/ppermute | solution.py:526
  29.1 1.8 %shard_map.66.source.middle_in._ = f32[3,36,72,128]{3,2,1,0:T(8,128)S(1)} custom-call(f32[3,36,72,128]{3,2,1,0:T(8,128)S(1)} %get-tuple-element.38.source.start_in, f32[3,36,72,128]{3,2,1,0:T(8,128)S(1)} %get-tuple-element.39.coef_ref, f32[72,128]{1,0:T(8,128)S(1)} %get-tuple-element.31.spin_ref), custom_call_target="tpu_custom_call" | custom-call | flops 2000000000 | bytes 6000000 | tf_op jit(solution)/shard_map/pallas_call | solution.py:589
  31.4 1.7 %collective-permute-done.9.second = f32[40,128]{1,0:T(8,128)S(1)} collective-permute-done((f32[40,128]{1,0:T(8,128)S(1)}, f32[40,128]{1,0:T(8,128)S(1)}, u32[]{:S(2)}, u32[]{:S(2)}) %collective-permute-start.9) | collective-permute-done | bytes 20512 | tf_op jit(solution)/shard_map/ppermute | solution.py:526
  33.9 0.9 %collective-permute-start.13 = (f32[40,128]{1,0:T(8,128)S(1)}, f32[40,128]{1,0:T(8,128)S(1)}, u32[]{:S(2)}, u32[]{:S(2)}) collective-permute-start(f32[40,128]{1,0:T(8,128)S(1)} %shard_map.69.first), channel_id=1, source_target_pairs={{0,4},{1,5},{2,6},{3,7},{4,0},{5,1},{6,2},{7,3},{8,12},{9,13},{10,... | collective-permute-start | bytes 61448 | tf_op jit(solution)/shard_map/ppermute | solution.py:526
  34.7 2.0 %collective-permute-start.14 = (f32[40,128]{1,0:T(8,128)S(1)}, f32[40,128]{1,0:T(8,128)S(1)}, u32[]{:S(2)}, u32[]{:S(2)}) collective-permute-start(f32[40,128]{1,0:T(8,128)S(1)} %shard_map.69.first), channel_id=1, source_target_pairs={{0,2},{1,3},{2,0},{3,1},{4,6},{5,7},{6,4},{7,5},{8,10},{9,11},{10,... | collective-permute-start | bytes 61448 | tf_op jit(solution)/shard_map/ppermute | solution.py:526
  36.7 1.7 %shard_map.67.state_in._ = f32[3,36,72,128]{3,2,1,0:T(8,128)S(1)} custom-call(f32[3,36,72,128]{3,2,1,0:T(8,128)S(1)} %shard_map.66.source.middle_in._, f32[3,36,72,128]{3,2,1,0:T(8,128)S(1)} %get-tuple-element.39.coef_ref, f32[72,128]{1,0:T(8,128)S(1)} %get-tuple-element.31.spin_ref), custom_call_target="tpu_custom_call" | custom-call | flops 2000000000 | bytes 6000000 | tf_op jit(solution)/shard_map/pallas_call | solution.py:589
  38.6 1.1 %shard_map.68 = (f32[3,36,72,128]{3,2,1,0:T(8,128)S(1)}, f32[3,36,72,128]{3,2,1,0:T(8,128)S(1)}, f32[3,36,72,128]{3,2,1,0:T(8,128)S(1)}) custom-call(s32[2]{0:T(128)S(1)} %pad_add_fusion.par, f32[3,36,72,128]{3,2,1,0:T(8,128)S(1)} %get-tuple-element.38.source.start_in, ...), custom_call_target="tpu_custom_call", output_to_operand_aliasing={{0}: (1, {}), {1}: (2, {}), {2}: (3, {})} | custom-call | flops 1000000000 | bytes 3000000 | tf_op jit(solution)/shard_map/pallas_call | solution.py:589
  39.8 3.0 %shard_map.71 = (f32[128,128]{1,0:T(8,128)S(1)}, f32[1,128]{1,0:T(1,128)S(1)}) custom-call(s32[2]{0:T(128)S(1)} %pad_add_fusion.par, f32[40,128]{1,0:T(8,128)S(1)} %shard_map.70.mine_ref, f32[40,128]{1,0:T(8,128)S(1)} %collective-permute-done.15.other_ref, f32[1,128]{1,0:T(1,128)S(1)} %broadcast_in_dim.3.prior_ref, ...), custom_call_target="tpu_custom_call" | custom-call | flops 10000000 | bytes 30000 | tf_op jit(solution)/shard_map/pallas_call | solution.py:589
  42.8 2.7 %shard_map.72 = (f32[3,32,64,128]{3,2,1,0:T(8,128)S(1)}, f32[40,128]{1,0:T(8,128)S(1)}, f32[40,128]{1,0:T(8,128)S(1)}) custom-call(s32[2]{0:T(128)S(1)} %pad_add_fusion.par, f32[3,36,72,128]{3,2,1,0:T(8,128)S(1)} %get-tuple-element.42._.state, f32[128,128]{1,0:T(8,128)S(1)} %get-tuple-element.45.inverse_ref), custom_call_target="tpu_custom_call" | custom-call | flops 2000000000 | bytes 6000000 | tf_op jit(solution)/shard_map/pallas_call | solution.py:589
  46.1 0.8 %collective-permute-done.16 = f32[40,128]{1,0:T(8,128)S(1)} collective-permute-done((f32[40,128]{1,0:T(8,128)S(1)}, f32[40,128]{1,0:T(8,128)S(1)}, u32[]{:S(2)}, u32[]{:S(2)}) %collective-permute-start.16) | collective-permute-done | bytes 20512 | tf_op jit(solution)/shard_map/ppermute | solution.py:526
  46.9 2.0 %collective-permute-start.17 = (f32[40,128]{1,0:T(8,128)S(1)}, f32[40,128]{1,0:T(8,128)S(1)}, u32[]{:S(2)}, u32[]{:S(2)}) collective-permute-start(f32[40,128]{1,0:T(8,128)S(1)} %add.25), channel_id=1, source_target_pairs={{0,6},{1,7},{2,4},{3,5},{4,2},{5,3},{6,0},{7,1},{8,14},{9,15},{10,... | collective-permute-start | bytes 61448 | tf_op jit(solution)/shard_map/ppermute | solution.py:526
  48.9 1.4 %collective-permute-start.18 = (f32[40,128]{1,0:T(8,128)S(1)}, f32[40,128]{1,0:T(8,128)S(1)}, u32[]{:S(2)}, u32[]{:S(2)}) collective-permute-start(f32[40,128]{1,0:T(8,128)S(1)} %add.25), channel_id=1, source_target_pairs={{0,4},{1,5},{2,6},{3,7},{4,0},{5,1},{6,2},{7,3},{8,12},{9,13},{10,... | collective-permute-start | bytes 61448 | tf_op jit(solution)/shard_map/ppermute | solution.py:526
  50.4 1.2 %collective-permute-done.17 = f32[40,128]{1,0:T(8,128)S(1)} collective-permute-done((f32[40,128]{1,0:T(8,128)S(1)}, f32[40,128]{1,0:T(8,128)S(1)}, u32[]{:S(2)}, u32[]{:S(2)}) %collective-permute-start.17) | collective-permute-done | bytes 20512 | tf_op jit(solution)/shard_map/ppermute | solution.py:526
  51.6 1.1 %collective-permute-done.18 = f32[40,128]{1,0:T(8,128)S(1)} collective-permute-done((f32[40,128]{1,0:T(8,128)S(1)}, f32[40,128]{1,0:T(8,128)S(1)}, u32[]{:S(2)}, u32[]{:S(2)}) %collective-permute-start.18) | collective-permute-done | bytes 20512 | tf_op jit(solution)/shard_map/ppermute | solution.py:526
  52.7 1.4 %collective-permute-done.19 = f32[40,128]{1,0:T(8,128)S(1)} collective-permute-done((f32[40,128]{1,0:T(8,128)S(1)}, f32[40,128]{1,0:T(8,128)S(1)}, u32[]{:S(2)}, u32[]{:S(2)}) %collective-permute-start.19) | collective-permute-done | bytes 20512 | tf_op jit(solution)/shard_map/ppermute | solution.py:526
  54.1 1.6 %collective-permute-start.20 = (f32[40,128]{1,0:T(8,128)S(1)}, f32[40,128]{1,0:T(8,128)S(1)}, u32[]{:S(2)}, u32[]{:S(2)}) collective-permute-start(f32[40,128]{1,0:T(8,128)S(1)} %add_add_fusion.1), channel_id=1, source_target_pairs={{0,24},{8,16},{16,8},{24,0},{1,25},{9,17},{17,9},{25,1},{2,26},{10... | collective-permute-start | bytes 61448 | tf_op jit(solution)/shard_map/ppermute | solution.py:526
  55.9 2.7 %collective-permute-start.22 = (f32[40,128]{1,0:T(8,128)S(1)}, f32[40,128]{1,0:T(8,128)S(1)}, u32[]{:S(2)}, u32[]{:S(2)}) collective-permute-start(f32[40,128]{1,0:T(8,128)S(1)} %add_add_fusion.1), channel_id=1, source_target_pairs={{0,8},{8,0},{16,24},{24,16},{1,9},{9,1},{17,25},{25,17},{2,10},{10... | collective-permute-start | bytes 61448 | tf_op jit(solution)/shard_map/ppermute | solution.py:526
  58.6 1.2 %collective-permute-done.20 = f32[40,128]{1,0:T(8,128)S(1)} collective-permute-done((f32[40,128]{1,0:T(8,128)S(1)}, f32[40,128]{1,0:T(8,128)S(1)}, u32[]{:S(2)}, u32[]{:S(2)}) %collective-permute-start.20) | collective-permute-done | bytes 20512 | tf_op jit(solution)/shard_map/ppermute | solution.py:526
  59.8 0.7 %collective-permute-done.21 = f32[40,128]{1,0:T(8,128)S(1)} collective-permute-done((f32[40,128]{1,0:T(8,128)S(1)}, f32[40,128]{1,0:T(8,128)S(1)}, u32[]{:S(2)}, u32[]{:S(2)}) %collective-permute-start.21) | collective-permute-done | bytes 20512 | tf_op jit(solution)/shard_map/ppermute | solution.py:526
  60.6 1.1 %shard_map.73 = bf16[3,64,32,256]{3,2,1,0:T(8,128)(2,1)S(1)} custom-call(f32[3,32,64,128]{3,2,1,0:T(8,128)S(1)} %get-tuple-element.49.turned), custom_call_target="tpu_custom_call" | custom-call | flops 1000000000 | bytes 3000000 | tf_op jit(solution)/shard_map/pallas_call | solution.py:589
  61.8 5.7 %shard_map.74 = (f32[24,256,128]{2,1,0:T(8,128)}, f32[1,128]{1,0:T(1,128)}) custom-call(s32[2]{0:T(128)S(1)} %pad_add_fusion.par, f32[40,128]{1,0:T(8,128)S(1)} %add_add_fusion.mine_ref, f32[40,128]{1,0:T(8,128)S(1)} %collective-permute-done.23.other_ref, f32[1,128]{1,0:T(1,128)S(1)} %get-tuple-element.48.prior_ref, bf16[24,256,256]{2,1,0:T(8,128)(2,1)S(1)} %bitcast.8), custom_call_target="tpu_custom_call" | custom-call | flops 1000000000 | bytes 3000000 | tf_op jit(solution)/shard_map/pallas_call | solution.py:589
  (40 shorter events, 5.2 us)
Async XLA Ops:
  0.7 5.7 %copy-start = (f32[3,64,32,128]{3,2,1,0:T(8,128)S(1)}, f32[3,64,32,128]{3,2,1,0:T(8,128)}, u32[]{:S(2)}) copy-start(f32[3,64,32,128]{3,2,1,0:T(8,128)} %t_ref.3) | copy-start | bytes 9437188
  2.6 10.6 %collective-permute-start = (f32[13,32,128]{2,1,0:T(8,128)S(1)}, f32[13,32,128]{2,1,0:T(8,128)S(1)}, u32[]{:S(2)}, u32[]{:S(2)}) collective-permute-start(f32[13,32,128]{2,1,0:T(8,128)S(1)} %get-tuple-element.29), channel_id=1, source_target_pairs={{0,8},{8,0},{16,24},{24,16},{1,9},{9,1},{17,25},{25,17},{2,10},{10... | collective-permute-start | bytes 638984 | tf_op jit(solution)/shard_map/ppermute | solution.py:522
  5.7 7.6 %collective-permute-start.1 = (f32[13,32,128]{2,1,0:T(8,128)S(1)}, f32[13,32,128]{2,1,0:T(8,128)S(1)}, u32[]{:S(2)}, u32[]{:S(2)}) collective-permute-start(f32[13,32,128]{2,1,0:T(8,128)S(1)} %get-tuple-element.30), channel_id=1, source_target_pairs={{8,16},{16,8},{9,17},{17,9},{10,18},{18,10},{11,19},{19,11},{12,20... | collective-permute-start | bytes 638984 | tf_op jit(solution)/shard_map/ppermute | solution.py:522
  9.5 7.9 %collective-permute-start.2 = (f32[392,128]{1,0:T(8,128)S(1)}, f32[392,128]{1,0:T(8,128)S(1)}, u32[]{:S(2)}, u32[]{:S(2)}) collective-permute-start(f32[392,128]{1,0:T(8,128)S(1)} %get-tuple-element.34), channel_id=1, source_target_pairs={{0,1},{1,0},{2,3},{3,2},{4,5},{5,4},{6,7},{7,6},{8,9},{9,8},{10,11... | collective-permute-start | bytes 602120 | tf_op jit(solution)/shard_map/ppermute | solution.py:522
  9.6 7.8 %collective-permute-start.3 = (f32[392,128]{1,0:T(8,128)S(1)}, f32[392,128]{1,0:T(8,128)S(1)}, u32[]{:S(2)}, u32[]{:S(2)}) collective-permute-start(f32[392,128]{1,0:T(8,128)S(1)} %get-tuple-element.35), channel_id=1, source_target_pairs={{0,7},{1,2},{2,1},{3,4},{4,3},{5,6},{6,5},{7,0},{8,15},{9,10},{10,... | collective-permute-start | bytes 602120 | tf_op jit(solution)/shard_map/ppermute | solution.py:522
  14.3 3.1 %collective-permute-start.4 = (f32[56,128]{1,0:T(8,128)S(1)}, f32[56,128]{1,0:T(8,128)S(1)}, u32[]{:S(2)}, u32[]{:S(2)}) collective-permute-start(f32[56,128]{1,0:T(8,128)S(1)} %get-tuple-element.36), channel_id=1, source_target_pairs={{0,1},{1,0},{2,3},{3,2},{4,5},{5,4},{6,7},{7,6},{8,9},{9,8},{10,11... | collective-permute-start | bytes 86024 | tf_op jit(solution)/shard_map/ppermute | solution.py:522
  14.4 4.3 %collective-permute-start.5 = (f32[56,128]{1,0:T(8,128)S(1)}, f32[56,128]{1,0:T(8,128)S(1)}, u32[]{:S(2)}, u32[]{:S(2)}) collective-permute-start(f32[56,128]{1,0:T(8,128)S(1)} %get-tuple-element.37), channel_id=1, source_target_pairs={{0,7},{1,2},{2,1},{3,4},{4,3},{5,6},{6,5},{7,0},{8,15},{9,10},{10,... | collective-permute-start | bytes 86024 | tf_op jit(solution)/shard_map/ppermute | solution.py:522
  20.8 1.4 %collective-permute-start.8 = (f32[40,128]{1,0:T(8,128)S(1)}, f32[40,128]{1,0:T(8,128)S(1)}, u32[]{:S(2)}, u32[]{:S(2)}) collective-permute-start(f32[40,128]{1,0:T(8,128)S(1)} %get-tuple-element.44), channel_id=1, source_target_pairs={{0,1},{1,0},{2,3},{3,2},{4,5},{5,4},{6,7},{7,6},{8,9},{9,8},{10,11... | collective-permute-start | bytes 61448 | tf_op jit(solution)/shard_map/ppermute | solution.py:526
  20.9 17.7 %collective-permute-start.6 = (f32[432,128]{1,0:T(8,128)S(1)}, f32[432,128]{1,0:T(8,128)S(1)}, u32[]{:S(2)}, u32[]{:S(2)}) collective-permute-start(f32[432,128]{1,0:T(8,128)S(1)} %get-tuple-element.40), channel_id=1, source_target_pairs={{0,1},{1,0},{2,3},{3,2},{4,5},{5,4},{6,7},{7,6},{8,9},{9,8},{10,11... | collective-permute-start | bytes 663560 | tf_op jit(solution)/shard_map/ppermute | solution.py:522
  21.4 17.2 %collective-permute-start.7 = (f32[432,128]{1,0:T(8,128)S(1)}, f32[432,128]{1,0:T(8,128)S(1)}, u32[]{:S(2)}, u32[]{:S(2)}) collective-permute-start(f32[432,128]{1,0:T(8,128)S(1)} %get-tuple-element.41), channel_id=1, source_target_pairs={{0,7},{1,2},{2,1},{3,4},{4,3},{5,6},{6,5},{7,0},{8,15},{9,10},{10,... | collective-permute-start | bytes 663560 | tf_op jit(solution)/shard_map/ppermute | solution.py:522
  22.2 8.7 %collective-permute-start.10 = (f32[40,128]{1,0:T(8,128)S(1)}, f32[40,128]{1,0:T(8,128)S(1)}, u32[]{:S(2)}, u32[]{:S(2)}) collective-permute-start(f32[40,128]{1,0:T(8,128)S(1)} %add.24.first), channel_id=1, source_target_pairs={{0,16},{8,24},{16,0},{24,8},{1,17},{9,25},{17,1},{25,9},{2,18},{10... | collective-permute-start | bytes 61448 | tf_op jit(solution)/shard_map/ppermute | solution.py:526
  27.5 3.9 %collective-permute-start.11 = (f32[40,128]{1,0:T(8,128)S(1)}, f32[40,128]{1,0:T(8,128)S(1)}, u32[]{:S(2)}, u32[]{:S(2)}) collective-permute-start(f32[40,128]{1,0:T(8,128)S(1)} %add.24.first), channel_id=1, source_target_pairs={{0,8},{8,0},{16,24},{24,16},{1,9},{9,1},{17,25},{25,17},{2,10},{10... | collective-permute-start | bytes 61448 | tf_op jit(solution)/shard_map/ppermute | solution.py:526
  27.5 5.6 %collective-permute-start.9 = (f32[40,128]{1,0:T(8,128)S(1)}, f32[40,128]{1,0:T(8,128)S(1)}, u32[]{:S(2)}, u32[]{:S(2)}) collective-permute-start(f32[40,128]{1,0:T(8,128)S(1)} %add.24.first), channel_id=1, source_target_pairs={{0,24},{8,16},{16,8},{24,0},{1,25},{9,17},{17,9},{25,1},{2,26},{10... | collective-permute-start | bytes 61448 | tf_op jit(solution)/shard_map/ppermute | solution.py:526
  33.1 5.3 %collective-permute-start.12 = (f32[40,128]{1,0:T(8,128)S(1)}, f32[40,128]{1,0:T(8,128)S(1)}, u32[]{:S(2)}, u32[]{:S(2)}) collective-permute-start(f32[40,128]{1,0:T(8,128)S(1)} %shard_map.69.first), channel_id=1, source_target_pairs={{0,6},{1,7},{2,4},{3,5},{4,2},{5,3},{6,0},{7,1},{8,14},{9,15},{10,... | collective-permute-start | bytes 61448 | tf_op jit(solution)/shard_map/ppermute | solution.py:526
  33.9 4.6 %collective-permute-start.13 = (f32[40,128]{1,0:T(8,128)S(1)}, f32[40,128]{1,0:T(8,128)S(1)}, u32[]{:S(2)}, u32[]{:S(2)}) collective-permute-start(f32[40,128]{1,0:T(8,128)S(1)} %shard_map.69.first), channel_id=1, source_target_pairs={{0,4},{1,5},{2,6},{3,7},{4,0},{5,1},{6,2},{7,3},{8,12},{9,13},{10,... | collective-permute-start | bytes 61448 | tf_op jit(solution)/shard_map/ppermute | solution.py:526
  34.7 3.8 %collective-permute-start.14 = (f32[40,128]{1,0:T(8,128)S(1)}, f32[40,128]{1,0:T(8,128)S(1)}, u32[]{:S(2)}, u32[]{:S(2)}) collective-permute-start(f32[40,128]{1,0:T(8,128)S(1)} %shard_map.69.first), channel_id=1, source_target_pairs={{0,2},{1,3},{2,0},{3,1},{4,6},{5,7},{6,4},{7,5},{8,10},{9,11},{10,... | collective-permute-start | bytes 61448 | tf_op jit(solution)/shard_map/ppermute | solution.py:526
  38.5 1.2 %collective-permute-start.15 = (f32[40,128]{1,0:T(8,128)S(1)}, f32[40,128]{1,0:T(8,128)S(1)}, u32[]{:S(2)}, u32[]{:S(2)}) collective-permute-start(f32[40,128]{1,0:T(8,128)S(1)} %shard_map.70.mine_ref), channel_id=1, source_target_pairs={{0,1},{1,0},{2,3},{3,2},{4,5},{5,4},{6,7},{7,6},{8,9},{9,8},{10,11... | collective-permute-start | bytes 61448 | tf_op jit(solution)/shard_map/ppermute | solution.py:526
  45.5 1.4 %collective-permute-start.16 = (f32[40,128]{1,0:T(8,128)S(1)}, f32[40,128]{1,0:T(8,128)S(1)}, u32[]{:S(2)}, u32[]{:S(2)}) collective-permute-start(f32[40,128]{1,0:T(8,128)S(1)} %get-tuple-element.47), channel_id=1, source_target_pairs={{0,1},{1,0},{2,3},{3,2},{4,5},{5,4},{6,7},{7,6},{8,9},{9,8},{10,11... | collective-permute-start | bytes 61448 | tf_op jit(solution)/shard_map/ppermute | solution.py:526
  46.9 4.7 %collective-permute-start.17 = (f32[40,128]{1,0:T(8,128)S(1)}, f32[40,128]{1,0:T(8,128)S(1)}, u32[]{:S(2)}, u32[]{:S(2)}) collective-permute-start(f32[40,128]{1,0:T(8,128)S(1)} %add.25), channel_id=1, source_target_pairs={{0,6},{1,7},{2,4},{3,5},{4,2},{5,3},{6,0},{7,1},{8,14},{9,15},{10,... | collective-permute-start | bytes 61448 | tf_op jit(solution)/shard_map/ppermute | solution.py:526
  48.9 3.8 %collective-permute-start.18 = (f32[40,128]{1,0:T(8,128)S(1)}, f32[40,128]{1,0:T(8,128)S(1)}, u32[]{:S(2)}, u32[]{:S(2)}) collective-permute-start(f32[40,128]{1,0:T(8,128)S(1)} %add.25), channel_id=1, source_target_pairs={{0,4},{1,5},{2,6},{3,7},{4,0},{5,1},{6,2},{7,3},{8,12},{9,13},{10,... | collective-permute-start | bytes 61448 | tf_op jit(solution)/shard_map/ppermute | solution.py:526
  50.3 3.8 %collective-permute-start.19 = (f32[40,128]{1,0:T(8,128)S(1)}, f32[40,128]{1,0:T(8,128)S(1)}, u32[]{:S(2)}, u32[]{:S(2)}) collective-permute-start(f32[40,128]{1,0:T(8,128)S(1)} %add.25), channel_id=1, source_target_pairs={{0,2},{1,3},{2,0},{3,1},{4,6},{5,7},{6,4},{7,5},{8,10},{9,11},{10,... | collective-permute-start | bytes 61448 | tf_op jit(solution)/shard_map/ppermute | solution.py:526
  54.1 5.6 %collective-permute-start.20 = (f32[40,128]{1,0:T(8,128)S(1)}, f32[40,128]{1,0:T(8,128)S(1)}, u32[]{:S(2)}, u32[]{:S(2)}) collective-permute-start(f32[40,128]{1,0:T(8,128)S(1)} %add_add_fusion.1), channel_id=1, source_target_pairs={{0,24},{8,16},{16,8},{24,0},{1,25},{9,17},{17,9},{25,1},{2,26},{10... | collective-permute-start | bytes 61448 | tf_op jit(solution)/shard_map/ppermute | solution.py:526
  55.7 4.8 %collective-permute-start.21 = (f32[40,128]{1,0:T(8,128)S(1)}, f32[40,128]{1,0:T(8,128)S(1)}, u32[]{:S(2)}, u32[]{:S(2)}) collective-permute-start(f32[40,128]{1,0:T(8,128)S(1)} %add_add_fusion.1), channel_id=1, source_target_pairs={{0,16},{8,24},{16,0},{24,8},{1,17},{9,25},{17,1},{25,9},{2,18},{10... | collective-permute-start | bytes 61448 | tf_op jit(solution)/shard_map/ppermute | solution.py:526
  55.9 4.7 %collective-permute-start.22 = (f32[40,128]{1,0:T(8,128)S(1)}, f32[40,128]{1,0:T(8,128)S(1)}, u32[]{:S(2)}, u32[]{:S(2)}) collective-permute-start(f32[40,128]{1,0:T(8,128)S(1)} %add_add_fusion.1), channel_id=1, source_target_pairs={{0,8},{8,0},{16,24},{24,16},{1,9},{9,1},{17,25},{25,17},{2,10},{10... | collective-permute-start | bytes 61448 | tf_op jit(solution)/shard_map/ppermute | solution.py:526
  60.6 1.2 %collective-permute-start.23 = (f32[40,128]{1,0:T(8,128)S(1)}, f32[40,128]{1,0:T(8,128)S(1)}, u32[]{:S(2)}, u32[]{:S(2)}) collective-permute-start(f32[40,128]{1,0:T(8,128)S(1)} %add_add_fusion.mine_ref), channel_id=1, source_target_pairs={{0,1},{1,0},{2,3},{3,2},{4,5},{5,4},{6,7},{7,6},{8,9},{9,8},{10,11... | collective-permute-start | bytes 61448 | tf_op jit(solution)/shard_map/ppermute | solution.py:526

commit v15 on v14

--- a/solution.py
+++ b/solution.py
@@ -146,7 +146,7 @@
                 ]
 
 
-def join_rows(par, state_in, coef_in, row_a, row_b, _, state, coef, col_a, col_b):
+def join_rows(par, state_in, coef_in, row_b, row_a, _, state, coef, col_a, col_b):
     comps, length, tall, _ = state.shape
     cols, rows = length - 2 * SIDE, tall - 2 * HALO
     norths, easts = sides_of(par)
@@ -519,7 +519,8 @@
     far = [(i, (i + 1 if i % 2 else i - 1) % count) for i in range(count)]
     if not closed:
         far = far[1:-1]
-    return lax.ppermute(near_value, axis, near), lax.ppermute(far_value, axis, far)
+    from_far = lax.ppermute(far_value, axis, far)
+    return lax.ppermute(near_value, axis, near), from_far
 
 
 def swapped(value, axis, mask):
@@ -658,7 +659,7 @@
         par,
         start,
         coef,
-        *row_halos,
+        *reversed(row_halos),
         middle,
         specs=[SMEM] + [VMEM] * 4 + [pl.BlockSpec(memory_space=pl.ANY)],
         aliases={1: 0, 2: 1},

time: 67.7 us -> 68 us (level)
    ppermute x8, starting transfers between devices: 8.42 us -> 11.2 us  [the longest x4 6.54 us: swap_pairs(): return (lax.ppermute(near_value, axis, near), from_far)]
    ppermute x16, starting transfers between devices: 19.1 us -> 16.7 us  [swapped(): lax.ppermute(value, axis, [(i, i ^ mask) for i in range(lax.axis_size(axi...]
  transfers between devices with their start and end apart: 24 -> 24, of which waited for: 11 -> 10; matrix products, arithmetic and copies ran while one was open for 0% -> 0% of each run, Pallas kernels for 20% -> 20%
where the time goes in v15:
time: 68 us; the launch traced here: 67.8 us
  Pallas kernels  28.9 us (42%)
  starting transfers between devices  27.9 us (41%)
  waiting for transfers between devices  10 us (15%)
  between operations  0.85 us (1%)
    pallas_call x14, Pallas kernels, call(): pl.pallas_call(kernel, out_shape=outs, in_specs=specs or [SMEM] + [VMEM]...  28.9 us
    ppermute x16, starting transfers between devices, swapped(): lax.ppermute(value, axis, [(i, i ^ mask) for i in range(lax.axis_size(axi...  16.7 us
    ppermute x16, waiting for transfers between devices, swapped(): lax.ppermute(value, axis, [(i, i ^ mask) for i in range(lax.axis_size(axi...  8.75 us
    ppermute x4, starting transfers between devices, swap_pairs(): return (lax.ppermute(near_value, axis, near), from_far)  6.54 us
    ppermute x4, starting transfers between devices, swap_pairs(): from_far = lax.ppermute(far_value, axis, far)  4.71 us
  transfers between devices with their start and end apart: 24, of which 10 were waited for; matrix products, arithmetic and copies ran while one was open for 0% of the time, Pallas kernels for 20%

profile of v15, /device:TPU:0, one launch (start us, length us, event | category | flops | bytes accessed | tf_op | source)
XLA Modules:
  0.0 67.8 jit_solution(6326070807686768127)
XLA Ops:
  0.7 1.9 %shard_map.60 = (f32[13,32,128]{2,1,0:T(8,128)S(1)}, f32[13,32,128]{2,1,0:T(8,128)S(1)}) custom-call(s32[2]{0:T(128)S(1)} %pad_add_fusion.par, f32[3,64,32,128]{3,2,1,0:T(8,128)} %t_ref.3, s32[32,64]{1,0:T(8,128)} %bitcast.9, s32[32,64]{1,0:T(8,128)} %bitcast.11, f32[32,64]{1,0:T(8,128)} %bitcast.13), custom_call_target="tpu_custom_call" | custom-call | flops 5000000000 | bytes 15000000 | tf_op jit(solution)/shard_map/pallas_call | solution.py:590
  3.3 5.9 %collective-permute-start.1 = (f32[13,32,128]{2,1,0:T(8,128)S(1)}, f32[13,32,128]{2,1,0:T(8,128)S(1)}, u32[]{:S(2)}, u32[]{:S(2)}) collective-permute-start(f32[13,32,128]{2,1,0:T(8,128)S(1)} %get-tuple-element.30), channel_id=1, source_target_pairs={{0,8},{8,0},{16,24},{24,16},{1,9},{9,1},{17,25},{25,17},{2,10},{10... | collective-permute-start | bytes 638984 | tf_op jit(solution)/shard_map/ppermute | solution.py:523
  9.2 3.1 %shard_map.59 = (f32[3,36,72,128]{3,2,1,0:T(8,128)S(1)}, f32[3,36,72,128]{3,2,1,0:T(8,128)S(1)}, f32[72,128]{1,0:T(8,128)S(1)}, f32[392,128]{1,0:T(8,128)S(1)}, f32[392,128]{1,0:T(8,128)S(1)}) custom-call(s32[2]{0:T(128)S(1)} %pad_add_fusion.par, f32[3,64,32,128]{3,2,1,0:T(8,128)S(1)} %copy-done, s32[32,64]{1,0:T(8,128)} %bitcast.10, s32[32,64]{1,0:T(8,128)} %bitcast.12, ...), custom_call_target="tpu_custom_call" | custom-call | flops 3000000000 | bytes 9000000 | tf_op jit(solution)/shard_map/pallas_call | solution.py:590
  12.4 2.5 %collective-permute-start.3 = (f32[392,128]{1,0:T(8,128)S(1)}, f32[392,128]{1,0:T(8,128)S(1)}, u32[]{:S(2)}, u32[]{:S(2)}) collective-permute-start(f32[392,128]{1,0:T(8,128)S(1)} %get-tuple-element.35), channel_id=1, source_target_pairs={{0,7},{1,2},{2,1},{3,4},{4,3},{5,6},{6,5},{7,0},{8,15},{9,10},{10,... | collective-permute-start | bytes 602120 | tf_op jit(solution)/shard_map/ppermute | solution.py:522
  14.9 1.2 %shard_map.61._.refs_0_ = f32[3,36,72,128]{3,2,1,0:T(8,128)S(1)} custom-call(f32[3,36,72,128]{3,2,1,0:T(8,128)S(1)} %get-tuple-element.27.source.state_in, f32[3,36,72,128]{3,2,1,0:T(8,128)S(1)} %get-tuple-element.28.coef_ref.coef_in, f32[72,128]{1,0:T(8,128)S(1)} %get-tuple-element.31.spin_ref), custom_call_target="tpu_custom_call" | custom-call | flops 2000000000 | bytes 6000000 | tf_op jit(solution)/shard_map/pallas_call | solution.py:590
  16.1 1.0 %shard_map.62 = (f32[3,36,72,128]{3,2,1,0:T(8,128)S(1)}, f32[3,36,72,128]{3,2,1,0:T(8,128)S(1)}, f32[56,128]{1,0:T(8,128)S(1)}, f32[56,128]{1,0:T(8,128)S(1)}) custom-call(s32[2]{0:T(128)S(1)} %pad_add_fusion.par, f32[3,36,72,128]{3,2,1,0:T(8,128)S(1)} %get-tuple-element.27.source.state_in, ...), custom_call_target="tpu_custom_call", output_to_operand_aliasing={{0}: (1, {}), {1}: (2, {})} | custom-call | flops 1000000000 | bytes 3000000 | tf_op jit(solution)/shard_map/pallas_call | solution.py:590
  18.5 1.6 %shard_map.64.state_in = f32[3,36,72,128]{3,2,1,0:T(8,128)S(1)} custom-call(f32[3,36,72,128]{3,2,1,0:T(8,128)S(1)} %shard_map.63.source.middle_in, f32[3,36,72,128]{3,2,1,0:T(8,128)S(1)} %get-tuple-element.33.coef_ref.coef_in, f32[72,128]{1,0:T(8,128)S(1)} %get-tuple-element.31.spin_ref), custom_call_target="tpu_custom_call" | custom-call | flops 2000000000 | bytes 6000000 | tf_op jit(solution)/shard_map/pallas_call | solution.py:590
  20.2 1.2 %collective-permute-done.5.d = f32[56,128]{1,0:T(8,128)S(1)} collective-permute-done((f32[56,128]{1,0:T(8,128)S(1)}, f32[56,128]{1,0:T(8,128)S(1)}, u32[]{:S(2)}, u32[]{:S(2)}) %collective-permute-start.5) | collective-permute-done | bytes 28704 | tf_op jit(solution)/shard_map/ppermute | solution.py:522
  21.4 2.2 %shard_map.65 = (f32[3,36,72,128]{3,2,1,0:T(8,128)S(1)}, f32[3,36,72,128]{3,2,1,0:T(8,128)S(1)}, f32[3,36,72,128]{3,2,1,0:T(8,128)S(1)}, f32[3,36,72,128]{3,2,1,...) custom-call(s32[2]{0:T(128)S(1)} %pad_add_fusion.par, ...), custom_call_target="tpu_custom_call", output_to_operand_aliasing={{0}: (1, {}), {1}: (2, {}), {2}: (3, {}), {3}: (4, {})} | custom-call | flops 2000000000 | bytes 6000000 | tf_op jit(solution)/shard_map/pallas_call | solution.py:590
  24.2 0.8 %collective-permute-start.7 = (f32[432,128]{1,0:T(8,128)S(1)}, f32[432,128]{1,0:T(8,128)S(1)}, u32[]{:S(2)}, u32[]{:S(2)}) collective-permute-start(f32[432,128]{1,0:T(8,128)S(1)} %get-tuple-element.41), channel_id=1, source_target_pairs={{0,7},{1,2},{2,1},{3,4},{4,3},{5,6},{6,5},{7,0},{8,15},{9,10},{10,... | collective-permute-start | bytes 663560 | tf_op jit(solution)/shard_map/ppermute | solution.py:522
  25.0 1.4 %collective-permute-start.10 = (f32[40,128]{1,0:T(8,128)S(1)}, f32[40,128]{1,0:T(8,128)S(1)}, u32[]{:S(2)}, u32[]{:S(2)}) collective-permute-start(f32[40,128]{1,0:T(8,128)S(1)} %add.24.first), channel_id=1, source_target_pairs={{0,16},{8,24},{16,0},{24,8},{1,17},{9,25},{17,1},{25,9},{2,18},{10... | collective-permute-start | bytes 61448 | tf_op jit(solution)/shard_map/ppermute | solution.py:527
  27.0 2.5 %collective-permute-start.9 = (f32[40,128]{1,0:T(8,128)S(1)}, f32[40,128]{1,0:T(8,128)S(1)}, u32[]{:S(2)}, u32[]{:S(2)}) collective-permute-start(f32[40,128]{1,0:T(8,128)S(1)} %add.24.first), channel_id=1, source_target_pairs={{0,24},{8,16},{16,8},{24,0},{1,25},{9,17},{17,9},{25,1},{2,26},{10... | collective-permute-start | bytes 61448 | tf_op jit(solution)/shard_map/ppermute | solution.py:527
  29.5 1.8 %shard_map.66.source.middle_in._ = f32[3,36,72,128]{3,2,1,0:T(8,128)S(1)} custom-call(f32[3,36,72,128]{3,2,1,0:T(8,128)S(1)} %get-tuple-element.38.source.start_in, f32[3,36,72,128]{3,2,1,0:T(8,128)S(1)} %get-tuple-element.39.coef_ref, f32[72,128]{1,0:T(8,128)S(1)} %get-tuple-element.31.spin_ref), custom_call_target="tpu_custom_call" | custom-call | flops 2000000000 | bytes 6000000 | tf_op jit(solution)/shard_map/pallas_call | solution.py:590
  31.3 1.2 %collective-permute-done.9.second = f32[40,128]{1,0:T(8,128)S(1)} collective-permute-done((f32[40,128]{1,0:T(8,128)S(1)}, f32[40,128]{1,0:T(8,128)S(1)}, u32[]{:S(2)}, u32[]{:S(2)}) %collective-permute-start.9) | collective-permute-done | bytes 20512 | tf_op jit(solution)/shard_map/ppermute | solution.py:527
  32.6 1.0 %collective-permute-start.12 = (f32[40,128]{1,0:T(8,128)S(1)}, f32[40,128]{1,0:T(8,128)S(1)}, u32[]{:S(2)}, u32[]{:S(2)}) collective-permute-start(f32[40,128]{1,0:T(8,128)S(1)} %shard_map.69.first), channel_id=1, source_target_pairs={{0,6},{1,7},{2,4},{3,5},{4,2},{5,3},{6,0},{7,1},{8,14},{9,15},{10,... | collective-permute-start | bytes 61448 | tf_op jit(solution)/shard_map/ppermute | solution.py:527
  33.6 1.3 %collective-permute-start.13 = (f32[40,128]{1,0:T(8,128)S(1)}, f32[40,128]{1,0:T(8,128)S(1)}, u32[]{:S(2)}, u32[]{:S(2)}) collective-permute-start(f32[40,128]{1,0:T(8,128)S(1)} %shard_map.69.first), channel_id=1, source_target_pairs={{0,4},{1,5},{2,6},{3,7},{4,0},{5,1},{6,2},{7,3},{8,12},{9,13},{10,... | collective-permute-start | bytes 61448 | tf_op jit(solution)/shard_map/ppermute | solution.py:527
  35.0 1.2 %collective-permute-start.14 = (f32[40,128]{1,0:T(8,128)S(1)}, f32[40,128]{1,0:T(8,128)S(1)}, u32[]{:S(2)}, u32[]{:S(2)}) collective-permute-start(f32[40,128]{1,0:T(8,128)S(1)} %shard_map.69.first), channel_id=1, source_target_pairs={{0,2},{1,3},{2,0},{3,1},{4,6},{5,7},{6,4},{7,5},{8,10},{9,11},{10,... | collective-permute-start | bytes 61448 | tf_op jit(solution)/shard_map/ppermute | solution.py:527
  36.1 1.7 %shard_map.67.state_in._ = f32[3,36,72,128]{3,2,1,0:T(8,128)S(1)} custom-call(f32[3,36,72,128]{3,2,1,0:T(8,128)S(1)} %shard_map.66.source.middle_in._, f32[3,36,72,128]{3,2,1,0:T(8,128)S(1)} %get-tuple-element.39.coef_ref, f32[72,128]{1,0:T(8,128)S(1)} %get-tuple-element.31.spin_ref), custom_call_target="tpu_custom_call" | custom-call | flops 2000000000 | bytes 6000000 | tf_op jit(solution)/shard_map/pallas_call | solution.py:590
  37.9 0.9 %collective-permute-done.14.fourth = f32[40,128]{1,0:T(8,128)S(1)} collective-permute-done((f32[40,128]{1,0:T(8,128)S(1)}, f32[40,128]{1,0:T(8,128)S(1)}, u32[]{:S(2)}, u32[]{:S(2)}) %collective-permute-start.14) | collective-permute-done | bytes 20512 | tf_op jit(solution)/shard_map/ppermute | solution.py:527
  38.9 1.1 %shard_map.68 = (f32[3,36,72,128]{3,2,1,0:T(8,128)S(1)}, f32[3,36,72,128]{3,2,1,0:T(8,128)S(1)}, f32[3,36,72,128]{3,2,1,0:T(8,128)S(1)}) custom-call(s32[2]{0:T(128)S(1)} %pad_add_fusion.par, f32[3,36,72,128]{3,2,1,0:T(8,128)S(1)} %get-tuple-element.38.source.start_in, ...), custom_call_target="tpu_custom_call", output_to_operand_aliasing={{0}: (1, {}), {1}: (2, {}), {2}: (3, {})} | custom-call | flops 1000000000 | bytes 3000000 | tf_op jit(solution)/shard_map/pallas_call | solution.py:590
  40.0 3.0 %shard_map.71 = (f32[128,128]{1,0:T(8,128)S(1)}, f32[1,128]{1,0:T(1,128)S(1)}) custom-call(s32[2]{0:T(128)S(1)} %pad_add_fusion.par, f32[40,128]{1,0:T(8,128)S(1)} %shard_map.70.mine_ref, f32[40,128]{1,0:T(8,128)S(1)} %collective-permute-done.15.other_ref, f32[1,128]{1,0:T(1,128)S(1)} %broadcast_in_dim.3.prior_ref, ...), custom_call_target="tpu_custom_call" | custom-call | flops 10000000 | bytes 30000 | tf_op jit(solution)/shard_map/pallas_call | solution.py:590
  43.1 2.7 %shard_map.72 = (f32[3,32,64,128]{3,2,1,0:T(8,128)S(1)}, f32[40,128]{1,0:T(8,128)S(1)}, f32[40,128]{1,0:T(8,128)S(1)}) custom-call(s32[2]{0:T(128)S(1)} %pad_add_fusion.par, f32[3,36,72,128]{3,2,1,0:T(8,128)S(1)} %get-tuple-element.42._.state, f32[128,128]{1,0:T(8,128)S(1)} %get-tuple-element.45.inverse_ref), custom_call_target="tpu_custom_call" | custom-call | flops 2000000000 | bytes 6000000 | tf_op jit(solution)/shard_map/pallas_call | solution.py:590
  47.2 2.0 %collective-permute-start.17 = (f32[40,128]{1,0:T(8,128)S(1)}, f32[40,128]{1,0:T(8,128)S(1)}, u32[]{:S(2)}, u32[]{:S(2)}) collective-permute-start(f32[40,128]{1,0:T(8,128)S(1)} %add.25), channel_id=1, source_target_pairs={{0,6},{1,7},{2,4},{3,5},{4,2},{5,3},{6,0},{7,1},{8,14},{9,15},{10,... | collective-permute-start | bytes 61448 | tf_op jit(solution)/shard_map/ppermute | solution.py:527
  49.8 0.9 %collective-permute-start.19 = (f32[40,128]{1,0:T(8,128)S(1)}, f32[40,128]{1,0:T(8,128)S(1)}, u32[]{:S(2)}, u32[]{:S(2)}) collective-permute-start(f32[40,128]{1,0:T(8,128)S(1)} %add.25), channel_id=1, source_target_pairs={{0,2},{1,3},{2,0},{3,1},{4,6},{5,7},{6,4},{7,5},{8,10},{9,11},{10,... | collective-permute-start | bytes 61448 | tf_op jit(solution)/shard_map/ppermute | solution.py:527
  50.7 1.2 %collective-permute-done.17 = f32[40,128]{1,0:T(8,128)S(1)} collective-permute-done((f32[40,128]{1,0:T(8,128)S(1)}, f32[40,128]{1,0:T(8,128)S(1)}, u32[]{:S(2)}, u32[]{:S(2)}) %collective-permute-start.17) | collective-permute-done | bytes 20512 | tf_op jit(solution)/shard_map/ppermute | solution.py:527
  51.8 1.1 %collective-permute-done.18 = f32[40,128]{1,0:T(8,128)S(1)} collective-permute-done((f32[40,128]{1,0:T(8,128)S(1)}, f32[40,128]{1,0:T(8,128)S(1)}, u32[]{:S(2)}, u32[]{:S(2)}) %collective-permute-start.18) | collective-permute-done | bytes 20512 | tf_op jit(solution)/shard_map/ppermute | solution.py:527
  53.6 2.5 %collective-permute-start.20 = (f32[40,128]{1,0:T(8,128)S(1)}, f32[40,128]{1,0:T(8,128)S(1)}, u32[]{:S(2)}, u32[]{:S(2)}) collective-permute-start(f32[40,128]{1,0:T(8,128)S(1)} %add_add_fusion.1), channel_id=1, source_target_pairs={{0,24},{8,16},{16,8},{24,0},{1,25},{9,17},{17,9},{25,1},{2,26},{10... | collective-permute-start | bytes 61448 | tf_op jit(solution)/shard_map/ppermute | solution.py:527
  56.1 1.9 %collective-permute-start.22 = (f32[40,128]{1,0:T(8,128)S(1)}, f32[40,128]{1,0:T(8,128)S(1)}, u32[]{:S(2)}, u32[]{:S(2)}) collective-permute-start(f32[40,128]{1,0:T(8,128)S(1)} %add_add_fusion.1), channel_id=1, source_target_pairs={{0,8},{8,0},{16,24},{24,16},{1,9},{9,1},{17,25},{25,17},{2,10},{10... | collective-permute-start | bytes 61448 | tf_op jit(solution)/shard_map/ppermute | solution.py:527
  58.0 1.3 %collective-permute-done.20 = f32[40,128]{1,0:T(8,128)S(1)} collective-permute-done((f32[40,128]{1,0:T(8,128)S(1)}, f32[40,128]{1,0:T(8,128)S(1)}, u32[]{:S(2)}, u32[]{:S(2)}) %collective-permute-start.20) | collective-permute-done | bytes 20512 | tf_op jit(solution)/shard_map/ppermute | solution.py:527
  59.3 1.5 %collective-permute-done.21 = f32[40,128]{1,0:T(8,128)S(1)} collective-permute-done((f32[40,128]{1,0:T(8,128)S(1)}, f32[40,128]{1,0:T(8,128)S(1)}, u32[]{:S(2)}, u32[]{:S(2)}) %collective-permute-start.21) | collective-permute-done | bytes 20512 | tf_op jit(solution)/shard_map/ppermute | solution.py:527
  60.9 1.1 %shard_map.73 = bf16[3,64,32,256]{3,2,1,0:T(8,128)(2,1)S(1)} custom-call(f32[3,32,64,128]{3,2,1,0:T(8,128)S(1)} %get-tuple-element.49.turned), custom_call_target="tpu_custom_call" | custom-call | flops 1000000000 | bytes 3000000 | tf_op jit(solution)/shard_map/pallas_call | solution.py:590
  62.1 5.7 %shard_map.74 = (f32[24,256,128]{2,1,0:T(8,128)}, f32[1,128]{1,0:T(1,128)}) custom-call(s32[2]{0:T(128)S(1)} %pad_add_fusion.par, f32[40,128]{1,0:T(8,128)S(1)} %add_add_fusion.mine_ref, f32[40,128]{1,0:T(8,128)S(1)} %collective-permute-done.23.other_ref, f32[1,128]{1,0:T(1,128)S(1)} %get-tuple-element.48.prior_ref, bf16[24,256,256]{2,1,0:T(8,128)(2,1)S(1)} %bitcast.8), custom_call_target="tpu_custom_call" | custom-call | flops 1000000000 | bytes 3000000 | tf_op jit(solution)/shard_map/pallas_call | solution.py:590
  (40 shorter events, 6.3 us)
Async XLA Ops:
  0.7 8.5 %copy-start = (f32[3,64,32,128]{3,2,1,0:T(8,128)S(1)}, f32[3,64,32,128]{3,2,1,0:T(8,128)}, u32[]{:S(2)}) copy-start(f32[3,64,32,128]{3,2,1,0:T(8,128)} %t_ref.3) | copy-start | bytes 9437188
  2.6 13.4 %collective-permute-start = (f32[13,32,128]{2,1,0:T(8,128)S(1)}, f32[13,32,128]{2,1,0:T(8,128)S(1)}, u32[]{:S(2)}, u32[]{:S(2)}) collective-permute-start(f32[13,32,128]{2,1,0:T(8,128)S(1)} %get-tuple-element.29), channel_id=1, source_target_pairs={{8,16},{16,8},{9,17},{17,9},{10,18},{18,10},{11,19},{19,11},{12,20... | collective-permute-start | bytes 638984 | tf_op jit(solution)/shard_map/ppermute | solution.py:522
  3.3 12.8 %collective-permute-start.1 = (f32[13,32,128]{2,1,0:T(8,128)S(1)}, f32[13,32,128]{2,1,0:T(8,128)S(1)}, u32[]{:S(2)}, u32[]{:S(2)}) collective-permute-start(f32[13,32,128]{2,1,0:T(8,128)S(1)} %get-tuple-element.30), channel_id=1, source_target_pairs={{0,8},{8,0},{16,24},{24,16},{1,9},{9,1},{17,25},{25,17},{2,10},{10... | collective-permute-start | bytes 638984 | tf_op jit(solution)/shard_map/ppermute | solution.py:523
  12.3 7.9 %collective-permute-start.2 = (f32[392,128]{1,0:T(8,128)S(1)}, f32[392,128]{1,0:T(8,128)S(1)}, u32[]{:S(2)}, u32[]{:S(2)}) collective-permute-start(f32[392,128]{1,0:T(8,128)S(1)} %get-tuple-element.34), channel_id=1, source_target_pairs={{0,1},{1,0},{2,3},{3,2},{4,5},{5,4},{6,7},{7,6},{8,9},{9,8},{10,11... | collective-permute-start | bytes 602120 | tf_op jit(solution)/shard_map/ppermute | solution.py:523
  12.4 7.8 %collective-permute-start.3 = (f32[392,128]{1,0:T(8,128)S(1)}, f32[392,128]{1,0:T(8,128)S(1)}, u32[]{:S(2)}, u32[]{:S(2)}) collective-permute-start(f32[392,128]{1,0:T(8,128)S(1)} %get-tuple-element.35), channel_id=1, source_target_pairs={{0,7},{1,2},{2,1},{3,4},{4,3},{5,6},{6,5},{7,0},{8,15},{9,10},{10,... | collective-permute-start | bytes 602120 | tf_op jit(solution)/shard_map/ppermute | solution.py:522
  17.1 3.1 %collective-permute-start.4 = (f32[56,128]{1,0:T(8,128)S(1)}, f32[56,128]{1,0:T(8,128)S(1)}, u32[]{:S(2)}, u32[]{:S(2)}) collective-permute-start(f32[56,128]{1,0:T(8,128)S(1)} %get-tuple-element.36), channel_id=1, source_target_pairs={{0,1},{1,0},{2,3},{3,2},{4,5},{5,4},{6,7},{7,6},{8,9},{9,8},{10,11... | collective-permute-start | bytes 86024 | tf_op jit(solution)/shard_map/ppermute | solution.py:523
  17.2 4.3 %collective-permute-start.5 = (f32[56,128]{1,0:T(8,128)S(1)}, f32[56,128]{1,0:T(8,128)S(1)}, u32[]{:S(2)}, u32[]{:S(2)}) collective-permute-start(f32[56,128]{1,0:T(8,128)S(1)} %get-tuple-element.37), channel_id=1, source_target_pairs={{0,7},{1,2},{2,1},{3,4},{4,3},{5,6},{6,5},{7,0},{8,15},{9,10},{10,... | collective-permute-start | bytes 86024 | tf_op jit(solution)/shard_map/ppermute | solution.py:522
  23.6 1.4 %collective-permute-start.8 = (f32[40,128]{1,0:T(8,128)S(1)}, f32[40,128]{1,0:T(8,128)S(1)}, u32[]{:S(2)}, u32[]{:S(2)}) collective-permute-start(f32[40,128]{1,0:T(8,128)S(1)} %get-tuple-element.44), channel_id=1, source_target_pairs={{0,1},{1,0},{2,3},{3,2},{4,5},{5,4},{6,7},{7,6},{8,9},{9,8},{10,11... | collective-permute-start | bytes 61448 | tf_op jit(solution)/shard_map/ppermute | solution.py:527
  23.7 15.2 %collective-permute-start.6 = (f32[432,128]{1,0:T(8,128)S(1)}, f32[432,128]{1,0:T(8,128)S(1)}, u32[]{:S(2)}, u32[]{:S(2)}) collective-permute-start(f32[432,128]{1,0:T(8,128)S(1)} %get-tuple-element.40), channel_id=1, source_target_pairs={{0,1},{1,0},{2,3},{3,2},{4,5},{5,4},{6,7},{7,6},{8,9},{9,8},{10,11... | collective-permute-start | bytes 663560 | tf_op jit(solution)/shard_map/ppermute | solution.py:523
  24.2 14.7 %collective-permute-start.7 = (f32[432,128]{1,0:T(8,128)S(1)}, f32[432,128]{1,0:T(8,128)S(1)}, u32[]{:S(2)}, u32[]{:S(2)}) collective-permute-start(f32[432,128]{1,0:T(8,128)S(1)} %get-tuple-element.41), channel_id=1, source_target_pairs={{0,7},{1,2},{2,1},{3,4},{4,3},{5,6},{6,5},{7,0},{8,15},{9,10},{10,... | collective-permute-start | bytes 663560 | tf_op jit(solution)/shard_map/ppermute | solution.py:522
  25.0 6.3 %collective-permute-start.10 = (f32[40,128]{1,0:T(8,128)S(1)}, f32[40,128]{1,0:T(8,128)S(1)}, u32[]{:S(2)}, u32[]{:S(2)}) collective-permute-start(f32[40,128]{1,0:T(8,128)S(1)} %add.24.first), channel_id=1, source_target_pairs={{0,16},{8,24},{16,0},{24,8},{1,17},{9,25},{17,1},{25,9},{2,18},{10... | collective-permute-start | bytes 61448 | tf_op jit(solution)/shard_map/ppermute | solution.py:527
  26.4 4.9 %collective-permute-start.11 = (f32[40,128]{1,0:T(8,128)S(1)}, f32[40,128]{1,0:T(8,128)S(1)}, u32[]{:S(2)}, u32[]{:S(2)}) collective-permute-start(f32[40,128]{1,0:T(8,128)S(1)} %add.24.first), channel_id=1, source_target_pairs={{0,8},{8,0},{16,24},{24,16},{1,9},{9,1},{17,25},{25,17},{2,10},{10... | collective-permute-start | bytes 61448 | tf_op jit(solution)/shard_map/ppermute | solution.py:527
  27.0 5.6 %collective-permute-start.9 = (f32[40,128]{1,0:T(8,128)S(1)}, f32[40,128]{1,0:T(8,128)S(1)}, u32[]{:S(2)}, u32[]{:S(2)}) collective-permute-start(f32[40,128]{1,0:T(8,128)S(1)} %add.24.first), channel_id=1, source_target_pairs={{0,24},{8,16},{16,8},{24,0},{1,25},{9,17},{17,9},{25,1},{2,26},{10... | collective-permute-start | bytes 61448 | tf_op jit(solution)/shard_map/ppermute | solution.py:527
  32.6 5.3 %collective-permute-start.12 = (f32[40,128]{1,0:T(8,128)S(1)}, f32[40,128]{1,0:T(8,128)S(1)}, u32[]{:S(2)}, u32[]{:S(2)}) collective-permute-start(f32[40,128]{1,0:T(8,128)S(1)} %shard_map.69.first), channel_id=1, source_target_pairs={{0,6},{1,7},{2,4},{3,5},{4,2},{5,3},{6,0},{7,1},{8,14},{9,15},{10,... | collective-permute-start | bytes 61448 | tf_op jit(solution)/shard_map/ppermute | solution.py:527
  33.6 4.3 %collective-permute-start.13 = (f32[40,128]{1,0:T(8,128)S(1)}, f32[40,128]{1,0:T(8,128)S(1)}, u32[]{:S(2)}, u32[]{:S(2)}) collective-permute-start(f32[40,128]{1,0:T(8,128)S(1)} %shard_map.69.first), channel_id=1, source_target_pairs={{0,4},{1,5},{2,6},{3,7},{4,0},{5,1},{6,2},{7,3},{8,12},{9,13},{10,... | collective-permute-start | bytes 61448 | tf_op jit(solution)/shard_map/ppermute | solution.py:527
  35.0 3.8 %collective-permute-start.14 = (f32[40,128]{1,0:T(8,128)S(1)}, f32[40,128]{1,0:T(8,128)S(1)}, u32[]{:S(2)}, u32[]{:S(2)}) collective-permute-start(f32[40,128]{1,0:T(8,128)S(1)} %shard_map.69.first), channel_id=1, source_target_pairs={{0,2},{1,3},{2,0},{3,1},{4,6},{5,7},{6,4},{7,5},{8,10},{9,11},{10,... | collective-permute-start | bytes 61448 | tf_op jit(solution)/shard_map/ppermute | solution.py:527
  38.8 1.2 %collective-permute-start.15 = (f32[40,128]{1,0:T(8,128)S(1)}, f32[40,128]{1,0:T(8,128)S(1)}, u32[]{:S(2)}, u32[]{:S(2)}) collective-permute-start(f32[40,128]{1,0:T(8,128)S(1)} %shard_map.70.mine_ref), channel_id=1, source_target_pairs={{0,1},{1,0},{2,3},{3,2},{4,5},{5,4},{6,7},{7,6},{8,9},{9,8},{10,11... | collective-permute-start | bytes 61448 | tf_op jit(solution)/shard_map/ppermute | solution.py:527
  45.8 1.4 %collective-permute-start.16 = (f32[40,128]{1,0:T(8,128)S(1)}, f32[40,128]{1,0:T(8,128)S(1)}, u32[]{:S(2)}, u32[]{:S(2)}) collective-permute-start(f32[40,128]{1,0:T(8,128)S(1)} %get-tuple-element.47), channel_id=1, source_target_pairs={{0,1},{1,0},{2,3},{3,2},{4,5},{5,4},{6,7},{7,6},{8,9},{9,8},{10,11... | collective-permute-start | bytes 61448 | tf_op jit(solution)/shard_map/ppermute | solution.py:527
  47.2 4.7 %collective-permute-start.17 = (f32[40,128]{1,0:T(8,128)S(1)}, f32[40,128]{1,0:T(8,128)S(1)}, u32[]{:S(2)}, u32[]{:S(2)}) collective-permute-start(f32[40,128]{1,0:T(8,128)S(1)} %add.25), channel_id=1, source_target_pairs={{0,6},{1,7},{2,4},{3,5},{4,2},{5,3},{6,0},{7,1},{8,14},{9,15},{10,... | collective-permute-start | bytes 61448 | tf_op jit(solution)/shard_map/ppermute | solution.py:527
  49.2 3.8 %collective-permute-start.18 = (f32[40,128]{1,0:T(8,128)S(1)}, f32[40,128]{1,0:T(8,128)S(1)}, u32[]{:S(2)}, u32[]{:S(2)}) collective-permute-start(f32[40,128]{1,0:T(8,128)S(1)} %add.25), channel_id=1, source_target_pairs={{0,4},{1,5},{2,6},{3,7},{4,0},{5,1},{6,2},{7,3},{8,12},{9,13},{10,... | collective-permute-start | bytes 61448 | tf_op jit(solution)/shard_map/ppermute | solution.py:527
  49.8 3.8 %collective-permute-start.19 = (f32[40,128]{1,0:T(8,128)S(1)}, f32[40,128]{1,0:T(8,128)S(1)}, u32[]{:S(2)}, u32[]{:S(2)}) collective-permute-start(f32[40,128]{1,0:T(8,128)S(1)} %add.25), channel_id=1, source_target_pairs={{0,2},{1,3},{2,0},{3,1},{4,6},{5,7},{6,4},{7,5},{8,10},{9,11},{10,... | collective-permute-start | bytes 61448 | tf_op jit(solution)/shard_map/ppermute | solution.py:527
  53.6 5.7 %collective-permute-start.20 = (f32[40,128]{1,0:T(8,128)S(1)}, f32[40,128]{1,0:T(8,128)S(1)}, u32[]{:S(2)}, u32[]{:S(2)}) collective-permute-start(f32[40,128]{1,0:T(8,128)S(1)} %add_add_fusion.1), channel_id=1, source_target_pairs={{0,24},{8,16},{16,8},{24,0},{1,25},{9,17},{17,9},{25,1},{2,26},{10... | collective-permute-start | bytes 61448 | tf_op jit(solution)/shard_map/ppermute | solution.py:527
  56.1 4.7 %collective-permute-start.21 = (f32[40,128]{1,0:T(8,128)S(1)}, f32[40,128]{1,0:T(8,128)S(1)}, u32[]{:S(2)}, u32[]{:S(2)}) collective-permute-start(f32[40,128]{1,0:T(8,128)S(1)} %add_add_fusion.1), channel_id=1, source_target_pairs={{0,16},{8,24},{16,0},{24,8},{1,17},{9,25},{17,1},{25,9},{2,18},{10... | collective-permute-start | bytes 61448 | tf_op jit(solution)/shard_map/ppermute | solution.py:527
  56.1 4.7 %collective-permute-start.22 = (f32[40,128]{1,0:T(8,128)S(1)}, f32[40,128]{1,0:T(8,128)S(1)}, u32[]{:S(2)}, u32[]{:S(2)}) collective-permute-start(f32[40,128]{1,0:T(8,128)S(1)} %add_add_fusion.1), channel_id=1, source_target_pairs={{0,8},{8,0},{16,24},{24,16},{1,9},{9,1},{17,25},{25,17},{2,10},{10... | collective-permute-start | bytes 61448 | tf_op jit(solution)/shard_map/ppermute | solution.py:527
  60.8 1.3 %collective-permute-start.23 = (f32[40,128]{1,0:T(8,128)S(1)}, f32[40,128]{1,0:T(8,128)S(1)}, u32[]{:S(2)}, u32[]{:S(2)}) collective-permute-start(f32[40,128]{1,0:T(8,128)S(1)} %add_add_fusion.mine_ref), channel_id=1, source_target_pairs={{0,1},{1,0},{2,3},{3,2},{4,5},{5,4},{6,7},{7,6},{8,9},{9,8},{10,11... | collective-permute-start | bytes 61448 | tf_op jit(solution)/shard_map/ppermute | solution.py:527

commit v16 on v14

--- a/solution.py
+++ b/solution.py
@@ -20,8 +20,8 @@
 FIELDS = 3
 HALO = STEPS * RENORMS
 SIDE = STEPS
-TILES = 24
-BATCH = 8
+TILES = 32
+BATCH = 4
 GROUP = 8
 VMEM_LIMIT = 16 * 1024 * 1024
 

time: 67.7 us -> 68.8 us (1.016)
  Pallas kernels: 28.9 us -> 29.8 us
    pallas_call x14, Pallas kernels: 28.8 us -> 29.8 us  [call(): pl.pallas_call(kernel, out_shape=outs, in_specs=specs or [SMEM] + [VMEM]...]
where the time goes in v16:
time: 68.8 us; the launch traced here: 68.6 us
  Pallas kernels  29.8 us (43%)
  starting transfers between devices  27.5 us (40%)
  waiting for transfers between devices  10.2 us (15%)
  between operations  1.02 us (1%)
    pallas_call x14, Pallas kernels, call(): pl.pallas_call(kernel, out_shape=outs, in_specs=specs or [SMEM] + [VMEM]...  29.8 us
    ppermute x16, starting transfers between devices, swapped(): lax.ppermute(value, axis, [(i, i ^ mask) for i in range(lax.axis_size(axi...  19.1 us
    ppermute x16, waiting for transfers between devices, swapped(): lax.ppermute(value, axis, [(i, i ^ mask) for i in range(lax.axis_size(axi...  8.9 us
    ppermute x4, starting transfers between devices, swap_pairs(): lax.ppermute(far_value, axis, far)  4.69 us
    ppermute x4, starting transfers between devices, swap_pairs(): lax.ppermute(near_value, axis, near)  3.72 us
  transfers between devices with their start and end apart: 24, of which 11 were waited for; matrix products, arithmetic and copies ran while one was open for 0% of the time, Pallas kernels for 20%

profile of v16, /device:TPU:0, one launch (start us, length us, event | category | flops | bytes accessed | tf_op | source)
XLA Modules:
  0.0 68.6 jit_solution(129820466950737921)
XLA Ops:
  0.7 1.9 %shard_map.60 = (f32[13,32,128]{2,1,0:T(8,128)S(1)}, f32[13,32,128]{2,1,0:T(8,128)S(1)}) custom-call(s32[2]{0:T(128)S(1)} %pad_add_fusion.par, f32[3,64,32,128]{3,2,1,0:T(8,128)} %t_ref.3, s32[32,64]{1,0:T(8,128)} %bitcast.9, s32[32,64]{1,0:T(8,128)} %bitcast.11, f32[32,64]{1,0:T(8,128)} %bitcast.13), custom_call_target="tpu_custom_call" | custom-call | flops 5000000000 | bytes 15000000 | tf_op jit(solution)/shard_map/pallas_call | solution.py:589
  2.6 3.1 %collective-permute-start = (f32[13,32,128]{2,1,0:T(8,128)S(1)}, f32[13,32,128]{2,1,0:T(8,128)S(1)}, u32[]{:S(2)}, u32[]{:S(2)}) collective-permute-start(f32[13,32,128]{2,1,0:T(8,128)S(1)} %get-tuple-element.29), channel_id=1, source_target_pairs={{0,8},{8,0},{16,24},{24,16},{1,9},{9,1},{17,25},{25,17},{2,10},{10... | collective-permute-start | bytes 638984 | tf_op jit(solution)/shard_map/ppermute | solution.py:522
  6.4 3.1 %shard_map.59 = (f32[3,36,72,128]{3,2,1,0:T(8,128)S(1)}, f32[3,36,72,128]{3,2,1,0:T(8,128)S(1)}, f32[72,128]{1,0:T(8,128)S(1)}, f32[392,128]{1,0:T(8,128)S(1)}, f32[392,128]{1,0:T(8,128)S(1)}) custom-call(s32[2]{0:T(128)S(1)} %pad_add_fusion.par, f32[3,64,32,128]{3,2,1,0:T(8,128)S(1)} %copy-done, s32[32,64]{1,0:T(8,128)} %bitcast.10, s32[32,64]{1,0:T(8,128)} %bitcast.12, ...), custom_call_target="tpu_custom_call" | custom-call | flops 3000000000 | bytes 9000000 | tf_op jit(solution)/shard_map/pallas_call | solution.py:589
  9.6 2.5 %collective-permute-start.3 = (f32[392,128]{1,0:T(8,128)S(1)}, f32[392,128]{1,0:T(8,128)S(1)}, u32[]{:S(2)}, u32[]{:S(2)}) collective-permute-start(f32[392,128]{1,0:T(8,128)S(1)} %get-tuple-element.35), channel_id=1, source_target_pairs={{0,7},{1,2},{2,1},{3,4},{4,3},{5,6},{6,5},{7,0},{8,15},{9,10},{10,... | collective-permute-start | bytes 602120 | tf_op jit(solution)/shard_map/ppermute | solution.py:522
  12.1 1.2 %shard_map.61._.refs_0_ = f32[3,36,72,128]{3,2,1,0:T(8,128)S(1)} custom-call(f32[3,36,72,128]{3,2,1,0:T(8,128)S(1)} %get-tuple-element.27.source.state_in, f32[3,36,72,128]{3,2,1,0:T(8,128)S(1)} %get-tuple-element.28.coef_ref.coef_in, f32[72,128]{1,0:T(8,128)S(1)} %get-tuple-element.31.spin_ref), custom_call_target="tpu_custom_call" | custom-call | flops 2000000000 | bytes 6000000 | tf_op jit(solution)/shard_map/pallas_call | solution.py:589
  13.3 1.0 %shard_map.62 = (f32[3,36,72,128]{3,2,1,0:T(8,128)S(1)}, f32[3,36,72,128]{3,2,1,0:T(8,128)S(1)}, f32[56,128]{1,0:T(8,128)S(1)}, f32[56,128]{1,0:T(8,128)S(1)}) custom-call(s32[2]{0:T(128)S(1)} %pad_add_fusion.par, f32[3,36,72,128]{3,2,1,0:T(8,128)S(1)} %get-tuple-element.27.source.state_in, ...), custom_call_target="tpu_custom_call", output_to_operand_aliasing={{0}: (1, {}), {1}: (2, {})} | custom-call | flops 1000000000 | bytes 3000000 | tf_op jit(solution)/shard_map/pallas_call | solution.py:589
  15.7 1.6 %shard_map.64.state_in = f32[3,36,72,128]{3,2,1,0:T(8,128)S(1)} custom-call(f32[3,36,72,128]{3,2,1,0:T(8,128)S(1)} %shard_map.63.source.middle_in, f32[3,36,72,128]{3,2,1,0:T(8,128)S(1)} %get-tuple-element.33.coef_ref.coef_in, f32[72,128]{1,0:T(8,128)S(1)} %get-tuple-element.31.spin_ref), custom_call_target="tpu_custom_call" | custom-call | flops 2000000000 | bytes 6000000 | tf_op jit(solution)/shard_map/pallas_call | solution.py:589
  17.4 1.2 %collective-permute-done.5.d = f32[56,128]{1,0:T(8,128)S(1)} collective-permute-done((f32[56,128]{1,0:T(8,128)S(1)}, f32[56,128]{1,0:T(8,128)S(1)}, u32[]{:S(2)}, u32[]{:S(2)}) %collective-permute-start.5) | collective-permute-done | bytes 28704 | tf_op jit(solution)/shard_map/ppermute | solution.py:522
  18.6 2.2 %shard_map.65 = (f32[3,36,72,128]{3,2,1,0:T(8,128)S(1)}, f32[3,36,72,128]{3,2,1,0:T(8,128)S(1)}, f32[3,36,72,128]{3,2,1,0:T(8,128)S(1)}, f32[3,36,72,128]{3,2,1,...) custom-call(s32[2]{0:T(128)S(1)} %pad_add_fusion.par, ...), custom_call_target="tpu_custom_call", output_to_operand_aliasing={{0}: (1, {}), {1}: (2, {}), {2}: (3, {}), {3}: (4, {})} | custom-call | flops 2000000000 | bytes 6000000 | tf_op jit(solution)/shard_map/pallas_call | solution.py:589
  21.4 0.8 %collective-permute-start.7 = (f32[432,128]{1,0:T(8,128)S(1)}, f32[432,128]{1,0:T(8,128)S(1)}, u32[]{:S(2)}, u32[]{:S(2)}) collective-permute-start(f32[432,128]{1,0:T(8,128)S(1)} %get-tuple-element.41), channel_id=1, source_target_pairs={{0,7},{1,2},{2,1},{3,4},{4,3},{5,6},{6,5},{7,0},{8,15},{9,10},{10,... | collective-permute-start | bytes 663560 | tf_op jit(solution)/shard_map/ppermute | solution.py:522
  22.2 5.3 %collective-permute-start.10 = (f32[40,128]{1,0:T(8,128)S(1)}, f32[40,128]{1,0:T(8,128)S(1)}, u32[]{:S(2)}, u32[]{:S(2)}) collective-permute-start(f32[40,128]{1,0:T(8,128)S(1)} %add.24.first), channel_id=1, source_target_pairs={{0,16},{8,24},{16,0},{24,8},{1,17},{9,25},{17,1},{25,9},{2,18},{10... | collective-permute-start | bytes 61448 | tf_op jit(solution)/shard_map/ppermute | solution.py:526
  27.5 1.5 %collective-permute-start.9 = (f32[40,128]{1,0:T(8,128)S(1)}, f32[40,128]{1,0:T(8,128)S(1)}, u32[]{:S(2)}, u32[]{:S(2)}) collective-permute-start(f32[40,128]{1,0:T(8,128)S(1)} %add.24.first), channel_id=1, source_target_pairs={{0,24},{8,16},{16,8},{24,0},{1,25},{9,17},{17,9},{25,1},{2,26},{10... | collective-permute-start | bytes 61448 | tf_op jit(solution)/shard_map/ppermute | solution.py:526
  29.1 1.8 %shard_map.66.source.middle_in._ = f32[3,36,72,128]{3,2,1,0:T(8,128)S(1)} custom-call(f32[3,36,72,128]{3,2,1,0:T(8,128)S(1)} %get-tuple-element.38.source.start_in, f32[3,36,72,128]{3,2,1,0:T(8,128)S(1)} %get-tuple-element.39.coef_ref, f32[72,128]{1,0:T(8,128)S(1)} %get-tuple-element.31.spin_ref), custom_call_target="tpu_custom_call" | custom-call | flops 2000000000 | bytes 6000000 | tf_op jit(solution)/shard_map/pallas_call | solution.py:589
  31.4 1.7 %collective-permute-done.9.second = f32[40,128]{1,0:T(8,128)S(1)} collective-permute-done((f32[40,128]{1,0:T(8,128)S(1)}, f32[40,128]{1,0:T(8,128)S(1)}, u32[]{:S(2)}, u32[]{:S(2)}) %collective-permute-start.9) | collective-permute-done | bytes 20512 | tf_op jit(solution)/shard_map/ppermute | solution.py:526
  33.9 0.9 %collective-permute-start.13 = (f32[40,128]{1,0:T(8,128)S(1)}, f32[40,128]{1,0:T(8,128)S(1)}, u32[]{:S(2)}, u32[]{:S(2)}) collective-permute-start(f32[40,128]{1,0:T(8,128)S(1)} %shard_map.69.first), channel_id=1, source_target_pairs={{0,4},{1,5},{2,6},{3,7},{4,0},{5,1},{6,2},{7,3},{8,12},{9,13},{10,... | collective-permute-start | bytes 61448 | tf_op jit(solution)/shard_map/ppermute | solution.py:526
  34.7 2.0 %collective-permute-start.14 = (f32[40,128]{1,0:T(8,128)S(1)}, f32[40,128]{1,0:T(8,128)S(1)}, u32[]{:S(2)}, u32[]{:S(2)}) collective-permute-start(f32[40,128]{1,0:T(8,128)S(1)} %shard_map.69.first), channel_id=1, source_target_pairs={{0,2},{1,3},{2,0},{3,1},{4,6},{5,7},{6,4},{7,5},{8,10},{9,11},{10,... | collective-permute-start | bytes 61448 | tf_op jit(solution)/shard_map/ppermute | solution.py:526
  36.7 1.7 %shard_map.67.state_in._ = f32[3,36,72,128]{3,2,1,0:T(8,128)S(1)} custom-call(f32[3,36,72,128]{3,2,1,0:T(8,128)S(1)} %shard_map.66.source.middle_in._, f32[3,36,72,128]{3,2,1,0:T(8,128)S(1)} %get-tuple-element.39.coef_ref, f32[72,128]{1,0:T(8,128)S(1)} %get-tuple-element.31.spin_ref), custom_call_target="tpu_custom_call" | custom-call | flops 2000000000 | bytes 6000000 | tf_op jit(solution)/shard_map/pallas_call | solution.py:589
  38.6 1.3 %shard_map.68 = (f32[3,36,72,128]{3,2,1,0:T(8,128)S(1)}, f32[3,36,72,128]{3,2,1,0:T(8,128)S(1)}, f32[3,36,72,128]{3,2,1,0:T(8,128)S(1)}) custom-call(s32[2]{0:T(128)S(1)} %pad_add_fusion.par, f32[3,36,72,128]{3,2,1,0:T(8,128)S(1)} %get-tuple-element.38.source.start_in, ...), custom_call_target="tpu_custom_call", output_to_operand_aliasing={{0}: (1, {}), {1}: (2, {}), {2}: (3, {})} | custom-call | flops 1000000000 | bytes 3000000 | tf_op jit(solution)/shard_map/pallas_call | solution.py:589
  40.0 3.0 %shard_map.71 = (f32[128,128]{1,0:T(8,128)S(1)}, f32[1,128]{1,0:T(1,128)S(1)}) custom-call(s32[2]{0:T(128)S(1)} %pad_add_fusion.par, f32[40,128]{1,0:T(8,128)S(1)} %shard_map.70.mine_ref, f32[40,128]{1,0:T(8,128)S(1)} %collective-permute-done.15.other_ref, f32[1,128]{1,0:T(1,128)S(1)} %broadcast_in_dim.3.prior_ref, ...), custom_call_target="tpu_custom_call" | custom-call | flops 10000000 | bytes 30000 | tf_op jit(solution)/shard_map/pallas_call | solution.py:589
  43.0 3.1 %shard_map.72 = (f32[3,32,64,128]{3,2,1,0:T(8,128)S(1)}, f32[40,128]{1,0:T(8,128)S(1)}, f32[40,128]{1,0:T(8,128)S(1)}) custom-call(s32[2]{0:T(128)S(1)} %pad_add_fusion.par, f32[3,36,72,128]{3,2,1,0:T(8,128)S(1)} %get-tuple-element.42._.state, f32[128,128]{1,0:T(8,128)S(1)} %get-tuple-element.45.inverse_ref), custom_call_target="tpu_custom_call" | custom-call | flops 2000000000 | bytes 6000000 | tf_op jit(solution)/shard_map/pallas_call | solution.py:589
  46.6 0.8 %collective-permute-done.16 = f32[40,128]{1,0:T(8,128)S(1)} collective-permute-done((f32[40,128]{1,0:T(8,128)S(1)}, f32[40,128]{1,0:T(8,128)S(1)}, u32[]{:S(2)}, u32[]{:S(2)}) %collective-permute-start.16) | collective-permute-done | bytes 20512 | tf_op jit(solution)/shard_map/ppermute | solution.py:526
  47.5 2.0 %collective-permute-start.17 = (f32[40,128]{1,0:T(8,128)S(1)}, f32[40,128]{1,0:T(8,128)S(1)}, u32[]{:S(2)}, u32[]{:S(2)}) collective-permute-start(f32[40,128]{1,0:T(8,128)S(1)} %add.25), channel_id=1, source_target_pairs={{0,6},{1,7},{2,4},{3,5},{4,2},{5,3},{6,0},{7,1},{8,14},{9,15},{10,... | collective-permute-start | bytes 61448 | tf_op jit(solution)/shard_map/ppermute | solution.py:526
  49.5 1.4 %collective-permute-start.18 = (f32[40,128]{1,0:T(8,128)S(1)}, f32[40,128]{1,0:T(8,128)S(1)}, u32[]{:S(2)}, u32[]{:S(2)}) collective-permute-start(f32[40,128]{1,0:T(8,128)S(1)} %add.25), channel_id=1, source_target_pairs={{0,4},{1,5},{2,6},{3,7},{4,0},{5,1},{6,2},{7,3},{8,12},{9,13},{10,... | collective-permute-start | bytes 61448 | tf_op jit(solution)/shard_map/ppermute | solution.py:526
  50.9 1.2 %collective-permute-done.17 = f32[40,128]{1,0:T(8,128)S(1)} collective-permute-done((f32[40,128]{1,0:T(8,128)S(1)}, f32[40,128]{1,0:T(8,128)S(1)}, u32[]{:S(2)}, u32[]{:S(2)}) %collective-permute-start.17) | collective-permute-done | bytes 20512 | tf_op jit(solution)/shard_map/ppermute | solution.py:526
  52.1 1.1 %collective-permute-done.18 = f32[40,128]{1,0:T(8,128)S(1)} collective-permute-done((f32[40,128]{1,0:T(8,128)S(1)}, f32[40,128]{1,0:T(8,128)S(1)}, u32[]{:S(2)}, u32[]{:S(2)}) %collective-permute-start.18) | collective-permute-done | bytes 20512 | tf_op jit(solution)/shard_map/ppermute | solution.py:526
  53.2 1.4 %collective-permute-done.19 = f32[40,128]{1,0:T(8,128)S(1)} collective-permute-done((f32[40,128]{1,0:T(8,128)S(1)}, f32[40,128]{1,0:T(8,128)S(1)}, u32[]{:S(2)}, u32[]{:S(2)}) %collective-permute-start.19) | collective-permute-done | bytes 20512 | tf_op jit(solution)/shard_map/ppermute | solution.py:526
  54.7 1.6 %collective-permute-start.20 = (f32[40,128]{1,0:T(8,128)S(1)}, f32[40,128]{1,0:T(8,128)S(1)}, u32[]{:S(2)}, u32[]{:S(2)}) collective-permute-start(f32[40,128]{1,0:T(8,128)S(1)} %add_add_fusion.1), channel_id=1, source_target_pairs={{0,24},{8,16},{16,8},{24,0},{1,25},{9,17},{17,9},{25,1},{2,26},{10... | collective-permute-start | bytes 61448 | tf_op jit(solution)/shard_map/ppermute | solution.py:526
  56.4 2.7 %collective-permute-start.22 = (f32[40,128]{1,0:T(8,128)S(1)}, f32[40,128]{1,0:T(8,128)S(1)}, u32[]{:S(2)}, u32[]{:S(2)}) collective-permute-start(f32[40,128]{1,0:T(8,128)S(1)} %add_add_fusion.1), channel_id=1, source_target_pairs={{0,8},{8,0},{16,24},{24,16},{1,9},{9,1},{17,25},{25,17},{2,10},{10... | collective-permute-start | bytes 61448 | tf_op jit(solution)/shard_map/ppermute | solution.py:526
  59.1 1.2 %collective-permute-done.20 = f32[40,128]{1,0:T(8,128)S(1)} collective-permute-done((f32[40,128]{1,0:T(8,128)S(1)}, f32[40,128]{1,0:T(8,128)S(1)}, u32[]{:S(2)}, u32[]{:S(2)}) %collective-permute-start.20) | collective-permute-done | bytes 20512 | tf_op jit(solution)/shard_map/ppermute | solution.py:526
  60.3 0.7 %collective-permute-done.21 = f32[40,128]{1,0:T(8,128)S(1)} collective-permute-done((f32[40,128]{1,0:T(8,128)S(1)}, f32[40,128]{1,0:T(8,128)S(1)}, u32[]{:S(2)}, u32[]{:S(2)}) %collective-permute-start.21) | collective-permute-done | bytes 20512 | tf_op jit(solution)/shard_map/ppermute | solution.py:526
  61.2 1.1 %shard_map.73 = bf16[3,64,32,256]{3,2,1,0:T(8,128)(2,1)S(1)} custom-call(f32[3,32,64,128]{3,2,1,0:T(8,128)S(1)} %get-tuple-element.49.turned), custom_call_target="tpu_custom_call" | custom-call | flops 1000000000 | bytes 3000000 | tf_op jit(solution)/shard_map/pallas_call | solution.py:589
  62.4 6.1 %shard_map.74 = (f32[32,192,128]{2,1,0:T(8,128)}, f32[1,128]{1,0:T(1,128)}) custom-call(s32[2]{0:T(128)S(1)} %pad_add_fusion.par, f32[40,128]{1,0:T(8,128)S(1)} %add_add_fusion.mine_ref, f32[40,128]{1,0:T(8,128)S(1)} %collective-permute-done.23.other_ref, f32[1,128]{1,0:T(1,128)S(1)} %get-tuple-element.48.prior_ref, bf16[32,192,256]{2,1,0:T(8,128)(2,1)S(1)} %bitcast.8), custom_call_target="tpu_custom_call" | custom-call | flops 1000000000 | bytes 3000000 | tf_op jit(solution)/shard_map/pallas_call | solution.py:589
  (40 shorter events, 5.2 us)
Async XLA Ops:
  0.7 5.7 %copy-start = (f32[3,64,32,128]{3,2,1,0:T(8,128)S(1)}, f32[3,64,32,128]{3,2,1,0:T(8,128)}, u32[]{:S(2)}) copy-start(f32[3,64,32,128]{3,2,1,0:T(8,128)} %t_ref.3) | copy-start | bytes 9437188
  2.6 10.6 %collective-permute-start = (f32[13,32,128]{2,1,0:T(8,128)S(1)}, f32[13,32,128]{2,1,0:T(8,128)S(1)}, u32[]{:S(2)}, u32[]{:S(2)}) collective-permute-start(f32[13,32,128]{2,1,0:T(8,128)S(1)} %get-tuple-element.29), channel_id=1, source_target_pairs={{0,8},{8,0},{16,24},{24,16},{1,9},{9,1},{17,25},{25,17},{2,10},{10... | collective-permute-start | bytes 638984 | tf_op jit(solution)/shard_map/ppermute | solution.py:522
  5.7 7.6 %collective-permute-start.1 = (f32[13,32,128]{2,1,0:T(8,128)S(1)}, f32[13,32,128]{2,1,0:T(8,128)S(1)}, u32[]{:S(2)}, u32[]{:S(2)}) collective-permute-start(f32[13,32,128]{2,1,0:T(8,128)S(1)} %get-tuple-element.30), channel_id=1, source_target_pairs={{8,16},{16,8},{9,17},{17,9},{10,18},{18,10},{11,19},{19,11},{12,20... | collective-permute-start | bytes 638984 | tf_op jit(solution)/shard_map/ppermute | solution.py:522
  9.5 7.9 %collective-permute-start.2 = (f32[392,128]{1,0:T(8,128)S(1)}, f32[392,128]{1,0:T(8,128)S(1)}, u32[]{:S(2)}, u32[]{:S(2)}) collective-permute-start(f32[392,128]{1,0:T(8,128)S(1)} %get-tuple-element.34), channel_id=1, source_target_pairs={{0,1},{1,0},{2,3},{3,2},{4,5},{5,4},{6,7},{7,6},{8,9},{9,8},{10,11... | collective-permute-start | bytes 602120 | tf_op jit(solution)/shard_map/ppermute | solution.py:522
  9.6 7.8 %collective-permute-start.3 = (f32[392,128]{1,0:T(8,128)S(1)}, f32[392,128]{1,0:T(8,128)S(1)}, u32[]{:S(2)}, u32[]{:S(2)}) collective-permute-start(f32[392,128]{1,0:T(8,128)S(1)} %get-tuple-element.35), channel_id=1, source_target_pairs={{0,7},{1,2},{2,1},{3,4},{4,3},{5,6},{6,5},{7,0},{8,15},{9,10},{10,... | collective-permute-start | bytes 602120 | tf_op jit(solution)/shard_map/ppermute | solution.py:522
  14.3 3.1 %collective-permute-start.4 = (f32[56,128]{1,0:T(8,128)S(1)}, f32[56,128]{1,0:T(8,128)S(1)}, u32[]{:S(2)}, u32[]{:S(2)}) collective-permute-start(f32[56,128]{1,0:T(8,128)S(1)} %get-tuple-element.36), channel_id=1, source_target_pairs={{0,1},{1,0},{2,3},{3,2},{4,5},{5,4},{6,7},{7,6},{8,9},{9,8},{10,11... | collective-permute-start | bytes 86024 | tf_op jit(solution)/shard_map/ppermute | solution.py:522
  14.4 4.3 %collective-permute-start.5 = (f32[56,128]{1,0:T(8,128)S(1)}, f32[56,128]{1,0:T(8,128)S(1)}, u32[]{:S(2)}, u32[]{:S(2)}) collective-permute-start(f32[56,128]{1,0:T(8,128)S(1)} %get-tuple-element.37), channel_id=1, source_target_pairs={{0,7},{1,2},{2,1},{3,4},{4,3},{5,6},{6,5},{7,0},{8,15},{9,10},{10,... | collective-permute-start | bytes 86024 | tf_op jit(solution)/shard_map/ppermute | solution.py:522
  20.8 1.4 %collective-permute-start.8 = (f32[40,128]{1,0:T(8,128)S(1)}, f32[40,128]{1,0:T(8,128)S(1)}, u32[]{:S(2)}, u32[]{:S(2)}) collective-permute-start(f32[40,128]{1,0:T(8,128)S(1)} %get-tuple-element.44), channel_id=1, source_target_pairs={{0,1},{1,0},{2,3},{3,2},{4,5},{5,4},{6,7},{7,6},{8,9},{9,8},{10,11... | collective-permute-start | bytes 61448 | tf_op jit(solution)/shard_map/ppermute | solution.py:526
  20.9 17.7 %collective-permute-start.6 = (f32[432,128]{1,0:T(8,128)S(1)}, f32[432,128]{1,0:T(8,128)S(1)}, u32[]{:S(2)}, u32[]{:S(2)}) collective-permute-start(f32[432,128]{1,0:T(8,128)S(1)} %get-tuple-element.40), channel_id=1, source_target_pairs={{0,1},{1,0},{2,3},{3,2},{4,5},{5,4},{6,7},{7,6},{8,9},{9,8},{10,11... | collective-permute-start | bytes 663560 | tf_op jit(solution)/shard_map/ppermute | solution.py:522
  21.4 17.2 %collective-permute-start.7 = (f32[432,128]{1,0:T(8,128)S(1)}, f32[432,128]{1,0:T(8,128)S(1)}, u32[]{:S(2)}, u32[]{:S(2)}) collective-permute-start(f32[432,128]{1,0:T(8,128)S(1)} %get-tuple-element.41), channel_id=1, source_target_pairs={{0,7},{1,2},{2,1},{3,4},{4,3},{5,6},{6,5},{7,0},{8,15},{9,10},{10,... | collective-permute-start | bytes 663560 | tf_op jit(solution)/shard_map/ppermute | solution.py:522
  22.2 8.7 %collective-permute-start.10 = (f32[40,128]{1,0:T(8,128)S(1)}, f32[40,128]{1,0:T(8,128)S(1)}, u32[]{:S(2)}, u32[]{:S(2)}) collective-permute-start(f32[40,128]{1,0:T(8,128)S(1)} %add.24.first), channel_id=1, source_target_pairs={{0,16},{8,24},{16,0},{24,8},{1,17},{9,25},{17,1},{25,9},{2,18},{10... | collective-permute-start | bytes 61448 | tf_op jit(solution)/shard_map/ppermute | solution.py:526
  27.5 3.9 %collective-permute-start.11 = (f32[40,128]{1,0:T(8,128)S(1)}, f32[40,128]{1,0:T(8,128)S(1)}, u32[]{:S(2)}, u32[]{:S(2)}) collective-permute-start(f32[40,128]{1,0:T(8,128)S(1)} %add.24.first), channel_id=1, source_target_pairs={{0,8},{8,0},{16,24},{24,16},{1,9},{9,1},{17,25},{25,17},{2,10},{10... | collective-permute-start | bytes 61448 | tf_op jit(solution)/shard_map/ppermute | solution.py:526
  27.5 5.6 %collective-permute-start.9 = (f32[40,128]{1,0:T(8,128)S(1)}, f32[40,128]{1,0:T(8,128)S(1)}, u32[]{:S(2)}, u32[]{:S(2)}) collective-permute-start(f32[40,128]{1,0:T(8,128)S(1)} %add.24.first), channel_id=1, source_target_pairs={{0,24},{8,16},{16,8},{24,0},{1,25},{9,17},{17,9},{25,1},{2,26},{10... | collective-permute-start | bytes 61448 | tf_op jit(solution)/shard_map/ppermute | solution.py:526
  33.1 5.3 %collective-permute-start.12 = (f32[40,128]{1,0:T(8,128)S(1)}, f32[40,128]{1,0:T(8,128)S(1)}, u32[]{:S(2)}, u32[]{:S(2)}) collective-permute-start(f32[40,128]{1,0:T(8,128)S(1)} %shard_map.69.first), channel_id=1, source_target_pairs={{0,6},{1,7},{2,4},{3,5},{4,2},{5,3},{6,0},{7,1},{8,14},{9,15},{10,... | collective-permute-start | bytes 61448 | tf_op jit(solution)/shard_map/ppermute | solution.py:526
  33.9 4.6 %collective-permute-start.13 = (f32[40,128]{1,0:T(8,128)S(1)}, f32[40,128]{1,0:T(8,128)S(1)}, u32[]{:S(2)}, u32[]{:S(2)}) collective-permute-start(f32[40,128]{1,0:T(8,128)S(1)} %shard_map.69.first), channel_id=1, source_target_pairs={{0,4},{1,5},{2,6},{3,7},{4,0},{5,1},{6,2},{7,3},{8,12},{9,13},{10,... | collective-permute-start | bytes 61448 | tf_op jit(solution)/shard_map/ppermute | solution.py:526
  34.7 3.8 %collective-permute-start.14 = (f32[40,128]{1,0:T(8,128)S(1)}, f32[40,128]{1,0:T(8,128)S(1)}, u32[]{:S(2)}, u32[]{:S(2)}) collective-permute-start(f32[40,128]{1,0:T(8,128)S(1)} %shard_map.69.first), channel_id=1, source_target_pairs={{0,2},{1,3},{2,0},{3,1},{4,6},{5,7},{6,4},{7,5},{8,10},{9,11},{10,... | collective-permute-start | bytes 61448 | tf_op jit(solution)/shard_map/ppermute | solution.py:526
  38.5 1.4 %collective-permute-start.15 = (f32[40,128]{1,0:T(8,128)S(1)}, f32[40,128]{1,0:T(8,128)S(1)}, u32[]{:S(2)}, u32[]{:S(2)}) collective-permute-start(f32[40,128]{1,0:T(8,128)S(1)} %shard_map.70.mine_ref), channel_id=1, source_target_pairs={{0,1},{1,0},{2,3},{3,2},{4,5},{5,4},{6,7},{7,6},{8,9},{9,8},{10,11... | collective-permute-start | bytes 61448 | tf_op jit(solution)/shard_map/ppermute | solution.py:526
  46.1 1.4 %collective-permute-start.16 = (f32[40,128]{1,0:T(8,128)S(1)}, f32[40,128]{1,0:T(8,128)S(1)}, u32[]{:S(2)}, u32[]{:S(2)}) collective-permute-start(f32[40,128]{1,0:T(8,128)S(1)} %get-tuple-element.47), channel_id=1, source_target_pairs={{0,1},{1,0},{2,3},{3,2},{4,5},{5,4},{6,7},{7,6},{8,9},{9,8},{10,11... | collective-permute-start | bytes 61448 | tf_op jit(solution)/shard_map/ppermute | solution.py:526
  47.5 4.7 %collective-permute-start.17 = (f32[40,128]{1,0:T(8,128)S(1)}, f32[40,128]{1,0:T(8,128)S(1)}, u32[]{:S(2)}, u32[]{:S(2)}) collective-permute-start(f32[40,128]{1,0:T(8,128)S(1)} %add.25), channel_id=1, source_target_pairs={{0,6},{1,7},{2,4},{3,5},{4,2},{5,3},{6,0},{7,1},{8,14},{9,15},{10,... | collective-permute-start | bytes 61448 | tf_op jit(solution)/shard_map/ppermute | solution.py:526
  49.5 3.8 %collective-permute-start.18 = (f32[40,128]{1,0:T(8,128)S(1)}, f32[40,128]{1,0:T(8,128)S(1)}, u32[]{:S(2)}, u32[]{:S(2)}) collective-permute-start(f32[40,128]{1,0:T(8,128)S(1)} %add.25), channel_id=1, source_target_pairs={{0,4},{1,5},{2,6},{3,7},{4,0},{5,1},{6,2},{7,3},{8,12},{9,13},{10,... | collective-permute-start | bytes 61448 | tf_op jit(solution)/shard_map/ppermute | solution.py:526
  50.9 3.8 %collective-permute-start.19 = (f32[40,128]{1,0:T(8,128)S(1)}, f32[40,128]{1,0:T(8,128)S(1)}, u32[]{:S(2)}, u32[]{:S(2)}) collective-permute-start(f32[40,128]{1,0:T(8,128)S(1)} %add.25), channel_id=1, source_target_pairs={{0,2},{1,3},{2,0},{3,1},{4,6},{5,7},{6,4},{7,5},{8,10},{9,11},{10,... | collective-permute-start | bytes 61448 | tf_op jit(solution)/shard_map/ppermute | solution.py:526
  54.7 5.6 %collective-permute-start.20 = (f32[40,128]{1,0:T(8,128)S(1)}, f32[40,128]{1,0:T(8,128)S(1)}, u32[]{:S(2)}, u32[]{:S(2)}) collective-permute-start(f32[40,128]{1,0:T(8,128)S(1)} %add_add_fusion.1), channel_id=1, source_target_pairs={{0,24},{8,16},{16,8},{24,0},{1,25},{9,17},{17,9},{25,1},{2,26},{10... | collective-permute-start | bytes 61448 | tf_op jit(solution)/shard_map/ppermute | solution.py:526
  56.3 4.8 %collective-permute-start.21 = (f32[40,128]{1,0:T(8,128)S(1)}, f32[40,128]{1,0:T(8,128)S(1)}, u32[]{:S(2)}, u32[]{:S(2)}) collective-permute-start(f32[40,128]{1,0:T(8,128)S(1)} %add_add_fusion.1), channel_id=1, source_target_pairs={{0,16},{8,24},{16,0},{24,8},{1,17},{9,25},{17,1},{25,9},{2,18},{10... | collective-permute-start | bytes 61448 | tf_op jit(solution)/shard_map/ppermute | solution.py:526
  56.4 4.7 %collective-permute-start.22 = (f32[40,128]{1,0:T(8,128)S(1)}, f32[40,128]{1,0:T(8,128)S(1)}, u32[]{:S(2)}, u32[]{:S(2)}) collective-permute-start(f32[40,128]{1,0:T(8,128)S(1)} %add_add_fusion.1), channel_id=1, source_target_pairs={{0,8},{8,0},{16,24},{24,16},{1,9},{9,1},{17,25},{25,17},{2,10},{10... | collective-permute-start | bytes 61448 | tf_op jit(solution)/shard_map/ppermute | solution.py:526
  61.1 1.2 %collective-permute-start.23 = (f32[40,128]{1,0:T(8,128)S(1)}, f32[40,128]{1,0:T(8,128)S(1)}, u32[]{:S(2)}, u32[]{:S(2)}) collective-permute-start(f32[40,128]{1,0:T(8,128)S(1)} %add_add_fusion.mine_ref), channel_id=1, source_target_pairs={{0,1},{1,0},{2,3},{3,2},{4,5},{5,4},{6,7},{7,6},{8,9},{9,8},{10,11... | collective-permute-start | bytes 61448 | tf_op jit(solution)/shard_map/ppermute | solution.py:526
